TPU v7x, 32 devices: a whole 2x2x4 slice. The times are simulated.
32 devices in a mesh: ctx: 2 (over x), vocab: 4 (over z), rep: 4 (over y, core).
Axes of the slice: x: 2, y: 2, z: 4, core: 2. Of those that a mesh axis runs over, the one named last changes fastest.
Arguments:
- queries: bfloat16 [8, 512, 8192], P('rep', 'ctx', 'vocab'), may hold values from -10 to 10
- key_value: bfloat16 [2, 8, 512, 512], P(None, 'rep', 'ctx'), may hold values from -10 to 10
- residual: bfloat16 [8, 512, 4096], P('rep', ('ctx', 'vocab')), may hold values from -6 to 6
- out_weight: bfloat16 [8192, 4096], P('vocab', ('ctx', 'rep')), may hold values from -0.5 to 0.5
- moe_gain: float32 [4096], replicated, may hold values from 0.1 to 1.9
- expert_ids: int32 [8, 512, 8], P('rep', ('ctx', 'vocab')), may hold values from 0 to 127, as said below
- route_gate: float32 [8, 512, 8], P('rep', ('ctx', 'vocab')), may hold values from 0.25 to 2.5
- gate_weight: bfloat16 [4, 1536, 4096], P('vocab', 'ctx'), may hold values from -0.09375 to 0.09375
- up_weight: bfloat16 [4, 1536, 4096], P('vocab', 'ctx'), may hold values from -0.09375 to 0.09375
- down_weight: bfloat16 [4, 1536, 4096], P('vocab', 'ctx'), may hold values from -0.15625 to 0.15625
- final_gain: float32 [4096], replicated, may hold values from 0.5 to 1.5
- teacher_head: bfloat16 [1536, 4096], P('vocab'), may hold values from -6 to 6
- learner_hidden: bfloat16 [8, 512, 4096], P('rep', ('ctx', 'vocab')), may hold values from -6 to 6
- learner_head: bfloat16 [1536, 4096], P('vocab', ('ctx', 'rep')), may hold values from -6 to 6
- lengths: int32 [8], P('rep'), may hold values from 128 to 512
Outputs:
- hidden_grad: bfloat16 [8, 512, 4096], P('rep', ('ctx', 'vocab'))
- head_grad: bfloat16 [1536, 4096], P('vocab', ('ctx', 'rep'))
- row_kl: float32 [8, 512], P('rep', ('ctx', 'vocab'))
Inputs may be any that keep to these rules, and one draw needn't show every extreme that they name: `expert_ids`: each token names 8 different experts. In the rows of one device (one index of every axis) every token names exactly one expert below 4, and each expert below 4 is named by exactly 32 of those tokens.
All inputs are finite; a program needn't handle non-finite values.
Results may differ from a plain program's by a relative error of at most 0.017.
Values may be sent and summed in bfloat16 or wider, within the bound.
No kernel may reach another device: no remote copies, remote signals or barrier semaphores. Data moves between devices by JAX's collectives and lax.ppermute only.
A program may use at most 128 MiB of HBM per device.

v0:
```python
import jax
import jax.numpy as jnp
from jax import lax
from jax.sharding import PartitionSpec as P

QH = 64
KVH = 4
HD = 128


EPSILON = 1e-06
MASKED = -1e30


def rms_scale(values, gain):
    mean_square = jnp.mean(values * values, axis=-1, keepdims=True)
    return values * lax.rsqrt(mean_square + EPSILON) * gain


def per_device(
    queries,
    key_value,
    residual,
    out_weight,
    moe_gain,
    expert_ids,
    route_gate,
    gate_weight,
    up_weight,
    down_weight,
    final_gain,
    teacher_head,
    learner_hidden,
    learner_head,
    lengths,
):
    seq_dev, pos_ctx, head_cols = queries.shape
    pos_dev = residual.shape[1]
    width = residual.shape[2]
    vocab_count = lax.axis_size("vocab")
    ctx_index = lax.axis_index("ctx")
    vocab_index = lax.axis_index("vocab")
    heads_dev = head_cols // HD
    shared_head = vocab_index * heads_dev // (QH // KVH)
    key_rows = lax.dynamic_slice_in_dim(key_value, shared_head * HD, HD, 3)
    query_heads = queries.reshape(seq_dev, pos_ctx, heads_dev, HD)
    query_pos = ctx_index * pos_ctx + jnp.arange(pos_ctx)
    score_scale = HD ** (-0.5)
    shard_rows = lax.all_gather(key_rows, "ctx", axis=2, tiled=True)
    running_max = jnp.full((seq_dev, pos_ctx, heads_dev), MASKED, jnp.float32)
    key_pos = jnp.arange(shard_rows.shape[2])
    scores = (
        jnp.einsum("sqhd,skd->sqhk", query_heads, shard_rows[0], preferred_element_type=jnp.float32)
        * score_scale
    )
    allowed = (key_pos[None, None, :] <= query_pos[None, :, None]) & (
        key_pos[None, None, :] < lengths[:, None, None]
    )
    allowed = allowed[:, :, None, :]
    scores = jnp.where(allowed, scores, MASKED)
    new_max = jnp.maximum(running_max, jnp.max(scores, axis=-1))
    exponent = jnp.where(allowed, jnp.exp(scores - new_max[..., None]), 0.0)
    running_sum = jnp.sum(exponent, axis=-1)
    weighted = jnp.einsum(
        "sqhk,skd->sqhd",
        exponent.astype(jnp.bfloat16),
        shard_rows[1],
        preferred_element_type=jnp.float32,
    )
    final_max, final_sum, weighted = (new_max, running_sum, weighted)
    heads_out = (
        (weighted / final_sum[..., None]).astype(jnp.bfloat16).reshape(seq_dev * pos_ctx, head_cols)
    )
    mixed = jnp.dot(
        heads_out,
        lax.all_gather(out_weight, ("ctx", "rep"), axis=1, tiled=True),
        preferred_element_type=jnp.float32,
    )
    attn_rows = lax.psum_scatter(
        mixed.reshape(seq_dev, pos_ctx, width).astype(jnp.bfloat16),
        "vocab",
        scatter_dimension=1,
        tiled=True,
    ).astype(jnp.float32)
    hidden_one = residual.astype(jnp.float32) + attn_rows
    own_count = seq_dev * pos_dev
    normed = rms_scale(hidden_one, moe_gain).astype(jnp.bfloat16).reshape(own_count, width)
    route_ids = expert_ids.reshape(own_count, -1)
    inside = route_ids < vocab_count
    chosen = jnp.sum(jnp.where(inside, route_ids, 0), axis=1)
    route_weight = jnp.sum(jnp.where(inside, route_gate.reshape(own_count, -1), 0.0), axis=1)
    per_expert = own_count // vocab_count
    member = (chosen[:, None] == jnp.arange(vocab_count)[None, :]).astype(jnp.int32)
    slot_rank = jnp.sum((jnp.cumsum(member, axis=0) - 1) * member, axis=1)
    target = chosen * per_expert + slot_rank
    placer = (target[None, :] == jnp.arange(own_count)[:, None]).astype(jnp.bfloat16)
    outgoing = jnp.dot(placer, normed, preferred_element_type=jnp.float32).astype(jnp.bfloat16)
    arrived = lax.all_to_all(
        outgoing.reshape(vocab_count, per_expert, width),
        "vocab",
        split_axis=0,
        concat_axis=0,
        tiled=True,
    )
    arrived = arrived.reshape(own_count, width)
    gate_slice = gate_weight[0]
    up_slice = up_weight[0]
    down_slice = down_weight[0]
    contract_last = (((1,), (1,)), ((), ()))
    shard_rows = lax.all_gather(arrived, "ctx", axis=0, tiled=True)
    gate_pre = lax.dot_general(
        shard_rows, gate_slice, contract_last, preferred_element_type=jnp.float32
    )
    up_pre = lax.dot_general(
        shard_rows, up_slice, contract_last, preferred_element_type=jnp.float32
    )
    activated = (jax.nn.silu(gate_pre) * up_pre).astype(jnp.bfloat16)
    expert_terms = jnp.dot(activated, down_slice, preferred_element_type=jnp.float32)
    expert_out = lax.psum_scatter(
        expert_terms.astype(jnp.bfloat16), "ctx", scatter_dimension=0, tiled=True
    )
    returned_rows = lax.all_to_all(
        expert_out.reshape(vocab_count, per_expert, width),
        "vocab",
        split_axis=0,
        concat_axis=0,
        tiled=True,
    )
    restored = lax.dot_general(
        placer,
        returned_rows.reshape(own_count, width),
        (((0,), (0,)), ((), ())),
        preferred_element_type=jnp.float32,
    )
    hidden_two = hidden_one.reshape(own_count, width) + route_weight[:, None] * restored
    final_rows = (
        rms_scale(hidden_two, final_gain).astype(jnp.bfloat16).reshape(seq_dev, pos_dev, width)
    )
    teacher_rows, learner_rows = (
        lax.all_gather(final_rows, "vocab", axis=1, tiled=True),
        lax.all_gather(learner_hidden, "vocab", axis=1, tiled=True),
    )
    learner_full = lax.all_gather(learner_head, ("ctx", "rep"), axis=1, tiled=True)
    teacher_flat = teacher_rows.reshape(-1, width)
    learner_flat = learner_rows.reshape(-1, width)
    teacher_logits = lax.dot_general(
        teacher_flat, teacher_head, contract_last, preferred_element_type=jnp.float32
    )
    learner_logits = lax.dot_general(
        learner_flat, learner_full, contract_last, preferred_element_type=jnp.float32
    )
    logit_gap = learner_logits - teacher_logits
    learner_peak = jnp.max(learner_logits, axis=1)
    teacher_peak = jnp.max(teacher_logits, axis=1)
    learner_peak, teacher_peak = lax.pmax((learner_peak, teacher_peak), "vocab")
    learner_exp = jnp.exp(learner_logits - learner_peak[:, None])
    learner_total, cross_total, teacher_total = lax.psum(
        (
            jnp.sum(learner_exp, axis=1),
            jnp.sum(learner_exp * logit_gap, axis=1),
            jnp.sum(jnp.exp(teacher_logits - teacher_peak[:, None]), axis=1),
        ),
        "vocab",
    )
    learner_lse = learner_peak + jnp.log(learner_total)
    teacher_lse = teacher_peak + jnp.log(teacher_total)
    mean_gap = cross_total / learner_total
    divergence = mean_gap - learner_lse + teacher_lse
    row_pos = ctx_index * pos_ctx + jnp.arange(pos_ctx)
    live_rows = (row_pos[None, :] < lengths[:, None]).reshape(-1)
    learner_prob = jnp.exp(learner_logits - learner_lse[:, None])
    dlogits = jnp.where(
        live_rows[:, None], learner_prob * (logit_gap - mean_gap[:, None]), 0.0
    ).astype(jnp.bfloat16)
    kl_block = jnp.where(live_rows, divergence, 0.0).reshape(seq_dev, pos_ctx)
    row_kl = lax.dynamic_slice_in_dim(kl_block, vocab_index * pos_dev, pos_dev, 1)
    by_position = jnp.swapaxes(dlogits.reshape(seq_dev, pos_ctx, -1), 0, 1)
    shard_rows = by_position
    grad_rows = lax.psum_scatter(
        jnp.einsum(
            "psv,vd->psd", shard_rows, learner_full, preferred_element_type=jnp.float32
        ).astype(jnp.bfloat16),
        "vocab",
        scatter_dimension=0,
        tiled=True,
    ).astype(jnp.float32)
    hidden_grad = jnp.swapaxes(grad_rows, 0, 1).astype(jnp.bfloat16)
    head_sum = lax.psum_scatter(
        lax.dot_general(
            learner_flat, dlogits, (((0,), (0,)), ((), ())), preferred_element_type=jnp.float32
        ).astype(jnp.bfloat16),
        ("ctx", "rep"),
        scatter_dimension=0,
        tiled=True,
    ).astype(jnp.float32)
    head_grad = jnp.transpose(head_sum).astype(jnp.bfloat16)
    return (hidden_grad, head_grad, row_kl)


def solution(mesh):
    placed = (
        P("rep", "ctx", "vocab"),
        P(None, "rep", "ctx", None),
        P("rep", ("ctx", "vocab"), None),
        P("vocab", ("ctx", "rep")),
        P(),
        P("rep", ("ctx", "vocab"), None),
        P("rep", ("ctx", "vocab"), None),
        P("vocab", "ctx", None),
        P("vocab", "ctx", None),
        P("vocab", "ctx", None),
        P(),
        P("vocab", None),
        P("rep", ("ctx", "vocab"), None),
        P("vocab", ("ctx", "rep")),
        P("rep"),
    )
    return jax.shard_map(
        per_device,
        mesh=mesh,
        in_specs=placed,
        out_specs=(
            P("rep", ("ctx", "vocab"), None),
            P("vocab", ("ctx", "rep")),
            P("rep", ("ctx", "vocab")),
        ),
        check_vma=False,
    )
```

profile of v0, /device:TPU:0, one launch (start us, length us, event | category | flops | bytes accessed | tf_op | source)
XLA Modules:
  0.0 678.5 jit_solution(14526473463836470970)
XLA Ops:
  7.2 0.0 copy-start
  7.2 0.0 all-gather.10.cloned.1.call-start
  7.2 0.7 all-gather.10.cloned.1.call-update
  7.9 0.0 reduce-scatter.5.cloned.1.call-start
  8.0 1.1 constant_dynamic-slice_fusion.1
  9.1 9.9 %all_gather.20 = bf16[2,2,512,128]{3,2,1,0:T(8,128)(2,1)S(1)} all-gather(bf16[2,2,256,128]{3,2,1,0:T(8,128)(2,1)S(1)} %constant_dynamic-slice_fusion.1), channel_id=1, replica_groups=mesh['ctx'=2,'vocab'=4,'rep'=4] {'ctx'}, dimensions={2}, use_global_device_ids=true | all-gather | bytes 786432 | tf_op jit(solution)/shard_map/all_gather | solution.py:49
  19.0 0.7 iota_compare_fusion.5
  19.7 0.1 iota_compare_fusion
  19.8 0.2 broadcast_and_fusion
  20.0 4.3 fusion.2
  24.4 4.0 fusion.3
  28.4 5.3 divide_convert_fusion
  33.7 72.1 %all-gather.10.cloned.1.call-done = bf16[2048,4096]{1,0:T(8,128)(2,1)} async-done(((bf16[2048,512]{1,0:T(8,128)(2,1)}), bf16[2048,4096]{1,0:T(8,128)(2,1)}) %all-gather.10.cloned.1.call-update) | async-done | bytes 16777232 | tf_op jit(solution)/shard_map/all_gather | solution.py:76
  105.7 14.5 %fusion.14 = bf16[2,256,4096]{2,1,0:T(8,128)(2,1)} fusion(bf16[2,256,2048]{1,2,0:T(8,128)(2,1)} %bitcast.103, bf16[2048,4096]{1,0:T(8,128)(2,1)} %all-gather.10.cloned.1.call-done), kind=kOutput, calls=%fused_computation.16 | convolution fusion | flops 8592031744 | bytes 23068672 | tf_op jit(solution)/shard_map/dot_general | solution.py:74
  120.2 0.0 reduce-scatter.5.cloned.1.call-update
  120.3 0.0 all-gather.12.cloned.1.call-start
  120.3 0.6 copy-done.1
  120.9 0.1 reduce_sum.87
  121.0 0.1 fusion.38
  121.1 0.2 reduce_window_sum.11
  121.3 0.2 select_reduce_fusion
  121.5 75.7 %reduce-scatter.5.cloned.1.call-done = bf16[2,64,4096]{2,1,0:T(8,128)(2,1)} async-done(((bf16[2,256,4096]{2,1,0:T(8,128)(2,1)}), bf16[2,64,4096]{2,1,0:T(8,128)(2,1)}) %reduce-scatter.5.cloned.1.call-update) | async-done | bytes 1048592 | tf_op jit(solution)/shard_map/reduce_scatter | solution.py:79
  197.2 2.0 multiply_reduce_fusion.1
  199.2 0.0 copy-done.2
  199.2 3.3 multiply_convert_fusion.1
  202.5 0.4 convolution_convert_fusion.2
  202.9 29.9 %all_to_all.10 = bf16[4,32,4096]{2,1,0:T(8,128)(2,1)} all-to-all(bf16[4,32,4096]{2,1,0:T(8,128)(2,1)S(1)} %bitcast.92), channel_id=1, replica_groups=mesh['ctx'=2,'vocab'=4,'rep'=4] {'vocab'}, dimensions={0} | all-to-all | bytes 2097152 | tf_op jit(solution)/shard_map/all_to_all | solution.py:98
  232.8 0.0 all-gather.12.cloned.1.call-update
  232.8 0.2 reduce-scatter.7.cloned.1.call-start
  233.0 32.1 %all-gather.12.cloned.1.call-done = bf16[256,4096]{1,0:T(8,128)(2,1)} async-done(((bf16[128,4096]{1,0:T(8,128)(2,1)}), bf16[256,4096]{1,0:T(8,128)(2,1)}) %all-gather.12.cloned.1.call-update) | async-done | bytes 2097168 | tf_op jit(solution)/shard_map/all_gather | solution.py:110
  265.1 6.1 fusion.12
  271.3 11.4 %fusion.18 = bf16[256,4096]{1,0:T(8,128)(2,1)} fusion(bf16[1,768,4096]{2,1,0:T(8,128)(2,1)} %param.24, bf16[256,4096]{1,0:T(8,128)(2,1)} %all-gather.12.cloned.1.call-done, bf16[1,768,4096]{2,1,0:T(8,128)(2,1)} %param.23, f32[256,768]{1,0:T(8,128)} %fusion.12), kind=kOutput, calls=%fused_computation.19 | convolution fusion | flops 3223453696 | bytes 17563648 | tf_op jit(solution)/shard_map/dot_general | solution.py:118
  282.6 0.0 reduce-scatter.7.cloned.1.call-update
  282.7 0.0 all-gather.8.cloned.1.call-start
  282.7 0.5 all-gather.8.cloned.1.call-update
  283.2 0.0 copy-start.3
  283.3 0.0 all-gather.6.cloned.1.call-start
  283.3 0.5 all-gather.6.cloned.1.call-update
  283.8 30.8 %reduce-scatter.7.cloned.1.call-done = bf16[128,4096]{1,0:T(8,128)(2,1)} async-done(((bf16[256,4096]{1,0:T(8,128)(2,1)}), bf16[128,4096]{1,0:T(8,128)(2,1)}) %reduce-scatter.7.cloned.1.call-update) | async-done | bytes 1048592 | tf_op jit(solution)/shard_map/reduce_scatter | solution.py:119
  314.7 4.6 all-to-all-start.1
  319.3 0.1 mul.102
  319.4 25.7 %all-to-all-done.1 = bf16[4,32,4096]{2,1,0:T(8,128)(2,1)} async-done(((bf16[4,32,4096]{2,1,0:T(8,128)(2,1)}), bf16[4,32,4096]{2,1,0:T(8,128)(2,1)}, u32[]{:S(2)}, u32[]{:S(2)}) %all-to-all-start.1) | async-done | bytes 1048608 | tf_op jit(solution)/shard_map/all_to_all | solution.py:122
  345.1 2.5 multiply_reduce_fusion
  347.7 1.3 multiply_convert_fusion
  348.9 0.0 all-gather.14.cloned.1.call-update
  348.9 0.0 reduce-scatter.11.cloned.1.call-start
  349.0 0.1 broadcast_compare_fusion
  349.1 0.1 all-gather.8.cloned.1.call-done
  349.2 82.2 %all-gather.6.cloned.1.call-done = bf16[2,256,4096]{2,1,0:T(8,128)(2,1)} async-done(((bf16[2,64,4096]{2,1,0:T(8,128)(2,1)}), bf16[2,256,4096]{2,1,0:T(8,128)(2,1)}) %all-gather.6.cloned.1.call-update) | async-done | bytes 4194320 | tf_op jit(solution)/shard_map/all_gather | solution.py:141
  431.5 6.4 fusion.47
  437.9 75.1 %all-gather.14.cloned.1.call-done = bf16[2,256,4096]{2,1,0:T(8,128)(2,1)} async-done(((bf16[2,64,4096]{2,1,0:T(8,128)(2,1)}), bf16[2,256,4096]{2,1,0:T(8,128)(2,1)}) %all-gather.14.cloned.1.call-update) | async-done | bytes 4194320 | tf_op jit(solution)/shard_map/all_gather | solution.py:140
  512.9 5.4 fusion.48
  518.4 8.9 %all-reduce.1 = (f32[512]{0:T(512)S(1)}, f32[512]{0:T(512)S(1)}) all-reduce(f32[512]{0:T(512)S(1)} %get-tuple-element.17, f32[512]{0:T(512)S(1)} %get-tuple-element.23), channel_id=1, replica_groups=mesh['ctx'=2,'vocab'=4,'rep'=4] {'vocab'}, use_global_device_ids=true, to_apply=%region_1.2 | all-reduce | flops 1024 | bytes 8192 | tf_op jit(solution)/shard_map/pmax | solution.py:155
  527.3 2.6 fusion.34
  529.9 10.1 %all-reduce = (f32[512]{0:T(512)S(1)}, f32[512]{0:T(512)S(1)}, f32[512]{0:T(512)S(1)}) all-reduce(f32[512]{0:T(512)S(1)} %get-tuple-element.4, f32[512]{0:T(512)S(1)} %get-tuple-element.3, f32[512]{0:T(512)S(1)} %get-tuple-element.16), channel_id=1, replica_groups=mesh['ctx'=2,'vocab'=4,'rep'=4] {'vocab'}, use_global_device_ids=true, to_apply=%region_15.16 | all-reduce | flops 1536 | bytes 12288 | tf_op jit(solution)/shard_map/psum | solution.py:157
  540.0 1.6 select_convert_fusion
  541.7 5.7 fusion.17
  547.4 0.0 reduce-scatter.11.cloned.1.call-update
  547.4 0.0 reduce-scatter.9.cloned.1.call-start
  547.4 6.2 convolution_convert_fusion
  553.6 0.0 reduce-scatter.9.cloned.1.call-update
  553.6 0.6 constant_dynamic-slice_fusion
  554.3 37.9 %reduce-scatter.11.cloned.1.call-done = bf16[512,384]{0,1:T(8,128)(2,1)} async-done(((bf16[4096,384]{0,1:T(8,128)(2,1)}), bf16[512,384]{0,1:T(8,128)(2,1)}) %reduce-scatter.11.cloned.1.call-update) | async-done | bytes 393232 | tf_op jit(solution)/shard_map/reduce_scatter | solution.py:188
  592.2 79.7 %reduce-scatter.9.cloned.1.call-done = bf16[64,2,4096]{2,0,1:T(8,128)(2,1)} async-done(((bf16[256,2,4096]{2,0,1:T(8,128)(2,1)}), bf16[64,2,4096]{2,0,1:T(8,128)(2,1)}) %reduce-scatter.9.cloned.1.call-update) | async-done | bytes 1048592 | tf_op jit(solution)/shard_map/reduce_scatter | solution.py:179
  (19 shorter events, 0.1 us)
Async XLA Ops:
  7.2 505.8 %copy-start = (bf16[384,4096]{1,0:T(8,128)(2,1)S(1)}, bf16[384,4096]{1,0:T(8,128)(2,1)}, u32[]{:S(2)}) copy-start(bf16[384,4096]{1,0:T(8,128)(2,1)} %param.26) | copy-start | bytes 9437188
  7.2 98.6 %all-gather.10.cloned.1.call-start = ((), (), s32[]{:S(2)}) async-start(), calls=%async_computation.8 | async-start | bytes 18874368 | tf_op jit(solution)/shard_map/all_gather | solution.py:76
  7.9 189.3 %reduce-scatter.5.cloned.1.call-start = ((), (), s32[]{:S(2)}) async-start(), calls=%async_computation.9 | async-start | bytes 5242880 | tf_op jit(solution)/shard_map/reduce_scatter | solution.py:79
  120.2 0.7 copy-start.1
  120.2 78.9 %copy-start.2 = (f32[4096]{0:T(1024)S(1)}, f32[4096]{0:T(1024)}, u32[]{:S(2)}) copy-start(f32[4096]{0:T(1024)} %param.19) | copy-start | bytes 49156
  120.3 144.9 %all-gather.12.cloned.1.call-start = ((), (), s32[]{:S(2)}) async-start(), calls=%async_computation.10 | async-start | bytes 3145728 | tf_op jit(solution)/shard_map/all_gather | solution.py:110
  232.8 81.9 %reduce-scatter.7.cloned.1.call-start = ((), (), s32[]{:S(2)}) async-start(), calls=%async_computation.11 | async-start | bytes 3145728 | tf_op jit(solution)/shard_map/reduce_scatter | solution.py:119
  282.6 36.6 %copy-start.4 = (f32[2,64,8]{1,2,0:T(8,128)S(1)}, f32[2,64,8]{1,2,0:T(8,128)}, u32[]{:S(2)}) copy-start(f32[2,64,8]{1,2,0:T(8,128)} %param.21) | copy-start | bytes 12292
  282.7 66.6 %all-gather.8.cloned.1.call-start = ((), (), s32[]{:S(2)}) async-start(), calls=%async_computation.7 | async-start | bytes 3538944 | tf_op jit(solution)/shard_map/all_gather | solution.py:143
  283.2 64.4 %copy-start.3 = (f32[4096]{0:T(1024)S(1)}, f32[4096]{0:T(1024)}, u32[]{:S(2)}) copy-start(f32[4096]{0:T(1024)} %param.25) | copy-start | bytes 49156
  283.3 148.2 %all-gather.6.cloned.1.call-start = ((), (), s32[]{:S(2)}) async-start(), calls=%async_computation.6 | async-start | bytes 5242880 | tf_op jit(solution)/shard_map/all_gather | solution.py:141
  314.7 30.4 %all-to-all-start.1 = ((bf16[4,32,4096]{2,1,0:T(8,128)(2,1)}), bf16[4,32,4096]{2,1,0:T(8,128)(2,1)}, u32[]{:S(2)}, u32[]{:S(2)}) async-start(bf16[4,32,4096]{2,1,0:T(8,128)(2,1)} %bitcast.99), calls=%async_computation.3 | async-start | bytes 2097152 | tf_op jit(solution)/shard_map/all_to_all | solution.py:122
  319.3 193.7 %all-gather.14.cloned.1.call-start = ((), (), s32[]{:S(2)}) async-start(), calls=%async_computation.12 | async-start | bytes 5242880 | tf_op jit(solution)/shard_map/all_gather | solution.py:140
  345.1 3.9 copy-start.5
  348.9 243.3 %reduce-scatter.11.cloned.1.call-start = ((), (), s32[]{:S(2)}) async-start(), calls=%async_computation.14 | async-start | bytes 3538944 | tf_op jit(solution)/shard_map/reduce_scatter | solution.py:188
  547.4 124.6 %reduce-scatter.9.cloned.1.call-start = ((), (), s32[]{:S(2)}) async-start(), calls=%async_computation.13 | async-start | bytes 5242880 | tf_op jit(solution)/shard_map/reduce_scatter | solution.py:179
Sparse Core Ops, SparseCore 0:
  9.9 95.8 all-gather.9
  120.4 76.7 reduce-scatter.4
  232.9 32.1 all-gather.11
  282.8 31.8 reduce-scatter.6
  316.4 32.8 all-gather.7
  350.7 80.7 all-gather.5
  433.6 79.2 all-gather.13
  547.5 44.6 reduce-scatter.10
  595.2 76.7 reduce-scatter.8
where the time goes:
time: 679 us; the launch traced here: 678 us
  waiting for transfers between devices  513 us (76%)
  matrix products  68.2 us (10%)
  blocking collectives  58.8 us (9%)
  other arithmetic  16.4 us (2%)
  between operations  14 us (2%)
    all_gather x1, waiting for transfers between devices, per_device(): lax.all_gather(learner_hidden, 'vocab', axis=1, tiled=True)  82.2 us
    reduce_scatter x1, waiting for transfers between devices, per_device(): lax.psum_scatter(jnp.einsum('psv,vd->psd', shard_rows, learner_full, pref...  79.7 us
    reduce_scatter x1, waiting for transfers between devices, per_device(): lax.psum_scatter(mixed.reshape(seq_dev, pos_ctx, width).astype(jnp.bfloat...  75.7 us
    all_gather x1, waiting for transfers between devices, per_device(): lax.all_gather(final_rows, 'vocab', axis=1, tiled=True)  75.1 us
    all_gather x1, waiting for transfers between devices, per_device(): lax.all_gather(out_weight, ('ctx', 'rep'), axis=1, tiled=True)  72.1 us
    reduce_scatter x1, waiting for transfers between devices, per_device(): lax.psum_scatter(lax.dot_general(learner_flat, dlogits, (((0,), (0,)), ((...  37.9 us
    all_gather x1, waiting for transfers between devices, per_device(): shard_rows = lax.all_gather(arrived, 'ctx', axis=0, tiled=True)  32.1 us
    reduce_scatter x1, waiting for transfers between devices, per_device(): lax.psum_scatter(expert_terms.astype(jnp.bfloat16), 'ctx', scatter_dimens...  30.8 us
  transfers between devices with their start and end apart: 10, of which 10 were waited for; matrix products, arithmetic and copies ran while one was open for 5% of the time, Pallas kernels for 0%

commit v1 on v0

v1 whole, which is shorter than its diff:
```python
import jax
import jax.numpy as jnp
from jax import lax
from jax.sharding import PartitionSpec as P

QH = 64
KVH = 4
HD = 128

EPSILON = 1e-06
MASKED = -1e30
PLANE = ("ctx", "rep")
LAST = (((1,), (1,)), ((), ()))
FIRST = (((0,), (0,)), ((), ()))
F32 = jnp.float32
BF16 = jnp.bfloat16


def matmul(left, right, dims=(((1,), (0,)), ((), ()))):
    return lax.dot_general(left, right, dims, preferred_element_type=F32)


def rms_scale(values, gain):
    mean_square = jnp.mean(values * values, axis=-1, keepdims=True)
    return values * lax.rsqrt(mean_square + EPSILON) * gain


def after(value, *earlier):
    return lax.optimization_barrier((value, *earlier))[0]


def plane_index():
    return lax.axis_index("ctx") * lax.axis_size("rep") + lax.axis_index("rep")


def is_square():
    return lax.axis_size("ctx") == 2 and lax.axis_size("rep") == 4


def plane_swap(value, offset):
    ranks = lax.axis_size("ctx") * lax.axis_size("rep")
    return lax.ppermute(value, PLANE, [(i, i ^ offset) for i in range(ranks)])


def plane_gather(own):
    if not is_square():
        gathered = lax.all_gather(own, PLANE, axis=0, tiled=False)
        index = plane_index()
        return [
            lax.dynamic_index_in_dim(gathered, index ^ r, 0, keepdims=False)
            for r in range(gathered.shape[0])
        ]
    core = plane_swap(own, 1)
    along_x = plane_swap(own, 4)
    along_y = plane_swap(own, 2)
    half = own.shape[0] // 2
    corner = jnp.concatenate([plane_swap(along_y[:half], 4), plane_swap(along_x[half:], 2)], axis=0)
    return [
        own,
        core,
        along_y,
        plane_swap(along_y, 1),
        along_x,
        plane_swap(along_x, 1),
        corner,
        plane_swap(corner, 1),
    ]


def plane_exchange(blocks):
    return [blocks[0]] + [plane_swap(blocks[r], r) for r in range(1, len(blocks))]


def pick(value, index, size, axis):
    return lax.dynamic_slice_in_dim(value, index * size, size, axis)


def split_relative(value, index, count, axis):
    size = value.shape[axis] // count
    return [pick(value, index ^ r, size, axis) for r in range(count)]


def join_absolute(blocks, index, axis):
    stacked = jnp.stack(blocks)
    return jnp.concatenate(
        [
            lax.dynamic_index_in_dim(stacked, index ^ j, 0, keepdims=False)
            for j in range(len(blocks))
        ],
        axis=axis,
    )


def line_exchange(value):
    count = lax.axis_size("vocab")
    index = lax.axis_index("vocab")
    blocks = split_relative(value, index, count, 0)
    received = [blocks[0]] + [
        lax.ppermute(blocks[r], "vocab", [(i, i ^ r) for i in range(count)])
        for r in range(1, count)
    ]
    return join_absolute(received, index, 0)


def line_gather(own):
    count = lax.axis_size("vocab")
    index = lax.axis_index("vocab")
    from_left, from_right = [own], [own]
    for _ in range(count - 1):
        from_left.append(
            lax.ppermute(from_left[-1], "vocab", [(i, i + 1) for i in range(count - 1)])
        )
        from_right.append(
            lax.ppermute(from_right[-1], "vocab", [(i + 1, i) for i in range(count - 1)])
        )
    blocks = []
    for j in range(count):
        block = own
        for distance in range(1, count):
            if j + distance < count:
                block = jnp.where(index == j + distance, from_left[distance], block)
            if j - distance >= 0:
                block = jnp.where(index == j - distance, from_right[distance], block)
        blocks.append(block)
    return jnp.stack(blocks)


def line_reduce(partial):
    count = lax.axis_size("vocab")
    index = lax.axis_index("vocab")
    size = partial.shape[0] // count
    to_right = to_left = None
    for step in range(1, count):
        ahead = count - step
        right = pick(partial, jnp.minimum(index + ahead, count - 1), size, 0)
        left = pick(partial, jnp.maximum(index - ahead, 0), size, 0)
        if to_right is not None:
            right = (right.astype(F32) + to_right.astype(F32)).astype(BF16)
            left = (left.astype(F32) + to_left.astype(F32)).astype(BF16)
        to_right = lax.ppermute(right, "vocab", [(i, i + 1) for i in range(min(step, count - 1))])
        to_left = lax.ppermute(
            left, "vocab", [(i, i - 1) for i in range(max(count - step, 1), count)]
        )
    own = pick(partial, index, size, 0).astype(F32)
    return own + to_right.astype(F32) + to_left.astype(F32)


def attend(queries, key_value, lengths):
    seq_dev, pos_ctx, head_cols = queries.shape
    heads_dev = head_cols // HD
    ctx_index = lax.axis_index("ctx")
    shared_head = lax.axis_index("vocab") * heads_dev // (QH // KVH)
    own_rows = lax.dynamic_slice_in_dim(key_value, shared_head * HD, HD, 3)
    query_heads = queries.reshape(seq_dev, pos_ctx, heads_dev, HD)
    query_pos = ctx_index * pos_ctx + jnp.arange(pos_ctx)
    if lax.axis_size("ctx") == 2:
        earlier = lax.ppermute(own_rows, "ctx", [(0, 1)])
        rows = jnp.concatenate([earlier, own_rows], axis=2)
        key_pos = jnp.arange(2 * pos_ctx) + (ctx_index - 1) * pos_ctx
    else:
        rows = lax.all_gather(own_rows, "ctx", axis=2, tiled=True)
        key_pos = jnp.arange(rows.shape[2])
    scores = jnp.einsum("sqhd,skd->sqhk", query_heads, rows[0], preferred_element_type=F32) * HD ** (
        -0.5
    )
    allowed = (
        (key_pos[None, None, :] <= query_pos[None, :, None])
        & (key_pos[None, None, :] < lengths[:, None, None])
        & (key_pos[None, None, :] >= 0)
    )
    allowed = allowed[:, :, None, :]
    scores = jnp.where(allowed, scores, MASKED)
    peak = jnp.max(scores, axis=-1)
    exponent = jnp.where(allowed, jnp.exp(scores - peak[..., None]), 0.0)
    total = jnp.sum(exponent, axis=-1)
    weighted = jnp.einsum(
        "sqhk,skd->sqhd", exponent.astype(BF16), rows[1], preferred_element_type=F32
    )
    return (weighted / total[..., None]).astype(BF16).reshape(seq_dev * pos_ctx, head_cols)


def per_device(
    queries,
    key_value,
    residual,
    out_weight,
    moe_gain,
    expert_ids,
    route_gate,
    gate_weight,
    up_weight,
    down_weight,
    final_gain,
    teacher_head,
    learner_hidden,
    learner_head,
    lengths,
):
    seq_dev, pos_ctx, _ = queries.shape
    pos_dev, width = residual.shape[1:]
    own_count = seq_dev * pos_dev
    vocab_count = lax.axis_size("vocab")
    plane_count = lax.axis_size("ctx") * lax.axis_size("rep")
    ctx_index = lax.axis_index("ctx")
    vocab_index = lax.axis_index("vocab")
    plane = plane_index()
    per_expert = own_count // vocab_count

    route_ids = expert_ids.reshape(own_count, -1)
    inside = route_ids < vocab_count
    chosen = jnp.sum(jnp.where(inside, route_ids, 0), axis=1)
    route_weight = jnp.sum(jnp.where(inside, route_gate.reshape(own_count, -1), 0.0), axis=1)
    member = (chosen[:, None] == jnp.arange(vocab_count)[None, :]).astype(jnp.int32)
    slot_rank = jnp.sum((jnp.cumsum(member, axis=0) - 1) * member, axis=1)
    target = chosen * per_expert + slot_rank
    placed = target[None, :] == jnp.arange(own_count)[:, None]
    placer = placed.astype(BF16)

    line_target = chosen * own_count + vocab_index * per_expert + slot_rank
    line_facts = line_gather(jnp.stack([line_target.astype(F32), route_weight]))
    line_target = line_facts[:, 0].astype(jnp.int32)
    line_weight = line_facts[:, 1]
    line_tokens = (
        jnp.swapaxes(line_target.reshape(vocab_count, seq_dev, pos_dev), 0, 1).reshape(-1)
    )
    line_placer = (line_tokens[None, :] == jnp.arange(seq_dev * pos_ctx)[:, None]).astype(BF16)
    mine = vocab_index * own_count + jnp.arange(own_count)
    my_weight = jnp.sum(
        jnp.where(line_target.reshape(1, -1) == mine[:, None], line_weight.reshape(1, -1), 0.0),
        axis=1,
    )

    residual_rows = line_exchange(
        matmul(placer, residual.reshape(own_count, width)).astype(BF16)
    )

    weight_blocks = plane_gather(out_weight)
    heads_out = attend(queries, key_value, lengths)
    heads_sorted = matmul(line_placer, heads_out).astype(BF16)

    teacher_line = line_gather(pick(teacher_head, plane, width // plane_count, 1))
    learner_line = line_gather(learner_head)

    attn_blocks = [None] * plane_count
    group = 2 if plane_count % 2 == 0 else 1
    order = [0, 2, 1, 3] if plane_count == 8 else range(plane_count // group)
    for start in order:
        members = range(start * group, start * group + group)
        part = jnp.concatenate(
            [matmul(heads_sorted, weight_blocks[r]).astype(BF16) for r in members], axis=1
        )
        for r, piece in zip(members, jnp.split(line_reduce(part), group, axis=1)):
            attn_blocks[r] = piece
    attn_rows = join_absolute(attn_blocks, plane, 1)

    vocab = vocab_count * teacher_head.shape[0]
    teacher_line = after(teacher_line, weight_blocks[-1])
    learner_line = after(learner_line, weight_blocks[-1])
    teacher_blocks = plane_gather(teacher_line.reshape(vocab, -1))
    learner_blocks = plane_gather(learner_line.reshape(vocab, -1))

    learner_rows = matmul(placer, learner_hidden.reshape(own_count, width)).astype(BF16)
    learner_columns = split_relative(learner_rows, plane, plane_count, 1)
    learner_logits = sum(
        matmul(rows, block, LAST) for rows, block in zip(learner_columns, learner_blocks)
    )
    learner_peak = jnp.max(learner_logits, axis=1, keepdims=True)
    learner_exp = jnp.exp(learner_logits - learner_peak)
    learner_total = jnp.sum(learner_exp, axis=1, keepdims=True)
    learner_lse = learner_peak + jnp.log(learner_total)
    plane_columns = jnp.concatenate(plane_exchange(learner_columns), axis=0)

    hidden_one = residual_rows.astype(F32) + attn_rows
    normed = rms_scale(hidden_one, moe_gain).astype(BF16)
    pair = lax.axis_size("ctx") == 2
    if pair:
        other = lax.ppermute(normed, "ctx", [(0, 1), (1, 0)])
        rows = jnp.concatenate([normed, other], axis=0)
    else:
        rows = lax.all_gather(normed, "ctx", axis=0, tiled=True)
    gate_pre = matmul(rows, gate_weight[0], LAST)
    up_pre = matmul(rows, up_weight[0], LAST)
    activated = (jax.nn.silu(gate_pre) * up_pre).astype(BF16)
    if pair:
        theirs = matmul(activated[own_count:], down_weight[0]).astype(BF16)
        theirs = lax.ppermute(theirs, "ctx", [(0, 1), (1, 0)])
        ours = matmul(activated[:own_count], down_weight[0]).astype(BF16)
        expert_out = (ours.astype(F32) + theirs.astype(F32)).astype(BF16)
    else:
        terms = matmul(activated, down_weight[0]).astype(BF16)
        expert_out = lax.psum_scatter(terms, "ctx", scatter_dimension=0, tiled=True)
    hidden_two = hidden_one + my_weight[:, None] * expert_out.astype(F32)
    final_rows = rms_scale(hidden_two, final_gain).astype(BF16)
    teacher_logits = sum(
        matmul(rows, block, LAST)
        for rows, block in zip(split_relative(final_rows, plane, plane_count, 1), teacher_blocks)
    )
    teacher_logits = line_exchange(teacher_logits)

    teacher_peak = jnp.max(teacher_logits, axis=1, keepdims=True)
    teacher_lse = teacher_peak + jnp.log(
        jnp.sum(jnp.exp(teacher_logits - teacher_peak), axis=1, keepdims=True)
    )
    logit_gap = learner_logits - teacher_logits
    mean_gap = jnp.sum(learner_exp * logit_gap, axis=1, keepdims=True) / learner_total
    divergence = mean_gap - learner_lse + teacher_lse
    row_pos = ctx_index * pos_ctx + vocab_index * pos_dev + jnp.arange(pos_dev)
    live = row_pos[None, :] < lengths[:, None]
    live_sorted = jnp.any(placed & live.reshape(1, -1), axis=1)
    kl_rows = jnp.sum(jnp.where(placed, divergence, 0.0), axis=0).reshape(seq_dev, pos_dev)
    row_kl = jnp.where(live, kl_rows, 0.0)
    learner_prob = jnp.exp(learner_logits - learner_lse)
    dlogits = jnp.where(
        live_sorted[:, None], learner_prob * (logit_gap - mean_gap), 0.0
    ).astype(BF16)

    plane_dlogits = jnp.concatenate(plane_gather(dlogits), axis=0)
    head_part = matmul(plane_dlogits, plane_columns, FIRST).astype(BF16)
    head_grad = line_reduce(head_part).astype(BF16)

    restored = matmul(placer, dlogits, FIRST).astype(BF16)
    hidden_grad = join_absolute(
        [matmul(restored, block).astype(BF16) for block in learner_blocks], plane, 1
    ).reshape(seq_dev, pos_dev, width)
    return (hidden_grad, head_grad, row_kl)


def solution(mesh):
    placed = (
        P("rep", "ctx", "vocab"),
        P(None, "rep", "ctx", None),
        P("rep", ("ctx", "vocab"), None),
        P("vocab", ("ctx", "rep")),
        P(),
        P("rep", ("ctx", "vocab"), None),
        P("rep", ("ctx", "vocab"), None),
        P("vocab", "ctx", None),
        P("vocab", "ctx", None),
        P("vocab", "ctx", None),
        P(),
        P("vocab", None),
        P("rep", ("ctx", "vocab"), None),
        P("vocab", ("ctx", "rep")),
        P("rep"),
    )
    return jax.shard_map(
        per_device,
        mesh=mesh,
        in_specs=placed,
        out_specs=(
            P("rep", ("ctx", "vocab"), None),
            P("vocab", ("ctx", "rep")),
            P("rep", ("ctx", "vocab")),
        ),
        check_vma=False,
    )
```

time: 679 us -> 521 us (0.77)
  waiting for transfers between devices: 513 us -> 208 us
  starting transfers between devices: 5.1 us -> 159 us
  blocking collectives: 58.8 us -> 0 us
  local copies, waits for them, and re-layouts: 2.58 us -> 42.1 us
  other arithmetic: 16.4 us -> 36.5 us
  between operations: 14 us -> 3.01 us
    all_gather x5 -> x0, waiting for transfers between devices: 262 us -> none  [the longest x1 82.2 us: per_device(): lax.all_gather(learner_hidden, 'vocab', axis=1, tiled=True)]
    reduce_scatter x4 -> x0, waiting for transfers between devices: 224 us -> none  [the longest x1 79.7 us: per_device(): lax.psum_scatter(jnp.einsum('psv,vd->psd', shard_rows, learner_full, pref...]
    ppermute x0 -> x96, waiting for transfers between devices: none -> 208 us  [the longest x39 87.7 us: plane_swap(): return lax.ppermute(value, PLANE, [(i, i ^ offset) for i in range(ranks)])]
    ppermute x0 -> x96, starting transfers between devices: none -> 159 us  [the longest x15 62.4 us: line_reduce(): lax.ppermute(right, 'vocab', [(i, i + 1) for i in range(min(step, count -...]
    all_to_all x1 -> x0, blocking collectives: 29.9 us -> none  [per_device(): lax.all_to_all(outgoing.reshape(vocab_count, per_expert, width), 'vocab',...]
    all_to_all x1 -> x0, waiting for transfers between devices: 25.7 us -> none  [per_device(): lax.all_to_all(expert_out.reshape(vocab_count, per_expert, width), 'vocab...]
    sub x0 -> x1, other arithmetic: none -> 17.2 us  [attend(): exponent = jnp.where(allowed, jnp.exp(scores - peak[..., None]), 0.0)]
    dynamic_slice x2 -> x13, local copies, waits for them, and re-layouts: 1.73 us -> 17.5 us  [the longest x10 14.7 us: join_absolute(): lax.dynamic_index_in_dim(stacked, index ^ j, 0, keepdims=False)]
  transfers between devices with their start and end apart: 10 -> 96, of which waited for: 10 -> 41; matrix products, arithmetic and copies ran while one was open for 5% -> 27% of each run, Pallas kernels for 0% -> 0%
where the time goes in v1:
time: 521 us; the launch traced here: 516 us
  waiting for transfers between devices  208 us (40%)
  starting transfers between devices  159 us (31%)
  matrix products  67.7 us (13%)
  local copies, waits for them, and re-layouts  42.1 us (8%)
  other arithmetic  36.5 us (7%)
    ppermute x39, waiting for transfers between devices, plane_swap(): return lax.ppermute(value, PLANE, [(i, i ^ offset) for i in range(ranks)])  87.7 us
    ppermute x15, starting transfers between devices, line_reduce(): lax.ppermute(right, 'vocab', [(i, i + 1) for i in range(min(step, count -...  62.4 us
    dot_general x41, matrix products, matmul(): return lax.dot_general(left, right, dims, preferred_element_type=F32)  52.6 us
    ppermute x9, starting transfers between devices, line_gather(): lax.ppermute(from_left[-1], 'vocab', [(i, i + 1) for i in range(count - 1)])  38.4 us
    ppermute x15, waiting for transfers between devices, line_reduce(): lax.ppermute(right, 'vocab', [(i, i + 1) for i in range(min(step, count -...  37.8 us
    ppermute x39, starting transfers between devices, plane_swap(): return lax.ppermute(value, PLANE, [(i, i ^ offset) for i in range(ranks)])  20.3 us
    ppermute x15, waiting for transfers between devices, line_reduce(): lax.ppermute(left, 'vocab', [(i, i - 1) for i in range(max(count - step,...  19.8 us
    ppermute x9, waiting for transfers between devices, line_gather(): lax.ppermute(from_right[-1], 'vocab', [(i + 1, i) for i in range(count -...  17.4 us
  transfers between devices with their start and end apart: 96, of which 41 were waited for; matrix products, arithmetic and copies ran while one was open for 27% of the time, Pallas kernels for 0%

profile of v1, /device:TPU:0, one launch (start us, length us, event | category | flops | bytes accessed | tf_op | source)
XLA Modules:
  0.0 516.3 jit_solution(839222370764169259)
XLA Ops:
  3.6 5.5 %collective-permute-start.22 = (f32[2,128]{1,0:T(2,128)}, f32[2,128]{1,0:T(2,128)}, u32[]{:S(2)}, u32[]{:S(2)}) collective-permute-start(f32[2,128]{1,0:T(2,128)} %pad_maximum_fusion.11), channel_id=1, source_target_pairs={{0,4},{4,8},{8,12},{1,5},{5,9},{9,13},{2,6},{6,10},{10,14},{3,7},{... | collective-permute-start | bytes 3080 | tf_op jit(solution)/shard_map/ppermute | solution.py:111
  12.2 5.3 %collective-permute-start.58 = (bf16[384,512]{1,0:T(8,128)(2,1)}, bf16[384,512]{1,0:T(8,128)(2,1)}, u32[]{:S(2)}, u32[]{:S(2)}) collective-permute-start(bf16[384,512]{1,0:T(8,128)(2,1)} %constant_dynamic-slice_fusion.13), channel_id=1, source_target_pairs={{0,4},{4,8},{8,12},{1,5},{5,9},{9,13},{2,6},{6,10},{10,14},{3,7},{... | collective-permute-start | bytes 1179656 | tf_op jit(solution)/shard_map/ppermute | solution.py:111
  18.5 4.1 collective-permute-start.28
  28.1 2.2 dynamic-slice_bitcast_fusion.4
  31.2 2.2 collective-permute-start.23
  34.9 5.1 collective-permute-start.24
  41.6 4.0 collective-permute-done.27
  54.7 2.0 collective-permute-done.86
  57.4 2.1 collective-permute-done.87
  62.4 9.1 %fusion.34 = f32[2,512,256,16]{2,1,3,0:T(8,128)} fusion(bf16[2,2,256,128]{3,2,1,0:T(8,128)(2,1)} %collective-permute-done.28, bf16[2,2,256,128]{3,2,1,0:T(8,128)(2,1)S(1)} %constant_dynamic-slice_fusion.22, bf16[2,256,2048]{2,1,0:T(8,128)(2,1)S(1)} %copy-done), kind=kOutput, calls=%fused_computation.42 | convolution fusion | flops 1074266112 | bytes 19398656 | tf_op jit(solution)/shard_map/sqhd,skd->sqhk/dot_general | solution.py:163
  71.5 17.2 %fusion.145 = (f32[2,256,16]{1,2,0:T(8,128)S(1)}, bf16[2,256,16,512]{1,3,2,0:T(8,128)(2,1)}) fusion(f32[2,512,256,16]{2,1,3,0:T(8,128)} %fusion.34, pred[2,256,512]{1,2,0:T(8,128)(4,1)S(1)} %copy-done.28), kind=kOutput, calls=%fused_computation.395 | output fusion | flops 33554944 | bytes 25460736 | tf_op jit(solution)/shard_map/sub | solution.py:174
  88.8 6.1 %divide_convert_fusion = bf16[2,256,16,128]{3,1,2,0:T(8,128)(2,1)S(1)} fusion(bf16[2,256,16,512]{1,3,2,0:T(8,128)(2,1)} %get-tuple-element.100, f32[2,256,16]{1,2,0:T(8,128)S(1)} %get-tuple-element.99, bf16[2,2,256,128]{3,2,1,0:T(8,128)(2,1)S(1)} %constant_dynamic-slice_fusion.22, bf16[2,2,256,128]{3,2,1,0:T(8,128)(2,1)} %collective-permute-done.28), kind=kOutput, calls=%fused_computation.22 | convolution fusion | flops 1076363264 | bytes 11042816 | tf_op jit(solution)/shard_map/sqhk,skd->sqhd/dot_general | solution.py:176
  96.3 4.6 collective-permute-start
  102.2 4.6 collective-permute-start.59
  106.9 2.2 collective-permute-done.61
  112.0 5.6 %collective-permute-done.3 = bf16[384,512]{1,0:T(8,128)(2,1)S(1)} collective-permute-done((bf16[384,512]{1,0:T(8,128)(2,1)S(1)}, bf16[384,512]{1,0:T(8,128)(2,1)S(1)}, u32[]{:S(2)}, u32[]{:S(2)}) %collective-permute-start.3) | collective-permute-done | bytes 393248 | tf_op jit(solution)/shard_map/ppermute | solution.py:114
  117.6 2.6 collective-permute-start.1
  126.3 4.2 collective-permute-start.2
  135.9 4.4 collective-permute-start.60
  140.3 2.7 collective-permute-done.5
  144.5 2.9 convolution_convert_fusion.11
  147.5 4.6 collective-permute-start.30
  156.1 4.4 collective-permute-start.31
  165.5 8.4 %collective-permute-done.8 = bf16[2048,512]{1,0:T(8,128)(2,1)S(1)} collective-permute-done((bf16[2048,512]{1,0:T(8,128)(2,1)S(1)}, bf16[2048,512]{1,0:T(8,128)(2,1)S(1)}, u32[]{:S(2)}, u32[]{:S(2)}) %collective-permute-start.8) | collective-permute-done | bytes 2097184 | tf_op jit(solution)/shard_map/ppermute | solution.py:42
  178.4 8.0 %collective-permute-done.35 = bf16[128,1024]{0,1:T(8,128)(2,1)S(1)} collective-permute-done((bf16[128,1024]{0,1:T(8,128)(2,1)S(1)}, bf16[128,1024]{0,1:T(8,128)(2,1)S(1)}, u32[]{:S(2)}, u32[]{:S(2)}) %collective-permute-start.35) | collective-permute-done | bytes 262176 | tf_op jit(solution)/shard_map/ppermute | solution.py:141
  186.4 2.2 collective-permute-start.32
  189.9 3.7 collective-permute-done.32
  195.4 4.4 collective-permute-start.37
  203.9 2.5 collective-permute-done.37
  206.5 4.4 collective-permute-start.38
  212.2 4.4 collective-permute-start.45
  220.9 1.9 collective-permute-done.45
  222.8 4.4 collective-permute-start.39
  228.7 4.7 collective-permute-start.46
  234.8 3.9 collective-permute-start.50
  239.5 4.3 collective-permute-done.50
  244.0 4.4 collective-permute-start.51
  249.4 3.0 collective-permute-done.51
  253.9 8.4 %collective-permute-start.52 = (bf16[128,1024]{0,1:T(8,128)(2,1)S(1)}, bf16[128,1024]{0,1:T(8,128)(2,1)S(1)}, u32[]{:S(2)}, u32[]{:S(2)}) collective-permute-start(bf16[128,1024]{0,1:T(8,128)(2,1)S(1)} %get-tuple-element.61), channel_id=1, source_target_pairs={{0,4},{4,8},{8,12},{1,5},{5,9},{9,13},{2,6},{6,10},{10,14},{3,7},{... | collective-permute-start | bytes 786440 | tf_op jit(solution)/shard_map/ppermute | solution.py:140
  288.4 11.6 %collective-permute-done.65 = bf16[1536,512]{1,0:T(8,128)(2,1)} collective-permute-done((bf16[1536,512]{1,0:T(8,128)(2,1)}, bf16[1536,512]{1,0:T(8,128)(2,1)}, u32[]{:S(2)}, u32[]{:S(2)}) %collective-permute-start.65) | collective-permute-done | bytes 1572896 | tf_op jit(solution)/shard_map/ppermute | solution.py:42
  307.7 23.2 %collective-permute-done.12 = bf16[1536,512]{1,0:T(8,128)(2,1)} collective-permute-done((bf16[1536,512]{1,0:T(8,128)(2,1)}, bf16[1536,512]{1,0:T(8,128)(2,1)}, u32[]{:S(2)}, u32[]{:S(2)}) %collective-permute-start.12) | collective-permute-done | bytes 1572896 | tf_op jit(solution)/shard_map/ppermute | solution.py:42
  332.5 3.3 collective-permute-done.14
  338.2 2.1 convolution_add_fusion.7
  340.3 2.1 convolution_add_fusion.6
  342.4 15.8 %collective-permute-done.56 = bf16[128,4096]{1,0:T(8,128)(2,1)S(1)} collective-permute-done((bf16[128,4096]{1,0:T(8,128)(2,1)S(1)}, bf16[128,4096]{1,0:T(8,128)(2,1)S(1)}, u32[]{:S(2)}, u32[]{:S(2)}) %collective-permute-start.56) | collective-permute-done | bytes 1048608 | tf_op jit(solution)/shard_map/ppermute | solution.py:277
  360.1 5.0 multiply_convert_fusion.2
  367.7 7.4 %collective-permute-done.69 = bf16[768,512]{1,0:T(8,128)(2,1)S(1)} collective-permute-done((bf16[768,512]{1,0:T(8,128)(2,1)S(1)}, bf16[768,512]{1,0:T(8,128)(2,1)S(1)}, u32[]{:S(2)}, u32[]{:S(2)}) %collective-permute-start.69) | collective-permute-done | bytes 786464 | tf_op jit(solution)/shard_map/ppermute | solution.py:42
  375.1 16.8 %collective-permute-done.16 = bf16[768,512]{1,0:T(8,128)(2,1)S(1)} collective-permute-done((bf16[768,512]{1,0:T(8,128)(2,1)S(1)}, bf16[768,512]{1,0:T(8,128)(2,1)S(1)}, u32[]{:S(2)}, u32[]{:S(2)}) %collective-permute-start.16) | collective-permute-done | bytes 786464 | tf_op jit(solution)/shard_map/ppermute | solution.py:42
  394.5 14.0 %collective-permute-done.57 = bf16[128,4096]{1,0:T(8,128)(2,1)S(1)} collective-permute-done((bf16[128,4096]{1,0:T(8,128)(2,1)S(1)}, bf16[128,4096]{1,0:T(8,128)(2,1)S(1)}, u32[]{:S(2)}, u32[]{:S(2)}) %collective-permute-start.57) | collective-permute-done | bytes 1048608 | tf_op jit(solution)/shard_map/ppermute | solution.py:286
  408.5 2.0 multiply_reduce_fusion
  412.6 2.1 convolution_add_fusion.3
  415.3 2.1 convolution_add_fusion.2
  417.4 2.1 fusion.110
  429.8 2.4 collective-permute-done.74
  432.2 11.4 %collective-permute-done.73 = f32[32,1536]{1,0:T(8,128)S(1)} collective-permute-done((f32[32,1536]{1,0:T(8,128)S(1)}, f32[32,1536]{1,0:T(8,128)S(1)}, u32[]{:S(2)}, u32[]{:S(2)}) %collective-permute-start.73) | collective-permute-done | bytes 196640 | tf_op jit(solution)/shard_map/ppermute | solution.py:99
  450.3 1.9 fusion.42
  453.0 4.6 collective-permute-done.76
  460.3 3.9 collective-permute-done.80
  471.8 7.3 %collective-permute-done.90 = bf16[384,512]{1,0:T(8,128)(2,1)S(1)} collective-permute-done((bf16[384,512]{1,0:T(8,128)(2,1)S(1)}, bf16[384,512]{1,0:T(8,128)(2,1)S(1)}, u32[]{:S(2)}, u32[]{:S(2)}) %collective-permute-start.90) | collective-permute-done | bytes 393248 | tf_op jit(solution)/shard_map/ppermute | solution.py:140
  479.2 4.4 collective-permute-start.91
  484.2 7.6 %collective-permute-done.91 = bf16[384,512]{1,0:T(8,128)(2,1)S(1)} collective-permute-done((bf16[384,512]{1,0:T(8,128)(2,1)S(1)}, bf16[384,512]{1,0:T(8,128)(2,1)S(1)}, u32[]{:S(2)}, u32[]{:S(2)}) %collective-permute-start.91) | collective-permute-done | bytes 393248 | tf_op jit(solution)/shard_map/ppermute | solution.py:140
  492.8 5.1 collective-permute-start.92
  499.4 5.7 %collective-permute-done.92 = bf16[384,512]{1,0:T(8,128)(2,1)S(1)} collective-permute-done((bf16[384,512]{1,0:T(8,128)(2,1)S(1)}, bf16[384,512]{1,0:T(8,128)(2,1)S(1)}, u32[]{:S(2)}, u32[]{:S(2)}) %collective-permute-start.92) | collective-permute-done | bytes 393248 | tf_op jit(solution)/shard_map/ppermute | solution.py:140
  505.1 10.1 %collective-permute-done.95 = bf16[384,512]{1,0:T(8,128)(2,1)S(1)} collective-permute-done((bf16[384,512]{1,0:T(8,128)(2,1)S(1)}, bf16[384,512]{1,0:T(8,128)(2,1)S(1)}, u32[]{:S(2)}, u32[]{:S(2)}) %collective-permute-start.95) | collective-permute-done | bytes 393248 | tf_op jit(solution)/shard_map/ppermute | solution.py:141
  (403 shorter events, 158.7 us)
Async XLA Ops:
  3.6 27.6 %collective-permute-start.22 = (f32[2,128]{1,0:T(2,128)}, f32[2,128]{1,0:T(2,128)}, u32[]{:S(2)}, u32[]{:S(2)}) collective-permute-start(f32[2,128]{1,0:T(2,128)} %pad_maximum_fusion.11), channel_id=1, source_target_pairs={{0,4},{4,8},{8,12},{1,5},{5,9},{9,13},{2,6},{6,10},{10,14},{3,7},{... | collective-permute-start | bytes 3080 | tf_op jit(solution)/shard_map/ppermute | solution.py:111
  9.1 24.3 %collective-permute-start.25 = (f32[2,128]{1,0:T(2,128)}, f32[2,128]{1,0:T(2,128)}, u32[]{:S(2)}, u32[]{:S(2)}) collective-permute-start(f32[2,128]{1,0:T(2,128)} %pad_maximum_fusion.11), channel_id=1, source_target_pairs={{4,0},{8,4},{12,8},{5,1},{9,5},{13,9},{6,2},{10,6},{14,10},{7,3},{... | collective-permute-start | bytes 3080 | tf_op jit(solution)/shard_map/ppermute | solution.py:114
  12.2 90.0 %collective-permute-start.58 = (bf16[384,512]{1,0:T(8,128)(2,1)}, bf16[384,512]{1,0:T(8,128)(2,1)}, u32[]{:S(2)}, u32[]{:S(2)}) collective-permute-start(bf16[384,512]{1,0:T(8,128)(2,1)} %constant_dynamic-slice_fusion.13), channel_id=1, source_target_pairs={{0,4},{4,8},{8,12},{1,5},{5,9},{9,13},{2,6},{6,10},{10,14},{3,7},{... | collective-permute-start | bytes 1179656 | tf_op jit(solution)/shard_map/ppermute | solution.py:111
  18.5 42.7 %collective-permute-start.28 = (bf16[2,2,256,128]{3,2,1,0:T(8,128)(2,1)S(1)}, bf16[2,2,256,128]{3,2,1,0:T(8,128)(2,1)}, u32[]{:S(2)}, u32[]{:S(2)}) collective-permute-start(bf16[2,2,256,128]{3,2,1,0:T(8,128)(2,1)S(1)} %constant_dynamic-slice_fusion.22), channel_id=1, source_target_pairs={{0,16},{1,17},{2,18},{3,19},{4,20},{5,21},{6,22},{7,23},{8,24},{9,... | collective-permute-start | bytes 786440 | tf_op jit(solution)/shard_map/ppermute | solution.py:157
  22.6 121.9 %collective-permute-start.29 = (bf16[2048,512]{1,0:T(8,128)(2,1)}, bf16[2048,512]{1,0:T(8,128)(2,1)}, u32[]{:S(2)}, u32[]{:S(2)}) collective-permute-start(bf16[2048,512]{1,0:T(8,128)(2,1)} %param.18), channel_id=1, source_target_pairs={{0,1},{1,0},{2,3},{3,2},{16,17},{17,16},{18,19},{19,18},{4,5},{5,4... | collective-permute-start | bytes 6291464 | tf_op jit(solution)/shard_map/ppermute | solution.py:42
  56.7 38.1 %collective-permute-start.21 = (bf16[32,4096]{1,0:T(8,128)(2,1)}, bf16[32,4096]{1,0:T(8,128)(2,1)S(1)}, u32[]{:S(2)}, u32[]{:S(2)}) collective-permute-start(bf16[32,4096]{1,0:T(8,128)(2,1)} %get-tuple-element.58), channel_id=1, source_target_pairs={{0,12},{4,8},{8,4},{12,0},{1,13},{5,9},{9,5},{13,1},{2,14},{6,10},... | collective-permute-start | bytes 786440 | tf_op jit(solution)/shard_map/ppermute | solution.py:99
  59.5 36.8 %collective-permute-start.20 = (bf16[32,4096]{1,0:T(8,128)(2,1)}, bf16[32,4096]{1,0:T(8,128)(2,1)S(1)}, u32[]{:S(2)}, u32[]{:S(2)}) collective-permute-start(bf16[32,4096]{1,0:T(8,128)(2,1)} %get-tuple-element.59), channel_id=1, source_target_pairs={{0,8},{4,12},{8,0},{12,4},{1,9},{5,13},{9,1},{13,5},{2,10},{6,14},... | collective-permute-start | bytes 786440 | tf_op jit(solution)/shard_map/ppermute | solution.py:99
  61.1 39.8 %collective-permute-start.19 = (bf16[32,4096]{1,0:T(8,128)(2,1)}, bf16[32,4096]{1,0:T(8,128)(2,1)S(1)}, u32[]{:S(2)}, u32[]{:S(2)}) collective-permute-start(bf16[32,4096]{1,0:T(8,128)(2,1)} %get-tuple-element.60), channel_id=1, source_target_pairs={{0,4},{4,0},{8,12},{12,8},{1,5},{5,1},{9,13},{13,9},{2,6},{6,2},{1... | collective-permute-start | bytes 786440 | tf_op jit(solution)/shard_map/ppermute | solution.py:99
  94.9 14.3 %collective-permute-start.61 = (bf16[384,512]{1,0:T(8,128)(2,1)}, bf16[384,512]{1,0:T(8,128)(2,1)S(1)}, u32[]{:S(2)}, u32[]{:S(2)}) collective-permute-start(bf16[384,512]{1,0:T(8,128)(2,1)} %constant_dynamic-slice_fusion.13), channel_id=1, source_target_pairs={{4,0},{8,4},{12,8},{5,1},{9,5},{13,9},{6,2},{10,6},{14,10},{7,3},{... | collective-permute-start | bytes 1179656 | tf_op jit(solution)/shard_map/ppermute | solution.py:114
  96.3 14.4 %collective-permute-start = (bf16[384,512]{1,0:T(8,128)(2,1)S(1)}, bf16[384,512]{1,0:T(8,128)(2,1)S(1)}, u32[]{:S(2)}, u32[]{:S(2)}) collective-permute-start(bf16[384,512]{1,0:T(8,128)(2,1)S(1)} %copy-done.27), channel_id=1, source_target_pairs={{0,4},{4,8},{8,12},{1,5},{5,9},{9,13},{2,6},{6,10},{10,14},{3,7},{... | collective-permute-start | bytes 1179656 | tf_op jit(solution)/shard_map/ppermute | solution.py:111
  100.9 16.7 %collective-permute-start.3 = (bf16[384,512]{1,0:T(8,128)(2,1)S(1)}, bf16[384,512]{1,0:T(8,128)(2,1)S(1)}, u32[]{:S(2)}, u32[]{:S(2)}) collective-permute-start(bf16[384,512]{1,0:T(8,128)(2,1)S(1)} %copy-done.27), channel_id=1, source_target_pairs={{4,0},{8,4},{12,8},{5,1},{9,5},{13,9},{6,2},{10,6},{14,10},{7,3},{... | collective-permute-start | bytes 1179656 | tf_op jit(solution)/shard_map/ppermute | solution.py:114
  102.2 18.0 %collective-permute-start.59 = (bf16[384,512]{1,0:T(8,128)(2,1)}, bf16[384,512]{1,0:T(8,128)(2,1)S(1)}, u32[]{:S(2)}, u32[]{:S(2)}) collective-permute-start(bf16[384,512]{1,0:T(8,128)(2,1)} %collective-permute-done.58), channel_id=1, source_target_pairs={{0,4},{4,8},{8,12},{1,5},{5,9},{9,13},{2,6},{6,10},{10,14},{3,7},{... | collective-permute-start | bytes 1179656 | tf_op jit(solution)/shard_map/ppermute | solution.py:111
  109.2 45.9 %collective-permute-start.6 = (bf16[2048,512]{1,0:T(8,128)(2,1)S(1)}, bf16[2048,512]{1,0:T(8,128)(2,1)S(1)}, u32[]{:S(2)}, u32[]{:S(2)}) collective-permute-start(bf16[2048,512]{1,0:T(8,128)(2,1)S(1)} %copy-done.39), channel_id=1, source_target_pairs={{0,2},{1,3},{2,0},{3,1},{16,18},{17,19},{18,16},{19,17},{4,6},{5,7... | collective-permute-start | bytes 6291464 | tf_op jit(solution)/shard_map/ppermute | solution.py:42
  110.7 15.2 %collective-permute-start.62 = (bf16[384,512]{1,0:T(8,128)(2,1)S(1)}, bf16[384,512]{1,0:T(8,128)(2,1)S(1)}, u32[]{:S(2)}, u32[]{:S(2)}) collective-permute-start(bf16[384,512]{1,0:T(8,128)(2,1)S(1)} %collective-permute-done.61), channel_id=1, source_target_pairs={{4,0},{8,4},{12,8},{5,1},{9,5},{13,9},{6,2},{10,6},{14,10},{7,3},{... | collective-permute-start | bytes 1179656 | tf_op jit(solution)/shard_map/ppermute | solution.py:114
  120.2 11.9 %collective-permute-start.4 = (bf16[384,512]{1,0:T(8,128)(2,1)S(1)}, bf16[384,512]{1,0:T(8,128)(2,1)S(1)}, u32[]{:S(2)}, u32[]{:S(2)}) collective-permute-start(bf16[384,512]{1,0:T(8,128)(2,1)S(1)} %collective-permute-done.3), channel_id=1, source_target_pairs={{4,0},{8,4},{12,8},{5,1},{9,5},{13,9},{6,2},{10,6},{14,10},{7,3},{... | collective-permute-start | bytes 1179656 | tf_op jit(solution)/shard_map/ppermute | solution.py:114
  125.9 48.1 %collective-permute-start.8 = (bf16[2048,512]{1,0:T(8,128)(2,1)S(1)}, bf16[2048,512]{1,0:T(8,128)(2,1)S(1)}, u32[]{:S(2)}, u32[]{:S(2)}) collective-permute-start(bf16[2048,512]{1,0:T(8,128)(2,1)S(1)} %copy-done.39), channel_id=1, source_target_pairs={{0,16},{1,17},{2,18},{3,19},{16,0},{17,1},{18,2},{19,3},{4,20},{5,... | collective-permute-start | bytes 6291464 | tf_op jit(solution)/shard_map/ppermute | solution.py:42
  132.1 10.9 %collective-permute-start.5 = (bf16[384,512]{1,0:T(8,128)(2,1)S(1)}, bf16[384,512]{1,0:T(8,128)(2,1)S(1)}, u32[]{:S(2)}, u32[]{:S(2)}) collective-permute-start(bf16[384,512]{1,0:T(8,128)(2,1)S(1)} %collective-permute-done.4), channel_id=1, source_target_pairs={{4,0},{8,4},{12,8},{5,1},{9,5},{13,9},{6,2},{10,6},{14,10},{7,3},{... | collective-permute-start | bytes 1179656 | tf_op jit(solution)/shard_map/ppermute | solution.py:114
  135.9 16.1 %collective-permute-start.60 = (bf16[384,512]{1,0:T(8,128)(2,1)S(1)}, bf16[384,512]{1,0:T(8,128)(2,1)S(1)}, u32[]{:S(2)}, u32[]{:S(2)}) collective-permute-start(bf16[384,512]{1,0:T(8,128)(2,1)S(1)} %collective-permute-done.59), channel_id=1, source_target_pairs={{0,4},{4,8},{8,12},{1,5},{5,9},{9,13},{2,6},{6,10},{10,14},{3,7},{... | collective-permute-start | bytes 1179656 | tf_op jit(solution)/shard_map/ppermute | solution.py:111
  143.0 10.4 %collective-permute-start.63 = (bf16[384,512]{1,0:T(8,128)(2,1)S(1)}, bf16[384,512]{1,0:T(8,128)(2,1)S(1)}, u32[]{:S(2)}, u32[]{:S(2)}) collective-permute-start(bf16[384,512]{1,0:T(8,128)(2,1)S(1)} %collective-permute-done.62), channel_id=1, source_target_pairs={{4,0},{8,4},{12,8},{5,1},{9,5},{13,9},{6,2},{10,6},{14,10},{7,3},{... | collective-permute-start | bytes 1179656 | tf_op jit(solution)/shard_map/ppermute | solution.py:114
  155.1 38.9 %collective-permute-start.36 = (bf16[2048,512]{1,0:T(8,128)(2,1)S(1)}, bf16[2048,512]{1,0:T(8,128)(2,1)S(1)}, u32[]{:S(2)}, u32[]{:S(2)}) collective-permute-start(bf16[2048,512]{1,0:T(8,128)(2,1)S(1)} %collective-permute-done.6), channel_id=1, source_target_pairs={{0,1},{1,0},{2,3},{3,2},{16,17},{17,16},{18,19},{19,18},{4,5},{5,4... | collective-permute-start | bytes 6291464 | tf_op jit(solution)/shard_map/ppermute | solution.py:42
  156.1 19.6 %collective-permute-start.31 = (bf16[128,1024]{0,1:T(8,128)(2,1)S(1)}, bf16[128,1024]{0,1:T(8,128)(2,1)S(1)}, u32[]{:S(2)}, u32[]{:S(2)}) collective-permute-start(bf16[128,1024]{0,1:T(8,128)(2,1)S(1)} %get-tuple-element.81), channel_id=1, source_target_pairs={{0,4},{4,8},{1,5},{5,9},{2,6},{6,10},{3,7},{7,11},{16,20},{20,24},... | collective-permute-start | bytes 786440 | tf_op jit(solution)/shard_map/ppermute | solution.py:140
  160.5 15.2 %collective-permute-start.34 = (bf16[128,1024]{0,1:T(8,128)(2,1)S(1)}, bf16[128,1024]{0,1:T(8,128)(2,1)S(1)}, u32[]{:S(2)}, u32[]{:S(2)}) collective-permute-start(bf16[128,1024]{0,1:T(8,128)(2,1)S(1)} %get-tuple-element.82), channel_id=1, source_target_pairs={{8,4},{12,8},{9,5},{13,9},{10,6},{14,10},{11,7},{15,11},{24,20},{2... | collective-permute-start | bytes 786440 | tf_op jit(solution)/shard_map/ppermute | solution.py:141
  164.0 29.8 %collective-permute-start.7 = (bf16[1024,512]{1,0:T(8,128)(2,1)S(1)}, bf16[1024,512]{1,0:T(8,128)(2,1)S(1)}, u32[]{:S(2)}, u32[]{:S(2)}) collective-permute-start(bf16[1024,512]{1,0:T(8,128)(2,1)S(1)} %slice.56), channel_id=1, source_target_pairs={{0,16},{1,17},{2,18},{3,19},{16,0},{17,1},{18,2},{19,3},{4,20},{5,... | collective-permute-start | bytes 3145736 | tf_op jit(solution)/shard_map/ppermute | solution.py:42
  174.0 19.8 %collective-permute-start.9 = (bf16[1024,512]{1,0:T(8,128)(2,1)S(1)}, bf16[1024,512]{1,0:T(8,128)(2,1)S(1)}, u32[]{:S(2)}, u32[]{:S(2)}) collective-permute-start(bf16[1024,512]{1,0:T(8,128)(2,1)S(1)} %slice.57), channel_id=1, source_target_pairs={{0,2},{1,3},{2,0},{3,1},{16,18},{17,19},{18,16},{19,17},{4,6},{5,7... | collective-permute-start | bytes 3145736 | tf_op jit(solution)/shard_map/ppermute | solution.py:42
  175.7 24.8 %collective-permute-start.43 = (bf16[2048,512]{1,0:T(8,128)(2,1)S(1)}, bf16[2048,512]{1,0:T(8,128)(2,1)S(1)}, u32[]{:S(2)}, u32[]{:S(2)}) collective-permute-start(bf16[2048,512]{1,0:T(8,128)(2,1)S(1)} %collective-permute-done.8), channel_id=1, source_target_pairs={{0,1},{1,0},{2,3},{3,2},{16,17},{17,16},{18,19},{19,18},{4,5},{5,4... | collective-permute-start | bytes 6291464 | tf_op jit(solution)/shard_map/ppermute | solution.py:42
  175.8 10.6 %collective-permute-start.35 = (bf16[128,1024]{0,1:T(8,128)(2,1)S(1)}, bf16[128,1024]{0,1:T(8,128)(2,1)S(1)}, u32[]{:S(2)}, u32[]{:S(2)}) collective-permute-start(bf16[128,1024]{0,1:T(8,128)(2,1)S(1)} %get-tuple-element.80), channel_id=1, source_target_pairs={{4,0},{8,4},{12,8},{5,1},{9,5},{13,9},{6,2},{10,6},{14,10},{7,3},{... | collective-permute-start | bytes 786440 | tf_op jit(solution)/shard_map/ppermute | solution.py:141
  193.9 34.8 %collective-permute-start.10 = (bf16[2048,512]{1,0:T(8,128)(2,1)S(1)}, bf16[2048,512]{1,0:T(8,128)(2,1)S(1)}, u32[]{:S(2)}, u32[]{:S(2)}) collective-permute-start(bf16[2048,512]{1,0:T(8,128)(2,1)S(1)} %constant_dynamic-update-slice_fusion), channel_id=1, source_target_pairs={{0,1},{1,0},{2,3},{3,2},{16,17},{17,16},{18,19},{19,18},{4,5},{5,4... | collective-permute-start | bytes 6291464 | tf_op jit(solution)/shard_map/ppermute | solution.py:42
  195.4 11.0 %collective-permute-start.37 = (bf16[128,1024]{0,1:T(8,128)(2,1)S(1)}, bf16[128,1024]{0,1:T(8,128)(2,1)S(1)}, u32[]{:S(2)}, u32[]{:S(2)}) collective-permute-start(bf16[128,1024]{0,1:T(8,128)(2,1)S(1)} %get-tuple-element.77), channel_id=1, source_target_pairs={{0,4},{1,5},{2,6},{3,7},{16,20},{17,21},{18,22},{19,23}} | collective-permute-start | bytes 786440 | tf_op jit(solution)/shard_map/ppermute | solution.py:140
  206.5 12.0 %collective-permute-start.38 = (bf16[128,1024]{0,1:T(8,128)(2,1)S(1)}, bf16[128,1024]{0,1:T(8,128)(2,1)S(1)}, u32[]{:S(2)}, u32[]{:S(2)}) collective-permute-start(bf16[128,1024]{0,1:T(8,128)(2,1)S(1)} %get-tuple-element.75), channel_id=1, source_target_pairs={{0,4},{4,8},{1,5},{5,9},{2,6},{6,10},{3,7},{7,11},{16,20},{20,24},... | collective-permute-start | bytes 786440 | tf_op jit(solution)/shard_map/ppermute | solution.py:140
  212.2 10.7 %collective-permute-start.45 = (bf16[128,1024]{0,1:T(8,128)(2,1)S(1)}, bf16[128,1024]{0,1:T(8,128)(2,1)S(1)}, u32[]{:S(2)}, u32[]{:S(2)}) collective-permute-start(bf16[128,1024]{0,1:T(8,128)(2,1)S(1)} %get-tuple-element.69), channel_id=1, source_target_pairs={{0,4},{4,8},{1,5},{5,9},{2,6},{6,10},{3,7},{7,11},{16,20},{20,24},... | collective-permute-start | bytes 786440 | tf_op jit(solution)/shard_map/ppermute | solution.py:140
  216.6 10.7 %collective-permute-start.48 = (bf16[128,1024]{0,1:T(8,128)(2,1)S(1)}, bf16[128,1024]{0,1:T(8,128)(2,1)S(1)}, u32[]{:S(2)}, u32[]{:S(2)}) collective-permute-start(bf16[128,1024]{0,1:T(8,128)(2,1)S(1)} %get-tuple-element.70), channel_id=1, source_target_pairs={{8,4},{12,8},{9,5},{13,9},{10,6},{14,10},{11,7},{15,11},{24,20},{2... | collective-permute-start | bytes 786440 | tf_op jit(solution)/shard_map/ppermute | solution.py:141
  218.6 67.7 %collective-permute-start.88 = (bf16[128,512]{1,0:T(8,128)(2,1)}, bf16[128,512]{1,0:T(8,128)(2,1)}, u32[]{:S(2)}, u32[]{:S(2)}) collective-permute-start(bf16[128,512]{1,0:T(8,128)(2,1)} %get-tuple-element.39), channel_id=1, source_target_pairs={{0,18},{1,19},{2,16},{3,17},{16,2},{17,3},{18,0},{19,1},{4,22},{5,... | collective-permute-start | bytes 393224 | tf_op jit(solution)/shard_map/ppermute | solution.py:42
  219.6 15.1 %collective-permute-start.42 = (bf16[128,1024]{0,1:T(8,128)(2,1)S(1)}, bf16[128,1024]{0,1:T(8,128)(2,1)S(1)}, u32[]{:S(2)}, u32[]{:S(2)}) collective-permute-start(bf16[128,1024]{0,1:T(8,128)(2,1)S(1)} %get-tuple-element.74), channel_id=1, source_target_pairs={{4,0},{8,4},{12,8},{5,1},{9,5},{13,9},{6,2},{10,6},{14,10},{7,3},{... | collective-permute-start | bytes 786440 | tf_op jit(solution)/shard_map/ppermute | solution.py:141
  222.8 15.9 %collective-permute-start.39 = (bf16[128,1024]{0,1:T(8,128)(2,1)S(1)}, bf16[128,1024]{0,1:T(8,128)(2,1)S(1)}, u32[]{:S(2)}, u32[]{:S(2)}) collective-permute-start(bf16[128,1024]{0,1:T(8,128)(2,1)S(1)} %get-tuple-element.73), channel_id=1, source_target_pairs={{0,4},{4,8},{8,12},{1,5},{5,9},{9,13},{2,6},{6,10},{10,14},{3,7},{... | collective-permute-start | bytes 786440 | tf_op jit(solution)/shard_map/ppermute | solution.py:140
  227.4 21.7 %collective-permute-start.49 = (bf16[128,1024]{0,1:T(8,128)(2,1)S(1)}, bf16[128,1024]{0,1:T(8,128)(2,1)S(1)}, u32[]{:S(2)}, u32[]{:S(2)}) collective-permute-start(bf16[128,1024]{0,1:T(8,128)(2,1)S(1)} %get-tuple-element.68), channel_id=1, source_target_pairs={{4,0},{8,4},{12,8},{5,1},{9,5},{13,9},{6,2},{10,6},{14,10},{7,3},{... | collective-permute-start | bytes 786440 | tf_op jit(solution)/shard_map/ppermute | solution.py:141
  228.7 20.5 %collective-permute-start.46 = (bf16[128,1024]{0,1:T(8,128)(2,1)S(1)}, bf16[128,1024]{0,1:T(8,128)(2,1)S(1)}, u32[]{:S(2)}, u32[]{:S(2)}) collective-permute-start(bf16[128,1024]{0,1:T(8,128)(2,1)S(1)} %get-tuple-element.67), channel_id=1, source_target_pairs={{0,4},{4,8},{8,12},{1,5},{5,9},{9,13},{2,6},{6,10},{10,14},{3,7},{... | collective-permute-start | bytes 786440 | tf_op jit(solution)/shard_map/ppermute | solution.py:140
  249.2 38.4 %collective-permute-start.89 = (bf16[128,512]{1,0:T(8,128)(2,1)}, bf16[128,512]{1,0:T(8,128)(2,1)}, u32[]{:S(2)}, u32[]{:S(2)}) collective-permute-start(bf16[128,512]{1,0:T(8,128)(2,1)} %get-tuple-element.38), channel_id=1, source_target_pairs={{0,19},{1,18},{2,17},{3,16},{16,3},{17,2},{18,1},{19,0},{4,23},{5,... | collective-permute-start | bytes 393224 | tf_op jit(solution)/shard_map/ppermute | solution.py:42
  252.6 11.9 %collective-permute-start.55 = (bf16[128,1024]{0,1:T(8,128)(2,1)S(1)}, bf16[128,1024]{0,1:T(8,128)(2,1)S(1)}, u32[]{:S(2)}, u32[]{:S(2)}) collective-permute-start(bf16[128,1024]{0,1:T(8,128)(2,1)S(1)} %get-tuple-element.62), channel_id=1, source_target_pairs={{4,0},{8,4},{12,8},{5,1},{9,5},{13,9},{6,2},{10,6},{14,10},{7,3},{... | collective-permute-start | bytes 786440 | tf_op jit(solution)/shard_map/ppermute | solution.py:141
  253.9 12.1 %collective-permute-start.52 = (bf16[128,1024]{0,1:T(8,128)(2,1)S(1)}, bf16[128,1024]{0,1:T(8,128)(2,1)S(1)}, u32[]{:S(2)}, u32[]{:S(2)}) collective-permute-start(bf16[128,1024]{0,1:T(8,128)(2,1)S(1)} %get-tuple-element.61), channel_id=1, source_target_pairs={{0,4},{4,8},{8,12},{1,5},{5,9},{9,13},{2,6},{6,10},{10,14},{3,7},{... | collective-permute-start | bytes 786440 | tf_op jit(solution)/shard_map/ppermute | solution.py:140
  262.3 37.7 %collective-permute-start.65 = (bf16[1536,512]{1,0:T(8,128)(2,1)}, bf16[1536,512]{1,0:T(8,128)(2,1)}, u32[]{:S(2)}, u32[]{:S(2)}) collective-permute-start(bf16[1536,512]{1,0:T(8,128)(2,1)} %bitcast.53), channel_id=1, source_target_pairs={{0,2},{1,3},{2,0},{3,1},{16,18},{17,19},{18,16},{19,17},{4,6},{5,7... | collective-permute-start | bytes 4718600 | tf_op jit(solution)/shard_map/ppermute | solution.py:42
  264.5 40.7 %collective-permute-start.67 = (bf16[1536,512]{1,0:T(8,128)(2,1)}, bf16[1536,512]{1,0:T(8,128)(2,1)}, u32[]{:S(2)}, u32[]{:S(2)}) collective-permute-start(bf16[1536,512]{1,0:T(8,128)(2,1)} %bitcast.53), channel_id=1, source_target_pairs={{0,16},{1,17},{2,18},{3,19},{16,0},{17,1},{18,2},{19,3},{4,20},{5,... | collective-permute-start | bytes 4718600 | tf_op jit(solution)/shard_map/ppermute | solution.py:42
  266.0 64.9 %collective-permute-start.12 = (bf16[1536,512]{1,0:T(8,128)(2,1)}, bf16[1536,512]{1,0:T(8,128)(2,1)}, u32[]{:S(2)}, u32[]{:S(2)}) collective-permute-start(bf16[1536,512]{1,0:T(8,128)(2,1)} %bitcast.5), channel_id=1, source_target_pairs={{0,2},{1,3},{2,0},{3,1},{16,18},{17,19},{18,16},{19,17},{4,6},{5,7... | collective-permute-start | bytes 4718600 | tf_op jit(solution)/shard_map/ppermute | solution.py:42
  286.3 49.5 %collective-permute-start.14 = (bf16[1536,512]{1,0:T(8,128)(2,1)}, bf16[1536,512]{1,0:T(8,128)(2,1)S(1)}, u32[]{:S(2)}, u32[]{:S(2)}) collective-permute-start(bf16[1536,512]{1,0:T(8,128)(2,1)} %bitcast.5), channel_id=1, source_target_pairs={{0,16},{1,17},{2,18},{3,19},{16,0},{17,1},{18,2},{19,3},{4,20},{5,... | collective-permute-start | bytes 4718600 | tf_op jit(solution)/shard_map/ppermute | solution.py:42
  287.6 49.0 %collective-permute-start.11 = (bf16[1536,512]{1,0:T(8,128)(2,1)}, bf16[1536,512]{1,0:T(8,128)(2,1)S(1)}, u32[]{:S(2)}, u32[]{:S(2)}) collective-permute-start(bf16[1536,512]{1,0:T(8,128)(2,1)} %bitcast.5), channel_id=1, source_target_pairs={{0,1},{1,0},{2,3},{3,2},{16,17},{17,16},{18,19},{19,18},{4,5},{5,4... | collective-permute-start | bytes 4718600 | tf_op jit(solution)/shard_map/ppermute | solution.py:42
  300.1 58.2 %collective-permute-start.56 = (bf16[128,4096]{1,0:T(8,128)(2,1)S(1)}, bf16[128,4096]{1,0:T(8,128)(2,1)S(1)}, u32[]{:S(2)}, u32[]{:S(2)}) collective-permute-start(bf16[128,4096]{1,0:T(8,128)(2,1)S(1)} %multiply_convert_fusion.1), channel_id=1, source_target_pairs={{0,16},{16,0},{1,17},{17,1},{2,18},{18,2},{3,19},{19,3},{4,20},{20... | collective-permute-start | bytes 3145736 | tf_op jit(solution)/shard_map/ppermute | solution.py:277
  305.2 69.9 %collective-permute-start.69 = (bf16[768,512]{1,0:T(8,128)(2,1)S(1)}, bf16[768,512]{1,0:T(8,128)(2,1)S(1)}, u32[]{:S(2)}, u32[]{:S(2)}) collective-permute-start(bf16[768,512]{1,0:T(8,128)(2,1)S(1)} %slice.66), channel_id=1, source_target_pairs={{0,16},{1,17},{2,18},{3,19},{16,0},{17,1},{18,2},{19,3},{4,20},{5,... | collective-permute-start | bytes 2359304 | tf_op jit(solution)/shard_map/ppermute | solution.py:42
  330.9 61.1 %collective-permute-start.70 = (bf16[768,512]{1,0:T(8,128)(2,1)S(1)}, bf16[768,512]{1,0:T(8,128)(2,1)S(1)}, u32[]{:S(2)}, u32[]{:S(2)}) collective-permute-start(bf16[768,512]{1,0:T(8,128)(2,1)S(1)} %slice.67), channel_id=1, source_target_pairs={{0,2},{1,3},{2,0},{3,1},{16,18},{17,19},{18,16},{19,17},{4,6},{5,7... | collective-permute-start | bytes 2359304 | tf_op jit(solution)/shard_map/ppermute | solution.py:42
  335.8 56.2 %collective-permute-start.16 = (bf16[768,512]{1,0:T(8,128)(2,1)S(1)}, bf16[768,512]{1,0:T(8,128)(2,1)S(1)}, u32[]{:S(2)}, u32[]{:S(2)}) collective-permute-start(bf16[768,512]{1,0:T(8,128)(2,1)S(1)} %slice.58), channel_id=1, source_target_pairs={{0,16},{1,17},{2,18},{3,19},{16,0},{17,1},{18,2},{19,3},{4,20},{5,... | collective-permute-start | bytes 2359304 | tf_op jit(solution)/shard_map/ppermute | solution.py:42
  336.6 56.0 %collective-permute-start.17 = (bf16[768,512]{1,0:T(8,128)(2,1)S(1)}, bf16[768,512]{1,0:T(8,128)(2,1)S(1)}, u32[]{:S(2)}, u32[]{:S(2)}) collective-permute-start(bf16[768,512]{1,0:T(8,128)(2,1)S(1)} %slice.59), channel_id=1, source_target_pairs={{0,2},{1,3},{2,0},{3,1},{16,18},{17,19},{18,16},{19,17},{4,6},{5,7... | collective-permute-start | bytes 2359304 | tf_op jit(solution)/shard_map/ppermute | solution.py:42
  366.2 42.4 %collective-permute-start.57 = (bf16[128,4096]{1,0:T(8,128)(2,1)S(1)}, bf16[128,4096]{1,0:T(8,128)(2,1)S(1)}, u32[]{:S(2)}, u32[]{:S(2)}) collective-permute-start(bf16[128,4096]{1,0:T(8,128)(2,1)S(1)} %fusion.21), channel_id=1, source_target_pairs={{0,16},{16,0},{1,17},{17,1},{2,18},{18,2},{3,19},{19,3},{4,20},{20... | collective-permute-start | bytes 3145736 | tf_op jit(solution)/shard_map/ppermute | solution.py:286
  375.1 36.3 %collective-permute-start.64 = (bf16[1536,512]{1,0:T(8,128)(2,1)}, bf16[1536,512]{1,0:T(8,128)(2,1)S(1)}, u32[]{:S(2)}, u32[]{:S(2)}) collective-permute-start(bf16[1536,512]{1,0:T(8,128)(2,1)} %bitcast.53), channel_id=1, source_target_pairs={{0,1},{1,0},{2,3},{3,2},{16,17},{17,16},{18,19},{19,18},{4,5},{5,4... | collective-permute-start | bytes 4718600 | tf_op jit(solution)/shard_map/ppermute | solution.py:42
  391.9 27.5 %collective-permute-start.66 = (bf16[1536,512]{1,0:T(8,128)(2,1)}, bf16[1536,512]{1,0:T(8,128)(2,1)S(1)}, u32[]{:S(2)}, u32[]{:S(2)}) collective-permute-start(bf16[1536,512]{1,0:T(8,128)(2,1)} %collective-permute-done.65), channel_id=1, source_target_pairs={{0,1},{1,0},{2,3},{3,2},{16,17},{17,16},{18,19},{19,18},{4,5},{5,4... | collective-permute-start | bytes 4718600 | tf_op jit(solution)/shard_map/ppermute | solution.py:42
  392.0 29.7 %collective-permute-start.68 = (bf16[1536,512]{1,0:T(8,128)(2,1)}, bf16[1536,512]{1,0:T(8,128)(2,1)S(1)}, u32[]{:S(2)}, u32[]{:S(2)}) collective-permute-start(bf16[1536,512]{1,0:T(8,128)(2,1)} %collective-permute-done.67), channel_id=1, source_target_pairs={{0,1},{1,0},{2,3},{3,2},{16,17},{17,16},{18,19},{19,18},{4,5},{5,4... | collective-permute-start | bytes 4718600 | tf_op jit(solution)/shard_map/ppermute | solution.py:42
  392.6 27.6 %collective-permute-start.13 = (bf16[1536,512]{1,0:T(8,128)(2,1)}, bf16[1536,512]{1,0:T(8,128)(2,1)S(1)}, u32[]{:S(2)}, u32[]{:S(2)}) collective-permute-start(bf16[1536,512]{1,0:T(8,128)(2,1)} %collective-permute-done.12), channel_id=1, source_target_pairs={{0,1},{1,0},{2,3},{3,2},{16,17},{17,16},{18,19},{19,18},{4,5},{5,4... | collective-permute-start | bytes 4718600 | tf_op jit(solution)/shard_map/ppermute | solution.py:42
  408.5 18.4 %collective-permute-start.18 = (bf16[1536,512]{1,0:T(8,128)(2,1)S(1)}, bf16[1536,512]{1,0:T(8,128)(2,1)S(1)}, u32[]{:S(2)}, u32[]{:S(2)}) collective-permute-start(bf16[1536,512]{1,0:T(8,128)(2,1)S(1)} %constant_dynamic-update-slice_fusion.2), channel_id=1, source_target_pairs={{0,1},{1,0},{2,3},{3,2},{16,17},{17,16},{18,19},{19,18},{4,5},{5,4... | collective-permute-start | bytes 4718600 | tf_op jit(solution)/shard_map/ppermute | solution.py:42
  424.1 19.5 %collective-permute-start.73 = (f32[32,1536]{1,0:T(8,128)S(1)}, f32[32,1536]{1,0:T(8,128)S(1)}, u32[]{:S(2)}, u32[]{:S(2)}) collective-permute-start(f32[32,1536]{1,0:T(8,128)S(1)} %get-tuple-element.91), channel_id=1, source_target_pairs={{0,8},{4,12},{8,0},{12,4},{1,9},{5,13},{9,1},{13,5},{2,10},{6,14},... | collective-permute-start | bytes 589832 | tf_op jit(solution)/shard_map/ppermute | solution.py:99
  425.8 17.9 %collective-permute-start.72 = (f32[32,1536]{1,0:T(8,128)S(1)}, f32[32,1536]{1,0:T(8,128)S(1)}, u32[]{:S(2)}, u32[]{:S(2)}) collective-permute-start(f32[32,1536]{1,0:T(8,128)S(1)} %get-tuple-element.92), channel_id=1, source_target_pairs={{0,4},{4,0},{8,12},{12,8},{1,5},{5,1},{9,13},{13,9},{2,6},{6,2},{1... | collective-permute-start | bytes 589832 | tf_op jit(solution)/shard_map/ppermute | solution.py:99
  446.0 14.2 %collective-permute-start.75 = (bf16[128,1536]{1,0:T(8,128)(2,1)S(1)}, bf16[128,1536]{1,0:T(8,128)(2,1)S(1)}, u32[]{:S(2)}, u32[]{:S(2)}) collective-permute-start(bf16[128,1536]{1,0:T(8,128)(2,1)S(1)} %get-tuple-element.16), channel_id=1, source_target_pairs={{0,1},{1,0},{2,3},{3,2},{16,17},{17,16},{18,19},{19,18},{4,5},{5,4... | collective-permute-start | bytes 1179656 | tf_op jit(solution)/shard_map/ppermute | solution.py:42
  446.1 11.5 %collective-permute-start.76 = (bf16[128,1536]{1,0:T(8,128)(2,1)S(1)}, bf16[128,1536]{1,0:T(8,128)(2,1)S(1)}, u32[]{:S(2)}, u32[]{:S(2)}) collective-permute-start(bf16[128,1536]{1,0:T(8,128)(2,1)S(1)} %get-tuple-element.16), channel_id=1, source_target_pairs={{0,2},{1,3},{2,0},{3,1},{16,18},{17,19},{18,16},{19,17},{4,6},{5,7... | collective-permute-start | bytes 1179656 | tf_op jit(solution)/shard_map/ppermute | solution.py:42
  447.0 11.7 %collective-permute-start.78 = (bf16[128,1536]{1,0:T(8,128)(2,1)S(1)}, bf16[128,1536]{1,0:T(8,128)(2,1)S(1)}, u32[]{:S(2)}, u32[]{:S(2)}) collective-permute-start(bf16[128,1536]{1,0:T(8,128)(2,1)S(1)} %get-tuple-element.16), channel_id=1, source_target_pairs={{0,16},{1,17},{2,18},{3,19},{16,0},{17,1},{18,2},{19,3},{4,20},{5,... | collective-permute-start | bytes 1179656 | tf_op jit(solution)/shard_map/ppermute | solution.py:42
  471.0 13.2 %collective-permute-start.93 = (bf16[384,512]{1,0:T(8,128)(2,1)S(1)}, bf16[384,512]{1,0:T(8,128)(2,1)S(1)}, u32[]{:S(2)}, u32[]{:S(2)}) collective-permute-start(bf16[384,512]{1,0:T(8,128)(2,1)S(1)} %get-tuple-element.28), channel_id=1, source_target_pairs={{12,8},{13,9},{14,10},{15,11},{28,24},{29,25},{30,26},{31,27}} | collective-permute-start | bytes 1179656 | tf_op jit(solution)/shard_map/ppermute | solution.py:141
  479.2 12.5 %collective-permute-start.91 = (bf16[384,512]{1,0:T(8,128)(2,1)S(1)}, bf16[384,512]{1,0:T(8,128)(2,1)S(1)}, u32[]{:S(2)}, u32[]{:S(2)}) collective-permute-start(bf16[384,512]{1,0:T(8,128)(2,1)S(1)} %add_convert_fusion.5), channel_id=1, source_target_pairs={{0,4},{4,8},{1,5},{5,9},{2,6},{6,10},{3,7},{7,11},{16,20},{20,24},... | collective-permute-start | bytes 1179656 | tf_op jit(solution)/shard_map/ppermute | solution.py:140
  492.8 12.4 %collective-permute-start.92 = (bf16[384,512]{1,0:T(8,128)(2,1)S(1)}, bf16[384,512]{1,0:T(8,128)(2,1)S(1)}, u32[]{:S(2)}, u32[]{:S(2)}) collective-permute-start(bf16[384,512]{1,0:T(8,128)(2,1)S(1)} %get-tuple-element.25), channel_id=1, source_target_pairs={{0,4},{4,8},{8,12},{1,5},{5,9},{9,13},{2,6},{6,10},{10,14},{3,7},{... | collective-permute-start | bytes 1179656 | tf_op jit(solution)/shard_map/ppermute | solution.py:140
  498.0 17.1 %collective-permute-start.95 = (bf16[384,512]{1,0:T(8,128)(2,1)S(1)}, bf16[384,512]{1,0:T(8,128)(2,1)S(1)}, u32[]{:S(2)}, u32[]{:S(2)}) collective-permute-start(bf16[384,512]{1,0:T(8,128)(2,1)S(1)} %add_convert_fusion.2), channel_id=1, source_target_pairs={{4,0},{8,4},{12,8},{5,1},{9,5},{13,9},{6,2},{10,6},{14,10},{7,3},{... | collective-permute-start | bytes 1179656 | tf_op jit(solution)/shard_map/ppermute | solution.py:141
  (76 other events, 796.2 us)

commit v2 on v0

--- a/solution.py
+++ b/solution.py
@@ -1,15 +1,25 @@
 import jax
 import jax.numpy as jnp
 from jax import lax
+from jax.experimental import pallas as pl
+from jax.experimental.pallas import tpu as pltpu
 from jax.sharding import PartitionSpec as P
 
 QH = 64
 KVH = 4
 HD = 128
 
-
 EPSILON = 1e-06
 MASKED = -1e30
+PLANE = ("ctx", "rep")
+LAST = (((1,), (1,)), ((), ()))
+FIRST = (((0,), (0,)), ((), ()))
+F32 = jnp.float32
+BF16 = jnp.bfloat16
+
+
+def matmul(left, right, dims=(((1,), (0,)), ((), ()))):
+    return lax.dot_general(left, right, dims, preferred_element_type=F32)
 
 
 def rms_scale(values, gain):
@@ -17,7 +27,331 @@
     return values * lax.rsqrt(mean_square + EPSILON) * gain
 
 
+def after(value, *earlier):
+    return lax.optimization_barrier((value, *earlier))[0]
+
+
+def swap_x(value):
+    return lax.ppermute(value, "ctx", [(0, 1), (1, 0)])
+
+
+def swap_rep(value, offset):
+    return lax.ppermute(value, "rep", [(i, i ^ offset) for i in range(4)])
+
+
+def swap_z(value, offset):
+    return lax.ppermute(value, "vocab", [(i, i ^ offset) for i in range(4)])
+
+
+def pick(value, index, size, axis):
+    return lax.dynamic_slice_in_dim(value, index * size, size, axis)
+
+
+def split_relative(value, index, count, axis):
+    size = value.shape[axis] // count
+    return [pick(value, index ^ r, size, axis) for r in range(count)]
+
+
+def join_absolute(blocks, index, axis):
+    count = len(blocks)
+    return jnp.concatenate(
+        [
+            lax.select_n(index, *[blocks[j ^ i] for i in range(count)])
+            for j in range(count)
+        ],
+        axis=axis,
+    )
+
+
+def rep_gather(own):
+    along_y = swap_rep(own, 2)
+    return [own, swap_rep(own, 1), along_y, swap_rep(along_y, 1)]
+
+
+def line_gather(own):
+    received = [own] + [swap_z(own, r) for r in (1, 2, 3)]
+    return join_absolute(received, lax.axis_index("vocab"), 0)
+
+
+def line_exchange(value):
+    index = lax.axis_index("vocab")
+    blocks = split_relative(value, index, 4, 0)
+    received = [blocks[0]] + [swap_z(blocks[r], r) for r in (1, 2, 3)]
+    return join_absolute(received, index, 0)
+
+
+def line_sum(partial):
+    blocks = split_relative(partial, lax.axis_index("vocab"), 4, 0)
+    received = [swap_z(blocks[r], r) for r in (3, 2, 1)]
+    return sum((block.astype(F32) for block in received), blocks[0].astype(F32))
+
+
+def line_reduce(far, near):
+    index = lax.axis_index("vocab")
+    size = near.shape[0] // 2
+    outer = lax.ppermute(far, "vocab", [(0, 1), (3, 2)])
+    far = (far.astype(F32) + outer.astype(F32)).astype(BF16)
+    inner = lax.ppermute(far, "vocab", [(1, 2), (2, 1)])
+    near = near.astype(F32) + inner.astype(F32)
+    beside = swap_z(pick(near, 1 - index % 2, size, 0).astype(BF16), 1)
+    return pick(near, index % 2, size, 0) + beside.astype(F32)
+
+
+def plane_rows(own):
+    half = own.shape[0] // 2
+    along_x = swap_x(own)
+    along_y = swap_rep(own, 2)
+    near = swap_x(along_y[:half])
+    far = swap_rep(along_x[half:], 2)
+    mine = jnp.concatenate([own, along_y, along_x, near, far], axis=0)
+    return jnp.concatenate([mine, swap_rep(mine, 1)], axis=0), along_x
+
+
+def plane_exchange(rows):
+    plane = lax.axis_index("ctx") * 4 + lax.axis_index("rep")
+    blocks = split_relative(rows, plane, 8, 1)
+    count, size = blocks[0].shape
+    there = swap_x(jnp.concatenate(blocks[4:], axis=1))
+    here = jnp.concatenate([jnp.concatenate(blocks[:4], axis=1), there], axis=0)
+    there = swap_rep(here[:, 2 * size :], 2)
+    here = here[:, : 2 * size]
+    here = jnp.concatenate([here[:count], there[:count], here[count:], there[count:]], axis=0)
+    return jnp.concatenate([here[:, :size], swap_rep(here[:, size:], 1)], axis=0)
+
+
+HEADS_STEP = 4
+
+
+def attend_kernel(facts, query, rows, out):
+    pos_ctx = query.shape[1]
+    keys = rows.shape[2]
+    length = facts[pl.program_id(0)]
+    query_pos = facts[pl.num_programs(0)] + lax.broadcasted_iota(jnp.int32, (pos_ctx, keys), 0)
+    key_pos = facts[pl.num_programs(0) + 1] + lax.broadcasted_iota(jnp.int32, (pos_ctx, keys), 1)
+    allowed = (key_pos <= query_pos) & (key_pos < length) & (key_pos >= 0)
+    bias = jnp.where(allowed, 0.0, MASKED)
+    for head in range(query.shape[2] // HD):
+        cols = slice(head * HD, (head + 1) * HD)
+        scores = matmul(query[0, :, cols], rows[0, 0], LAST) * HD ** (-0.5) + bias
+        peak = jnp.max(scores, axis=-1, keepdims=True)
+        exponent = jnp.exp(scores - peak)
+        total = jnp.sum(exponent, axis=-1, keepdims=True)
+        weighted = matmul(exponent.astype(BF16), rows[1, 0])
+        out[:, cols] = (weighted / total).astype(BF16)
+
+
+def attend(queries, key_value, lengths):
+    seq_dev, pos_ctx, head_cols = queries.shape
+    heads_dev = head_cols // HD
+    ctx_index = lax.axis_index("ctx")
+    shared_head = lax.axis_index("vocab") * heads_dev // (QH // KVH)
+    own_rows = lax.dynamic_slice_in_dim(key_value, shared_head * HD, HD, 3)
+    other = swap_x(own_rows)
+    rows = jnp.concatenate([other, own_rows], axis=2)
+    facts = jnp.concatenate([lengths, jnp.stack([ctx_index * pos_ctx, (ctx_index - 1) * pos_ctx])])
+    step_cols = HEADS_STEP * HD
+    heads_out = pl.pallas_call(
+        attend_kernel,
+        out_shape=jax.ShapeDtypeStruct((seq_dev * pos_ctx, head_cols), BF16),
+        grid_spec=pltpu.PrefetchScalarGridSpec(
+            num_scalar_prefetch=1,
+            grid=(seq_dev, head_cols // step_cols),
+            in_specs=[
+                pl.BlockSpec((1, pos_ctx, step_cols), lambda s, h, facts: (s, 0, h)),
+                pl.BlockSpec((2, 1, rows.shape[2], HD), lambda s, h, facts: (0, s, 0, 0)),
+            ],
+            out_specs=pl.BlockSpec((pos_ctx, step_cols), lambda s, h, facts: (s, h)),
+        ),
+        cost_estimate=pl.CostEstimate(
+            flops=4 * seq_dev * pos_ctx * rows.shape[2] * head_cols,
+            bytes_accessed=4 * queries.size,
+            transcendentals=seq_dev * heads_dev * pos_ctx * rows.shape[2],
+        ),
+        compiler_params=pltpu.CompilerParams(vmem_limit_bytes=32 * 2**20),
+        name="attend",
+    )(facts, queries, rows)
+    return heads_out, other
+
+
 def per_device(
+    queries,
+    key_value,
+    residual,
+    out_weight,
+    moe_gain,
+    expert_ids,
+    route_gate,
+    gate_weight,
+    up_weight,
+    down_weight,
+    final_gain,
+    teacher_head,
+    learner_hidden,
+    learner_head,
+    lengths,
+):
+    seq_dev, pos_ctx, _ = queries.shape
+    pos_dev, width = residual.shape[1:]
+    own_count = seq_dev * pos_dev
+    half = width // 2
+    ctx_index = lax.axis_index("ctx")
+    vocab_index = lax.axis_index("vocab")
+    rep_index = lax.axis_index("rep")
+    per_expert = own_count // 4
+    vocab = 4 * teacher_head.shape[0]
+
+    route_ids = expert_ids.reshape(own_count, -1)
+    inside = route_ids < 4
+    chosen = jnp.sum(jnp.where(inside, route_ids, 0), axis=1)
+    route_weight = jnp.sum(jnp.where(inside, route_gate.reshape(own_count, -1), 0.0), axis=1)
+    member = (chosen[:, None] == jnp.arange(4)[None, :]).astype(jnp.int32)
+    slot_rank = jnp.sum((jnp.cumsum(member, axis=0) - 1) * member, axis=1)
+    target = chosen * per_expert + slot_rank
+    placed = target[None, :] == jnp.arange(own_count)[:, None]
+    placer = placed.astype(BF16)
+
+    line_target = chosen * own_count + vocab_index * per_expert + slot_rank
+    pair_facts = jnp.stack([line_target.astype(F32), route_weight])[None]
+    beside = swap_z(pair_facts, 1)
+    pair_facts = join_absolute([pair_facts, beside], vocab_index % 2, 0)
+    line_facts = join_absolute([pair_facts, swap_z(pair_facts, 2)], vocab_index // 2, 0)
+    line_target = line_facts[:, 0].astype(jnp.int32)
+    line_weight = line_facts[:, 1]
+    line_tokens = jnp.swapaxes(line_target.reshape(4, seq_dev, pos_dev), 0, 1).reshape(-1)
+    line_placer = (line_tokens[None, :] == jnp.arange(seq_dev * pos_ctx)[:, None]).astype(BF16)
+    mine = vocab_index * own_count + jnp.arange(own_count)
+    my_weight = jnp.sum(
+        jnp.where(line_target.reshape(1, -1) == mine[:, None], line_weight.reshape(1, -1), 0.0),
+        axis=1,
+        keepdims=True,
+    )
+
+    heads_out, keys = attend(queries, key_value, lengths)
+    weight_blocks = rep_gather(out_weight)
+    residual_rows = matmul(placer, residual.reshape(own_count, width)).astype(BF16)
+    other_residual = swap_x(after(pick(residual_rows, 1 - ctx_index, half, 1), keys))
+    both_residual = (pick(residual_rows, ctx_index, half, 1), other_residual)
+    other_weight = swap_x(my_weight)
+
+    learner_line = line_gather(learner_head)
+    learner_line = after(learner_line, weight_blocks[2])
+    learner_blocks = rep_gather(learner_line)
+
+    heads_sorted = matmul(line_placer, heads_out).astype(BF16)
+    far_pair, near_pair = 1 - vocab_index // 2, vocab_index // 2
+    pair_rows = 2 * own_count
+    own_far = pick(heads_sorted, far_pair, pair_rows, 0)
+    own_near = pick(heads_sorted, near_pair, pair_rows, 0)
+    other_far = swap_x(own_far)
+    other_near = swap_x(after(own_near, other_far))
+    owner = (jnp.arange(4) == vocab_index).reshape(1, 4, 1, 1)
+
+    def project(rows, weight, residual_part, pair, block):
+        added = pick(residual_part, pair, 2 * per_expert, 0)
+        added = pick(added, rep_index ^ block, weight.shape[1], 1).astype(F32)
+        added = jnp.where(owner, added.reshape(2, 1, per_expert, -1), 0.0)
+        added = added.reshape(pair_rows, -1)
+        return (matmul(rows, weight) + added).astype(BF16)
+
+    def projected(far, near, residual_part, members):
+        parts = [
+            jnp.concatenate(
+                [project(rows, weight_blocks[r], residual_part, pair, r) for r in members], axis=1
+            )
+            for rows, pair in ((far, far_pair), (near, near_pair))
+        ]
+        return jnp.split(line_reduce(*parts), 2, axis=1)
+
+    own_blocks = projected(own_far, own_near, both_residual[0], (0, 1))
+    own_blocks += projected(own_far, own_near, both_residual[0], (2, 3))
+    other_blocks = projected(other_far, other_near, both_residual[1], (0, 1))
+    other_blocks += projected(other_far, other_near, both_residual[1], (2, 3))
+
+    hidden_one = jnp.concatenate(
+        [join_absolute(own_blocks, rep_index, 1), join_absolute(other_blocks, rep_index, 1)], axis=0
+    )
+    sent = hidden_one.astype(BF16)
+    got = swap_x(sent)
+    got = jnp.concatenate([got[own_count:], got[:own_count]], axis=0)
+    rows = join_absolute([sent, got], ctx_index, 1).astype(F32)
+    normed = rms_scale(rows, moe_gain).astype(BF16)
+
+    learner_own = learner_hidden.reshape(own_count, width)
+    learner_rows = matmul(placer, learner_own).astype(BF16)
+    other_rows = swap_x(after(pick(learner_rows, 1 - ctx_index, half, 1), other_near))
+    both_rows = jnp.concatenate([pick(learner_rows, ctx_index, half, 1), other_rows], axis=0)
+    learner_part = sum(
+        matmul(part, block, LAST)
+        for part, block in zip(split_relative(both_rows, rep_index, 4, 1), learner_blocks)
+    )
+    learner_logits = learner_part[:own_count] + swap_x(learner_part[own_count:])
+    learner_peak = jnp.max(learner_logits, axis=1, keepdims=True)
+    learner_exp = jnp.exp(learner_logits - learner_peak)
+    learner_total = jnp.sum(learner_exp, axis=1, keepdims=True)
+    learner_lse = learner_peak + jnp.log(learner_total)
+    plane_columns = plane_exchange(after(learner_own, learner_logits))
+
+    teacher_slice = pick(teacher_head, ctx_index * 4 + rep_index, width // 8, 1)
+    teacher_line = line_gather(after(teacher_slice, other_blocks[0], other_blocks[2]))
+    teacher_blocks = rep_gather(teacher_line)
+
+    gate_pre = matmul(normed, gate_weight[0], LAST)
+    up_pre = matmul(normed, up_weight[0], LAST)
+    activated = (jax.nn.silu(gate_pre) * up_pre).astype(BF16)
+    theirs = matmul(activated, pick(down_weight[0], 1 - ctx_index, half, 1)).astype(BF16)
+    theirs = swap_x(theirs)
+    theirs = jnp.concatenate([theirs[own_count:], theirs[:own_count]], axis=0)
+    ours = matmul(activated, pick(down_weight[0], ctx_index, half, 1)).astype(BF16)
+    expert_out = (ours.astype(F32) + theirs.astype(F32)).astype(BF16).astype(F32)
+    both_weight = jnp.concatenate([my_weight, other_weight], axis=0)
+    hidden_two = hidden_one + both_weight * expert_out
+
+    squares = jnp.sum(hidden_two * hidden_two, axis=1, keepdims=True)
+    own_squares = squares[:own_count] + swap_x(squares[own_count:])
+    scale = lax.rsqrt(own_squares / width + EPSILON)
+    final_rows = (hidden_two * pick(final_gain, ctx_index, half, 0)).astype(BF16)
+    teacher_part = sum(
+        matmul(part, block, LAST)
+        for part, block in zip(split_relative(final_rows, rep_index, 4, 1), teacher_blocks)
+    )
+    teacher_logits = (teacher_part[:own_count] + swap_x(teacher_part[own_count:])) * scale
+    teacher_logits = line_exchange(teacher_logits)
+
+    teacher_peak = jnp.max(teacher_logits, axis=1, keepdims=True)
+    teacher_lse = teacher_peak + jnp.log(
+        jnp.sum(jnp.exp(teacher_logits - teacher_peak), axis=1, keepdims=True)
+    )
+    logit_gap = learner_logits - teacher_logits
+    mean_gap = jnp.sum(learner_exp * logit_gap, axis=1, keepdims=True) / learner_total
+    divergence = mean_gap - learner_lse + teacher_lse
+    row_pos = ctx_index * pos_ctx + vocab_index * pos_dev + jnp.arange(pos_dev)
+    live = row_pos[None, :] < lengths[:, None]
+    live_sorted = jnp.any(placed & live.reshape(1, -1), axis=1)
+    kl_rows = jnp.sum(jnp.where(placed, divergence, 0.0), axis=0).reshape(seq_dev, pos_dev)
+    row_kl = jnp.where(live, kl_rows, 0.0)
+    learner_prob = jnp.exp(learner_logits - learner_lse)
+    dlogits = jnp.where(
+        live_sorted[:, None], learner_prob * (logit_gap - mean_gap), 0.0
+    ).astype(BF16)
+    dlogits = matmul(placer, dlogits, FIRST).astype(BF16)
+
+    plane_dlogits, other_dlogits = plane_rows(dlogits)
+    head_part = matmul(plane_dlogits, plane_columns, FIRST).astype(BF16)
+    head_grad = line_sum(head_part).astype(BF16)
+
+    other_grad = swap_x(
+        join_absolute(
+            [matmul(other_dlogits, block).astype(BF16) for block in learner_blocks], rep_index, 1
+        )
+    )
+    own_grad = join_absolute(
+        [matmul(dlogits, block).astype(BF16) for block in learner_blocks], rep_index, 1
+    )
+    hidden_grad = join_absolute([own_grad, other_grad], ctx_index, 1)
+    return (hidden_grad.reshape(seq_dev, pos_dev, width), head_grad, row_kl)
+
+
+def per_device_general(
     queries,
     key_value,
     residual,
@@ -215,8 +549,10 @@
         P("vocab", ("ctx", "rep")),
         P("rep"),
     )
+    shape = dict(mesh.shape)
+    swaps = (shape["ctx"], shape["vocab"], shape["rep"]) == (2, 4, 4)
     return jax.shard_map(
-        per_device,
+        per_device if swaps else per_device_general,
         mesh=mesh,
         in_specs=placed,
         out_specs=(

time: 679 us -> 454 us (0.67); the launches traced: 678 us -> 445 us
  waiting for transfers between devices: 513 us -> 227 us
  starting transfers between devices: 5.1 us -> 102 us
  blocking collectives: 58.8 us -> 0 us
  matrix products: 68.2 us -> 42.3 us
  other arithmetic: 16.4 us -> 38.1 us
  local copies, waits for them, and re-layouts: 2.58 us -> 20.2 us
  Pallas kernels: 0 us -> 11.9 us
  between operations: 14 us -> 2.91 us
    all_gather x5 -> x0, waiting for transfers between devices: 262 us -> none  [the longest x1 82.2 us: per_device(): lax.all_gather(learner_hidden, 'vocab', axis=1, tiled=True)]
    ppermute x0 -> x55, waiting for transfers between devices: none -> 227 us  [the longest x15 122 us: swap_x(): return lax.ppermute(value, 'ctx', [(0, 1), (1, 0)])]
    reduce_scatter x4 -> x0, waiting for transfers between devices: 224 us -> none  [the longest x1 79.7 us: per_device(): lax.psum_scatter(jnp.einsum('psv,vd->psd', shard_rows, learner_full, pref...]
    ppermute x0 -> x55, starting transfers between devices: none -> 102 us  [the longest x18 61.1 us: swap_z(): return lax.ppermute(value, 'vocab', [(i, i ^ offset) for i in range(4)])]
    all_to_all x1 -> x0, blocking collectives: 29.9 us -> none  [per_device(): lax.all_to_all(outgoing.reshape(vocab_count, per_expert, width), 'vocab',...]
    dot_general x11 -> x41, matrix products: 68.2 us -> 42.3 us  [matmul(): return lax.dot_general(left, right, dims, preferred_element_type=F32)]
    all_to_all x1 -> x0, waiting for transfers between devices: 25.7 us -> none  [per_device(): lax.all_to_all(expert_out.reshape(vocab_count, per_expert, width), 'vocab...]
    broadcast_in_dim x0 -> x17, other arithmetic: none -> 12.1 us  [the longest x16 12.1 us: project(): added = jnp.where(owner, added.reshape(2, 1, per_expert, -1), 0.0)]
  transfers between devices with their start and end apart: 10 -> 55, of which waited for: 10 -> 25; matrix products, arithmetic and copies ran while one was open for 5% -> 20% of each run, Pallas kernels for 0% -> 3%
where the time goes in v2:
time: 454 us; the launch traced here: 445 us
  waiting for transfers between devices  227 us (50%)
  starting transfers between devices  102 us (22%)
  matrix products  42.3 us (9%)
  other arithmetic  38.1 us (8%)
  local copies, waits for them, and re-layouts  20.2 us (4%)
  Pallas kernels  11.9 us (3%)
    ppermute x15, waiting for transfers between devices, swap_x(): return lax.ppermute(value, 'ctx', [(0, 1), (1, 0)])  122 us
    ppermute x18, waiting for transfers between devices, swap_z(): return lax.ppermute(value, 'vocab', [(i, i ^ offset) for i in range(4)])  73.9 us
    ppermute x18, starting transfers between devices, swap_z(): return lax.ppermute(value, 'vocab', [(i, i ^ offset) for i in range(4)])  61.1 us
    dot_general x41, matrix products, matmul(): return lax.dot_general(left, right, dims, preferred_element_type=F32)  42.3 us
    ppermute x4, waiting for transfers between devices, line_reduce(): outer = lax.ppermute(far, 'vocab', [(0, 1), (3, 2)])  22.7 us
    ppermute x15, starting transfers between devices, swap_x(): return lax.ppermute(value, 'ctx', [(0, 1), (1, 0)])  22.5 us
    broadcast_in_dim x16, other arithmetic, project(): added = jnp.where(owner, added.reshape(2, 1, per_expert, -1), 0.0)  12.1 us
    pallas_call x1, Pallas kernels, attend(): pl.pallas_call(attend_kernel, out_shape=jax.ShapeDtypeStruct((seq_dev * p...  11.9 us
  transfers between devices with their start and end apart: 55, of which 25 were waited for; matrix products, arithmetic and copies ran while one was open for 20% of the time, Pallas kernels for 3%

profile of v2, /device:TPU:0, one launch (start us, length us, event | category | flops | bytes accessed | tf_op | source)
XLA Modules:
  0.0 445.1 jit_solution(4176995840036997334)
XLA Ops:
  0.7 1.9 copy-done
  2.6 3.1 collective-permute-start.32
  5.7 2.6 collective-permute-start.33
  8.3 1.7 constant_dynamic-slice_fusion.18
  9.9 1.7 collective-permute-start.2
  15.1 1.7 convolution_convert_fusion.1
  20.5 10.5 %collective-permute-done = f32[1,2,128]{2,1,0:T(2,128)} collective-permute-done((f32[1,2,128]{2,1,0:T(2,128)S(1)}, f32[1,2,128]{2,1,0:T(2,128)}, u32[]{:S(2)}, u32[]{:S(2)}) %collective-permute-start) | collective-permute-done | bytes 1056 | tf_op jit(solution)/shard_map/ppermute | solution.py:43
  31.7 3.6 collective-permute-start.1
  36.8 1.5 convert.17
  38.3 1.5 convert.18
  49.6 1.9 collective-permute-start.7
  52.6 11.9 %attend.1 = bf16[512,2048]{1,0:T(8,128)(2,1)S(1)} custom-call(s32[4]{0:T(128)S(1)} %pad_add_fusion.facts, bf16[2,256,2048]{2,1,0:T(8,128)(2,1)S(1)} %copy-done.2, bf16[2,2,512,128]{3,2,1,0:T(8,128)(2,1)S(1)} %pad_maximum_fusion.11.rows), custom_call_target="tpu_custom_call" | custom-call | flops 2147483648 | bytes 4194304 | tf_op jit(solution)/shard_map/attend/pallas_call | solution.py:153
  64.5 2.5 collective-permute-start.8
  68.4 1.6 collective-permute-start.9
  70.1 1.6 collective-permute-start.3
  71.7 7.8 %collective-permute-done.7 = bf16[384,512]{1,0:T(8,128)(2,1)S(1)} collective-permute-done((bf16[384,512]{1,0:T(8,128)(2,1)}, bf16[384,512]{1,0:T(8,128)(2,1)S(1)}, u32[]{:S(2)}, u32[]{:S(2)}) %collective-permute-start.7) | collective-permute-done | bytes 393248 | tf_op jit(solution)/shard_map/ppermute | solution.py:43
  81.0 2.7 select_select_fusion.3
  83.9 23.1 %collective-permute-done.22 = bf16[128,2048]{1,0:T(8,128)(2,1)S(1)} collective-permute-done((bf16[128,2048]{1,0:T(8,128)(2,1)S(1)}, bf16[128,2048]{1,0:T(8,128)(2,1)S(1)}, u32[]{:S(2)}, u32[]{:S(2)}) %collective-permute-start.22) | collective-permute-done | bytes 524320 | tf_op jit(solution)/shard_map/ppermute | solution.py:35
  110.3 1.6 collective-permute-start.4
  113.5 1.5 collective-permute-start.11
  122.3 12.9 %collective-permute-done.4 = bf16[256,2048]{1,0:T(8,128)(2,1)S(1)} collective-permute-done((bf16[256,2048]{1,0:T(8,128)(2,1)S(1)}, bf16[256,2048]{1,0:T(8,128)(2,1)S(1)}, u32[]{:S(2)}, u32[]{:S(2)}) %collective-permute-start.4) | collective-permute-done | bytes 1048608 | tf_op jit(solution)/shard_map/ppermute | solution.py:35
  136.8 3.4 collective-permute-done.23
  141.9 1.6 collective-permute-start.5
  143.7 19.0 %collective-permute-start.17 = (bf16[128,1024]{1,0:T(8,128)(2,1)S(1)}, bf16[128,1024]{1,0:T(8,128)(2,1)S(1)}, u32[]{:S(2)}, u32[]{:S(2)}) collective-permute-start(bf16[128,1024]{1,0:T(8,128)(2,1)S(1)} %dynamic-slice_convert_fusion.3), channel_id=1, source_target_pairs={{0,4},{4,0},{8,12},{12,8},{1,5},{5,1},{9,13},{13,9},{2,6},{6,2},{1... | collective-permute-start | bytes 786440 | tf_op jit(solution)/shard_map/ppermute | solution.py:43
  162.9 6.0 %collective-permute-done.17 = bf16[128,1024]{1,0:T(8,128)(2,1)S(1)} collective-permute-done((bf16[128,1024]{1,0:T(8,128)(2,1)S(1)}, bf16[128,1024]{1,0:T(8,128)(2,1)S(1)}, u32[]{:S(2)}, u32[]{:S(2)}) %collective-permute-start.17) | collective-permute-done | bytes 262176 | tf_op jit(solution)/shard_map/ppermute | solution.py:43
  168.9 1.7 collective-permute-start.25
  171.4 4.8 %collective-permute-done.25 = bf16[128,1024]{1,0:T(8,128)(2,1)S(1)} collective-permute-done((bf16[128,1024]{1,0:T(8,128)(2,1)S(1)}, bf16[128,1024]{1,0:T(8,128)(2,1)S(1)}, u32[]{:S(2)}, u32[]{:S(2)}) %collective-permute-start.25) | collective-permute-done | bytes 262176 | tf_op jit(solution)/shard_map/ppermute | solution.py:43
  180.2 3.4 collective-permute-start.19
  186.4 9.4 %collective-permute-done.19 = bf16[256,1024]{1,0:T(8,128)(2,1)S(1)} collective-permute-done((bf16[256,1024]{1,0:T(8,128)(2,1)S(1)}, bf16[256,1024]{1,0:T(8,128)(2,1)S(1)}, u32[]{:S(2)}, u32[]{:S(2)}) %collective-permute-start.19) | collective-permute-done | bytes 524320 | tf_op jit(solution)/shard_map/ppermute | solution.py:92
  196.6 10.0 %collective-permute-done.26 = bf16[256,1024]{1,0:T(8,128)(2,1)S(1)} collective-permute-done((bf16[256,1024]{1,0:T(8,128)(2,1)S(1)}, bf16[256,1024]{1,0:T(8,128)(2,1)S(1)}, u32[]{:S(2)}, u32[]{:S(2)}) %collective-permute-start.26) | collective-permute-done | bytes 524320 | tf_op jit(solution)/shard_map/ppermute | solution.py:92
  208.6 5.1 %collective-permute-start.21 = (bf16[128,1024]{1,0:T(8,128)(2,1)S(1)}, bf16[128,1024]{1,0:T(8,128)(2,1)S(1)}, u32[]{:S(2)}, u32[]{:S(2)}) collective-permute-start(bf16[128,1024]{1,0:T(8,128)(2,1)S(1)} %dynamic-slice_convert_fusion.2), channel_id=1, source_target_pairs={{0,4},{4,0},{8,12},{12,8},{1,5},{5,1},{9,13},{13,9},{2,6},{6,2},{1... | collective-permute-start | bytes 786440 | tf_op jit(solution)/shard_map/ppermute | solution.py:43
  213.9 11.0 %collective-permute-start.28 = (bf16[128,1024]{1,0:T(8,128)(2,1)S(1)}, bf16[128,1024]{1,0:T(8,128)(2,1)S(1)}, u32[]{:S(2)}, u32[]{:S(2)}) collective-permute-start(bf16[128,1024]{1,0:T(8,128)(2,1)S(1)} %dynamic-slice_convert_fusion), channel_id=1, source_target_pairs={{0,4},{4,0},{8,12},{12,8},{1,5},{5,1},{9,13},{13,9},{2,6},{6,2},{1... | collective-permute-start | bytes 786440 | tf_op jit(solution)/shard_map/ppermute | solution.py:43
  232.3 1.6 collective-permute-start.30
  233.8 2.7 pad_maximum_fusion.2
  237.2 10.8 %collective-permute-done.13 = f32[128,1536]{1,0:T(8,128)} collective-permute-done((f32[128,1536]{1,0:T(8,128)}, f32[128,1536]{1,0:T(8,128)}, u32[]{:S(2)}, u32[]{:S(2)}) %collective-permute-start.13) | collective-permute-done | bytes 786464 | tf_op jit(solution)/shard_map/ppermute | solution.py:35
  247.9 2.1 fusion.108
  250.0 17.8 %collective-permute-done.30 = bf16[256,2048]{1,0:T(8,128)(2,1)} collective-permute-done((bf16[256,2048]{1,0:T(8,128)(2,1)}, bf16[256,2048]{1,0:T(8,128)(2,1)}, u32[]{:S(2)}, u32[]{:S(2)}) %collective-permute-start.30) | collective-permute-done | bytes 1048608 | tf_op jit(solution)/shard_map/ppermute | solution.py:35
  270.4 5.0 %fusion.2 = f32[256,768]{1,0:T(8,128)S(1)} fusion(bf16[1,768,4096]{2,1,0:T(8,128)(2,1)} %param.22, f32[4096]{0:T(1024)S(1)} %copy-done.58, f32[256]{0:T(256)S(1)} %add_rsqrt_fusion, bf16[256,2048]{1,0:T(8,128)(2,1)S(1)} %get-tuple-element.30, bf16[256,2048]{1,0:T(8,128)(2,1)S(1)} %get-tuple-element.29), kind=kOutput, calls=%fused_computation.2 | convolution fusion | flops 1617952768 | bytes 9192448 | tf_op jit(solution)/shard_map/dot_general | solution.py:22
  275.5 2.0 fusion.26
  277.5 2.0 fusion.17
  283.9 1.6 collective-permute-start.29
  285.4 28.3 %collective-permute-done.29 = f32[128,1]{0,1:T(1,128)S(1)} collective-permute-done((f32[128,1]{0,1:T(1,128)S(1)}, f32[128,1]{0,1:T(1,128)S(1)}, u32[]{:S(2)}, u32[]{:S(2)}) %collective-permute-start.29) | collective-permute-done | bytes 544 | tf_op jit(solution)/shard_map/ppermute | solution.py:35
  318.0 3.3 multiply_reduce_fusion
  321.4 2.1 fusion.67
  324.2 2.0 convolution_add_fusion.1
  326.9 1.8 collective-permute-start.38
  329.5 1.6 collective-permute-start.39
  331.2 15.7 %collective-permute-done.39 = f32[128,1]{0,1:T(1,128)S(1)} collective-permute-done((f32[128,1]{0,1:T(1,128)S(1)}, f32[128,1]{0,1:T(1,128)S(1)}, u32[]{:S(2)}, u32[]{:S(2)}) %collective-permute-start.39) | collective-permute-done | bytes 544 | tf_op jit(solution)/shard_map/ppermute | solution.py:35
  349.3 2.4 collective-permute-start.42
  352.7 3.7 collective-permute-done.40
  356.4 8.2 %collective-permute-done.41 = f32[32,1536]{1,0:T(8,128)S(1)} collective-permute-done((f32[32,1536]{1,0:T(8,128)S(1)}, f32[32,1536]{1,0:T(8,128)S(1)}, u32[]{:S(2)}, u32[]{:S(2)}) %collective-permute-start.41) | collective-permute-done | bytes 196640 | tf_op jit(solution)/shard_map/ppermute | solution.py:43
  367.8 1.8 constant_dynamic-update-slice_fusion.4
  369.6 1.7 collective-permute-start.45
  373.5 5.1 %collective-permute-done.45 = bf16[128,1536]{1,0:T(8,128)(2,1)S(1)} collective-permute-done((bf16[128,1536]{1,0:T(8,128)(2,1)S(1)}, bf16[128,1536]{1,0:T(8,128)(2,1)S(1)}, u32[]{:S(2)}, u32[]{:S(2)}) %collective-permute-start.45) | collective-permute-done | bytes 393248 | tf_op jit(solution)/shard_map/ppermute | solution.py:39
  378.7 1.6 collective-permute-start.46
  380.8 1.9 collective-permute-start.47
  384.4 2.2 collective-permute-done.47
  387.2 1.6 collective-permute-start.44
  389.5 12.0 %collective-permute-done.44 = bf16[128,2048]{1,0:T(8,128)(2,1)S(1)} collective-permute-done((bf16[128,2048]{1,0:T(8,128)(2,1)S(1)}, bf16[128,2048]{1,0:T(8,128)(2,1)S(1)}, u32[]{:S(2)}, u32[]{:S(2)}) %collective-permute-start.44) | collective-permute-done | bytes 524320 | tf_op jit(solution)/shard_map/ppermute | solution.py:35
  402.8 2.9 convolution_convert_fusion.2
  405.8 2.1 collective-permute-start.52
  407.9 3.2 collective-permute-start.53
  412.1 7.7 %collective-permute-done.52 = bf16[384,512]{1,0:T(8,128)(2,1)S(1)} collective-permute-done((bf16[384,512]{1,0:T(8,128)(2,1)S(1)}, bf16[384,512]{1,0:T(8,128)(2,1)S(1)}, u32[]{:S(2)}, u32[]{:S(2)}) %collective-permute-start.52) | collective-permute-done | bytes 393248 | tf_op jit(solution)/shard_map/ppermute | solution.py:43
  419.8 23.8 %collective-permute-done.53 = bf16[384,512]{1,0:T(8,128)(2,1)S(1)} collective-permute-done((bf16[384,512]{1,0:T(8,128)(2,1)S(1)}, bf16[384,512]{1,0:T(8,128)(2,1)S(1)}, u32[]{:S(2)}, u32[]{:S(2)}) %collective-permute-start.53) | collective-permute-done | bytes 393248 | tf_op jit(solution)/shard_map/ppermute | solution.py:43
  (342 shorter events, 85.8 us)
Async XLA Ops:
  2.6 61.9 %collective-permute-start.32 = (bf16[384,512]{1,0:T(8,128)(2,1)S(1)}, bf16[384,512]{1,0:T(8,128)(2,1)}, u32[]{:S(2)}, u32[]{:S(2)}) collective-permute-start(bf16[384,512]{1,0:T(8,128)(2,1)S(1)} %constant_dynamic-slice_fusion.14), channel_id=1, source_target_pairs={{0,4},{4,0},{8,12},{12,8},{1,5},{5,1},{9,13},{13,9},{2,6},{6,2},{1... | collective-permute-start | bytes 1179656 | tf_op jit(solution)/shard_map/ppermute | solution.py:43
  5.7 62.7 %collective-permute-start.33 = (bf16[384,512]{1,0:T(8,128)(2,1)S(1)}, bf16[384,512]{1,0:T(8,128)(2,1)}, u32[]{:S(2)}, u32[]{:S(2)}) collective-permute-start(bf16[384,512]{1,0:T(8,128)(2,1)S(1)} %constant_dynamic-slice_fusion.14), channel_id=1, source_target_pairs={{0,8},{4,12},{8,0},{12,4},{1,9},{5,13},{9,1},{13,5},{2,10},{6,14},... | collective-permute-start | bytes 1179656 | tf_op jit(solution)/shard_map/ppermute | solution.py:43
  8.2 61.7 %collective-permute-start.34 = (bf16[384,512]{1,0:T(8,128)(2,1)S(1)}, bf16[384,512]{1,0:T(8,128)(2,1)}, u32[]{:S(2)}, u32[]{:S(2)}) collective-permute-start(bf16[384,512]{1,0:T(8,128)(2,1)S(1)} %constant_dynamic-slice_fusion.14), channel_id=1, source_target_pairs={{0,12},{4,8},{8,4},{12,0},{1,13},{5,9},{9,5},{13,1},{2,14},{6,10},... | collective-permute-start | bytes 1179656 | tf_op jit(solution)/shard_map/ppermute | solution.py:43
  9.9 39.7 %collective-permute-start.2 = (bf16[2,2,256,128]{3,2,1,0:T(8,128)(2,1)}, bf16[2,2,256,128]{3,2,1,0:T(8,128)(2,1)}, u32[]{:S(2)}, u32[]{:S(2)}) collective-permute-start(bf16[2,2,256,128]{3,2,1,0:T(8,128)(2,1)} %constant_dynamic-slice_fusion.18), channel_id=1, source_target_pairs={{0,16},{16,0},{1,17},{17,1},{2,18},{18,2},{3,19},{19,3},{4,20},{20... | collective-permute-start | bytes 786440 | tf_op jit(solution)/shard_map/ppermute | solution.py:35
  13.8 17.2 %collective-permute-start = (f32[1,2,128]{2,1,0:T(2,128)S(1)}, f32[1,2,128]{2,1,0:T(2,128)}, u32[]{:S(2)}, u32[]{:S(2)}) collective-permute-start(f32[1,2,128]{2,1,0:T(2,128)S(1)} %maximum_bitcast_fusion), channel_id=1, source_target_pairs={{0,4},{4,0},{8,12},{12,8},{1,5},{5,1},{9,13},{13,9},{2,6},{6,2},{1... | collective-permute-start | bytes 3080 | tf_op jit(solution)/shard_map/ppermute | solution.py:43
  19.2 33.3 %copy-start.2 = (bf16[2,256,2048]{2,1,0:T(8,128)(2,1)S(1)}, bf16[2,256,2048]{2,1,0:T(8,128)(2,1)}, u32[]{:S(2)}) copy-start(bf16[2,256,2048]{2,1,0:T(8,128)(2,1)} %query.1) | copy-start | bytes 6291460
  31.7 16.5 %collective-permute-start.1 = (f32[2,2,128]{2,1,0:T(2,128)S(1)}, f32[2,2,128]{2,1,0:T(2,128)S(1)}, u32[]{:S(2)}, u32[]{:S(2)}) collective-permute-start(f32[2,2,128]{2,1,0:T(2,128)S(1)} %pad_maximum_fusion.20), channel_id=1, source_target_pairs={{0,8},{4,12},{8,0},{12,4},{1,9},{5,13},{9,1},{13,5},{2,10},{6,14},... | collective-permute-start | bytes 6152 | tf_op jit(solution)/shard_map/ppermute | solution.py:43
  48.1 22.0 %collective-permute-start.6 = (bf16[384,512]{1,0:T(8,128)(2,1)}, bf16[384,512]{1,0:T(8,128)(2,1)S(1)}, u32[]{:S(2)}, u32[]{:S(2)}) collective-permute-start(bf16[384,512]{1,0:T(8,128)(2,1)} %param.28), channel_id=1, source_target_pairs={{0,4},{4,0},{8,12},{12,8},{1,5},{5,1},{9,13},{13,9},{2,6},{6,2},{1... | collective-permute-start | bytes 1179656 | tf_op jit(solution)/shard_map/ppermute | solution.py:43
  49.6 29.9 %collective-permute-start.7 = (bf16[384,512]{1,0:T(8,128)(2,1)}, bf16[384,512]{1,0:T(8,128)(2,1)S(1)}, u32[]{:S(2)}, u32[]{:S(2)}) collective-permute-start(bf16[384,512]{1,0:T(8,128)(2,1)} %param.28), channel_id=1, source_target_pairs={{0,8},{4,12},{8,0},{12,4},{1,9},{5,13},{9,1},{13,5},{2,10},{6,14},... | collective-permute-start | bytes 1179656 | tf_op jit(solution)/shard_map/ppermute | solution.py:43
  64.5 16.4 %collective-permute-start.8 = (bf16[384,512]{1,0:T(8,128)(2,1)S(1)}, bf16[384,512]{1,0:T(8,128)(2,1)S(1)}, u32[]{:S(2)}, u32[]{:S(2)}) collective-permute-start(bf16[384,512]{1,0:T(8,128)(2,1)S(1)} %copy-done.52), channel_id=1, source_target_pairs={{0,12},{4,8},{8,4},{12,0},{1,13},{5,9},{9,5},{13,1},{2,14},{6,10},... | collective-permute-start | bytes 1179656 | tf_op jit(solution)/shard_map/ppermute | solution.py:43
  68.4 45.1 %collective-permute-start.9 = (bf16[2048,512]{1,0:T(8,128)(2,1)S(1)}, bf16[2048,512]{1,0:T(8,128)(2,1)S(1)}, u32[]{:S(2)}, u32[]{:S(2)}) collective-permute-start(bf16[2048,512]{1,0:T(8,128)(2,1)S(1)} %copy-done.57), channel_id=1, source_target_pairs={{0,2},{1,3},{2,0},{3,1},{4,6},{5,7},{6,4},{7,5},{8,10},{9,11},{10,... | collective-permute-start | bytes 6291464 | tf_op jit(solution)/shard_map/ppermute | solution.py:39
  70.0 45.1 %collective-permute-start.14 = (bf16[2048,512]{1,0:T(8,128)(2,1)S(1)}, bf16[2048,512]{1,0:T(8,128)(2,1)S(1)}, u32[]{:S(2)}, u32[]{:S(2)}) collective-permute-start(bf16[2048,512]{1,0:T(8,128)(2,1)S(1)} %copy-done.57), channel_id=1, source_target_pairs={{0,1},{1,0},{2,3},{3,2},{4,5},{5,4},{6,7},{7,6},{8,9},{9,8},{10,11... | collective-permute-start | bytes 6291464 | tf_op jit(solution)/shard_map/ppermute | solution.py:39
  70.1 40.2 %collective-permute-start.3 = (bf16[256,2048]{1,0:T(8,128)(2,1)S(1)}, bf16[256,2048]{1,0:T(8,128)(2,1)S(1)}, u32[]{:S(2)}, u32[]{:S(2)}) collective-permute-start(bf16[256,2048]{1,0:T(8,128)(2,1)S(1)} %get-tuple-element.31), channel_id=1, source_target_pairs={{0,16},{16,0},{1,17},{17,1},{2,18},{18,2},{3,19},{19,3},{4,20},{20... | collective-permute-start | bytes 3145736 | tf_op jit(solution)/shard_map/ppermute | solution.py:35
  79.5 27.5 %collective-permute-start.22 = (bf16[128,2048]{1,0:T(8,128)(2,1)S(1)}, bf16[128,2048]{1,0:T(8,128)(2,1)S(1)}, u32[]{:S(2)}, u32[]{:S(2)}) collective-permute-start(bf16[128,2048]{1,0:T(8,128)(2,1)S(1)} %copy-done.49), channel_id=1, source_target_pairs={{0,16},{16,0},{1,17},{17,1},{2,18},{18,2},{3,19},{19,3},{4,20},{20... | collective-permute-start | bytes 1572872 | tf_op jit(solution)/shard_map/ppermute | solution.py:35
  110.3 24.9 %collective-permute-start.4 = (bf16[256,2048]{1,0:T(8,128)(2,1)S(1)}, bf16[256,2048]{1,0:T(8,128)(2,1)S(1)}, u32[]{:S(2)}, u32[]{:S(2)}) collective-permute-start(bf16[256,2048]{1,0:T(8,128)(2,1)S(1)} %get-tuple-element.9), channel_id=1, source_target_pairs={{0,16},{16,0},{1,17},{17,1},{2,18},{18,2},{3,19},{19,3},{4,20},{20... | collective-permute-start | bytes 3145736 | tf_op jit(solution)/shard_map/ppermute | solution.py:35
  113.5 63.5 %collective-permute-start.10 = (bf16[1536,512]{1,0:T(8,128)(2,1)S(1)}, bf16[1536,512]{1,0:T(8,128)(2,1)S(1)}, u32[]{:S(2)}, u32[]{:S(2)}) collective-permute-start(bf16[1536,512]{1,0:T(8,128)(2,1)S(1)} %pad_maximum_fusion.1), channel_id=1, source_target_pairs={{0,1},{1,0},{2,3},{3,2},{4,5},{5,4},{6,7},{7,6},{8,9},{9,8},{10,11... | collective-permute-start | bytes 4718600 | tf_op jit(solution)/shard_map/ppermute | solution.py:39
  113.5 62.8 %collective-permute-start.11 = (bf16[1536,512]{1,0:T(8,128)(2,1)S(1)}, bf16[1536,512]{1,0:T(8,128)(2,1)S(1)}, u32[]{:S(2)}, u32[]{:S(2)}) collective-permute-start(bf16[1536,512]{1,0:T(8,128)(2,1)S(1)} %pad_maximum_fusion.1), channel_id=1, source_target_pairs={{0,2},{1,3},{2,0},{3,1},{4,6},{5,7},{6,4},{7,5},{8,10},{9,11},{10,... | collective-permute-start | bytes 4718600 | tf_op jit(solution)/shard_map/ppermute | solution.py:39
  115.8 20.1 %collective-permute-start.15 = (bf16[256,1024]{1,0:T(8,128)(2,1)S(1)}, bf16[256,1024]{1,0:T(8,128)(2,1)S(1)}, u32[]{:S(2)}, u32[]{:S(2)}) collective-permute-start(bf16[256,1024]{1,0:T(8,128)(2,1)S(1)} %pad_maximum_fusion.12), channel_id=1, source_target_pairs={{0,4},{12,8},{1,5},{13,9},{2,6},{14,10},{3,7},{15,11},{16,20},{28,... | collective-permute-start | bytes 1572872 | tf_op jit(solution)/shard_map/ppermute | solution.py:92
  118.0 22.2 %collective-permute-start.23 = (bf16[256,1024]{1,0:T(8,128)(2,1)S(1)}, bf16[256,1024]{1,0:T(8,128)(2,1)S(1)}, u32[]{:S(2)}, u32[]{:S(2)}) collective-permute-start(bf16[256,1024]{1,0:T(8,128)(2,1)S(1)} %pad_maximum_fusion.14), channel_id=1, source_target_pairs={{0,4},{12,8},{1,5},{13,9},{2,6},{14,10},{3,7},{15,11},{16,20},{28,... | collective-permute-start | bytes 1572872 | tf_op jit(solution)/shard_map/ppermute | solution.py:92
  135.2 44.2 %collective-permute-start.18 = (bf16[2048,512]{1,0:T(8,128)(2,1)S(1)}, bf16[2048,512]{1,0:T(8,128)(2,1)S(1)}, u32[]{:S(2)}, u32[]{:S(2)}) collective-permute-start(bf16[2048,512]{1,0:T(8,128)(2,1)S(1)} %collective-permute-done.9), channel_id=1, source_target_pairs={{0,1},{1,0},{2,3},{3,2},{4,5},{5,4},{6,7},{7,6},{8,9},{9,8},{10,11... | collective-permute-start | bytes 6291464 | tf_op jit(solution)/shard_map/ppermute | solution.py:39
  136.1 5.8 %collective-permute-start.16 = (bf16[256,1024]{1,0:T(8,128)(2,1)S(1)}, bf16[256,1024]{1,0:T(8,128)(2,1)S(1)}, u32[]{:S(2)}, u32[]{:S(2)}) collective-permute-start(bf16[256,1024]{1,0:T(8,128)(2,1)S(1)} %add_convert_fusion.4), channel_id=1, source_target_pairs={{4,8},{8,4},{5,9},{9,5},{6,10},{10,6},{7,11},{11,7},{20,24},{24,20... | collective-permute-start | bytes 1572872 | tf_op jit(solution)/shard_map/ppermute | solution.py:94
  140.4 3.3 collective-permute-start.24
  141.9 34.5 %collective-permute-start.5 = (bf16[128,2048]{1,0:T(8,128)(2,1)S(1)}, bf16[128,2048]{1,0:T(8,128)(2,1)S(1)}, u32[]{:S(2)}, u32[]{:S(2)}) collective-permute-start(bf16[128,2048]{1,0:T(8,128)(2,1)S(1)} %copy-done.50), channel_id=1, source_target_pairs={{0,16},{16,0},{1,17},{17,1},{2,18},{18,2},{3,19},{19,3},{4,20},{20... | collective-permute-start | bytes 1572872 | tf_op jit(solution)/shard_map/ppermute | solution.py:35
  143.7 25.2 %collective-permute-start.17 = (bf16[128,1024]{1,0:T(8,128)(2,1)S(1)}, bf16[128,1024]{1,0:T(8,128)(2,1)S(1)}, u32[]{:S(2)}, u32[]{:S(2)}) collective-permute-start(bf16[128,1024]{1,0:T(8,128)(2,1)S(1)} %dynamic-slice_convert_fusion.3), channel_id=1, source_target_pairs={{0,4},{4,0},{8,12},{12,8},{1,5},{5,1},{9,13},{13,9},{2,6},{6,2},{1... | collective-permute-start | bytes 786440 | tf_op jit(solution)/shard_map/ppermute | solution.py:43
  168.9 7.4 %collective-permute-start.25 = (bf16[128,1024]{1,0:T(8,128)(2,1)S(1)}, bf16[128,1024]{1,0:T(8,128)(2,1)S(1)}, u32[]{:S(2)}, u32[]{:S(2)}) collective-permute-start(bf16[128,1024]{1,0:T(8,128)(2,1)S(1)} %dynamic-slice_convert_fusion.1), channel_id=1, source_target_pairs={{0,4},{4,0},{8,12},{12,8},{1,5},{5,1},{9,13},{13,9},{2,6},{6,2},{1... | collective-permute-start | bytes 786440 | tf_op jit(solution)/shard_map/ppermute | solution.py:43
  176.3 48.6 %collective-permute-start.12 = (bf16[1536,512]{1,0:T(8,128)(2,1)S(1)}, bf16[1536,512]{1,0:T(8,128)(2,1)S(1)}, u32[]{:S(2)}, u32[]{:S(2)}) collective-permute-start(bf16[1536,512]{1,0:T(8,128)(2,1)S(1)} %collective-permute-done.11), channel_id=1, source_target_pairs={{0,1},{1,0},{2,3},{3,2},{4,5},{5,4},{6,7},{7,6},{8,9},{9,8},{10,11... | collective-permute-start | bytes 4718600 | tf_op jit(solution)/shard_map/ppermute | solution.py:39
  180.2 15.5 %collective-permute-start.19 = (bf16[256,1024]{1,0:T(8,128)(2,1)S(1)}, bf16[256,1024]{1,0:T(8,128)(2,1)S(1)}, u32[]{:S(2)}, u32[]{:S(2)}) collective-permute-start(bf16[256,1024]{1,0:T(8,128)(2,1)S(1)} %pad_maximum_fusion.13), channel_id=1, source_target_pairs={{0,4},{12,8},{1,5},{13,9},{2,6},{14,10},{3,7},{15,11},{16,20},{28,... | collective-permute-start | bytes 1572872 | tf_op jit(solution)/shard_map/ppermute | solution.py:92
  184.3 22.2 %collective-permute-start.26 = (bf16[256,1024]{1,0:T(8,128)(2,1)S(1)}, bf16[256,1024]{1,0:T(8,128)(2,1)S(1)}, u32[]{:S(2)}, u32[]{:S(2)}) collective-permute-start(bf16[256,1024]{1,0:T(8,128)(2,1)S(1)} %pad_maximum_fusion.15), channel_id=1, source_target_pairs={{0,4},{12,8},{1,5},{13,9},{2,6},{14,10},{3,7},{15,11},{16,20},{28,... | collective-permute-start | bytes 1572872 | tf_op jit(solution)/shard_map/ppermute | solution.py:92
  195.9 12.5 %collective-permute-start.20 = (bf16[256,1024]{1,0:T(8,128)(2,1)S(1)}, bf16[256,1024]{1,0:T(8,128)(2,1)S(1)}, u32[]{:S(2)}, u32[]{:S(2)}) collective-permute-start(bf16[256,1024]{1,0:T(8,128)(2,1)S(1)} %add_convert_fusion.3), channel_id=1, source_target_pairs={{4,8},{8,4},{5,9},{9,5},{6,10},{10,6},{7,11},{11,7},{20,24},{24,20... | collective-permute-start | bytes 1572872 | tf_op jit(solution)/shard_map/ppermute | solution.py:94
  206.7 6.9 %collective-permute-start.27 = (bf16[256,1024]{1,0:T(8,128)(2,1)S(1)}, bf16[256,1024]{1,0:T(8,128)(2,1)S(1)}, u32[]{:S(2)}, u32[]{:S(2)}) collective-permute-start(bf16[256,1024]{1,0:T(8,128)(2,1)S(1)} %add_convert_fusion.1), channel_id=1, source_target_pairs={{4,8},{8,4},{5,9},{9,5},{6,10},{10,6},{7,11},{11,7},{20,24},{24,20... | collective-permute-start | bytes 1572872 | tf_op jit(solution)/shard_map/ppermute | solution.py:94
  208.6 20.0 %collective-permute-start.21 = (bf16[128,1024]{1,0:T(8,128)(2,1)S(1)}, bf16[128,1024]{1,0:T(8,128)(2,1)S(1)}, u32[]{:S(2)}, u32[]{:S(2)}) collective-permute-start(bf16[128,1024]{1,0:T(8,128)(2,1)S(1)} %dynamic-slice_convert_fusion.2), channel_id=1, source_target_pairs={{0,4},{4,0},{8,12},{12,8},{1,5},{5,1},{9,13},{13,9},{2,6},{6,2},{1... | collective-permute-start | bytes 786440 | tf_op jit(solution)/shard_map/ppermute | solution.py:43
  213.9 16.3 %collective-permute-start.28 = (bf16[128,1024]{1,0:T(8,128)(2,1)S(1)}, bf16[128,1024]{1,0:T(8,128)(2,1)S(1)}, u32[]{:S(2)}, u32[]{:S(2)}) collective-permute-start(bf16[128,1024]{1,0:T(8,128)(2,1)S(1)} %dynamic-slice_convert_fusion), channel_id=1, source_target_pairs={{0,4},{4,0},{8,12},{12,8},{1,5},{5,1},{9,13},{13,9},{2,6},{6,2},{1... | collective-permute-start | bytes 786440 | tf_op jit(solution)/shard_map/ppermute | solution.py:43
  227.1 20.8 %collective-permute-start.13 = (f32[128,1536]{1,0:T(8,128)}, f32[128,1536]{1,0:T(8,128)}, u32[]{:S(2)}, u32[]{:S(2)}) collective-permute-start(f32[128,1536]{1,0:T(8,128)} %slice.98), channel_id=1, source_target_pairs={{0,16},{16,0},{1,17},{17,1},{2,18},{18,2},{3,19},{19,3},{4,20},{20... | collective-permute-start | bytes 2359304 | tf_op jit(solution)/shard_map/ppermute | solution.py:35
  232.3 35.6 %collective-permute-start.30 = (bf16[256,2048]{1,0:T(8,128)(2,1)}, bf16[256,2048]{1,0:T(8,128)(2,1)}, u32[]{:S(2)}, u32[]{:S(2)}) collective-permute-start(bf16[256,2048]{1,0:T(8,128)(2,1)} %fusion.107), channel_id=1, source_target_pairs={{0,16},{16,0},{1,17},{17,1},{2,18},{18,2},{3,19},{19,3},{4,20},{20... | collective-permute-start | bytes 3145736 | tf_op jit(solution)/shard_map/ppermute | solution.py:35
  236.6 32.6 %copy-start.11 = (f32[128,512]{1,0:T(8,128)S(1)}, f32[128,512]{1,0:T(8,128)}, u32[]{:S(2)}) copy-start(f32[128,512]{1,0:T(8,128)} %copy-done.10) | copy-start | bytes 786436
  236.6 32.6 %copy-start.14 = (f32[128,512]{1,0:T(8,128)S(1)}, f32[128,512]{1,0:T(8,128)}, u32[]{:S(2)}) copy-start(f32[128,512]{1,0:T(8,128)} %copy-done.13) | copy-start | bytes 786436
  236.6 32.6 %copy-start.17 = (f32[128,512]{1,0:T(8,128)S(1)}, f32[128,512]{1,0:T(8,128)}, u32[]{:S(2)}) copy-start(f32[128,512]{1,0:T(8,128)} %copy-done.16) | copy-start | bytes 786436
  236.6 32.6 %copy-start.20 = (f32[128,512]{1,0:T(8,128)S(1)}, f32[128,512]{1,0:T(8,128)}, u32[]{:S(2)}) copy-start(f32[128,512]{1,0:T(8,128)} %copy-done.19) | copy-start | bytes 786436
  236.6 32.6 %copy-start.23 = (f32[128,512]{1,0:T(8,128)S(1)}, f32[128,512]{1,0:T(8,128)}, u32[]{:S(2)}) copy-start(f32[128,512]{1,0:T(8,128)} %copy-done.22) | copy-start | bytes 786436
  236.6 32.6 %copy-start.26 = (f32[128,512]{1,0:T(8,128)S(1)}, f32[128,512]{1,0:T(8,128)}, u32[]{:S(2)}) copy-start(f32[128,512]{1,0:T(8,128)} %copy-done.25) | copy-start | bytes 786436
  236.6 32.6 %copy-start.29 = (f32[128,512]{1,0:T(8,128)S(1)}, f32[128,512]{1,0:T(8,128)}, u32[]{:S(2)}) copy-start(f32[128,512]{1,0:T(8,128)} %copy-done.28) | copy-start | bytes 786436
  236.6 77.1 %collective-permute-start.36 = (bf16[1536,512]{1,0:T(8,128)(2,1)}, bf16[1536,512]{1,0:T(8,128)(2,1)}, u32[]{:S(2)}, u32[]{:S(2)}) collective-permute-start(bf16[1536,512]{1,0:T(8,128)(2,1)} %pad_maximum_fusion.2), channel_id=1, source_target_pairs={{0,2},{1,3},{2,0},{3,1},{4,6},{5,7},{6,4},{7,5},{8,10},{9,11},{10,... | collective-permute-start | bytes 4718600 | tf_op jit(solution)/shard_map/ppermute | solution.py:39
  279.5 37.2 %collective-permute-start.31 = (bf16[256,2048]{1,0:T(8,128)(2,1)}, bf16[256,2048]{1,0:T(8,128)(2,1)}, u32[]{:S(2)}, u32[]{:S(2)}) collective-permute-start(bf16[256,2048]{1,0:T(8,128)(2,1)} %fusion.17), channel_id=1, source_target_pairs={{0,16},{16,0},{1,17},{17,1},{2,18},{18,2},{3,19},{19,3},{4,20},{20... | collective-permute-start | bytes 3145736 | tf_op jit(solution)/shard_map/ppermute | solution.py:35
  282.6 31.2 %collective-permute-start.49 = (bf16[128,2048]{1,0:T(8,128)(2,1)}, bf16[128,2048]{1,0:T(8,128)(2,1)}, u32[]{:S(2)}, u32[]{:S(2)}) collective-permute-start(bf16[128,2048]{1,0:T(8,128)(2,1)} %pad_maximum_fusion.18), channel_id=1, source_target_pairs={{0,16},{16,0},{1,17},{17,1},{2,18},{18,2},{3,19},{19,3},{4,20},{20... | collective-permute-start | bytes 1572872 | tf_op jit(solution)/shard_map/ppermute | solution.py:35
  283.2 38.2 %collective-permute-start.35 = (bf16[1536,512]{1,0:T(8,128)(2,1)}, bf16[1536,512]{1,0:T(8,128)(2,1)}, u32[]{:S(2)}, u32[]{:S(2)}) collective-permute-start(bf16[1536,512]{1,0:T(8,128)(2,1)} %pad_maximum_fusion.2), channel_id=1, source_target_pairs={{0,1},{1,0},{2,3},{3,2},{4,5},{5,4},{6,7},{7,6},{8,9},{9,8},{10,11... | collective-permute-start | bytes 4718600 | tf_op jit(solution)/shard_map/ppermute | solution.py:39
  283.9 29.8 %collective-permute-start.29 = (f32[128,1]{0,1:T(1,128)S(1)}, f32[128,1]{0,1:T(1,128)S(1)}, u32[]{:S(2)}, u32[]{:S(2)}) collective-permute-start(f32[128,1]{0,1:T(1,128)S(1)} %bitcast.208), channel_id=1, source_target_pairs={{0,16},{16,0},{1,17},{17,1},{2,18},{18,2},{3,19},{19,3},{4,20},{20... | collective-permute-start | bytes 1544 | tf_op jit(solution)/shard_map/ppermute | solution.py:35
  313.7 12.5 %collective-permute-start.37 = (bf16[1536,512]{1,0:T(8,128)(2,1)}, bf16[1536,512]{1,0:T(8,128)(2,1)S(1)}, u32[]{:S(2)}, u32[]{:S(2)}) collective-permute-start(bf16[1536,512]{1,0:T(8,128)(2,1)} %collective-permute-done.36), channel_id=1, source_target_pairs={{0,1},{1,0},{2,3},{3,2},{4,5},{5,4},{6,7},{7,6},{8,9},{9,8},{10,11... | collective-permute-start | bytes 4718600 | tf_op jit(solution)/shard_map/ppermute | solution.py:39
  315.1 14.4 %collective-permute-start.50 = (bf16[256,1024]{1,0:T(8,128)(2,1)S(1)}, bf16[256,1024]{1,0:T(8,128)(2,1)S(1)}, u32[]{:S(2)}, u32[]{:S(2)}) collective-permute-start(bf16[256,1024]{1,0:T(8,128)(2,1)S(1)} %pad_maximum_fusion.7), channel_id=1, source_target_pairs={{0,2},{1,3},{2,0},{3,1},{4,6},{5,7},{6,4},{7,5},{8,10},{9,11},{10,... | collective-permute-start | bytes 1572872 | tf_op jit(solution)/shard_map/ppermute | solution.py:39
  326.9 20.0 %collective-permute-start.38 = (f32[128,1536]{1,0:T(8,128)S(1)}, f32[128,1536]{1,0:T(8,128)S(1)}, u32[]{:S(2)}, u32[]{:S(2)}) collective-permute-start(f32[128,1536]{1,0:T(8,128)S(1)} %slice.104), channel_id=1, source_target_pairs={{0,16},{16,0},{1,17},{17,1},{2,18},{18,2},{3,19},{19,3},{4,20},{20... | collective-permute-start | bytes 2359304 | tf_op jit(solution)/shard_map/ppermute | solution.py:35
  329.5 17.4 %collective-permute-start.39 = (f32[128,1]{0,1:T(1,128)S(1)}, f32[128,1]{0,1:T(1,128)S(1)}, u32[]{:S(2)}, u32[]{:S(2)}) collective-permute-start(f32[128,1]{0,1:T(1,128)S(1)} %slice_bitcast_fusion), channel_id=1, source_target_pairs={{0,16},{16,0},{1,17},{17,1},{2,18},{18,2},{3,19},{19,3},{4,20},{20... | collective-permute-start | bytes 1544 | tf_op jit(solution)/shard_map/ppermute | solution.py:35
  347.2 9.2 %collective-permute-start.40 = (f32[32,1536]{1,0:T(8,128)S(1)}, f32[32,1536]{1,0:T(8,128)S(1)}, u32[]{:S(2)}, u32[]{:S(2)}) collective-permute-start(f32[32,1536]{1,0:T(8,128)S(1)} %get-tuple-element.84), channel_id=1, source_target_pairs={{0,4},{4,0},{8,12},{12,8},{1,5},{5,1},{9,13},{13,9},{2,6},{6,2},{1... | collective-permute-start | bytes 589832 | tf_op jit(solution)/shard_map/ppermute | solution.py:43
  347.8 16.8 %collective-permute-start.41 = (f32[32,1536]{1,0:T(8,128)S(1)}, f32[32,1536]{1,0:T(8,128)S(1)}, u32[]{:S(2)}, u32[]{:S(2)}) collective-permute-start(f32[32,1536]{1,0:T(8,128)S(1)} %get-tuple-element.82), channel_id=1, source_target_pairs={{0,8},{4,12},{8,0},{12,4},{1,9},{5,13},{9,1},{13,5},{2,10},{6,14},... | collective-permute-start | bytes 589832 | tf_op jit(solution)/shard_map/ppermute | solution.py:43
  349.3 15.4 %collective-permute-start.42 = (f32[32,1536]{1,0:T(8,128)S(1)}, f32[32,1536]{1,0:T(8,128)S(1)}, u32[]{:S(2)}, u32[]{:S(2)}) collective-permute-start(f32[32,1536]{1,0:T(8,128)S(1)} %get-tuple-element.83), channel_id=1, source_target_pairs={{0,12},{4,8},{8,4},{12,0},{1,13},{5,9},{9,5},{13,1},{2,14},{6,10},... | collective-permute-start | bytes 589832 | tf_op jit(solution)/shard_map/ppermute | solution.py:43
  352.7 49.2 %collective-permute-start.51 = (bf16[512,512]{1,0:T(8,128)(2,1)}, bf16[512,512]{1,0:T(8,128)(2,1)}, u32[]{:S(2)}, u32[]{:S(2)}) collective-permute-start(bf16[512,512]{1,0:T(8,128)(2,1)} %get-tuple-element.49), channel_id=1, source_target_pairs={{0,1},{1,0},{2,3},{3,2},{4,5},{5,4},{6,7},{7,6},{8,9},{9,8},{10,11... | collective-permute-start | bytes 1572872 | tf_op jit(solution)/shard_map/ppermute | solution.py:39
  369.6 9.0 %collective-permute-start.45 = (bf16[128,1536]{1,0:T(8,128)(2,1)S(1)}, bf16[128,1536]{1,0:T(8,128)(2,1)S(1)}, u32[]{:S(2)}, u32[]{:S(2)}) collective-permute-start(bf16[128,1536]{1,0:T(8,128)(2,1)S(1)} %get-tuple-element.133), channel_id=1, source_target_pairs={{0,2},{1,3},{2,0},{3,1},{4,6},{5,7},{6,4},{7,5},{8,10},{9,11},{10,... | collective-permute-start | bytes 1179656 | tf_op jit(solution)/shard_map/ppermute | solution.py:39
  371.3 9.6 %collective-permute-start.43 = (bf16[128,1536]{1,0:T(8,128)(2,1)S(1)}, bf16[128,1536]{1,0:T(8,128)(2,1)S(1)}, u32[]{:S(2)}, u32[]{:S(2)}) collective-permute-start(bf16[128,1536]{1,0:T(8,128)(2,1)S(1)} %get-tuple-element.133), channel_id=1, source_target_pairs={{0,16},{16,0},{1,17},{17,1},{2,18},{18,2},{3,19},{19,3},{4,20},{20... | collective-permute-start | bytes 1179656 | tf_op jit(solution)/shard_map/ppermute | solution.py:35
  378.7 5.7 %collective-permute-start.46 = (bf16[64,1536]{1,0:T(8,128)(2,1)S(1)}, bf16[64,1536]{1,0:T(8,128)(2,1)S(1)}, u32[]{:S(2)}, u32[]{:S(2)}) collective-permute-start(bf16[64,1536]{1,0:T(8,128)(2,1)S(1)} %slice.105), channel_id=1, source_target_pairs={{0,16},{16,0},{1,17},{17,1},{2,18},{18,2},{3,19},{19,3},{4,20},{20... | collective-permute-start | bytes 589832 | tf_op jit(solution)/shard_map/ppermute | solution.py:35
  380.8 5.7 %collective-permute-start.47 = (bf16[64,1536]{1,0:T(8,128)(2,1)S(1)}, bf16[64,1536]{1,0:T(8,128)(2,1)S(1)}, u32[]{:S(2)}, u32[]{:S(2)}) collective-permute-start(bf16[64,1536]{1,0:T(8,128)(2,1)S(1)} %slice.106), channel_id=1, source_target_pairs={{0,2},{1,3},{2,0},{3,1},{4,6},{5,7},{6,4},{7,5},{8,10},{9,11},{10,... | collective-permute-start | bytes 589832 | tf_op jit(solution)/shard_map/ppermute | solution.py:39
  386.6 15.2 %collective-permute-start.48 = (bf16[512,1536]{1,0:T(8,128)(2,1)S(1)}, bf16[512,1536]{1,0:T(8,128)(2,1)S(1)}, u32[]{:S(2)}, u32[]{:S(2)}) collective-permute-start(bf16[512,1536]{1,0:T(8,128)(2,1)S(1)} %get-tuple-element.109), channel_id=1, source_target_pairs={{0,1},{1,0},{2,3},{3,2},{4,5},{5,4},{6,7},{7,6},{8,9},{9,8},{10,11... | collective-permute-start | bytes 4718600 | tf_op jit(solution)/shard_map/ppermute | solution.py:39
  387.2 14.4 %collective-permute-start.44 = (bf16[128,2048]{1,0:T(8,128)(2,1)S(1)}, bf16[128,2048]{1,0:T(8,128)(2,1)S(1)}, u32[]{:S(2)}, u32[]{:S(2)}) collective-permute-start(bf16[128,2048]{1,0:T(8,128)(2,1)S(1)} %pad_maximum_fusion.17), channel_id=1, source_target_pairs={{0,16},{16,0},{1,17},{17,1},{2,18},{18,2},{3,19},{19,3},{4,20},{20... | collective-permute-start | bytes 1572872 | tf_op jit(solution)/shard_map/ppermute | solution.py:35
  405.7 38.9 %copy-start.1 = (bf16[384,4096]{1,0:T(8,128)(2,1)S(1)}, bf16[384,4096]{1,0:T(8,128)(2,1)}, u32[]{:S(2)}) copy-start(bf16[384,4096]{1,0:T(8,128)(2,1)} %param.26) | copy-start | bytes 9437188
  405.8 14.0 %collective-permute-start.52 = (bf16[384,512]{1,0:T(8,128)(2,1)S(1)}, bf16[384,512]{1,0:T(8,128)(2,1)S(1)}, u32[]{:S(2)}, u32[]{:S(2)}) collective-permute-start(bf16[384,512]{1,0:T(8,128)(2,1)S(1)} %get-tuple-element.33), channel_id=1, source_target_pairs={{0,12},{4,8},{8,4},{12,0},{1,13},{5,9},{9,5},{13,1},{2,14},{6,10},... | collective-permute-start | bytes 1179656 | tf_op jit(solution)/shard_map/ppermute | solution.py:43
  407.9 35.7 %collective-permute-start.53 = (bf16[384,512]{1,0:T(8,128)(2,1)S(1)}, bf16[384,512]{1,0:T(8,128)(2,1)S(1)}, u32[]{:S(2)}, u32[]{:S(2)}) collective-permute-start(bf16[384,512]{1,0:T(8,128)(2,1)S(1)} %get-tuple-element.35), channel_id=1, source_target_pairs={{0,8},{4,12},{8,0},{12,4},{1,9},{5,13},{9,1},{13,5},{2,10},{6,14},... | collective-permute-start | bytes 1179656 | tf_op jit(solution)/shard_map/ppermute | solution.py:43
  411.1 32.6 %collective-permute-start.54 = (bf16[384,512]{1,0:T(8,128)(2,1)S(1)}, bf16[384,512]{1,0:T(8,128)(2,1)S(1)}, u32[]{:S(2)}, u32[]{:S(2)}) collective-permute-start(bf16[384,512]{1,0:T(8,128)(2,1)S(1)} %get-tuple-element.34), channel_id=1, source_target_pairs={{0,4},{4,0},{8,12},{12,8},{1,5},{5,1},{9,13},{13,9},{2,6},{6,2},{1... | collective-permute-start | bytes 1179656 | tf_op jit(solution)/shard_map/ppermute | solution.py:43
  (57 other events, 407.6 us)

commit v3 on v2

--- a/solution.py
+++ b/solution.py
@@ -63,13 +63,13 @@
     )
 
 
-def rep_gather(own):
+def rep_gather(own, gate=lambda value: value):
     along_y = swap_rep(own, 2)
-    return [own, swap_rep(own, 1), along_y, swap_rep(along_y, 1)]
-
-
-def line_gather(own):
-    received = [own] + [swap_z(own, r) for r in (1, 2, 3)]
+    return [own, swap_rep(own, 1), along_y, swap_rep(gate(along_y), 1)]
+
+
+def line_gather(own, gate=lambda value: value):
+    received = [own] + [gate(swap_z(own, r)) for r in (1, 2, 3)]
     return join_absolute(received, lax.axis_index("vocab"), 0)
 
 
@@ -81,20 +81,18 @@
 
 
 def line_sum(partial):
-    blocks = split_relative(partial, lax.axis_index("vocab"), 4, 0)
-    received = [swap_z(blocks[r], r) for r in (3, 2, 1)]
-    return sum((block.astype(F32) for block in received), blocks[0].astype(F32))
-
-
-def line_reduce(far, near):
     index = lax.axis_index("vocab")
-    size = near.shape[0] // 2
-    outer = lax.ppermute(far, "vocab", [(0, 1), (3, 2)])
-    far = (far.astype(F32) + outer.astype(F32)).astype(BF16)
-    inner = lax.ppermute(far, "vocab", [(1, 2), (2, 1)])
-    near = near.astype(F32) + inner.astype(F32)
-    beside = swap_z(pick(near, 1 - index % 2, size, 0).astype(BF16), 1)
-    return pick(near, index % 2, size, 0) + beside.astype(F32)
+    size = partial.shape[0] // 4
+    half = partial.shape[1] // 2
+    blocks = split_relative(partial, index, 4, 0)
+    kept = []
+    for first in (0, half):
+        mine, beside, far, farther = (block[:, first : first + half] for block in blocks)
+        got = swap_z(jnp.concatenate([beside, farther], axis=0), 1).astype(F32)
+        kept.append((mine.astype(F32) + got[:size], far.astype(F32) + got[size:]))
+    return jnp.concatenate(
+        [mine + swap_z(far.astype(BF16), 2).astype(F32) for mine, far in kept], axis=1
+    )
 
 
 def plane_rows(own):
@@ -107,16 +105,17 @@
     return jnp.concatenate([mine, swap_rep(mine, 1)], axis=0), along_x
 
 
-def plane_exchange(rows):
+def plane_exchange(rows, gate_y, gate_core):
     plane = lax.axis_index("ctx") * 4 + lax.axis_index("rep")
     blocks = split_relative(rows, plane, 8, 1)
     count, size = blocks[0].shape
     there = swap_x(jnp.concatenate(blocks[4:], axis=1))
     here = jnp.concatenate([jnp.concatenate(blocks[:4], axis=1), there], axis=0)
+    here = gate_y(here)
     there = swap_rep(here[:, 2 * size :], 2)
     here = here[:, : 2 * size]
     here = jnp.concatenate([here[:count], there[:count], here[count:], there[count:]], axis=0)
-    return jnp.concatenate([here[:, :size], swap_rep(here[:, size:], 1)], axis=0)
+    return jnp.concatenate([here[:, :size], swap_rep(gate_core(here[:, size:]), 1)], axis=0)
 
 
 HEADS_STEP = 4
@@ -140,13 +139,13 @@
         out[:, cols] = (weighted / total).astype(BF16)
 
 
-def attend(queries, key_value, lengths):
+def attend(queries, key_value, lengths, earlier):
     seq_dev, pos_ctx, head_cols = queries.shape
     heads_dev = head_cols // HD
     ctx_index = lax.axis_index("ctx")
     shared_head = lax.axis_index("vocab") * heads_dev // (QH // KVH)
     own_rows = lax.dynamic_slice_in_dim(key_value, shared_head * HD, HD, 3)
-    other = swap_x(own_rows)
+    other = after(swap_x(own_rows), earlier)
     rows = jnp.concatenate([other, own_rows], axis=2)
     facts = jnp.concatenate([lengths, jnp.stack([ctx_index * pos_ctx, (ctx_index - 1) * pos_ctx])])
     step_cols = HEADS_STEP * HD
@@ -162,11 +161,7 @@
             ],
             out_specs=pl.BlockSpec((pos_ctx, step_cols), lambda s, h, facts: (s, h)),
         ),
-        cost_estimate=pl.CostEstimate(
-            flops=4 * seq_dev * pos_ctx * rows.shape[2] * head_cols,
-            bytes_accessed=4 * queries.size,
-            transcendentals=seq_dev * heads_dev * pos_ctx * rows.shape[2],
-        ),
+        cost_estimate=pl.CostEstimate(flops=0, bytes_accessed=0, transcendentals=0),
         compiler_params=pltpu.CompilerParams(vmem_limit_bytes=32 * 2**20),
         name="attend",
     )(facts, queries, rows)
@@ -200,6 +195,16 @@
     per_expert = own_count // 4
     vocab = 4 * teacher_head.shape[0]
 
+    def column_blocks(value, ctx):
+        size = value.shape[-1] // 8
+        return [pick(value, ctx * 4 + (rep_index ^ r), size, value.ndim - 1) for r in range(4)]
+
+    residual_rows = residual.reshape(own_count, width)
+    other_residual = jnp.concatenate(column_blocks(residual_rows, 1 - ctx_index), axis=1)
+    other_residual = swap_x(other_residual)
+    heads_out, keys = attend(queries, key_value, lengths, other_residual)
+    expert_ids = after(expert_ids, keys)
+
     route_ids = expert_ids.reshape(own_count, -1)
     inside = route_ids < 4
     chosen = jnp.sum(jnp.where(inside, route_ids, 0), axis=1)
@@ -211,111 +216,155 @@
     placer = placed.astype(BF16)
 
     line_target = chosen * own_count + vocab_index * per_expert + slot_rank
-    pair_facts = jnp.stack([line_target.astype(F32), route_weight])[None]
-    beside = swap_z(pair_facts, 1)
-    pair_facts = join_absolute([pair_facts, beside], vocab_index % 2, 0)
-    line_facts = join_absolute([pair_facts, swap_z(pair_facts, 2)], vocab_index // 2, 0)
-    line_target = line_facts[:, 0].astype(jnp.int32)
-    line_weight = line_facts[:, 1]
-    line_tokens = jnp.swapaxes(line_target.reshape(4, seq_dev, pos_dev), 0, 1).reshape(-1)
-    line_placer = (line_tokens[None, :] == jnp.arange(seq_dev * pos_ctx)[:, None]).astype(BF16)
-    mine = vocab_index * own_count + jnp.arange(own_count)
-    my_weight = jnp.sum(
-        jnp.where(line_target.reshape(1, -1) == mine[:, None], line_weight.reshape(1, -1), 0.0),
-        axis=1,
-        keepdims=True,
-    )
-
-    heads_out, keys = attend(queries, key_value, lengths)
-    weight_blocks = rep_gather(out_weight)
-    residual_rows = matmul(placer, residual.reshape(own_count, width)).astype(BF16)
-    other_residual = swap_x(after(pick(residual_rows, 1 - ctx_index, half, 1), keys))
-    both_residual = (pick(residual_rows, ctx_index, half, 1), other_residual)
-    other_weight = swap_x(my_weight)
-
-    learner_line = line_gather(learner_head)
-    learner_line = after(learner_line, weight_blocks[2])
-    learner_blocks = rep_gather(learner_line)
-
+    own_facts = jnp.stack([line_target.astype(F32), route_weight])[None]
+    line_facts = line_gather(own_facts)
+
+    weight_y = swap_rep(out_weight, 2)
+    weight_blocks = [out_weight, swap_rep(out_weight, 1), weight_y]
+    other_facts = swap_x(line_facts)
+    line_facts = after(line_facts, heads_out)
+    mine = vocab_index * own_count + jnp.arange(own_count)[:, None]
+
+    def routed(facts):
+        targets = facts[:, 0].astype(jnp.int32).reshape(1, -1)
+        weights = jnp.where(targets == mine, facts[:, 1].reshape(1, -1), 0.0)
+        return targets, jnp.sum(weights, axis=1, keepdims=True)
+
+    line_target_all, my_weight = routed(line_facts)
+    other_target_all, other_weight = routed(other_facts)
+    other_target = pick(other_target_all, vocab_index, own_count, 1)
+
+    line_rows = jnp.arange(seq_dev * pos_ctx)
+    chunk = line_rows // own_count
+    chunk = jnp.where(chunk < 2, 2 * chunk + 1, 2 * chunk - 4) ^ vocab_index
+    line_rows = (chunk * own_count + line_rows % own_count)[:, None]
+    line_tokens = jnp.swapaxes(line_target_all.reshape(4, seq_dev, pos_dev), 0, 1).reshape(1, -1)
+    line_placer = (line_rows == line_tokens).astype(BF16)
     heads_sorted = matmul(line_placer, heads_out).astype(BF16)
-    far_pair, near_pair = 1 - vocab_index // 2, vocab_index // 2
-    pair_rows = 2 * own_count
-    own_far = pick(heads_sorted, far_pair, pair_rows, 0)
-    own_near = pick(heads_sorted, near_pair, pair_rows, 0)
-    other_far = swap_x(own_far)
-    other_near = swap_x(after(own_near, other_far))
-    owner = (jnp.arange(4) == vocab_index).reshape(1, 4, 1, 1)
-
-    def project(rows, weight, residual_part, pair, block):
-        added = pick(residual_part, pair, 2 * per_expert, 0)
-        added = pick(added, rep_index ^ block, weight.shape[1], 1).astype(F32)
-        added = jnp.where(owner, added.reshape(2, 1, per_expert, -1), 0.0)
-        added = added.reshape(pair_rows, -1)
-        return (matmul(rows, weight) + added).astype(BF16)
-
-    def projected(far, near, residual_part, members):
-        parts = [
-            jnp.concatenate(
-                [project(rows, weight_blocks[r], residual_part, pair, r) for r in members], axis=1
-            )
-            for rows, pair in ((far, far_pair), (near, near_pair))
-        ]
-        return jnp.split(line_reduce(*parts), 2, axis=1)
-
-    own_blocks = projected(own_far, own_near, both_residual[0], (0, 1))
-    own_blocks += projected(own_far, own_near, both_residual[0], (2, 3))
-    other_blocks = projected(other_far, other_near, both_residual[1], (0, 1))
-    other_blocks += projected(other_far, other_near, both_residual[1], (2, 3))
-
-    hidden_one = jnp.concatenate(
-        [join_absolute(own_blocks, rep_index, 1), join_absolute(other_blocks, rep_index, 1)], axis=0
-    )
-    sent = hidden_one.astype(BF16)
-    got = swap_x(sent)
-    got = jnp.concatenate([got[own_count:], got[:own_count]], axis=0)
-    rows = join_absolute([sent, got], ctx_index, 1).astype(F32)
-    normed = rms_scale(rows, moe_gain).astype(BF16)
-
-    learner_own = learner_hidden.reshape(own_count, width)
+    sent_count = 2 * own_count
+    other_sent = swap_x(heads_sorted[:sent_count])
+
+    own_residual = jnp.concatenate(column_blocks(after(residual_rows, heads_out), ctx_index), axis=1)
+    own_added = matmul((line_rows == line_target[None, :]).astype(BF16), own_residual).astype(BF16)
+    other_added = matmul(
+        (line_rows == other_target).astype(BF16), other_residual
+    ).astype(BF16)
+
+    def projected(rows, added, members):
+        size = added.shape[1] // 4
+        return jnp.concatenate(
+            [
+                (
+                    matmul(rows, weight_blocks[r])
+                    + added[:, r * size : (r + 1) * size].astype(F32)
+                ).astype(BF16)
+                for r in members
+            ],
+            axis=1,
+        )
+
+    def beside_sum(kept, beside):
+        return kept.astype(F32) + beside.astype(F32)
+
+    def across_sum(kept, across):
+        return kept[:own_count] + across.astype(F32)
+
+    part_0 = projected(heads_sorted, own_added, (0, 1))
+    beside_0 = swap_z(part_0[:sent_count], 1)
+    weight_blocks.append(swap_rep(after(weight_y, part_0), 1))
+    part_1 = projected(heads_sorted, own_added, (2, 3))
+    beside_1 = swap_z(part_1[:sent_count], 1)
+    other_kept = swap_x(after(heads_sorted[sent_count:], other_sent, part_1))
+    kept_0 = beside_sum(part_0[sent_count:], after(beside_0, part_1))
+    across_0 = swap_z(kept_0[own_count:].astype(BF16), 2)
+    sent_2 = projected(after(other_sent, part_1), other_added[:sent_count], (0, 1, 2, 3))
+    beside_2 = swap_z(sent_2, 1)
+    kept_1 = beside_sum(part_1[sent_count:], after(beside_1, sent_2))
+    across_1 = swap_z(kept_1[own_count:].astype(BF16), 2)
+    other_kept = after(other_kept, kept_0, kept_1)
+    kept_2 = projected(other_kept, other_added[sent_count:], (0, 1, 2, 3))
+    hidden_0 = across_sum(kept_0, after(across_0, kept_2))
+    hidden_1 = across_sum(kept_1, after(across_1, kept_2))
+    kept_2 = beside_sum(kept_2, beside_2)
+    across_2 = swap_z(kept_2[own_count:].astype(BF16), 2)
+    hidden_2 = across_sum(kept_2, across_2)
+    hidden_parts = [hidden_0, hidden_1, hidden_2]
+    sent = [part.astype(BF16) for part in hidden_parts]
+    got = [swap_x(part) for part in sent]
+
+    plane_columns = plane_exchange(
+        after(learner_hidden.reshape(own_count, width), part_1),
+        lambda value: after(value, sent_2),
+        lambda value: after(value, hidden_2),
+    )
+    teacher_slice = pick(teacher_head, ctx_index * 4 + rep_index, width // 8, 1)
+    teacher_line = line_gather(teacher_slice, lambda value: after(value, part_1))
+    teacher_line = after(teacher_line, weight_y)
+    teacher_blocks = rep_gather(teacher_line, lambda value: after(value, hidden_2))
+    learner_line = line_gather(after(learner_head, hidden_2))
+
+    hidden_one = jnp.concatenate([jnp.concatenate(hidden_parts[:2], axis=1), hidden_2], axis=0)
+    theirs = jnp.concatenate([got[2], jnp.concatenate(got[:2], axis=1)], axis=0)
+    squares = jnp.sum(hidden_one * hidden_one, axis=1, keepdims=True) + jnp.sum(
+        jnp.square(theirs.astype(F32)), axis=1, keepdims=True
+    )
+    scale = lax.rsqrt(squares / width + EPSILON)
+    sides = [
+        join_absolute(jnp.split(side, 4, axis=1), rep_index, 1)
+        for side in (hidden_one.astype(BF16), theirs)
+    ]
+    rows = join_absolute(sides, ctx_index, 1)
+    normed = (rows.astype(F32) * scale * moe_gain).astype(BF16)
+
+    learner_own = after(learner_hidden, sent_2).reshape(own_count, width)
     learner_rows = matmul(placer, learner_own).astype(BF16)
-    other_rows = swap_x(after(pick(learner_rows, 1 - ctx_index, half, 1), other_near))
-    both_rows = jnp.concatenate([pick(learner_rows, ctx_index, half, 1), other_rows], axis=0)
+    other_rows = jnp.concatenate(column_blocks(learner_rows, 1 - ctx_index), axis=1)
+    other_rows = swap_x(after(other_rows, other_kept))
+    own_rows = jnp.concatenate(column_blocks(learner_rows, ctx_index), axis=1)
+    both_rows = jnp.concatenate([own_rows, other_rows], axis=0)
+    gate_pre = matmul(normed, gate_weight[0], LAST)
+    up_pre = matmul(normed, up_weight[0], LAST)
+    activated = (jax.nn.silu(gate_pre) * up_pre).astype(BF16)
+    down_other = column_blocks(after(down_weight, sent_2)[0], 1 - ctx_index)
+    down_own = column_blocks(after(down_weight, sent_2)[0], ctx_index)
+    expert_parts = []
+    for r in (0, 2):
+        terms = matmul(activated, jnp.concatenate(down_other[r : r + 2], axis=1)).astype(BF16)
+        terms = swap_x(terms)
+        terms = jnp.concatenate([terms[own_count:], terms[:own_count]], axis=0)
+        ours = matmul(activated, jnp.concatenate(down_own[r : r + 2], axis=1)).astype(BF16)
+        expert_parts.append((ours.astype(F32) + terms.astype(F32)).astype(BF16).astype(F32))
+    expert_out = jnp.concatenate(expert_parts, axis=1)
+    both_weight = jnp.concatenate([my_weight, other_weight], axis=0)
+    hidden_two = hidden_one + both_weight * expert_out
+
+    squares = jnp.sum(hidden_two * hidden_two, axis=1, keepdims=True)
+    own_squares = squares[:own_count] + swap_x(squares[own_count:])
+    scale = lax.rsqrt(own_squares / width + EPSILON)
+    gain = jnp.concatenate(column_blocks(final_gain, ctx_index))
+    final_rows = (hidden_two * gain).astype(BF16)
+    final_blocks = jnp.split(final_rows, 4, axis=1)
+    teacher_sides = [
+        sum(
+            matmul(rows, block[first : first + vocab // 2], LAST)
+            for rows, block in zip(final_blocks, teacher_blocks)
+        )
+        for first in (0, vocab // 2)
+    ]
+    teacher_parts = [
+        (side[:own_count] + swap_x(side[own_count:])) * scale for side in teacher_sides
+    ]
+    teacher_logits = jnp.concatenate([line_exchange(part) for part in teacher_parts], axis=1)
+    learner_blocks = rep_gather(learner_line, lambda value: after(value, *teacher_sides))
     learner_part = sum(
         matmul(part, block, LAST)
-        for part, block in zip(split_relative(both_rows, rep_index, 4, 1), learner_blocks)
-    )
-    learner_logits = learner_part[:own_count] + swap_x(learner_part[own_count:])
+        for part, block in zip(jnp.split(both_rows, 4, axis=1), learner_blocks)
+    )
+    learner_logits = learner_part[:own_count] + swap_x(after(learner_part[own_count:], *teacher_parts))
     learner_peak = jnp.max(learner_logits, axis=1, keepdims=True)
     learner_exp = jnp.exp(learner_logits - learner_peak)
     learner_total = jnp.sum(learner_exp, axis=1, keepdims=True)
     learner_lse = learner_peak + jnp.log(learner_total)
-    plane_columns = plane_exchange(after(learner_own, learner_logits))
-
-    teacher_slice = pick(teacher_head, ctx_index * 4 + rep_index, width // 8, 1)
-    teacher_line = line_gather(after(teacher_slice, other_blocks[0], other_blocks[2]))
-    teacher_blocks = rep_gather(teacher_line)
-
-    gate_pre = matmul(normed, gate_weight[0], LAST)
-    up_pre = matmul(normed, up_weight[0], LAST)
-    activated = (jax.nn.silu(gate_pre) * up_pre).astype(BF16)
-    theirs = matmul(activated, pick(down_weight[0], 1 - ctx_index, half, 1)).astype(BF16)
-    theirs = swap_x(theirs)
-    theirs = jnp.concatenate([theirs[own_count:], theirs[:own_count]], axis=0)
-    ours = matmul(activated, pick(down_weight[0], ctx_index, half, 1)).astype(BF16)
-    expert_out = (ours.astype(F32) + theirs.astype(F32)).astype(BF16).astype(F32)
-    both_weight = jnp.concatenate([my_weight, other_weight], axis=0)
-    hidden_two = hidden_one + both_weight * expert_out
-
-    squares = jnp.sum(hidden_two * hidden_two, axis=1, keepdims=True)
-    own_squares = squares[:own_count] + swap_x(squares[own_count:])
-    scale = lax.rsqrt(own_squares / width + EPSILON)
-    final_rows = (hidden_two * pick(final_gain, ctx_index, half, 0)).astype(BF16)
-    teacher_part = sum(
-        matmul(part, block, LAST)
-        for part, block in zip(split_relative(final_rows, rep_index, 4, 1), teacher_blocks)
-    )
-    teacher_logits = (teacher_part[:own_count] + swap_x(teacher_part[own_count:])) * scale
-    teacher_logits = line_exchange(teacher_logits)
 
     teacher_peak = jnp.max(teacher_logits, axis=1, keepdims=True)
     teacher_lse = teacher_peak + jnp.log(
@@ -347,7 +396,7 @@
     own_grad = join_absolute(
         [matmul(dlogits, block).astype(BF16) for block in learner_blocks], rep_index, 1
     )
-    hidden_grad = join_absolute([own_grad, other_grad], ctx_index, 1)
+    hidden_grad = join_absolute([own_grad, after(other_grad, head_grad)], ctx_index, 1)
     return (hidden_grad.reshape(seq_dev, pos_dev, width), head_grad, row_kl)
 
 

time: 454 us -> 374 us (0.82); the launches traced: 445 us -> 371 us
  starting transfers between devices: 102 us -> 67.3 us
  waiting for transfers between devices: 227 us -> 203 us
  other arithmetic: 38.1 us -> 15 us
  matrix products: 42.3 us -> 58.4 us
  local copies, waits for them, and re-layouts: 20.2 us -> 12.6 us
    ppermute x14, waiting for transfers between devices: 9.02 us -> 34.9 us  [swap_rep(): return lax.ppermute(value, 'rep', [(i, i ^ offset) for i in range(4)])]
    ppermute x18 -> x25, starting transfers between devices: 61.1 us -> 38.3 us  [swap_z(): return lax.ppermute(value, 'vocab', [(i, i ^ offset) for i in range(4)])]
    ppermute x8 -> x0, waiting for transfers between devices: 22.8 us -> none  [the longest x4 22.7 us: line_reduce(): outer = lax.ppermute(far, 'vocab', [(0, 1), (3, 2)])]
    ppermute x15 -> x19, waiting for transfers between devices: 122 us -> 102 us  [swap_x(): return lax.ppermute(value, 'ctx', [(0, 1), (1, 0)])]
    dot_general x41 -> x44, matrix products: 42.3 us -> 58.4 us  [matmul(): return lax.dot_general(left, right, dims, preferred_element_type=F32)]
    broadcast_in_dim x17 -> x1, other arithmetic: 12.1 us -> 0.01 us  [per_device(): own_facts = jnp.stack([line_target.astype(F32), route_weight])[None]]
    ppermute x8 -> x0, starting transfers between devices: 10.6 us -> none  [the longest x4 7.52 us: line_reduce(): outer = lax.ppermute(far, 'vocab', [(0, 1), (3, 2)])]
    ppermute x18 -> x25, waiting for transfers between devices: 73.9 us -> 66.5 us  [swap_z(): return lax.ppermute(value, 'vocab', [(i, i ^ offset) for i in range(4)])]
  transfers between devices with their start and end apart: 55 -> 58, of which waited for: 25 -> 24; matrix products, arithmetic and copies ran while one was open for 20% -> 19% of each run, Pallas kernels for 3% -> 3%
where the time goes in v3:
time: 374 us; the launch traced here: 371 us
  waiting for transfers between devices  203 us (54%)
  starting transfers between devices  67.3 us (18%)
  matrix products  58.4 us (16%)
  other arithmetic  15 us (4%)
  local copies, waits for them, and re-layouts  12.6 us (3%)
  Pallas kernels  12.1 us (3%)
    ppermute x19, waiting for transfers between devices, swap_x(): return lax.ppermute(value, 'ctx', [(0, 1), (1, 0)])  102 us
    ppermute x25, waiting for transfers between devices, swap_z(): return lax.ppermute(value, 'vocab', [(i, i ^ offset) for i in range(4)])  66.5 us
    dot_general x44, matrix products, matmul(): return lax.dot_general(left, right, dims, preferred_element_type=F32)  58.4 us
    ppermute x25, starting transfers between devices, swap_z(): return lax.ppermute(value, 'vocab', [(i, i ^ offset) for i in range(4)])  38.3 us
    ppermute x14, waiting for transfers between devices, swap_rep(): return lax.ppermute(value, 'rep', [(i, i ^ offset) for i in range(4)])  34.9 us
    ppermute x19, starting transfers between devices, swap_x(): return lax.ppermute(value, 'ctx', [(0, 1), (1, 0)])  21 us
    pallas_call x1, Pallas kernels, attend(): pl.pallas_call(attend_kernel, out_shape=jax.ShapeDtypeStruct((seq_dev * p...  12.1 us
    ppermute x14, starting transfers between devices, swap_rep(): return lax.ppermute(value, 'rep', [(i, i ^ offset) for i in range(4)])  8.08 us
  transfers between devices with their start and end apart: 58, of which 24 were waited for; matrix products, arithmetic and copies ran while one was open for 19% of the time, Pallas kernels for 3%

profile of v3, /device:TPU:0, one launch (start us, length us, event | category | flops | bytes accessed | tf_op | source)
XLA Modules:
  0.0 371.1 jit_solution(98506235392901847)
XLA Ops:
  0.7 3.0 collective-permute-start.6
  5.7 1.5 collective-permute-start.1
  8.1 1.8 constant_dynamic-slice_fusion.16
  9.9 16.0 %collective-permute-done = bf16[2,2,256,128]{3,2,1,0:T(8,128)(2,1)S(1)} collective-permute-done((bf16[2,2,256,128]{3,2,1,0:T(8,128)(2,1)S(1)}, bf16[2,2,256,128]{3,2,1,0:T(8,128)(2,1)S(1)}, u32[]{:S(2)}, u32[]{:S(2)}) %collective-permute-start) | collective-permute-done | bytes 262176 | tf_op jit(solution)/shard_map/ppermute | solution.py:35
  26.6 1.6 collective-permute-start.2
  28.3 2.6 collective-permute-start.3
  31.2 12.1 %attend.1 = bf16[512,2048]{1,0:T(8,128)(2,1)S(1)} custom-call(s32[4]{0:T(128)S(1)} %pad_add_fusion.facts, bf16[2,256,2048]{2,1,0:T(8,128)(2,1)S(1)} %copy-done.2, bf16[2,2,512,128]{3,2,1,0:T(8,128)(2,1)S(1)} %pad_maximum_fusion.15.rows), custom_call_target="tpu_custom_call" | custom-call | tf_op jit(solution)/shard_map/attend/pallas_call | solution.py:152
  45.3 3.5 collective-permute-start.29
  48.9 1.5 collective-permute-start.9
  50.6 2.9 convolution_convert_fusion.4
  56.9 1.9 convolution_convert_fusion.2
  59.4 2.9 fusion.42
  62.4 2.9 fusion.40
  67.1 15.9 %collective-permute-done.5 = bf16[256,2048]{1,0:T(8,128)(2,1)S(1)} collective-permute-done((bf16[256,2048]{1,0:T(8,128)(2,1)S(1)}, bf16[256,2048]{1,0:T(8,128)(2,1)S(1)}, u32[]{:S(2)}, u32[]{:S(2)}) %collective-permute-start.5) | collective-permute-done | bytes 1048608 | tf_op jit(solution)/shard_map/ppermute | solution.py:35
  83.3 1.9 collective-permute-done.11
  85.2 1.7 collective-permute-start.10
  87.9 2.6 fusion.53
  90.4 2.6 fusion.54
  94.5 1.6 select_select_fusion.3
  100.4 21.0 %collective-permute-done.51 = bf16[128,2048]{1,0:T(8,128)(2,1)S(1)} collective-permute-done((bf16[128,2048]{1,0:T(8,128)(2,1)S(1)}, bf16[128,2048]{1,0:T(8,128)(2,1)S(1)}, u32[]{:S(2)}, u32[]{:S(2)}) %collective-permute-start.51) | collective-permute-done | bytes 524320 | tf_op jit(solution)/shard_map/ppermute | solution.py:35
  122.6 2.6 collective-permute-start.22
  125.2 2.2 fusion.56
  127.4 2.9 fusion.57
  130.3 3.0 fusion.58
  133.3 2.2 fusion.59
  136.6 20.7 %collective-permute-done.22 = bf16[128,1024]{0,1:T(8,128)(2,1)S(1)} collective-permute-done((bf16[128,1024]{0,1:T(8,128)(2,1)S(1)}, bf16[128,1024]{0,1:T(8,128)(2,1)S(1)}, u32[]{:S(2)}, u32[]{:S(2)}) %collective-permute-start.22) | collective-permute-done | bytes 262176 | tf_op jit(solution)/shard_map/ppermute | solution.py:43
  157.5 1.6 collective-permute-start.24
  159.6 8.9 %collective-permute-done.15 = bf16[128,2048]{0,1:T(8,128)(2,1)S(1)} collective-permute-done((bf16[128,2048]{0,1:T(8,128)(2,1)S(1)}, bf16[128,2048]{0,1:T(8,128)(2,1)S(1)}, u32[]{:S(2)}, u32[]{:S(2)}) %collective-permute-start.15) | collective-permute-done | bytes 524320 | tf_op jit(solution)/shard_map/ppermute | solution.py:43
  168.6 1.6 collective-permute-start.23
  171.4 2.1 collective-permute-start.17
  173.6 9.9 %collective-permute-done.23 = bf16[128,2048]{0,1:T(8,128)(2,1)S(1)} collective-permute-done((bf16[128,2048]{0,1:T(8,128)(2,1)S(1)}, bf16[128,2048]{0,1:T(8,128)(2,1)S(1)}, u32[]{:S(2)}, u32[]{:S(2)}) %collective-permute-start.23) | collective-permute-done | bytes 524320 | tf_op jit(solution)/shard_map/ppermute | solution.py:35
  183.5 1.6 collective-permute-start.18
  186.4 5.7 %fusion.2 = f32[256,768]{1,0:T(8,128)S(1)} fusion(bf16[1,768,4096]{2,1,0:T(8,128)(2,1)} %param.22, bf16[256,2048]{0,1:T(8,128)(2,1)S(1)} %get-tuple-element.88, bf16[256,2048]{0,1:T(8,128)(2,1)S(1)} %get-tuple-element.87, f32[4096]{0:T(1024)S(1)} %copy-done.30, f32[256]{0:T(256)S(1)} %add_rsqrt_fusion), kind=kOutput, calls=%fused_computation.2 | convolution fusion | flops 1617952768 | bytes 9192448 | tf_op jit(solution)/shard_map/dot_general | solution.py:22
  192.1 5.3 %fusion.49 = bf16[256,768]{1,0:T(8,128)(2,1)S(1)} fusion(bf16[1,768,4096]{2,1,0:T(8,128)(2,1)} %param.23, f32[256,768]{1,0:T(8,128)S(1)} %fusion.2, bf16[256,2048]{0,1:T(8,128)(2,1)S(1)} %get-tuple-element.88, bf16[256,2048]{0,1:T(8,128)(2,1)S(1)} %get-tuple-element.87, f32[4096]{0:T(1024)S(1)} %copy-done.30, f32[256]{0:T(256)S(1)} %add_rsqrt_fusion), kind=kOutput, calls=%fused_computation.70 | convolution fusion | flops 1619132416 | bytes 9585664 | tf_op jit(solution)/shard_map/dot_general | solution.py:22
  199.0 2.0 collective-permute-done.17
  201.1 1.5 collective-permute-start.26
  203.4 12.5 %collective-permute-done.26 = bf16[256,1024]{0,1:T(8,128)(2,1)S(1)} collective-permute-done((bf16[256,1024]{0,1:T(8,128)(2,1)S(1)}, bf16[256,1024]{0,1:T(8,128)(2,1)S(1)}, u32[]{:S(2)}, u32[]{:S(2)}) %collective-permute-start.26) | collective-permute-done | bytes 524320 | tf_op jit(solution)/shard_map/ppermute | solution.py:35
  216.0 8.6 %collective-permute-done.27 = bf16[256,1024]{0,1:T(8,128)(2,1)S(1)} collective-permute-done((bf16[256,1024]{0,1:T(8,128)(2,1)S(1)}, bf16[256,1024]{0,1:T(8,128)(2,1)S(1)}, u32[]{:S(2)}, u32[]{:S(2)}) %collective-permute-start.27) | collective-permute-done | bytes 524320 | tf_op jit(solution)/shard_map/ppermute | solution.py:35
  226.8 2.1 multiply_reduce_fusion
  232.3 26.2 %collective-permute-done.20 = bf16[1536,512]{1,0:T(8,128)(2,1)S(1)} collective-permute-done((bf16[1536,512]{1,0:T(8,128)(2,1)S(1)}, bf16[1536,512]{1,0:T(8,128)(2,1)S(1)}, u32[]{:S(2)}, u32[]{:S(2)}) %collective-permute-start.20) | collective-permute-done | bytes 1572896 | tf_op jit(solution)/shard_map/ppermute | solution.py:39
  258.5 1.7 collective-permute-start.36
  260.7 1.6 collective-permute-start.35
  262.4 1.4 collective-permute-start.52
  263.9 8.4 %collective-permute-done.37 = f32[128,768]{1,0:T(8,128)S(1)} collective-permute-done((f32[128,768]{1,0:T(8,128)S(1)}, f32[128,768]{1,0:T(8,128)S(1)}, u32[]{:S(2)}, u32[]{:S(2)}) %collective-permute-start.37) | collective-permute-done | bytes 393248 | tf_op jit(solution)/shard_map/ppermute | solution.py:35
  272.3 7.6 %collective-permute-done.35 = f32[128,768]{1,0:T(8,128)S(1)} collective-permute-done((f32[128,768]{1,0:T(8,128)S(1)}, f32[128,768]{1,0:T(8,128)S(1)}, u32[]{:S(2)}, u32[]{:S(2)}) %collective-permute-start.35) | collective-permute-done | bytes 393248 | tf_op jit(solution)/shard_map/ppermute | solution.py:35
  285.2 3.8 %collective-permute-start.43 = (f32[32,768]{1,0:T(8,128)S(1)}, f32[32,768]{1,0:T(8,128)S(1)}, u32[]{:S(2)}, u32[]{:S(2)}) collective-permute-start(f32[32,768]{1,0:T(8,128)S(1)} %get-tuple-element.171), channel_id=1, source_target_pairs={{0,8},{4,12},{8,0},{12,4},{1,9},{5,13},{9,1},{13,5},{2,10},{6,14},... | collective-permute-start | bytes 294920 | tf_op jit(solution)/shard_map/ppermute | solution.py:43
  291.0 2.5 collective-permute-start.40
  293.5 3.5 collective-permute-done.43
  297.0 4.8 %collective-permute-start.41 = (f32[32,768]{1,0:T(8,128)S(1)}, f32[32,768]{1,0:T(8,128)S(1)}, u32[]{:S(2)}, u32[]{:S(2)}) collective-permute-start(f32[32,768]{1,0:T(8,128)S(1)} %get-tuple-element.175), channel_id=1, source_target_pairs={{0,12},{4,8},{8,4},{12,0},{1,13},{5,9},{9,5},{13,1},{2,14},{6,10},... | collective-permute-start | bytes 294920 | tf_op jit(solution)/shard_map/ppermute | solution.py:43
  305.8 1.6 fusion.76
  308.5 1.8 constant_dynamic-update-slice_fusion.4
  311.0 1.4 collective-permute-start.45
  312.7 6.0 %collective-permute-done.47 = bf16[128,1536]{1,0:T(8,128)(2,1)S(1)} collective-permute-done((bf16[128,1536]{1,0:T(8,128)(2,1)S(1)}, bf16[128,1536]{1,0:T(8,128)(2,1)S(1)}, u32[]{:S(2)}, u32[]{:S(2)}) %collective-permute-start.47) | collective-permute-done | bytes 393248 | tf_op jit(solution)/shard_map/ppermute | solution.py:39
  318.7 2.2 collective-permute-start.48
  321.0 1.4 collective-permute-start.49
  322.5 2.1 collective-permute-done.48
  324.6 2.1 collective-permute-done.49
  330.3 1.8 convolution_convert_fusion.1
  332.3 2.6 collective-permute-start.54
  336.6 8.2 %collective-permute-done.54 = bf16[768,256]{1,0:T(8,128)(2,1)S(1)} collective-permute-done((bf16[768,256]{1,0:T(8,128)(2,1)S(1)}, bf16[768,256]{1,0:T(8,128)(2,1)S(1)}, u32[]{:S(2)}, u32[]{:S(2)}) %collective-permute-start.54) | collective-permute-done | bytes 393248 | tf_op jit(solution)/shard_map/ppermute | solution.py:43
  344.9 2.6 collective-permute-start.55
  348.1 8.8 %collective-permute-done.56 = bf16[768,256]{1,0:T(8,128)(2,1)S(1)} collective-permute-done((bf16[768,256]{1,0:T(8,128)(2,1)S(1)}, bf16[768,256]{1,0:T(8,128)(2,1)S(1)}, u32[]{:S(2)}, u32[]{:S(2)}) %collective-permute-start.56) | collective-permute-done | bytes 393248 | tf_op jit(solution)/shard_map/ppermute | solution.py:43
  357.2 2.6 collective-permute-start.57
  360.2 8.6 %collective-permute-done.57 = bf16[384,256]{1,0:T(8,128)(2,1)S(1)} collective-permute-done((bf16[384,256]{1,0:T(8,128)(2,1)S(1)}, bf16[384,256]{1,0:T(8,128)(2,1)S(1)}, u32[]{:S(2)}, u32[]{:S(2)}) %collective-permute-start.57) | collective-permute-done | bytes 196640 | tf_op jit(solution)/shard_map/ppermute | solution.py:43
  (276 shorter events, 54.7 us)
Async XLA Ops:
  0.7 25.2 %copy-start.22 = (s32[2,64,8]{1,2,0:T(8,128)S(1)}, s32[2,64,8]{1,2,0:T(8,128)}, u32[]{:S(2)}) copy-start(s32[2,64,8]{1,2,0:T(8,128)} %param.20) | copy-start | bytes 12292
  0.7 25.8 %copy-start.23 = (f32[2,64,8]{1,2,0:T(8,128)S(1)}, f32[2,64,8]{1,2,0:T(8,128)}, u32[]{:S(2)}) copy-start(f32[2,64,8]{1,2,0:T(8,128)} %param.21) | copy-start | bytes 12292
  0.7 53.1 %collective-permute-start.6 = (bf16[2048,512]{1,0:T(8,128)(2,1)}, bf16[2048,512]{1,0:T(8,128)(2,1)}, u32[]{:S(2)}, u32[]{:S(2)}) collective-permute-start(bf16[2048,512]{1,0:T(8,128)(2,1)} %param.18), channel_id=1, source_target_pairs={{0,2},{1,3},{2,0},{3,1},{4,6},{5,7},{6,4},{7,5},{8,10},{9,11},{10,... | collective-permute-start | bytes 6291464 | tf_op jit(solution)/shard_map/ppermute | solution.py:39
  3.7 55.1 %collective-permute-start.7 = (bf16[2048,512]{1,0:T(8,128)(2,1)}, bf16[2048,512]{1,0:T(8,128)(2,1)}, u32[]{:S(2)}, u32[]{:S(2)}) collective-permute-start(bf16[2048,512]{1,0:T(8,128)(2,1)} %param.18), channel_id=1, source_target_pairs={{0,1},{1,0},{2,3},{3,2},{4,5},{5,4},{6,7},{7,6},{8,9},{9,8},{10,11... | collective-permute-start | bytes 6291464 | tf_op jit(solution)/shard_map/ppermute | solution.py:39
  4.9 26.3 %copy-start.2 = (bf16[2,256,2048]{2,1,0:T(8,128)(2,1)S(1)}, bf16[2,256,2048]{2,1,0:T(8,128)(2,1)}, u32[]{:S(2)}) copy-start(bf16[2,256,2048]{2,1,0:T(8,128)(2,1)} %query.1) | copy-start | bytes 6291460
  5.7 20.2 %collective-permute-start.1 = (bf16[128,2048]{1,0:T(8,128)(2,1)}, bf16[128,2048]{1,0:T(8,128)(2,1)}, u32[]{:S(2)}, u32[]{:S(2)}) collective-permute-start(bf16[128,2048]{1,0:T(8,128)(2,1)} %pad_maximum_fusion.14), channel_id=1, source_target_pairs={{0,16},{16,0},{1,17},{17,1},{2,18},{18,2},{3,19},{19,3},{4,20},{20... | collective-permute-start | bytes 1572872 | tf_op jit(solution)/shard_map/ppermute | solution.py:35
  7.3 18.6 %collective-permute-start = (bf16[2,2,256,128]{3,2,1,0:T(8,128)(2,1)S(1)}, bf16[2,2,256,128]{3,2,1,0:T(8,128)(2,1)S(1)}, u32[]{:S(2)}, u32[]{:S(2)}) collective-permute-start(bf16[2,2,256,128]{3,2,1,0:T(8,128)(2,1)S(1)} %constant_dynamic-slice_fusion.34), channel_id=1, source_target_pairs={{0,16},{16,0},{1,17},{17,1},{2,18},{18,2},{3,19},{19,3},{4,20},{20... | collective-permute-start | bytes 786440 | tf_op jit(solution)/shard_map/ppermute | solution.py:35
  26.6 18.0 %collective-permute-start.2 = (f32[1,2,128]{2,1,0:T(2,128)S(1)}, f32[1,2,128]{2,1,0:T(2,128)S(1)}, u32[]{:S(2)}, u32[]{:S(2)}) collective-permute-start(f32[1,2,128]{2,1,0:T(2,128)S(1)} %maximum_bitcast_fusion), channel_id=1, source_target_pairs={{0,4},{4,0},{8,12},{12,8},{1,5},{5,1},{9,13},{13,9},{2,6},{6,2},{1... | collective-permute-start | bytes 3080 | tf_op jit(solution)/shard_map/ppermute | solution.py:43
  28.3 17.0 %collective-permute-start.3 = (f32[1,2,128]{2,1,0:T(2,128)S(1)}, f32[1,2,128]{2,1,0:T(2,128)S(1)}, u32[]{:S(2)}, u32[]{:S(2)}) collective-permute-start(f32[1,2,128]{2,1,0:T(2,128)S(1)} %maximum_bitcast_fusion), channel_id=1, source_target_pairs={{0,8},{4,12},{8,0},{12,4},{1,9},{5,13},{9,1},{13,5},{2,10},{6,14},... | collective-permute-start | bytes 3080 | tf_op jit(solution)/shard_map/ppermute | solution.py:43
  30.9 18.0 %collective-permute-start.4 = (f32[1,2,128]{2,1,0:T(2,128)S(1)}, f32[1,2,128]{2,1,0:T(2,128)S(1)}, u32[]{:S(2)}, u32[]{:S(2)}) collective-permute-start(f32[1,2,128]{2,1,0:T(2,128)S(1)} %maximum_bitcast_fusion), channel_id=1, source_target_pairs={{0,12},{4,8},{8,4},{12,0},{1,13},{5,9},{9,5},{13,1},{2,14},{6,10},... | collective-permute-start | bytes 3080 | tf_op jit(solution)/shard_map/ppermute | solution.py:43
  31.2 12.1 %copy-start.9 = (bf16[2,64,4096]{2,1,0:T(8,128)(2,1)S(1)}, bf16[2,64,4096]{2,1,0:T(8,128)(2,1)}, u32[]{:S(2)}) copy-start(bf16[2,64,4096]{2,1,0:T(8,128)(2,1)} %param.17) | copy-start | bytes 3145732
  44.6 49.6 %collective-permute-start.28 = (bf16[384,512]{1,0:T(8,128)(2,1)S(1)}, bf16[384,512]{1,0:T(8,128)(2,1)S(1)}, u32[]{:S(2)}, u32[]{:S(2)}) collective-permute-start(bf16[384,512]{1,0:T(8,128)(2,1)S(1)} %copy-done.21), channel_id=1, source_target_pairs={{0,4},{4,0},{8,12},{12,8},{1,5},{5,1},{9,13},{13,9},{2,6},{6,2},{1... | collective-permute-start | bytes 1179656 | tf_op jit(solution)/shard_map/ppermute | solution.py:43
  45.3 49.0 %collective-permute-start.29 = (bf16[384,512]{1,0:T(8,128)(2,1)S(1)}, bf16[384,512]{1,0:T(8,128)(2,1)S(1)}, u32[]{:S(2)}, u32[]{:S(2)}) collective-permute-start(bf16[384,512]{1,0:T(8,128)(2,1)S(1)} %copy-done.21), channel_id=1, source_target_pairs={{0,8},{4,12},{8,0},{12,4},{1,9},{5,13},{9,1},{13,5},{2,10},{6,14},... | collective-permute-start | bytes 1179656 | tf_op jit(solution)/shard_map/ppermute | solution.py:43
  48.9 7.5 %collective-permute-start.9 = (f32[4,2,128]{2,1,0:T(2,128)S(1)}, f32[4,2,128]{2,1,0:T(2,128)S(1)}, u32[]{:S(2)}, u32[]{:S(2)}) collective-permute-start(f32[4,2,128]{2,1,0:T(2,128)S(1)} %pad_maximum_fusion.24), channel_id=1, source_target_pairs={{0,16},{16,0},{1,17},{17,1},{2,18},{18,2},{3,19},{19,3},{4,20},{20... | collective-permute-start | bytes 12296 | tf_op jit(solution)/shard_map/ppermute | solution.py:35
  53.8 11.5 %collective-permute-start.8 = (bf16[2048,512]{1,0:T(8,128)(2,1)}, bf16[2048,512]{1,0:T(8,128)(2,1)S(1)}, u32[]{:S(2)}, u32[]{:S(2)}) collective-permute-start(bf16[2048,512]{1,0:T(8,128)(2,1)} %collective-permute-done.6), channel_id=1, source_target_pairs={{0,1},{1,0},{2,3},{3,2},{4,5},{5,4},{6,7},{7,6},{8,9},{9,8},{10,11... | collective-permute-start | bytes 6291464 | tf_op jit(solution)/shard_map/ppermute | solution.py:39
  56.4 38.1 %collective-permute-start.30 = (bf16[384,512]{1,0:T(8,128)(2,1)S(1)}, bf16[384,512]{1,0:T(8,128)(2,1)S(1)}, u32[]{:S(2)}, u32[]{:S(2)}) collective-permute-start(bf16[384,512]{1,0:T(8,128)(2,1)S(1)} %copy-done.21), channel_id=1, source_target_pairs={{0,12},{4,8},{8,4},{12,0},{1,13},{5,9},{9,5},{13,1},{2,14},{6,10},... | collective-permute-start | bytes 1179656 | tf_op jit(solution)/shard_map/ppermute | solution.py:43
  58.8 24.2 %collective-permute-start.5 = (bf16[256,2048]{1,0:T(8,128)(2,1)S(1)}, bf16[256,2048]{1,0:T(8,128)(2,1)S(1)}, u32[]{:S(2)}, u32[]{:S(2)}) collective-permute-start(bf16[256,2048]{1,0:T(8,128)(2,1)S(1)} %get-tuple-element.90), channel_id=1, source_target_pairs={{0,16},{16,0},{1,17},{17,1},{2,18},{18,2},{3,19},{19,3},{4,20},{20... | collective-permute-start | bytes 3145736 | tf_op jit(solution)/shard_map/ppermute | solution.py:35
  65.3 27.7 %copy-start.28 = (bf16[2048,512]{1,0:T(8,128)(2,1)}, bf16[2048,512]{1,0:T(8,128)(2,1)S(1)}, u32[]{:S(2)}) copy-start(bf16[2048,512]{1,0:T(8,128)(2,1)S(1)} %collective-permute-done.8) | copy-start | bytes 6291460
  65.3 19.9 %collective-permute-start.11 = (bf16[256,1024]{0,1:T(8,128)(2,1)S(1)}, bf16[256,1024]{0,1:T(8,128)(2,1)S(1)}, u32[]{:S(2)}, u32[]{:S(2)}) collective-permute-start(bf16[256,1024]{0,1:T(8,128)(2,1)S(1)} %fusion.80), channel_id=1, source_target_pairs={{0,4},{4,0},{8,12},{12,8},{1,5},{5,1},{9,13},{13,9},{2,6},{6,2},{1... | collective-permute-start | bytes 1572872 | tf_op jit(solution)/shard_map/ppermute | solution.py:43
  83.0 16.8 %collective-permute-start.12 = (bf16[256,1024]{0,1:T(8,128)(2,1)S(1)}, bf16[256,1024]{0,1:T(8,128)(2,1)S(1)}, u32[]{:S(2)}, u32[]{:S(2)}) collective-permute-start(bf16[256,1024]{0,1:T(8,128)(2,1)S(1)} %fusion.78), channel_id=1, source_target_pairs={{0,4},{4,0},{8,12},{12,8},{1,5},{5,1},{9,13},{13,9},{2,6},{6,2},{1... | collective-permute-start | bytes 1572872 | tf_op jit(solution)/shard_map/ppermute | solution.py:43
  85.2 37.5 %collective-permute-start.10 = (bf16[256,2048]{1,0:T(8,128)(2,1)S(1)}, bf16[256,2048]{1,0:T(8,128)(2,1)}, u32[]{:S(2)}, u32[]{:S(2)}) collective-permute-start(bf16[256,2048]{1,0:T(8,128)(2,1)S(1)} %get-tuple-element.37), channel_id=1, source_target_pairs={{0,16},{16,0},{1,17},{17,1},{2,18},{18,2},{3,19},{19,3},{4,20},{20... | collective-permute-start | bytes 3145736 | tf_op jit(solution)/shard_map/ppermute | solution.py:35
  94.3 41.2 %collective-permute-start.14 = (bf16[256,2048]{0,1:T(8,128)(2,1)S(1)}, bf16[256,2048]{0,1:T(8,128)(2,1)S(1)}, u32[]{:S(2)}, u32[]{:S(2)}) collective-permute-start(bf16[256,2048]{0,1:T(8,128)(2,1)S(1)} %pad_maximum_fusion.5), channel_id=1, source_target_pairs={{0,4},{4,0},{8,12},{12,8},{1,5},{5,1},{9,13},{13,9},{2,6},{6,2},{1... | collective-permute-start | bytes 3145736 | tf_op jit(solution)/shard_map/ppermute | solution.py:43
  96.3 132.6 %collective-permute-start.31 = (bf16[1536,512]{1,0:T(8,128)(2,1)S(1)}, bf16[1536,512]{1,0:T(8,128)(2,1)S(1)}, u32[]{:S(2)}, u32[]{:S(2)}) collective-permute-start(bf16[1536,512]{1,0:T(8,128)(2,1)S(1)} %pad_maximum_fusion.2), channel_id=1, source_target_pairs={{0,1},{1,0},{2,3},{3,2},{4,5},{5,4},{6,7},{7,6},{8,9},{9,8},{10,11... | collective-permute-start | bytes 4718600 | tf_op jit(solution)/shard_map/ppermute | solution.py:39
  98.2 23.2 %collective-permute-start.51 = (bf16[128,2048]{1,0:T(8,128)(2,1)S(1)}, bf16[128,2048]{1,0:T(8,128)(2,1)S(1)}, u32[]{:S(2)}, u32[]{:S(2)}) collective-permute-start(bf16[128,2048]{1,0:T(8,128)(2,1)S(1)} %pad_maximum_fusion.19), channel_id=1, source_target_pairs={{0,16},{16,0},{1,17},{17,1},{2,18},{18,2},{3,19},{19,3},{4,20},{20... | collective-permute-start | bytes 1572872 | tf_op jit(solution)/shard_map/ppermute | solution.py:35
  99.8 70.9 %collective-permute-start.32 = (bf16[1536,512]{1,0:T(8,128)(2,1)S(1)}, bf16[1536,512]{1,0:T(8,128)(2,1)S(1)}, u32[]{:S(2)}, u32[]{:S(2)}) collective-permute-start(bf16[1536,512]{1,0:T(8,128)(2,1)S(1)} %pad_maximum_fusion.2), channel_id=1, source_target_pairs={{0,2},{1,3},{2,0},{3,1},{4,6},{5,7},{6,4},{7,5},{8,10},{9,11},{10,... | collective-permute-start | bytes 4718600 | tf_op jit(solution)/shard_map/ppermute | solution.py:39
  121.4 35.9 %collective-permute-start.21 = (bf16[128,1024]{0,1:T(8,128)(2,1)S(1)}, bf16[128,1024]{0,1:T(8,128)(2,1)S(1)}, u32[]{:S(2)}, u32[]{:S(2)}) collective-permute-start(bf16[128,1024]{0,1:T(8,128)(2,1)S(1)} %slice.453), channel_id=1, source_target_pairs={{0,8},{4,12},{8,0},{12,4},{1,9},{5,13},{9,1},{13,5},{2,10},{6,14},... | collective-permute-start | bytes 786440 | tf_op jit(solution)/shard_map/ppermute | solution.py:43
  122.6 34.7 %collective-permute-start.22 = (bf16[128,1024]{0,1:T(8,128)(2,1)S(1)}, bf16[128,1024]{0,1:T(8,128)(2,1)S(1)}, u32[]{:S(2)}, u32[]{:S(2)}) collective-permute-start(bf16[128,1024]{0,1:T(8,128)(2,1)S(1)} %slice.452), channel_id=1, source_target_pairs={{0,8},{4,12},{8,0},{12,4},{1,9},{5,13},{9,1},{13,5},{2,10},{6,14},... | collective-permute-start | bytes 786440 | tf_op jit(solution)/shard_map/ppermute | solution.py:43
  135.8 32.7 %collective-permute-start.15 = (bf16[128,2048]{0,1:T(8,128)(2,1)S(1)}, bf16[128,2048]{0,1:T(8,128)(2,1)S(1)}, u32[]{:S(2)}, u32[]{:S(2)}) collective-permute-start(bf16[128,2048]{0,1:T(8,128)(2,1)S(1)} %slice.451), channel_id=1, source_target_pairs={{0,8},{4,12},{8,0},{12,4},{1,9},{5,13},{9,1},{13,5},{2,10},{6,14},... | collective-permute-start | bytes 1572872 | tf_op jit(solution)/shard_map/ppermute | solution.py:43
  157.5 13.9 %collective-permute-start.24 = (bf16[128,1024]{0,1:T(8,128)(2,1)S(1)}, bf16[128,1024]{0,1:T(8,128)(2,1)S(1)}, u32[]{:S(2)}, u32[]{:S(2)}) collective-permute-start(bf16[128,1024]{0,1:T(8,128)(2,1)S(1)} %get-tuple-element.73), channel_id=1, source_target_pairs={{0,16},{16,0},{1,17},{17,1},{2,18},{18,2},{3,19},{19,3},{4,20},{20... | collective-permute-start | bytes 786440 | tf_op jit(solution)/shard_map/ppermute | solution.py:35
  159.1 12.4 %collective-permute-start.25 = (bf16[128,1024]{0,1:T(8,128)(2,1)S(1)}, bf16[128,1024]{0,1:T(8,128)(2,1)S(1)}, u32[]{:S(2)}, u32[]{:S(2)}) collective-permute-start(bf16[128,1024]{0,1:T(8,128)(2,1)S(1)} %get-tuple-element.207), channel_id=1, source_target_pairs={{0,16},{16,0},{1,17},{17,1},{2,18},{18,2},{3,19},{19,3},{4,20},{20... | collective-permute-start | bytes 786440 | tf_op jit(solution)/shard_map/ppermute | solution.py:35
  168.6 14.8 %collective-permute-start.23 = (bf16[128,2048]{0,1:T(8,128)(2,1)S(1)}, bf16[128,2048]{0,1:T(8,128)(2,1)S(1)}, u32[]{:S(2)}, u32[]{:S(2)}) collective-permute-start(bf16[128,2048]{0,1:T(8,128)(2,1)S(1)} %get-tuple-element.71), channel_id=1, source_target_pairs={{0,16},{16,0},{1,17},{17,1},{2,18},{18,2},{3,19},{19,3},{4,20},{20... | collective-permute-start | bytes 1572872 | tf_op jit(solution)/shard_map/ppermute | solution.py:35
  170.6 90.1 %collective-permute-start.13 = (bf16[128,2048]{1,0:T(8,128)(2,1)S(1)}, bf16[128,2048]{1,0:T(8,128)(2,1)S(1)}, u32[]{:S(2)}, u32[]{:S(2)}) collective-permute-start(bf16[128,2048]{1,0:T(8,128)(2,1)S(1)} %pad_maximum_fusion.16), channel_id=1, source_target_pairs={{0,16},{16,0},{1,17},{17,1},{2,18},{18,2},{3,19},{19,3},{4,20},{20... | collective-permute-start | bytes 1572872 | tf_op jit(solution)/shard_map/ppermute | solution.py:35
  171.4 27.6 %collective-permute-start.16 = (bf16[384,512]{1,0:T(8,128)(2,1)S(1)}, bf16[384,512]{1,0:T(8,128)(2,1)S(1)}, u32[]{:S(2)}, u32[]{:S(2)}) collective-permute-start(bf16[384,512]{1,0:T(8,128)(2,1)S(1)} %copy-done.20), channel_id=1, source_target_pairs={{0,4},{4,0},{8,12},{12,8},{1,5},{5,1},{9,13},{13,9},{2,6},{6,2},{1... | collective-permute-start | bytes 1179656 | tf_op jit(solution)/shard_map/ppermute | solution.py:43
  171.4 29.6 %collective-permute-start.17 = (bf16[384,512]{1,0:T(8,128)(2,1)S(1)}, bf16[384,512]{1,0:T(8,128)(2,1)S(1)}, u32[]{:S(2)}, u32[]{:S(2)}) collective-permute-start(bf16[384,512]{1,0:T(8,128)(2,1)S(1)} %copy-done.20), channel_id=1, source_target_pairs={{0,8},{4,12},{8,0},{12,4},{1,9},{5,13},{9,1},{13,5},{2,10},{6,14},... | collective-permute-start | bytes 1179656 | tf_op jit(solution)/shard_map/ppermute | solution.py:43
  183.5 19.1 %collective-permute-start.18 = (bf16[384,512]{1,0:T(8,128)(2,1)S(1)}, bf16[384,512]{1,0:T(8,128)(2,1)S(1)}, u32[]{:S(2)}, u32[]{:S(2)}) collective-permute-start(bf16[384,512]{1,0:T(8,128)(2,1)S(1)} %copy-done.20), channel_id=1, source_target_pairs={{0,12},{4,8},{8,4},{12,0},{1,13},{5,9},{9,5},{13,1},{2,14},{6,10},... | collective-permute-start | bytes 1179656 | tf_op jit(solution)/shard_map/ppermute | solution.py:43
  199.0 31.6 %collective-permute-start.33 = (bf16[1536,512]{1,0:T(8,128)(2,1)S(1)}, bf16[1536,512]{1,0:T(8,128)(2,1)S(1)}, u32[]{:S(2)}, u32[]{:S(2)}) collective-permute-start(bf16[1536,512]{1,0:T(8,128)(2,1)S(1)} %collective-permute-done.32), channel_id=1, source_target_pairs={{0,1},{1,0},{2,3},{3,2},{4,5},{5,4},{6,7},{7,6},{8,9},{9,8},{10,11... | collective-permute-start | bytes 4718600 | tf_op jit(solution)/shard_map/ppermute | solution.py:39
  201.1 14.9 %collective-permute-start.26 = (bf16[256,1024]{0,1:T(8,128)(2,1)S(1)}, bf16[256,1024]{0,1:T(8,128)(2,1)S(1)}, u32[]{:S(2)}, u32[]{:S(2)}) collective-permute-start(bf16[256,1024]{0,1:T(8,128)(2,1)S(1)} %fusion.28), channel_id=1, source_target_pairs={{0,16},{16,0},{1,17},{17,1},{2,18},{18,2},{3,19},{19,3},{4,20},{20... | collective-permute-start | bytes 1572872 | tf_op jit(solution)/shard_map/ppermute | solution.py:35
  202.6 22.0 %collective-permute-start.27 = (bf16[256,1024]{0,1:T(8,128)(2,1)S(1)}, bf16[256,1024]{0,1:T(8,128)(2,1)S(1)}, u32[]{:S(2)}, u32[]{:S(2)}) collective-permute-start(bf16[256,1024]{0,1:T(8,128)(2,1)S(1)} %fusion.22), channel_id=1, source_target_pairs={{0,16},{16,0},{1,17},{17,1},{2,18},{18,2},{3,19},{19,3},{4,20},{20... | collective-permute-start | bytes 1572872 | tf_op jit(solution)/shard_map/ppermute | solution.py:35
  215.9 64.8 %collective-permute-start.19 = (bf16[1536,512]{1,0:T(8,128)(2,1)S(1)}, bf16[1536,512]{1,0:T(8,128)(2,1)S(1)}, u32[]{:S(2)}, u32[]{:S(2)}) collective-permute-start(bf16[1536,512]{1,0:T(8,128)(2,1)S(1)} %pad_maximum_fusion.1), channel_id=1, source_target_pairs={{0,1},{1,0},{2,3},{3,2},{4,5},{5,4},{6,7},{7,6},{8,9},{9,8},{10,11... | collective-permute-start | bytes 4718600 | tf_op jit(solution)/shard_map/ppermute | solution.py:39
  224.6 33.8 %collective-permute-start.20 = (bf16[1536,512]{1,0:T(8,128)(2,1)S(1)}, bf16[1536,512]{1,0:T(8,128)(2,1)S(1)}, u32[]{:S(2)}, u32[]{:S(2)}) collective-permute-start(bf16[1536,512]{1,0:T(8,128)(2,1)S(1)} %pad_maximum_fusion.1), channel_id=1, source_target_pairs={{0,2},{1,3},{2,0},{3,1},{4,6},{5,7},{6,4},{7,5},{8,10},{9,11},{10,... | collective-permute-start | bytes 4718600 | tf_op jit(solution)/shard_map/ppermute | solution.py:39
  258.4 21.6 %copy-start.7 = (bf16[1536,512]{1,0:T(8,128)(2,1)}, bf16[1536,512]{1,0:T(8,128)(2,1)S(1)}, u32[]{:S(2)}) copy-start(bf16[1536,512]{1,0:T(8,128)(2,1)S(1)} %collective-permute-done.20) | copy-start | bytes 4718596
  258.5 22.9 %collective-permute-start.34 = (bf16[1536,512]{1,0:T(8,128)(2,1)S(1)}, bf16[1536,512]{1,0:T(8,128)(2,1)S(1)}, u32[]{:S(2)}, u32[]{:S(2)}) collective-permute-start(bf16[1536,512]{1,0:T(8,128)(2,1)S(1)} %collective-permute-done.20), channel_id=1, source_target_pairs={{0,1},{1,0},{2,3},{3,2},{4,5},{5,4},{6,7},{7,6},{8,9},{9,8},{10,11... | collective-permute-start | bytes 4718600 | tf_op jit(solution)/shard_map/ppermute | solution.py:39
  258.5 4.0 %collective-permute-start.36 = (f32[128,1]{0,1:T(1,128)S(1)}, f32[128,1]{0,1:T(1,128)S(1)}, u32[]{:S(2)}, u32[]{:S(2)}) collective-permute-start(f32[128,1]{0,1:T(1,128)S(1)} %slice_bitcast_fusion), channel_id=1, source_target_pairs={{0,16},{16,0},{1,17},{17,1},{2,18},{18,2},{3,19},{19,3},{4,20},{20... | collective-permute-start | bytes 1544 | tf_op jit(solution)/shard_map/ppermute | solution.py:35
  260.2 12.0 %collective-permute-start.37 = (f32[128,768]{1,0:T(8,128)S(1)}, f32[128,768]{1,0:T(8,128)S(1)}, u32[]{:S(2)}, u32[]{:S(2)}) collective-permute-start(f32[128,768]{1,0:T(8,128)S(1)} %slice.345), channel_id=1, source_target_pairs={{0,16},{16,0},{1,17},{17,1},{2,18},{18,2},{3,19},{19,3},{4,20},{20... | collective-permute-start | bytes 1179656 | tf_op jit(solution)/shard_map/ppermute | solution.py:35
  260.7 19.2 %collective-permute-start.35 = (f32[128,768]{1,0:T(8,128)S(1)}, f32[128,768]{1,0:T(8,128)S(1)}, u32[]{:S(2)}, u32[]{:S(2)}) collective-permute-start(f32[128,768]{1,0:T(8,128)S(1)} %slice.343), channel_id=1, source_target_pairs={{0,16},{16,0},{1,17},{17,1},{2,18},{18,2},{3,19},{19,3},{4,20},{20... | collective-permute-start | bytes 1179656 | tf_op jit(solution)/shard_map/ppermute | solution.py:35
  262.4 21.8 %collective-permute-start.52 = (bf16[256,1024]{1,0:T(8,128)(2,1)S(1)}, bf16[256,1024]{1,0:T(8,128)(2,1)S(1)}, u32[]{:S(2)}, u32[]{:S(2)}) collective-permute-start(bf16[256,1024]{1,0:T(8,128)(2,1)S(1)} %slice.282), channel_id=1, source_target_pairs={{0,2},{1,3},{2,0},{3,1},{4,6},{5,7},{6,4},{7,5},{8,10},{9,11},{10,... | collective-permute-start | bytes 1572872 | tf_op jit(solution)/shard_map/ppermute | solution.py:39
  283.8 21.0 %collective-permute-start.38 = (f32[128,1536]{1,0:T(8,128)S(1)}, f32[128,1536]{1,0:T(8,128)S(1)}, u32[]{:S(2)}, u32[]{:S(2)}) collective-permute-start(f32[128,1536]{1,0:T(8,128)S(1)} %slice.341), channel_id=1, source_target_pairs={{0,16},{16,0},{1,17},{17,1},{2,18},{18,2},{3,19},{19,3},{4,20},{20... | collective-permute-start | bytes 2359304 | tf_op jit(solution)/shard_map/ppermute | solution.py:35
  285.1 5.9 %collective-permute-start.42 = (f32[32,768]{1,0:T(8,128)S(1)}, f32[32,768]{1,0:T(8,128)S(1)}, u32[]{:S(2)}, u32[]{:S(2)}) collective-permute-start(f32[32,768]{1,0:T(8,128)S(1)} %get-tuple-element.173), channel_id=1, source_target_pairs={{0,4},{4,0},{8,12},{12,8},{1,5},{5,1},{9,13},{13,9},{2,6},{6,2},{1... | collective-permute-start | bytes 294920 | tf_op jit(solution)/shard_map/ppermute | solution.py:43
  285.2 11.9 %collective-permute-start.43 = (f32[32,768]{1,0:T(8,128)S(1)}, f32[32,768]{1,0:T(8,128)S(1)}, u32[]{:S(2)}, u32[]{:S(2)}) collective-permute-start(f32[32,768]{1,0:T(8,128)S(1)} %get-tuple-element.171), channel_id=1, source_target_pairs={{0,8},{4,12},{8,0},{12,4},{1,9},{5,13},{9,1},{13,5},{2,10},{6,14},... | collective-permute-start | bytes 294920 | tf_op jit(solution)/shard_map/ppermute | solution.py:43
  289.0 12.8 %collective-permute-start.44 = (f32[32,768]{1,0:T(8,128)S(1)}, f32[32,768]{1,0:T(8,128)S(1)}, u32[]{:S(2)}, u32[]{:S(2)}) collective-permute-start(f32[32,768]{1,0:T(8,128)S(1)} %get-tuple-element.172), channel_id=1, source_target_pairs={{0,12},{4,8},{8,4},{12,0},{1,13},{5,9},{9,5},{13,1},{2,14},{6,10},... | collective-permute-start | bytes 294920 | tf_op jit(solution)/shard_map/ppermute | solution.py:43
  289.6 12.5 %collective-permute-start.39 = (f32[32,768]{1,0:T(8,128)S(1)}, f32[32,768]{1,0:T(8,128)S(1)}, u32[]{:S(2)}, u32[]{:S(2)}) collective-permute-start(f32[32,768]{1,0:T(8,128)S(1)} %get-tuple-element.176), channel_id=1, source_target_pairs={{0,4},{4,0},{8,12},{12,8},{1,5},{5,1},{9,13},{13,9},{2,6},{6,2},{1... | collective-permute-start | bytes 294920 | tf_op jit(solution)/shard_map/ppermute | solution.py:43
  291.0 12.4 %collective-permute-start.40 = (f32[32,768]{1,0:T(8,128)S(1)}, f32[32,768]{1,0:T(8,128)S(1)}, u32[]{:S(2)}, u32[]{:S(2)}) collective-permute-start(f32[32,768]{1,0:T(8,128)S(1)} %get-tuple-element.174), channel_id=1, source_target_pairs={{0,8},{4,12},{8,0},{12,4},{1,9},{5,13},{9,1},{13,5},{2,10},{6,14},... | collective-permute-start | bytes 294920 | tf_op jit(solution)/shard_map/ppermute | solution.py:43
  297.0 7.5 %collective-permute-start.41 = (f32[32,768]{1,0:T(8,128)S(1)}, f32[32,768]{1,0:T(8,128)S(1)}, u32[]{:S(2)}, u32[]{:S(2)}) collective-permute-start(f32[32,768]{1,0:T(8,128)S(1)} %get-tuple-element.175), channel_id=1, source_target_pairs={{0,12},{4,8},{8,4},{12,0},{1,13},{5,9},{9,5},{13,1},{2,14},{6,10},... | collective-permute-start | bytes 294920 | tf_op jit(solution)/shard_map/ppermute | solution.py:43
  310.3 8.4 %collective-permute-start.47 = (bf16[128,1536]{1,0:T(8,128)(2,1)S(1)}, bf16[128,1536]{1,0:T(8,128)(2,1)S(1)}, u32[]{:S(2)}, u32[]{:S(2)}) collective-permute-start(bf16[128,1536]{1,0:T(8,128)(2,1)S(1)} %get-tuple-element.198), channel_id=1, source_target_pairs={{0,2},{1,3},{2,0},{3,1},{4,6},{5,7},{6,4},{7,5},{8,10},{9,11},{10,... | collective-permute-start | bytes 1179656 | tf_op jit(solution)/shard_map/ppermute | solution.py:39
  311.0 9.9 %collective-permute-start.45 = (bf16[128,1536]{1,0:T(8,128)(2,1)S(1)}, bf16[128,1536]{1,0:T(8,128)(2,1)S(1)}, u32[]{:S(2)}, u32[]{:S(2)}) collective-permute-start(bf16[128,1536]{1,0:T(8,128)(2,1)S(1)} %get-tuple-element.198), channel_id=1, source_target_pairs={{0,16},{16,0},{1,17},{17,1},{2,18},{18,2},{3,19},{19,3},{4,20},{20... | collective-permute-start | bytes 1179656 | tf_op jit(solution)/shard_map/ppermute | solution.py:35
  312.6 17.7 %collective-permute-start.53 = (bf16[512,512]{1,0:T(8,128)(2,1)S(1)}, bf16[512,512]{1,0:T(8,128)(2,1)S(1)}, u32[]{:S(2)}, u32[]{:S(2)}) collective-permute-start(bf16[512,512]{1,0:T(8,128)(2,1)S(1)} %get-tuple-element.55), channel_id=1, source_target_pairs={{0,1},{1,0},{2,3},{3,2},{4,5},{5,4},{6,7},{7,6},{8,9},{9,8},{10,11... | collective-permute-start | bytes 1572872 | tf_op jit(solution)/shard_map/ppermute | solution.py:39
  318.7 5.9 %collective-permute-start.48 = (bf16[64,1536]{1,0:T(8,128)(2,1)S(1)}, bf16[64,1536]{1,0:T(8,128)(2,1)S(1)}, u32[]{:S(2)}, u32[]{:S(2)}) collective-permute-start(bf16[64,1536]{1,0:T(8,128)(2,1)S(1)} %slice.346), channel_id=1, source_target_pairs={{0,16},{16,0},{1,17},{17,1},{2,18},{18,2},{3,19},{19,3},{4,20},{20... | collective-permute-start | bytes 589832 | tf_op jit(solution)/shard_map/ppermute | solution.py:35
  321.0 5.7 %collective-permute-start.49 = (bf16[64,1536]{1,0:T(8,128)(2,1)S(1)}, bf16[64,1536]{1,0:T(8,128)(2,1)S(1)}, u32[]{:S(2)}, u32[]{:S(2)}) collective-permute-start(bf16[64,1536]{1,0:T(8,128)(2,1)S(1)} %slice.347), channel_id=1, source_target_pairs={{0,2},{1,3},{2,0},{3,1},{4,6},{5,7},{6,4},{7,5},{8,10},{9,11},{10,... | collective-permute-start | bytes 589832 | tf_op jit(solution)/shard_map/ppermute | solution.py:39
  326.7 3.5 collective-permute-start.50
  332.3 12.5 %collective-permute-start.54 = (bf16[768,256]{1,0:T(8,128)(2,1)S(1)}, bf16[768,256]{1,0:T(8,128)(2,1)S(1)}, u32[]{:S(2)}, u32[]{:S(2)}) collective-permute-start(bf16[768,256]{1,0:T(8,128)(2,1)S(1)} %pad_maximum_fusion.20), channel_id=1, source_target_pairs={{0,4},{4,0},{8,12},{12,8},{1,5},{5,1},{9,13},{13,9},{2,6},{6,2},{1... | collective-permute-start | bytes 1179656 | tf_op jit(solution)/shard_map/ppermute | solution.py:43
  335.3 21.6 %collective-permute-start.56 = (bf16[768,256]{1,0:T(8,128)(2,1)S(1)}, bf16[768,256]{1,0:T(8,128)(2,1)S(1)}, u32[]{:S(2)}, u32[]{:S(2)}) collective-permute-start(bf16[768,256]{1,0:T(8,128)(2,1)S(1)} %pad_maximum_fusion.21), channel_id=1, source_target_pairs={{0,4},{4,0},{8,12},{12,8},{1,5},{5,1},{9,13},{13,9},{2,6},{6,2},{1... | collective-permute-start | bytes 1179656 | tf_op jit(solution)/shard_map/ppermute | solution.py:43
  344.9 12.1 %collective-permute-start.55 = (bf16[384,256]{1,0:T(8,128)(2,1)S(1)}, bf16[384,256]{1,0:T(8,128)(2,1)S(1)}, u32[]{:S(2)}, u32[]{:S(2)}) collective-permute-start(bf16[384,256]{1,0:T(8,128)(2,1)S(1)} %fusion.93), channel_id=1, source_target_pairs={{0,8},{4,12},{8,0},{12,4},{1,9},{5,13},{9,1},{13,5},{2,10},{6,14},... | collective-permute-start | bytes 589832 | tf_op jit(solution)/shard_map/ppermute | solution.py:43
  347.6 22.0 %collective-permute-start.46 = (bf16[128,2048]{1,0:T(8,128)(2,1)S(1)}, bf16[128,2048]{1,0:T(8,128)(2,1)S(1)}, u32[]{:S(2)}, u32[]{:S(2)}) collective-permute-start(bf16[128,2048]{1,0:T(8,128)(2,1)S(1)} %pad_maximum_fusion.18), channel_id=1, source_target_pairs={{0,16},{16,0},{1,17},{17,1},{2,18},{18,2},{3,19},{19,3},{4,20},{20... | collective-permute-start | bytes 1572872 | tf_op jit(solution)/shard_map/ppermute | solution.py:35
  357.2 11.6 %collective-permute-start.57 = (bf16[384,256]{1,0:T(8,128)(2,1)S(1)}, bf16[384,256]{1,0:T(8,128)(2,1)S(1)}, u32[]{:S(2)}, u32[]{:S(2)}) collective-permute-start(bf16[384,256]{1,0:T(8,128)(2,1)S(1)} %get-tuple-element.92), channel_id=1, source_target_pairs={{0,8},{4,12},{8,0},{12,4},{1,9},{5,13},{9,1},{13,5},{2,10},{6,14},... | collective-permute-start | bytes 589832 | tf_op jit(solution)/shard_map/ppermute | solution.py:43
  (27 other events, 85.0 us)

commit v4 on v0

--- a/solution.py
+++ b/solution.py
@@ -1,15 +1,27 @@
+import functools
+
 import jax
 import jax.numpy as jnp
 from jax import lax
+from jax.experimental import pallas as pl
+from jax.experimental.pallas import tpu as pltpu
 from jax.sharding import PartitionSpec as P
 
 QH = 64
 KVH = 4
 HD = 128
 
-
 EPSILON = 1e-06
 MASKED = -1e30
+PLANE = ("ctx", "rep")
+LAST = (((1,), (1,)), ((), ()))
+FIRST = (((0,), (0,)), ((), ()))
+F32 = jnp.float32
+BF16 = jnp.bfloat16
+
+
+def matmul(left, right, dims=(((1,), (0,)), ((), ()))):
+    return lax.dot_general(left, right, dims, preferred_element_type=F32)
 
 
 def rms_scale(values, gain):
@@ -17,7 +29,773 @@
     return values * lax.rsqrt(mean_square + EPSILON) * gain
 
 
+class Order:
+    def __init__(self):
+        self.last = None
+
+    def take(self, *values):
+        if self.last is None:
+            return values if len(values) > 1 else values[0]
+        values = lax.optimization_barrier((*values, self.last))[:-1]
+        return values if len(values) > 1 else values[0]
+
+    def ends(self, value):
+        self.last = value
+        return value
+
+    def waits(self, *values):
+        values = lax.optimization_barrier((*values, self.last))[:-1]
+        self.last = values[0]
+        return values if len(values) > 1 else values[0]
+
+
+def swap_x(value):
+    return lax.ppermute(value, "ctx", [(0, 1), (1, 0)])
+
+
+def swap_rep(value, offset):
+    return lax.ppermute(value, "rep", [(i, i ^ offset) for i in range(4)])
+
+
+def swap_z(value, offset):
+    return lax.ppermute(value, "vocab", [(i, i ^ offset) for i in range(4)])
+
+
+def pick(value, index, size, axis):
+    return lax.dynamic_slice_in_dim(value, index * size, size, axis)
+
+
+def split_relative(value, index, count, axis):
+    size = value.shape[axis] // count
+    return [pick(value, index ^ r, size, axis) for r in range(count)]
+
+
+def join_absolute(blocks, index, axis):
+    count = len(blocks)
+    return jnp.concatenate(
+        [
+            lax.select_n(index, *[blocks[j ^ i] for i in range(count)])
+            for j in range(count)
+        ],
+        axis=axis,
+    )
+
+
+def line_gather(own):
+    return [own] + [swap_z(own, r) for r in (1, 2, 3)]
+
+
+def line_exchange(value):
+    blocks = split_relative(value, lax.axis_index("vocab"), 4, 0)
+    return [blocks[0]] + [swap_z(blocks[r], r) for r in (1, 2, 3)]
+
+
+def line_joined(received):
+    return join_absolute(received, lax.axis_index("vocab"), 0)
+
+
+HEADS_STEP = 4
+
+
+def attend_kernel(facts, query, rows, out):
+    pos_ctx = query.shape[1]
+    keys = rows.shape[2]
+    length = facts[pl.program_id(0)]
+    query_pos = facts[pl.num_programs(0)] + lax.broadcasted_iota(jnp.int32, (pos_ctx, keys), 0)
+    key_pos = facts[pl.num_programs(0) + 1] + lax.broadcasted_iota(jnp.int32, (pos_ctx, keys), 1)
+    allowed = (key_pos <= query_pos) & (key_pos < length) & (key_pos >= 0)
+    bias = jnp.where(allowed, 0.0, MASKED)
+    for head in range(query.shape[2] // HD):
+        cols = slice(head * HD, (head + 1) * HD)
+        scores = matmul(query[0, :, cols], rows[0, 0], LAST) * HD ** (-0.5) + bias
+        peak = jnp.max(scores, axis=-1, keepdims=True)
+        exponent = jnp.exp(scores - peak)
+        total = jnp.sum(exponent, axis=-1, keepdims=True)
+        weighted = matmul(exponent.astype(BF16), rows[1, 0])
+        out[:, cols] = (weighted / total).astype(BF16)
+
+
+def attend(queries, rows, lengths):
+    seq_dev, pos_ctx, head_cols = queries.shape
+    ctx_index = lax.axis_index("ctx")
+    facts = jnp.concatenate([lengths, jnp.stack([ctx_index * pos_ctx, (ctx_index - 1) * pos_ctx])])
+    step_cols = HEADS_STEP * HD
+    return pl.pallas_call(
+        attend_kernel,
+        out_shape=jax.ShapeDtypeStruct((seq_dev * pos_ctx, head_cols), BF16),
+        grid_spec=pltpu.PrefetchScalarGridSpec(
+            num_scalar_prefetch=1,
+            grid=(seq_dev, head_cols // step_cols),
+            in_specs=[
+                pl.BlockSpec(
+                    (1, pos_ctx, step_cols), lambda s, h, facts: (s, 0, h)
+                ),
+                pl.BlockSpec((2, 1, rows.shape[2], HD), lambda s, h, facts: (0, s, 0, 0)),
+            ],
+            out_specs=pl.BlockSpec((pos_ctx, step_cols), lambda s, h, facts: (s, h)),
+        ),
+        cost_estimate=pl.CostEstimate(flops=0, bytes_accessed=0, transcendentals=0),
+        compiler_params=pltpu.CompilerParams(vmem_limit_bytes=32 * 2**20),
+        name="attend",
+    )(facts, queries, rows)
+
+
+FREE = pl.CostEstimate(flops=0, bytes_accessed=0, transcendentals=0)
+VMEM_BYTES = 48 * 2**20
+
+
+def whole(shape):
+    return pl.BlockSpec(shape, lambda *_: (0,) * len(shape))
+
+
+def project_kernel(count, parts, *refs):
+    groups = len(parts)
+    rows, placers, refs = refs[:groups], refs[groups : 2 * groups], refs[2 * groups :]
+    residual, weights, outs = refs[0], refs[1 : 1 + count], list(refs[1 + count :])
+    for row, placer, part in zip(rows, placers, parts):
+        targets = [outs.pop(0) for _ in part]
+        for r in range(count):
+            total = matmul(row[...], weights[r][...]) + matmul(placer[...], residual[r])
+            first = 0
+            for target, size in zip(targets, part):
+                target[r] = total[first : first + size].astype(BF16)
+                first += size
+
+
+def project(rows, placers, residual, weights, parts):
+    count = len(weights)
+    size = weights[0].shape[1]
+    tile = size // 2
+    cuts = [part for group in parts for part in group]
+    return pl.pallas_call(
+        functools.partial(project_kernel, count, parts),
+        out_shape=[jax.ShapeDtypeStruct((count, part, size), BF16) for part in cuts],
+        grid=(2,),
+        in_specs=[whole(value.shape) for value in (*rows, *placers)]
+        + [pl.BlockSpec((count, residual.shape[1], tile), lambda j: (0, 0, j))]
+        + [pl.BlockSpec((weights[0].shape[0], tile), lambda j: (0, j))] * count,
+        out_specs=[pl.BlockSpec((count, part, tile), lambda j: (0, 0, j)) for part in cuts],
+        cost_estimate=FREE,
+        compiler_params=pltpu.CompilerParams(vmem_limit_bytes=VMEM_BYTES),
+        name="project",
+    )(*rows, *placers, residual, *weights)
+
+
+def sort_kernel(placer, heads, sent, kept):
+    half = sent.shape[0]
+    sent[...] = matmul(placer[:half], heads[...]).astype(BF16)
+    kept[...] = matmul(placer[half:], heads[...]).astype(BF16)
+
+
+def sorted_rows(placer, heads):
+    rows, width = heads.shape
+    tile = width // 4
+    return pl.pallas_call(
+        sort_kernel,
+        out_shape=[jax.ShapeDtypeStruct((rows // 2, width), BF16)] * 2,
+        grid=(4,),
+        in_specs=[whole(placer.shape), pl.BlockSpec((rows, tile), lambda j: (0, j))],
+        out_specs=[pl.BlockSpec((rows // 2, tile), lambda j: (0, j))] * 2,
+        cost_estimate=FREE,
+        compiler_params=pltpu.CompilerParams(vmem_limit_bytes=VMEM_BYTES),
+        name="sorted_rows",
+    )(placer, heads)
+
+
+def logits_kernel(rows, *refs):
+    blocks, (own, other) = refs[:-2], refs[-2:]
+    count = own.shape[0]
+    total = 0.0
+    for r, block in enumerate(blocks):
+        total += matmul(rows[r], block[...].reshape(own.shape[1], -1), LAST)
+    own[...] = total[:count]
+    other[...] = total[count:]
+
+
+def logits_part(rows, heads, part):
+    vocab_count, entries, size = heads[0].shape
+    tile = vocab_count // 2 * entries
+    count = rows.shape[1] // 2
+    block = (vocab_count // 2, entries, size)
+    return pl.pallas_call(
+        logits_kernel,
+        out_shape=[jax.ShapeDtypeStruct((count, tile), F32)] * 2,
+        grid=(1,),
+        in_specs=[whole(rows.shape)] + [pl.BlockSpec(block, lambda j: (part, 0, 0))] * len(heads),
+        out_specs=[whole((count, tile))] * 2,
+        cost_estimate=FREE,
+        compiler_params=pltpu.CompilerParams(vmem_limit_bytes=VMEM_BYTES),
+        name="logits",
+    )(rows, *heads)
+
+
+def learner_logits_kernel(facts, rows, *refs):
+    logits_kernel(rows, *[ref.at[:, 0] for ref in refs[:4]], *refs[4:])
+
+
+def learner_logits_part(facts, rows, heads, part):
+    vocab_count, rep_count, entries, size = heads.shape
+    tile = vocab_count // 2 * entries
+    count = rows.shape[1] // 2
+    block = (vocab_count // 2, 1, entries, size)
+    return pl.pallas_call(
+        learner_logits_kernel,
+        out_shape=[jax.ShapeDtypeStruct((count, tile), F32)] * 2,
+        grid_spec=pltpu.PrefetchScalarGridSpec(
+            num_scalar_prefetch=1,
+            grid=(1,),
+            in_specs=[whole(rows.shape)]
+            + [
+                pl.BlockSpec(block, lambda j, facts, r=r: (part, facts[r], 0, 0))
+                for r in range(rep_count)
+            ],
+            out_specs=[whole((count, tile))] * 2,
+        ),
+        cost_estimate=FREE,
+        compiler_params=pltpu.CompilerParams(vmem_limit_bytes=VMEM_BYTES),
+        name="logits",
+    )(facts, rows, *[heads] * rep_count)
+
+
+def join_kernel(facts, *refs):
+    sources, out = refs[:-1], refs[-1]
+    for r, source in enumerate(sources):
+
+        @pl.when((facts[0] ^ pl.program_id(0)) == r)
+        def _():
+            out[0] = source[...]
+
+
+def joined(index, blocks):
+    count = len(blocks)
+    shape = blocks[0].shape
+    return pl.pallas_call(
+        join_kernel,
+        out_shape=jax.ShapeDtypeStruct((count, *shape), blocks[0].dtype),
+        grid_spec=pltpu.PrefetchScalarGridSpec(
+            num_scalar_prefetch=1,
+            grid=(count,),
+            in_specs=[whole(shape)] * count,
+            out_specs=pl.BlockSpec((1, *shape), lambda j, facts: (j, 0, 0)),
+        ),
+        cost_estimate=FREE,
+        compiler_params=pltpu.CompilerParams(vmem_limit_bytes=VMEM_BYTES),
+        name="joined",
+    )(index.reshape(1).astype(jnp.int32), *blocks)
+
+
+def learner_kernel(facts, placer, other_placer, own, other, rows, near, far):
+    r = pl.program_id(0)
+    count = own.shape[0]
+    rows[0, :count] = matmul(placer[...], own[...]).astype(BF16)
+    rows[0, count:] = matmul(other_placer[...], other[...]).astype(BF16)
+    for out, here in ((near, r < 2), (far, r >= 2)):
+
+        @pl.when(here)
+        def _():
+            out[0, :count] = own[...]
+            out[0, count:] = other[...]
+
+
+def learner_parts(facts, placer, other_placer, own, other):
+    count = own.shape[0]
+    size = own.shape[1] // 8
+    shape = (1, 2 * count, size)
+    return pl.pallas_call(
+        learner_kernel,
+        out_shape=[
+            jax.ShapeDtypeStruct((blocks, 2 * count, size), BF16) for blocks in (4, 2, 2)
+        ],
+        grid_spec=pltpu.PrefetchScalarGridSpec(
+            num_scalar_prefetch=1,
+            grid=(4,),
+            in_specs=[
+                whole(placer.shape),
+                whole(placer.shape),
+                pl.BlockSpec((count, size), lambda r, facts: (0, facts[r])),
+                pl.BlockSpec((count, size), lambda r, facts: (0, r)),
+            ],
+            out_specs=[
+                pl.BlockSpec(shape, lambda r, facts: (r, 0, 0)),
+                pl.BlockSpec(shape, lambda r, facts: (jnp.minimum(r, 1), 0, 0)),
+                pl.BlockSpec(shape, lambda r, facts: (jnp.maximum(r - 2, 0), 0, 0)),
+            ],
+        ),
+        cost_estimate=FREE,
+        compiler_params=pltpu.CompilerParams(vmem_limit_bytes=VMEM_BYTES),
+        name="learner_parts",
+    )(facts, placer, other_placer, own, other)
+
+
+def head_kernel(facts, mine, core, here, along_y, other, *outs):
+    i = pl.program_id(0)
+    count = here.shape[1]
+    total = matmul(mine[:count], here[0], FIRST) + matmul(mine[count:], along_y[0], FIRST)
+    total += matmul(core[:count], other[0], FIRST) + matmul(core[count:], other[1], FIRST)
+    total = total.astype(BF16)
+    size = total.shape[1] // 2
+    for group, now in ((outs[:2], i < 2), (outs[2:], i >= 2)):
+
+        @pl.when(now)
+        def _():
+            for k, out in enumerate(group):
+                out[0] = total[:, k * size : (k + 1) * size]
+
+
+def head_parts(facts, mine, core, here, along_y, other):
+    rows, vocab = mine.shape
+    tile, size = vocab // 4, here.shape[2] // 2
+    shape = (1, tile, size)
+    first = pl.BlockSpec(shape, lambda i, facts: (jnp.minimum(i, 1), 0, 0))
+    rest = pl.BlockSpec(shape, lambda i, facts: (jnp.maximum(i - 2, 0), 0, 0))
+    return pl.pallas_call(
+        head_kernel,
+        out_shape=[jax.ShapeDtypeStruct((2, tile, size), BF16)] * 4,
+        grid_spec=pltpu.PrefetchScalarGridSpec(
+            num_scalar_prefetch=1,
+            grid=(4,),
+            in_specs=[pl.BlockSpec((rows, tile), lambda i, facts: (0, facts[i]))] * 2
+            + [whole(value.shape) for value in (here, along_y, other)],
+            out_specs=[first, first, rest, rest],
+        ),
+        cost_estimate=FREE,
+        compiler_params=pltpu.CompilerParams(vmem_limit_bytes=VMEM_BYTES),
+        name="head_parts",
+    )(facts, mine, core, here, along_y, other)
+
+
+def grad_kernel(rows, block, out):
+    out[...] = matmul(rows[...], block[:, 0].reshape(rows.shape[1], -1)).astype(BF16)
+
+
+def grad_part(rows, heads):
+    vocab_count, rep_count, entries, size = heads.shape
+    return pl.pallas_call(
+        grad_kernel,
+        out_shape=jax.ShapeDtypeStruct((rows.shape[0], rep_count * size), BF16),
+        grid=(rep_count,),
+        in_specs=[
+            whole(rows.shape),
+            pl.BlockSpec((vocab_count, 1, entries, size), lambda r: (0, r, 0, 0)),
+        ],
+        out_specs=pl.BlockSpec((rows.shape[0], size), lambda r: (0, r)),
+        cost_estimate=FREE,
+        compiler_params=pltpu.CompilerParams(vmem_limit_bytes=VMEM_BYTES),
+        name="hidden_grad",
+    )(rows, heads)
+
+
+def expert_kernel(facts, *refs):
+    hidden, got, (gain, gate, up, out, normed) = refs[:4], refs[4:8], refs[8:]
+    count, size = hidden[0].shape[1:]
+    width = normed.shape[1]
+
+    @pl.when(pl.program_id(0) == 0)
+    def _():
+        own = [part[r] for part in hidden[:2] for r in range(2)]
+        own += [part[r].astype(F32) for part in got[2:] for r in range(2)]
+        partner = [part[r] for part in hidden[2:] for r in range(2)]
+        partner += [part[r].astype(F32) for part in got[:2] for r in range(2)]
+        for first, blocks in ((0, own), (count, partner)):
+            squares = sum(jnp.sum(block * block, axis=1, keepdims=True) for block in blocks)
+            scale = lax.rsqrt(squares / width + EPSILON)
+            for i, block in enumerate(blocks):
+                column = pl.multiple_of(facts[i] * size, size)
+                normed[first : first + count, pl.ds(column, size)] = (
+                    block * scale * gain[:, pl.ds(column, size)]
+                ).astype(BF16)
+
+    rows = normed[...]
+    gate_pre = matmul(rows, gate[0], LAST)
+    up_pre = matmul(rows, up[0], LAST)
+    out[...] = (gate_pre / (1.0 + jnp.exp(-gate_pre)) * up_pre).astype(BF16)
+
+
+def expert_hidden(facts, hidden, got, gain, gate, up):
+    count, size = hidden[0].shape[1:]
+    units, width = gate.shape[1:]
+    tile = units // 3
+    return pl.pallas_call(
+        expert_kernel,
+        out_shape=jax.ShapeDtypeStruct((2 * count, units), BF16),
+        grid_spec=pltpu.PrefetchScalarGridSpec(
+            num_scalar_prefetch=1,
+            grid=(3,),
+            in_specs=[whole(part.shape) for part in (*hidden, *got)]
+            + [whole((1, width))]
+            + [pl.BlockSpec((1, tile, width), lambda j, facts: (0, j, 0))] * 2,
+            out_specs=pl.BlockSpec((2 * count, tile), lambda j, facts: (0, j)),
+            scratch_shapes=[pltpu.VMEM((2 * count, width), BF16)],
+        ),
+        cost_estimate=FREE,
+        compiler_params=pltpu.CompilerParams(vmem_limit_bytes=VMEM_BYTES),
+        name="expert_hidden",
+    )(facts, *hidden, *got, gain[None], gate, up)
+
+
+def down_kernel(turned, facts, rows, weight, out):
+    total = matmul(rows[...], weight[0]).astype(BF16)
+    half = total.shape[0] // 2
+    if turned:
+        out[0, :half] = total[half:]
+        out[0, half:] = total[:half]
+    else:
+        out[0] = total
+
+
+def expert_down(facts, rows, weight, turned):
+    count = facts.shape[0]
+    units = rows.shape[1]
+    size = weight.shape[2] // 8
+    return pl.pallas_call(
+        functools.partial(down_kernel, turned),
+        out_shape=jax.ShapeDtypeStruct((count, rows.shape[0], size), BF16),
+        grid_spec=pltpu.PrefetchScalarGridSpec(
+            num_scalar_prefetch=1,
+            grid=(count,),
+            in_specs=[
+                whole(rows.shape),
+                pl.BlockSpec((1, units, size), lambda r, facts: (0, 0, facts[r])),
+            ],
+            out_specs=pl.BlockSpec((1, rows.shape[0], size), lambda r, facts: (r, 0, 0)),
+        ),
+        cost_estimate=FREE,
+        compiler_params=pltpu.CompilerParams(vmem_limit_bytes=VMEM_BYTES),
+        name="expert_down",
+    )(facts, rows, weight)
+
+
+def final_kernel(*refs):
+    hidden_parts, (ours, terms, weight, gain, rows, squares) = refs[:4], refs[4:]
+    total = 0.0
+    for r in range(4):
+        parts = [part[r % 2] for part in hidden_parts[r // 2 :: 2]]
+        hidden = jnp.concatenate(parts, axis=0)
+        out = (ours[r].astype(F32) + terms[r].astype(F32)).astype(BF16).astype(F32)
+        hidden = hidden + weight[...] * out
+        total += jnp.sum(hidden * hidden, axis=1, keepdims=True)
+        rows[r] = (hidden * gain[r]).astype(BF16)
+    squares[...] = jnp.broadcast_to(total, squares.shape)
+
+
+def final_hidden(hidden, ours, terms, weight, gain):
+    values = (*hidden, ours, terms, weight, gain)
+    return pl.pallas_call(
+        final_kernel,
+        grid=(1,),
+        in_specs=[whole(value.shape) for value in values],
+        out_specs=[whole(ours.shape), whole((ours.shape[1], 128))],
+        out_shape=[
+            jax.ShapeDtypeStruct(ours.shape, BF16),
+            jax.ShapeDtypeStruct((ours.shape[1], 128), F32),
+        ],
+        cost_estimate=FREE,
+        compiler_params=pltpu.CompilerParams(vmem_limit_bytes=VMEM_BYTES),
+        name="final_hidden",
+    )(*values)
+
+
 def per_device(
+    queries,
+    key_value,
+    residual,
+    out_weight,
+    moe_gain,
+    expert_ids,
+    route_gate,
+    gate_weight,
+    up_weight,
+    down_weight,
+    final_gain,
+    teacher_head,
+    learner_hidden,
+    learner_head,
+    lengths,
+):
+    seq_dev, pos_ctx, head_cols = queries.shape
+    pos_dev, width = residual.shape[1:]
+    own_count = seq_dev * pos_dev
+    half = width // 2
+    ctx_index = lax.axis_index("ctx")
+    vocab_index = lax.axis_index("vocab")
+    rep_index = lax.axis_index("rep")
+    plane = ctx_index * 4 + rep_index
+    per_expert = own_count // 4
+    vocab = 4 * teacher_head.shape[0]
+    order = Order()
+
+    def column_blocks(value, ctx):
+        size = value.shape[-1] // 8
+        return [pick(value, ctx * 4 + (rep_index ^ r), size, value.ndim - 1) for r in range(4)]
+
+    def columns(value, ctx):
+        return jnp.concatenate(column_blocks(value, ctx), axis=-1)
+
+    shared_head = vocab_index * (head_cols // HD) // (QH // KVH)
+    own_keys = lax.dynamic_slice_in_dim(key_value, shared_head * HD, HD, 3)
+    other_keys = swap_x(own_keys)
+    weight_y = swap_rep(out_weight, 2)
+    weight_core = swap_rep(out_weight, 1)
+    teacher_slice = pick(teacher_head, plane, width // 8, 1)
+    teacher = line_gather(teacher_slice[None])
+
+    expert_ids = lax.optimization_barrier((expert_ids, own_keys))[0]
+    route_ids = expert_ids.reshape(own_count, -1)
+    inside = route_ids < 4
+    chosen = jnp.sum(jnp.where(inside, route_ids, 0), axis=1)
+    route_weight = jnp.sum(jnp.where(inside, route_gate.reshape(own_count, -1), 0.0), axis=1)
+    member = (chosen[:, None] == jnp.arange(4)[None, :]).astype(jnp.int32)
+    slot_rank = jnp.sum((jnp.cumsum(member, axis=0) - 1) * member, axis=1)
+    target = chosen * per_expert + slot_rank
+    placed = target[None, :] == jnp.arange(own_count)[:, None]
+    placer = placed.astype(BF16)
+    line_target = chosen * own_count + vocab_index * per_expert + slot_rank
+    line_facts = line_joined(line_gather(jnp.stack([line_target.astype(F32), route_weight])[None]))
+    other_facts = swap_x(line_facts)
+    order.ends(line_facts)
+    mine = vocab_index * own_count + jnp.arange(own_count)[:, None]
+
+    def routed(facts):
+        targets = facts[:, 0].astype(jnp.int32).reshape(1, -1)
+        weights = jnp.where(targets == mine, facts[:, 1].reshape(1, -1), 0.0)
+        return targets, jnp.sum(weights, axis=1, keepdims=True)
+
+    line_rows = jnp.arange(seq_dev * pos_ctx)
+    chunk = line_rows // own_count
+    chunk = jnp.where(chunk < 2, 2 * chunk + 1, 2 * chunk - 4) ^ vocab_index
+    line_rows = (chunk * own_count + line_rows % own_count)[:, None]
+    line_targets, my_weight = routed(line_facts)
+    line_tokens = jnp.swapaxes(line_targets.reshape(4, seq_dev, pos_dev), 0, 1).reshape(1, -1)
+    line_placer = (line_rows == line_tokens).astype(BF16)
+    sent_count = 2 * own_count
+
+    residual_rows = order.take(residual).reshape(own_count, width)
+    own_residual = column_blocks(residual_rows, ctx_index)
+    own_blocks = [jnp.stack(own_residual[:2]), jnp.stack(own_residual[2:])]
+    own_placer = (line_rows == line_target[None, :]).astype(BF16)
+    own_placers = (own_placer[:sent_count], own_placer[sent_count:])
+    other_blocks = swap_x(jnp.stack(column_blocks(residual_rows, 1 - ctx_index)))
+    learner_own = order.take(learner_hidden).reshape(own_count, width)
+    other_targets, other_weight = routed(other_facts)
+    other_target = pick(other_targets, vocab_index, own_count, 1)
+    other_placer = (line_rows == other_target).astype(BF16)
+    both_weight = jnp.concatenate([my_weight, other_weight], axis=0)
+
+    other_slot = other_target.reshape(-1)
+    other_slot = other_slot // own_count * per_expert + other_slot % per_expert
+    other_place = (other_slot[None, :] == jnp.arange(own_count)[:, None]).astype(BF16)
+    places = (rep_index ^ jnp.arange(4)).astype(jnp.int32)
+    here, there = ctx_index * 4 + places, (1 - ctx_index) * 4 + places
+
+    rows = jnp.concatenate([other_keys, own_keys], axis=2)
+    ready = (queries, rows, line_placer, *own_blocks, *own_placers, other_placer, both_weight)
+    ready += (weight_core,)
+    ready = lax.optimization_barrier(ready)
+    queries, rows, line_placer, *own_blocks = ready[:5]
+    own_placers, (other_placer, both_weight, weight_core) = ready[5:7], ready[7:]
+    heads_out = order.ends(attend(queries, rows, lengths))
+
+    cuts = ((sent_count,), (own_count, own_count))
+
+    def halved(far, beside):
+        return order.ends((far.astype(F32) + beside[:, own_count:].astype(F32)).astype(BF16))
+
+    def summed(mine, beside, across):
+        total = mine.astype(F32) + beside[:, :own_count].astype(F32)
+        return order.ends(total + across.astype(F32))
+
+    other_blocks = order.waits(other_blocks)
+    sent_rows, kept_rows = sorted_rows(order.take(line_placer), heads_out)
+    order.ends(kept_rows)
+    other_sent = swap_x(sent_rows)
+    sent_0, mine_0, far_0 = project(
+        order.take(sent_rows, kept_rows),
+        own_placers,
+        own_blocks[0],
+        (out_weight, weight_core),
+        cuts,
+    )
+    order.ends(mine_0)
+    teacher = order.ends(line_joined(order.waits(*teacher)))
+    beside_0 = swap_z(order.take(sent_0), 1)
+    other_sent = order.waits(other_sent)
+    beside_0 = order.waits(beside_0)
+    across_0 = swap_z(halved(far_0, beside_0), 2)
+    weight_y = order.waits(weight_y)
+    weight_y_core = swap_rep(weight_y, 1)
+    teacher_y = swap_rep(order.take(teacher), 2)
+    weight_y_core, across_0 = order.waits(weight_y_core, across_0)
+
+    sent_1, mine_1, far_1 = project(
+        order.take(sent_rows, kept_rows),
+        own_placers,
+        own_blocks[1],
+        (weight_y, weight_y_core),
+        cuts,
+    )
+    order.ends(mine_1)
+    beside_1 = swap_z(sent_1, 1)
+
+    weights = (out_weight, weight_core, weight_y, weight_y_core)
+
+    def other_part(rows, placer, first, cuts):
+        return project(
+            (rows,), (placer,), other_blocks[first : first + 2], weights[first : first + 2], (cuts,)
+        )
+
+    (sent_2,) = other_part(order.take(other_sent), other_placer[:sent_count], 0, (sent_count,))
+    order.ends(sent_2)
+    beside_2 = swap_z(sent_2, 1)
+    other_kept = swap_x(order.take(kept_rows))
+    (sent_3,) = other_part(order.take(other_sent), other_placer[:sent_count], 2, (sent_count,))
+    order.ends(sent_3)
+    beside_3 = swap_z(sent_3, 1)
+
+    beside_1, beside_2, other_kept, teacher_y = order.waits(
+        beside_1, beside_2, other_kept, teacher_y
+    )
+    across_1 = swap_z(halved(far_1, beside_1), 2)
+    mine_2, far_2 = other_part(
+        order.take(other_kept), other_placer[sent_count:], 0, (own_count, own_count)
+    )
+    order.ends(mine_2)
+    across_2 = swap_z(halved(far_2, beside_2), 2)
+    mine_3, far_3 = other_part(
+        order.take(other_kept), other_placer[sent_count:], 2, (own_count, own_count)
+    )
+    order.ends(mine_3)
+    beside_3 = order.waits(beside_3)
+    across_3 = swap_z(halved(far_3, beside_3), 2)
+    hidden_0 = summed(mine_0, beside_0, across_0)
+    got_0 = swap_x(hidden_0.astype(BF16))
+    hidden_1 = summed(mine_1, beside_1, order.waits(across_1))
+    got_0, across_2 = order.waits(got_0, across_2)
+    hidden_2 = summed(mine_2, beside_2, across_2)
+    got_1, got_2 = (swap_x(order.take(part.astype(BF16))) for part in (hidden_1, hidden_2))
+    across_3, got_1, got_2 = order.waits(across_3, got_1, got_2)
+    hidden_3 = summed(mine_3, beside_3, across_3)
+    got_3 = swap_x(hidden_3.astype(BF16))
+    heads = lax.all_gather(order.take(learner_head), ("vocab", "rep"))
+    heads = heads.reshape(4, 4, *learner_head.shape)
+    got_3 = order.waits(got_3)
+    learner_x = swap_x(columns(order.take(learner_own), 1 - ctx_index))
+
+    hidden = (hidden_0, hidden_1, hidden_2, hidden_3)
+    activated = expert_hidden(
+        jnp.concatenate([here, there]).astype(jnp.int32),
+        hidden,
+        (got_0, got_1, got_2, got_3),
+        moe_gain,
+        gate_weight,
+        up_weight,
+    )
+    order.ends(activated)
+    terms = order.ends(expert_down(there, order.take(activated), down_weight, True))
+    learner_x = order.waits(learner_x)
+    terms = swap_x(order.take(terms))
+    ours = order.ends(expert_down(here, order.take(activated), down_weight, False))
+    learner_rows, plane_here, plane_there = learner_parts(
+        here, placer, other_place, order.take(learner_own), order.take(learner_x)
+    )
+    order.ends(learner_rows)
+    plane_y = swap_rep(plane_there, 2)
+    terms = order.waits(terms)
+
+    places = places.astype(jnp.int32)
+    final_rows, squares = final_hidden(
+        hidden,
+        ours,
+        order.take(terms),
+        both_weight,
+        jnp.stack(column_blocks(final_gain, ctx_index))[:, None],
+    )
+    order.ends(final_rows)
+    other_squares = swap_x(squares[own_count:])
+    cores = [swap_rep(order.take(block), 1) for block in (teacher, teacher_y)]
+    other_squares, *cores = order.waits(other_squares, *cores)
+    teacher = (teacher, cores[0], teacher_y, cores[1])
+    teacher_own, teacher_other = [None, None], [None, None]
+    teacher_own[0], teacher_other[0] = logits_part(order.take(final_rows), teacher, 0)
+    order.ends(teacher_other[0])
+    teacher_got = swap_x(teacher_other[0])
+    teacher_own[1], teacher_other[1] = logits_part(order.take(final_rows), teacher, 1)
+    order.ends(teacher_own[1])
+    scale = lax.rsqrt((squares[:own_count, :1] + other_squares[:, :1]) / width + EPSILON)
+    teacher_got, plane_y = order.waits(teacher_got, plane_y)
+    part = order.ends((teacher_own[0] + teacher_got) * scale)
+    teacher_got = swap_x(order.take(teacher_other[1]))
+    teacher_logits = [line_exchange(part)]
+
+    heads = order.waits(heads)
+    learner_own_part, learner_other = (
+        jnp.concatenate(parts, axis=1)
+        for parts in zip(*(learner_logits_part(places, order.take(learner_rows), heads, i) for i in (0, 1)))
+    )
+    order.ends(learner_own_part)
+    part = order.ends((teacher_own[1] + order.waits(teacher_got)) * scale)
+    learner_other = swap_x(order.take(learner_other))
+    teacher_logits[0] = order.waits(*teacher_logits[0])
+    teacher_logits.append(line_exchange(order.take(part)))
+    teacher_logits = [line_joined(order.take(*received)) for received in teacher_logits]
+    teacher_logits = order.ends(jnp.concatenate(teacher_logits, axis=1))
+    teacher_peak = jnp.max(teacher_logits, axis=1, keepdims=True)
+    teacher_lse = teacher_peak + jnp.log(
+        jnp.sum(jnp.exp(teacher_logits - teacher_peak), axis=1, keepdims=True)
+    )
+    plane_core = swap_rep(jnp.stack([plane_here[1], plane_y[1]]), 1)
+    learner_other, plane_core = order.waits(learner_other, plane_core)
+    learner_logits = learner_own_part + learner_other
+    learner_peak = jnp.max(learner_logits, axis=1, keepdims=True)
+    learner_exp = jnp.exp(learner_logits - learner_peak)
+    learner_total = jnp.sum(learner_exp, axis=1, keepdims=True)
+    learner_lse = learner_peak + jnp.log(learner_total)
+
+    logit_gap = learner_logits - teacher_logits
+    mean_gap = jnp.sum(learner_exp * logit_gap, axis=1, keepdims=True) / learner_total
+    divergence = mean_gap - learner_lse + teacher_lse
+    row_pos = ctx_index * pos_ctx + vocab_index * pos_dev + jnp.arange(pos_dev)
+    live = row_pos[None, :] < lengths[:, None]
+    live_sorted = jnp.any(placed & live.reshape(1, -1), axis=1)
+    learner_prob = jnp.exp(learner_logits - learner_lse)
+    dlogits = jnp.where(
+        live_sorted[:, None], learner_prob * (logit_gap - mean_gap), 0.0
+    ).astype(BF16)
+    dlogits = order.ends(matmul(placer, dlogits, FIRST).astype(BF16))
+
+    rows = own_count // 2
+    along_x, along_y = swap_x(dlogits), swap_rep(dlogits, 2)
+    along_x, along_y = order.waits(along_x, along_y)
+    near, far = swap_x(along_y[:rows]), swap_rep(along_x[rows:], 2)
+    near, far = order.waits(near, far)
+    mine = order.ends(jnp.concatenate([dlogits, along_x, along_y, near, far], axis=0))
+    core = order.waits(swap_rep(mine, 1))
+    blocks = (vocab_index ^ jnp.array([1, 3, 0, 2])).astype(jnp.int32)
+    parts = head_parts(blocks, mine, core, plane_here, plane_y, plane_core)
+    order.ends(parts[0])
+    sums = [(kept, swap_z(sent, 1)) for sent, kept in zip(parts[:2], parts[2:])]
+    other_grad = order.ends(grad_part(order.take(along_x), heads))
+    other_grad = swap_x(other_grad)
+    own_grad = order.ends(grad_part(order.take(dlogits), heads))
+    for i, (kept, beside) in enumerate(sums):
+        beside = order.waits(beside)
+        far = order.ends((kept[1].astype(F32) + beside[1].astype(F32)).astype(BF16))
+        sums[i] = (kept[0], beside[0], swap_z(far, 2))
+    kl_rows = jnp.sum(jnp.where(placed, order.take(divergence), 0.0), axis=0)
+    row_kl = order.ends(jnp.where(live, kl_rows.reshape(seq_dev, pos_dev), 0.0))
+    other_grad = order.take(other_grad)
+    hidden_grad = join_absolute([own_grad, other_grad], ctx_index, 1)
+    order.ends(hidden_grad)
+    head_grad = jnp.concatenate(
+        [
+            mine.astype(F32) + beside.astype(F32) + order.take(across).astype(F32)
+            for mine, beside, across in sums
+        ],
+        axis=1,
+    ).astype(BF16)
+    return (hidden_grad.reshape(seq_dev, pos_dev, width), head_grad, row_kl)
+
+
+def per_device_general(
     queries,
     key_value,
     residual,
@@ -215,8 +993,10 @@
         P("vocab", ("ctx", "rep")),
         P("rep"),
     )
+    shape = dict(mesh.shape)
+    swaps = (shape["ctx"], shape["vocab"], shape["rep"]) == (2, 4, 4)
     return jax.shard_map(
-        per_device,
+        per_device if swaps else per_device_general,
         mesh=mesh,
         in_specs=placed,
         out_specs=(

time: 679 us -> 358 us (0.53)
  waiting for transfers between devices: 513 us -> 144 us
  Pallas kernels: 0 us -> 85.1 us
  matrix products: 68.2 us -> 0.38 us
  blocking collectives: 58.8 us -> 0 us
  starting transfers between devices: 5.1 us -> 62.8 us
  local copies, waits for them, and re-layouts: 2.58 us -> 19.1 us
  other arithmetic: 16.4 us -> 30.2 us
    all_gather x5 -> x1, waiting for transfers between devices: 262 us -> 0.01 us  [per_device(): heads = lax.all_gather(order.take(learner_head), ('vocab', 'rep'))]
    reduce_scatter x4 -> x0, waiting for transfers between devices: 224 us -> none  [the longest x1 79.7 us: per_device(): lax.psum_scatter(jnp.einsum('psv,vd->psd', shard_rows, learner_full, pref...]
    ppermute x0 -> x53, waiting for transfers between devices: none -> 144 us  [the longest x24 83 us: swap_z(): return lax.ppermute(value, 'vocab', [(i, i ^ offset) for i in range(4)])]
    pallas_call x0 -> x20, Pallas kernels: none -> 85.1 us  [the longest x6 20 us: project(): pl.pallas_call(functools.partial(project_kernel, count, parts), out_shape...]
    dot_general x11 -> x1, matrix products: 68.2 us -> 0.38 us  [matmul(): return lax.dot_general(left, right, dims, preferred_element_type=F32)]
    ppermute x0 -> x53, starting transfers between devices: none -> 62.7 us  [the longest x24 36.4 us: swap_z(): return lax.ppermute(value, 'vocab', [(i, i ^ offset) for i in range(4)])]
    all_to_all x1 -> x0, blocking collectives: 29.9 us -> none  [per_device(): lax.all_to_all(outgoing.reshape(vocab_count, per_expert, width), 'vocab',...]
    all_to_all x1 -> x0, waiting for transfers between devices: 25.7 us -> none  [per_device(): lax.all_to_all(expert_out.reshape(vocab_count, per_expert, width), 'vocab...]
  transfers between devices with their start and end apart: 10 -> 54, of which waited for: 10 -> 29; matrix products, arithmetic and copies ran while one was open for 5% -> 8% of each run, Pallas kernels for 0% -> 22%
where the time goes in v4:
time: 358 us; the launch traced here: 357 us
  waiting for transfers between devices  144 us (40%)
  Pallas kernels  85.1 us (24%)
  starting transfers between devices  62.8 us (18%)
  other arithmetic  30.2 us (8%)
  local copies, waits for them, and re-layouts  19.1 us (5%)
  between operations  15.1 us (4%)
    ppermute x24, waiting for transfers between devices, swap_z(): return lax.ppermute(value, 'vocab', [(i, i ^ offset) for i in range(4)])  83 us
    ppermute x18, waiting for transfers between devices, swap_x(): return lax.ppermute(value, 'ctx', [(0, 1), (1, 0)])  52.4 us
    ppermute x24, starting transfers between devices, swap_z(): return lax.ppermute(value, 'vocab', [(i, i ^ offset) for i in range(4)])  36.4 us
    ppermute x18, starting transfers between devices, swap_x(): return lax.ppermute(value, 'ctx', [(0, 1), (1, 0)])  21.2 us
    pallas_call x6, Pallas kernels, project(): pl.pallas_call(functools.partial(project_kernel, count, parts), out_shape...  20 us
    unnamed x120, local copies, waits for them, and re-layouts  13.2 us
    pallas_call x1, Pallas kernels, attend(): pl.pallas_call(attend_kernel, out_shape=jax.ShapeDtypeStruct((seq_dev * p...  12.1 us
    pallas_call x2, Pallas kernels, expert_down(): pl.pallas_call(functools.partial(down_kernel, turned), out_shape=jax.Shap...  9.76 us
  transfers between devices with their start and end apart: 54, of which 29 were waited for; matrix products, arithmetic and copies ran while one was open for 8% of the time, Pallas kernels for 22%

profile of v4, /device:TPU:0, one launch (start us, length us, event | category | flops | bytes accessed | tf_op | source)
XLA Modules:
  0.0 356.6 jit_solution(6162626681241361044)
XLA Ops:
  7.2 1.8 constant_dynamic-slice_fusion.13
  11.8 3.0 collective-permute-start
  14.8 2.6 collective-permute-start.1
  17.4 1.7 collective-permute-start.4
  23.8 1.6 collective-permute-start.3
  29.4 2.2 collective-permute-start.8
  32.9 12.1 %attend.1.heads = bf16[512,2048]{1,0:T(8,128)(2,1)S(1)} custom-call(s32[4]{0:T(128)S(1)} %pad_add_fusion.1.facts, bf16[2,256,2048]{2,1,0:T(8,128)(2,1)S(1)} %copy-done.24, bf16[2,2,512,128]{3,2,1,0:T(8,128)(2,1)S(1)} %pad_maximum_fusion.3.rows), custom_call_target="tpu_custom_call" | custom-call | tf_op jit(solution)/shard_map/attend/pallas_call | solution.py:123
  45.0 2.1 sorted_rows.1
  47.1 1.6 collective-permute-start.11
  48.6 4.1 %project.6 = (bf16[2,256,512]{2,1,0:T(8,128)(2,1)S(1)}, bf16[2,128,512]{2,1,0:T(8,128)(2,1)S(1)}, bf16[2,128,512]{2,1,0:T(8,128)(2,1)S(1)}) custom-call(bf16[256,2048]{1,0:T(8,128)(2,1)S(1)} %get-tuple-element.161.refs_0_, bf16[256,2048]{1,0:T(8,128)(2,1)S(1)} %get-tuple-element.168.refs_1_, bf16[256,128]{1,0:T(8,128)(2,1)S(1)} %get-tuple-element.144.refs_2_, ...), custom_call_target="tpu_custom_call" | custom-call | tf_op jit(solution)/shard_map/project/pallas_call | solution.py:170
  52.8 6.5 %collective-permute-done.8 = bf16[1,384,512]{2,1,0:T(8,128)(2,1)S(1)} collective-permute-done((bf16[1,384,512]{2,1,0:T(8,128)(2,1)S(1)}, bf16[1,384,512]{2,1,0:T(8,128)(2,1)S(1)}, u32[]{:S(2)}, u32[]{:S(2)}) %collective-permute-start.8) | collective-permute-done | bytes 393248 | tf_op jit(solution)/shard_map/ppermute | solution.py:61
  60.6 6.8 %collective-permute-start.10 = (bf16[2,256,512]{2,1,0:T(8,128)(2,1)S(1)}, bf16[2,256,512]{2,1,0:T(8,128)(2,1)}, u32[]{:S(2)}, u32[]{:S(2)}) collective-permute-start(bf16[2,256,512]{2,1,0:T(8,128)(2,1)S(1)} %get-tuple-element.154), channel_id=1, source_target_pairs={{0,4},{4,0},{8,12},{12,8},{1,5},{5,1},{9,13},{13,9},{2,6},{6,2},{1... | collective-permute-start | bytes 1572872 | tf_op jit(solution)/shard_map/ppermute | solution.py:61
  67.4 3.6 collective-permute-done.11.refs_0_
  70.9 6.6 %collective-permute-done.10 = bf16[2,256,512]{2,1,0:T(8,128)(2,1)} collective-permute-done((bf16[2,256,512]{2,1,0:T(8,128)(2,1)S(1)}, bf16[2,256,512]{2,1,0:T(8,128)(2,1)}, u32[]{:S(2)}, u32[]{:S(2)}) %collective-permute-start.10) | collective-permute-done | bytes 524320 | tf_op jit(solution)/shard_map/ppermute | solution.py:61
  78.7 3.7 %collective-permute-start.14 = (bf16[2,128,512]{2,1,0:T(8,128)(2,1)S(1)}, bf16[2,128,512]{2,1,0:T(8,128)(2,1)S(1)}, u32[]{:S(2)}, u32[]{:S(2)}) collective-permute-start(bf16[2,128,512]{2,1,0:T(8,128)(2,1)S(1)} %add_convert_fusion.3), channel_id=1, source_target_pairs={{0,8},{4,12},{8,0},{12,4},{1,9},{5,13},{9,1},{13,5},{2,10},{6,14},... | collective-permute-start | bytes 786440 | tf_op jit(solution)/shard_map/ppermute | solution.py:61
  82.4 12.4 %collective-permute-done.14 = bf16[2,128,512]{2,1,0:T(8,128)(2,1)S(1)} collective-permute-done((bf16[2,128,512]{2,1,0:T(8,128)(2,1)S(1)}, bf16[2,128,512]{2,1,0:T(8,128)(2,1)S(1)}, u32[]{:S(2)}, u32[]{:S(2)}) %collective-permute-start.14) | collective-permute-done | bytes 262176 | tf_op jit(solution)/shard_map/ppermute | solution.py:61
  96.1 4.4 %project.7 = (bf16[2,256,512]{2,1,0:T(8,128)(2,1)S(1)}, bf16[2,128,512]{2,1,0:T(8,128)(2,1)S(1)}, bf16[2,128,512]{2,1,0:T(8,128)(2,1)S(1)}) custom-call(bf16[256,2048]{1,0:T(8,128)(2,1)S(1)} %get-tuple-element.161.refs_0_, bf16[256,2048]{1,0:T(8,128)(2,1)S(1)} %get-tuple-element.168.refs_1_, bf16[256,128]{1,0:T(8,128)(2,1)S(1)} %get-tuple-element.144.refs_2_, ...), custom_call_target="tpu_custom_call" | custom-call | tf_op jit(solution)/shard_map/project/pallas_call | solution.py:170
  100.5 3.0 project.8
  103.5 1.8 collective-permute-start.17
  105.3 2.0 collective-permute-start.15
  107.3 2.8 project.9
  110.2 1.9 fusion.38
  112.1 3.3 collective-permute-done.18.refs_2_
  116.6 1.7 collective-permute-start.20
  118.3 2.0 collective-permute-done.16
  120.3 11.2 %collective-permute-done.15 = bf16[2,256,512]{2,1,0:T(8,128)(2,1)} collective-permute-done((bf16[2,256,512]{2,1,0:T(8,128)(2,1)S(1)}, bf16[2,256,512]{2,1,0:T(8,128)(2,1)}, u32[]{:S(2)}, u32[]{:S(2)}) %collective-permute-start.15) | collective-permute-done | bytes 524320 | tf_op jit(solution)/shard_map/ppermute | solution.py:61
  133.5 2.9 project.10
  137.4 2.1 collective-permute-start.21
  139.5 2.8 project.11
  142.3 5.9 %collective-permute-done.22 = bf16[2,256,512]{2,1,0:T(8,128)(2,1)S(1)} collective-permute-done((bf16[2,256,512]{2,1,0:T(8,128)(2,1)S(1)}, bf16[2,256,512]{2,1,0:T(8,128)(2,1)S(1)}, u32[]{:S(2)}, u32[]{:S(2)}) %collective-permute-start.22) | collective-permute-done | bytes 524320 | tf_op jit(solution)/shard_map/ppermute | solution.py:61
  148.4 11.0 %collective-permute-done.19 = bf16[2,128,512]{2,1,0:T(8,128)(2,1)S(1)} collective-permute-done((bf16[2,128,512]{2,1,0:T(8,128)(2,1)S(1)}, bf16[2,128,512]{2,1,0:T(8,128)(2,1)S(1)}, u32[]{:S(2)}, u32[]{:S(2)}) %collective-permute-start.19) | collective-permute-done | bytes 262176 | tf_op jit(solution)/shard_map/ppermute | solution.py:61
  160.4 4.5 %collective-permute-done.21 = bf16[2,128,512]{2,1,0:T(8,128)(2,1)S(1)} collective-permute-done((bf16[2,128,512]{2,1,0:T(8,128)(2,1)S(1)}, bf16[2,128,512]{2,1,0:T(8,128)(2,1)S(1)}, u32[]{:S(2)}, u32[]{:S(2)}) %collective-permute-start.21) | collective-permute-done | bytes 262176 | tf_op jit(solution)/shard_map/ppermute | solution.py:61
  166.2 2.0 collective-permute-start.25
  168.2 4.3 %collective-permute-done.24.refs_5_ = bf16[2,128,512]{2,1,0:T(8,128)(2,1)S(1)} collective-permute-done((bf16[2,128,512]{2,1,0:T(8,128)(2,1)S(1)}, bf16[2,128,512]{2,1,0:T(8,128)(2,1)S(1)}, u32[]{:S(2)}, u32[]{:S(2)}) %collective-permute-start.24) | collective-permute-done | bytes 262176 | tf_op jit(solution)/shard_map/ppermute | solution.py:53
  173.2 3.7 %collective-permute-done.25.refs_6_ = bf16[2,128,512]{2,1,0:T(8,128)(2,1)S(1)} collective-permute-done((bf16[2,128,512]{2,1,0:T(8,128)(2,1)S(1)}, bf16[2,128,512]{2,1,0:T(8,128)(2,1)S(1)}, u32[]{:S(2)}, u32[]{:S(2)}) %collective-permute-start.25) | collective-permute-done | bytes 262176 | tf_op jit(solution)/shard_map/ppermute | solution.py:53
  178.6 9.4 %collective-permute-done.26.refs_7_ = bf16[2,128,512]{2,1,0:T(8,128)(2,1)S(1)} collective-permute-done((bf16[2,128,512]{2,1,0:T(8,128)(2,1)}, bf16[2,128,512]{2,1,0:T(8,128)(2,1)S(1)}, u32[]{:S(2)}, u32[]{:S(2)}) %collective-permute-start.26) | collective-permute-done | bytes 262176 | tf_op jit(solution)/shard_map/ppermute | solution.py:53
  188.4 8.6 %expert_hidden.1.rows = bf16[256,768]{1,0:T(8,128)(2,1)S(1)} custom-call(s32[8]{0:T(128)S(1)} %pad_add_fusion.facts, f32[2,128,512]{2,1,0:T(8,128)S(1)} %copy-done.10, f32[2,128,512]{2,1,0:T(8,128)S(1)} %get-tuple-element.278.refs_1_, f32[2,128,512]{2,1,0:T(8,128)S(1)} %get-tuple-element.276.refs_2_, f32[2,128,512]{2,1,0:T(8,128)S(1)} %get-tuple-element.274.refs_3_, ...), custom_call_target="tpu_custom_call" | custom-call | tf_op jit(solution)/shard_map/expert_hidden/pallas_call | solution.py:418
  197.0 5.1 %expert_down.2 = bf16[4,256,512]{2,1,0:T(8,128)(2,1)} custom-call(s32[4]{0:T(128)S(1)} %get-tuple-element.344.facts, bf16[256,768]{1,0:T(8,128)(2,1)S(1)} %expert_hidden.1.rows, bf16[1,768,4096]{2,1,0:T(8,128)(2,1)} %weight.3), custom_call_target="tpu_custom_call" | custom-call | tf_op jit(solution)/shard_map/expert_down/pallas_call | solution.py:450
  202.9 2.0 collective-permute-start.28
  206.2 4.7 %expert_down.3.refs_4_ = bf16[4,256,512]{2,1,0:T(8,128)(2,1)S(1)} custom-call(s32[4]{0:T(128)S(1)} %get-tuple-element.345.facts, bf16[256,768]{1,0:T(8,128)(2,1)S(1)} %expert_hidden.1.rows, bf16[1,768,4096]{2,1,0:T(8,128)(2,1)} %weight.3), custom_call_target="tpu_custom_call" | custom-call | tf_op jit(solution)/shard_map/expert_down/pallas_call | solution.py:450
  211.0 2.3 learner_parts.1
  215.1 4.9 %collective-permute-done.28.refs_5_ = bf16[4,256,512]{2,1,0:T(8,128)(2,1)} collective-permute-done((bf16[4,256,512]{2,1,0:T(8,128)(2,1)}, bf16[4,256,512]{2,1,0:T(8,128)(2,1)}, u32[]{:S(2)}, u32[]{:S(2)}) %collective-permute-start.28) | collective-permute-done | bytes 1048608 | tf_op jit(solution)/shard_map/ppermute | solution.py:53
  220.0 2.3 final_hidden.1
  224.9 3.5 collective-permute-done.29
  229.6 3.7 %logits.4 = (f32[128,768]{1,0:T(8,128)S(1)}, f32[128,768]{1,0:T(8,128)}) custom-call(bf16[4,256,512]{2,1,0:T(8,128)(2,1)S(1)} %get-tuple-element.214.rows, bf16[4,384,512]{2,1,0:T(8,128)(2,1)S(1)} %copy-done.6, bf16[4,384,512]{2,1,0:T(8,128)(2,1)S(1)} %collective-permute-done.30.refs_1_, bf16[4,384,512]{2,1,0:T(8,128)(2,1)} %copy-done.43, ...), custom_call_target="tpu_custom_call" | custom-call | tf_op jit(solution)/shard_map/logits/pallas_call | solution.py:220
  237.6 3.3 logits.5
  241.0 3.5 collective-permute-done.32
  247.2 3.1 collective-permute-start.38
  253.5 3.4 logits.7
  256.9 3.4 logits.6
  263.0 3.6 %collective-permute-start.41 = (f32[32,768]{1,0:T(8,128)S(1)}, f32[32,768]{1,0:T(8,128)S(1)}, u32[]{:S(2)}, u32[]{:S(2)}) collective-permute-start(f32[32,768]{1,0:T(8,128)S(1)} %get-tuple-element.306), channel_id=1, source_target_pairs={{0,8},{4,12},{8,0},{12,4},{1,9},{5,13},{9,1},{13,5},{2,10},{6,14},... | collective-permute-start | bytes 294920 | tf_op jit(solution)/shard_map/ppermute | solution.py:61
  269.5 5.0 %collective-permute-done.41 = f32[32,768]{1,0:T(8,128)S(1)} collective-permute-done((f32[32,768]{1,0:T(8,128)S(1)}, f32[32,768]{1,0:T(8,128)S(1)}, u32[]{:S(2)}, u32[]{:S(2)}) %collective-permute-start.41) | collective-permute-done | bytes 98336 | tf_op jit(solution)/shard_map/ppermute | solution.py:61
  275.0 6.7 %collective-permute-done.35 = f32[128,1536]{1,0:T(8,128)S(1)} collective-permute-done((f32[128,1536]{1,0:T(8,128)S(1)}, f32[128,1536]{1,0:T(8,128)S(1)}, u32[]{:S(2)}, u32[]{:S(2)}) %collective-permute-start.35) | collective-permute-done | bytes 786464 | tf_op jit(solution)/shard_map/ppermute | solution.py:53
  285.2 8.6 %collective-permute-done.43.rows = bf16[128,1536]{1,0:T(8,128)(2,1)S(1)} collective-permute-done((bf16[128,1536]{1,0:T(8,128)(2,1)S(1)}, bf16[128,1536]{1,0:T(8,128)(2,1)S(1)}, u32[]{:S(2)}, u32[]{:S(2)}) %collective-permute-start.43) | collective-permute-done | bytes 393248 | tf_op jit(solution)/shard_map/ppermute | solution.py:53
  296.4 4.0 %collective-permute-done.45 = bf16[64,1536]{1,0:T(8,128)(2,1)S(1)} collective-permute-done((bf16[64,1536]{1,0:T(8,128)(2,1)S(1)}, bf16[64,1536]{1,0:T(8,128)(2,1)S(1)}, u32[]{:S(2)}, u32[]{:S(2)}) %collective-permute-start.45) | collective-permute-done | bytes 196640 | tf_op jit(solution)/shard_map/ppermute | solution.py:53
  301.5 3.4 collective-permute-done.47.core
  306.1 5.6 %head_parts.1 = (bf16[2,384,256]{2,1,0:T(8,128)(2,1)}, bf16[2,384,256]{2,1,0:T(8,128)(2,1)}, bf16[2,384,256]{2,1,0:T(8,128)(2,1)S(1)}, bf16[2,384,256]{2,1,0:T(8,128)(2,1)S(1)}) custom-call(s32[4]{0:T(128)S(1)} %broadcast_xor_fusion.facts, bf16[512,1536]{1,0:T(8,128)(2,1)S(1)} %constant_dynamic-update-slice_fusion.2.mine, bf16[512,1536]{1,0:T(8,128)(2,1)} %copy-done.46, ...), custom_call_target="tpu_custom_call" | custom-call | tf_op jit(solution)/shard_map/head_parts/pallas_call | solution.py:351
  311.8 2.0 collective-permute-start.49
  313.8 4.2 %hidden_grad.2 = bf16[128,2048]{1,0:T(8,128)(2,1)S(1)} custom-call(bf16[128,1536]{1,0:T(8,128)(2,1)S(1)} %collective-permute-done.43.rows, bf16[4,4,384,512]{3,2,1,0:T(8,128)(2,1)} %bitcast.84), custom_call_target="tpu_custom_call" | custom-call | tf_op jit(solution)/shard_map/hidden_grad/pallas_call | solution.py:373
  319.3 4.2 %hidden_grad.3 = bf16[128,2048]{1,0:T(8,128)(2,1)S(1)} custom-call(bf16[128,1536]{1,0:T(8,128)(2,1)S(1)} %get-tuple-element.251.rows, bf16[4,4,384,512]{3,2,1,0:T(8,128)(2,1)} %bitcast.85), custom_call_target="tpu_custom_call" | custom-call | tf_op jit(solution)/shard_map/hidden_grad/pallas_call | solution.py:373
  324.1 1.6 fusion.7
  326.9 9.0 %collective-permute-done.49 = bf16[2,384,256]{2,1,0:T(8,128)(2,1)} collective-permute-done((bf16[2,384,256]{2,1,0:T(8,128)(2,1)}, bf16[2,384,256]{2,1,0:T(8,128)(2,1)}, u32[]{:S(2)}, u32[]{:S(2)}) %collective-permute-start.49) | collective-permute-done | bytes 393248 | tf_op jit(solution)/shard_map/ppermute | solution.py:61
  335.9 1.6 fusion.8
  341.0 6.9 %collective-permute-done.52 = bf16[384,256]{1,0:T(8,128)(2,1)S(1)} collective-permute-done((bf16[384,256]{1,0:T(8,128)(2,1)}, bf16[384,256]{1,0:T(8,128)(2,1)S(1)}, u32[]{:S(2)}, u32[]{:S(2)}) %collective-permute-start.52) | collective-permute-done | bytes 196640 | tf_op jit(solution)/shard_map/ppermute | solution.py:61
  (280 shorter events, 66.1 us)
Async XLA Ops:
  7.2 246.3 %all-gather.3.cloned.1.call-start = ((), (), s32[]{:S(2)}) async-start(), calls=%async_computation | async-start | bytes 6684672 | tf_op jit(solution)/shard_map/all_gather | solution.py:678
  11.8 8.7 %collective-permute-start = (f32[1,2,128]{2,1,0:T(2,128)}, f32[1,2,128]{2,1,0:T(2,128)}, u32[]{:S(2)}, u32[]{:S(2)}) collective-permute-start(f32[1,2,128]{2,1,0:T(2,128)} %maximum_bitcast_fusion), channel_id=1, source_target_pairs={{0,4},{4,0},{8,12},{12,8},{1,5},{5,1},{9,13},{13,9},{2,6},{6,2},{1... | collective-permute-start | bytes 3080 | tf_op jit(solution)/shard_map/ppermute | solution.py:61
  14.8 7.2 %collective-permute-start.1 = (f32[1,2,128]{2,1,0:T(2,128)}, f32[1,2,128]{2,1,0:T(2,128)}, u32[]{:S(2)}, u32[]{:S(2)}) collective-permute-start(f32[1,2,128]{2,1,0:T(2,128)} %maximum_bitcast_fusion), channel_id=1, source_target_pairs={{0,8},{4,12},{8,0},{12,4},{1,9},{5,13},{9,1},{13,5},{2,10},{6,14},... | collective-permute-start | bytes 3080 | tf_op jit(solution)/shard_map/ppermute | solution.py:61
  17.4 5.7 %collective-permute-start.2 = (f32[1,2,128]{2,1,0:T(2,128)}, f32[1,2,128]{2,1,0:T(2,128)}, u32[]{:S(2)}, u32[]{:S(2)}) collective-permute-start(f32[1,2,128]{2,1,0:T(2,128)} %maximum_bitcast_fusion), channel_id=1, source_target_pairs={{0,12},{4,8},{8,4},{12,0},{1,13},{5,9},{9,5},{13,1},{2,14},{6,10},... | collective-permute-start | bytes 3080 | tf_op jit(solution)/shard_map/ppermute | solution.py:61
  17.4 11.9 %collective-permute-start.4 = (bf16[2,2,256,128]{3,2,1,0:T(8,128)(2,1)}, bf16[2,2,256,128]{3,2,1,0:T(8,128)(2,1)}, u32[]{:S(2)}, u32[]{:S(2)}) collective-permute-start(bf16[2,2,256,128]{3,2,1,0:T(8,128)(2,1)} %constant_dynamic-slice_fusion.13), channel_id=1, source_target_pairs={{0,16},{16,0},{1,17},{17,1},{2,18},{18,2},{3,19},{19,3},{4,20},{20... | collective-permute-start | bytes 786440 | tf_op jit(solution)/shard_map/ppermute | solution.py:53
  19.1 12.4 %collective-permute-start.5 = (bf16[2048,512]{1,0:T(8,128)(2,1)}, bf16[2048,512]{1,0:T(8,128)(2,1)}, u32[]{:S(2)}, u32[]{:S(2)}) collective-permute-start(bf16[2048,512]{1,0:T(8,128)(2,1)} %refs_3_.3), channel_id=1, source_target_pairs={{0,1},{1,0},{2,3},{3,2},{4,5},{5,4},{6,7},{7,6},{8,9},{9,8},{10,11... | collective-permute-start | bytes 6291464 | tf_op jit(solution)/shard_map/ppermute | solution.py:57
  20.5 58.1 %collective-permute-start.12 = (bf16[2048,512]{1,0:T(8,128)(2,1)}, bf16[2048,512]{1,0:T(8,128)(2,1)}, u32[]{:S(2)}, u32[]{:S(2)}) collective-permute-start(bf16[2048,512]{1,0:T(8,128)(2,1)} %refs_3_.3), channel_id=1, source_target_pairs={{0,2},{1,3},{2,0},{3,1},{4,6},{5,7},{6,4},{7,5},{8,10},{9,11},{10,... | collective-permute-start | bytes 6291464 | tf_op jit(solution)/shard_map/ppermute | solution.py:57
  22.0 30.8 %collective-permute-start.7 = (bf16[1,384,512]{2,1,0:T(8,128)(2,1)S(1)}, bf16[1,384,512]{2,1,0:T(8,128)(2,1)}, u32[]{:S(2)}, u32[]{:S(2)}) collective-permute-start(bf16[1,384,512]{2,1,0:T(8,128)(2,1)S(1)} %dynamic-slice_bitcast_fusion), channel_id=1, source_target_pairs={{0,4},{4,0},{8,12},{12,8},{1,5},{5,1},{9,13},{13,9},{2,6},{6,2},{1... | collective-permute-start | bytes 1179656 | tf_op jit(solution)/shard_map/ppermute | solution.py:61
  23.8 3.7 %collective-permute-start.3 = (f32[4,2,128]{2,1,0:T(2,128)S(1)}, f32[4,2,128]{2,1,0:T(2,128)S(1)}, u32[]{:S(2)}, u32[]{:S(2)}) collective-permute-start(f32[4,2,128]{2,1,0:T(2,128)S(1)} %pad_maximum_fusion.11), channel_id=1, source_target_pairs={{0,16},{16,0},{1,17},{17,1},{2,18},{18,2},{3,19},{19,3},{4,20},{20... | collective-permute-start | bytes 12296 | tf_op jit(solution)/shard_map/ppermute | solution.py:53
  27.5 17.5 %collective-permute-start.6 = (bf16[4,128,512]{2,1,0:T(8,128)(2,1)S(1)}, bf16[4,128,512]{2,1,0:T(8,128)(2,1)S(1)}, u32[]{:S(2)}, u32[]{:S(2)}) collective-permute-start(bf16[4,128,512]{2,1,0:T(8,128)(2,1)S(1)} %pad_maximum_fusion.4), channel_id=1, source_target_pairs={{0,16},{16,0},{1,17},{17,1},{2,18},{18,2},{3,19},{19,3},{4,20},{20... | collective-permute-start | bytes 1572872 | tf_op jit(solution)/shard_map/ppermute | solution.py:53
  29.4 29.9 %collective-permute-start.8 = (bf16[1,384,512]{2,1,0:T(8,128)(2,1)S(1)}, bf16[1,384,512]{2,1,0:T(8,128)(2,1)S(1)}, u32[]{:S(2)}, u32[]{:S(2)}) collective-permute-start(bf16[1,384,512]{2,1,0:T(8,128)(2,1)S(1)} %dynamic-slice_bitcast_fusion), channel_id=1, source_target_pairs={{0,8},{4,12},{8,0},{12,4},{1,9},{5,13},{9,1},{13,5},{2,10},{6,14},... | collective-permute-start | bytes 1179656 | tf_op jit(solution)/shard_map/ppermute | solution.py:61
  31.5 27.7 %collective-permute-start.9 = (bf16[1,384,512]{2,1,0:T(8,128)(2,1)S(1)}, bf16[1,384,512]{2,1,0:T(8,128)(2,1)S(1)}, u32[]{:S(2)}, u32[]{:S(2)}) collective-permute-start(bf16[1,384,512]{2,1,0:T(8,128)(2,1)S(1)} %dynamic-slice_bitcast_fusion), channel_id=1, source_target_pairs={{0,12},{4,8},{8,4},{12,0},{1,13},{5,9},{9,5},{13,1},{2,14},{6,10},... | collective-permute-start | bytes 1179656 | tf_op jit(solution)/shard_map/ppermute | solution.py:61
  47.1 23.9 %collective-permute-start.11 = (bf16[256,2048]{1,0:T(8,128)(2,1)S(1)}, bf16[256,2048]{1,0:T(8,128)(2,1)S(1)}, u32[]{:S(2)}, u32[]{:S(2)}) collective-permute-start(bf16[256,2048]{1,0:T(8,128)(2,1)S(1)} %get-tuple-element.161.refs_0_), channel_id=1, source_target_pairs={{0,16},{16,0},{1,17},{17,1},{2,18},{18,2},{3,19},{19,3},{4,20},{20... | collective-permute-start | bytes 3145736 | tf_op jit(solution)/shard_map/ppermute | solution.py:53
  60.6 39.9 %copy-start.5 = (bf16[4,384,512]{2,1,0:T(8,128)(2,1)}, bf16[4,384,512]{2,1,0:T(8,128)(2,1)S(1)}, u32[]{:S(2)}) copy-start(bf16[4,384,512]{2,1,0:T(8,128)(2,1)S(1)} %pad_maximum_fusion.refs_0_) | copy-start | bytes 4718596
  60.6 16.9 %collective-permute-start.10 = (bf16[2,256,512]{2,1,0:T(8,128)(2,1)S(1)}, bf16[2,256,512]{2,1,0:T(8,128)(2,1)}, u32[]{:S(2)}, u32[]{:S(2)}) collective-permute-start(bf16[2,256,512]{2,1,0:T(8,128)(2,1)S(1)} %get-tuple-element.154), channel_id=1, source_target_pairs={{0,4},{4,0},{8,12},{12,8},{1,5},{5,1},{9,13},{13,9},{2,6},{6,2},{1... | collective-permute-start | bytes 1572872 | tf_op jit(solution)/shard_map/ppermute | solution.py:61
  78.5 16.2 %collective-permute-start.13 = (bf16[2048,512]{1,0:T(8,128)(2,1)}, bf16[2048,512]{1,0:T(8,128)(2,1)S(1)}, u32[]{:S(2)}, u32[]{:S(2)}) collective-permute-start(bf16[2048,512]{1,0:T(8,128)(2,1)} %collective-permute-done.12.refs_5_.refs_3_), channel_id=1, source_target_pairs={{0,1},{1,0},{2,3},{3,2},{4,5},{5,4},{6,7},{7,6},{8,9},{9,8},{10,11... | collective-permute-start | bytes 6291464 | tf_op jit(solution)/shard_map/ppermute | solution.py:57
  78.6 36.8 %collective-permute-start.18 = (bf16[4,384,512]{2,1,0:T(8,128)(2,1)S(1)}, bf16[4,384,512]{2,1,0:T(8,128)(2,1)S(1)}, u32[]{:S(2)}, u32[]{:S(2)}) collective-permute-start(bf16[4,384,512]{2,1,0:T(8,128)(2,1)S(1)} %pad_maximum_fusion.refs_0_), channel_id=1, source_target_pairs={{0,2},{1,3},{2,0},{3,1},{4,6},{5,7},{6,4},{7,5},{8,10},{9,11},{10,... | collective-permute-start | bytes 4718600 | tf_op jit(solution)/shard_map/ppermute | solution.py:57
  78.7 16.1 %collective-permute-start.14 = (bf16[2,128,512]{2,1,0:T(8,128)(2,1)S(1)}, bf16[2,128,512]{2,1,0:T(8,128)(2,1)S(1)}, u32[]{:S(2)}, u32[]{:S(2)}) collective-permute-start(bf16[2,128,512]{2,1,0:T(8,128)(2,1)S(1)} %add_convert_fusion.3), channel_id=1, source_target_pairs={{0,8},{4,12},{8,0},{12,4},{1,9},{5,13},{9,1},{13,5},{2,10},{6,14},... | collective-permute-start | bytes 786440 | tf_op jit(solution)/shard_map/ppermute | solution.py:61
  103.5 28.0 %collective-permute-start.17 = (bf16[256,2048]{1,0:T(8,128)(2,1)S(1)}, bf16[256,2048]{1,0:T(8,128)(2,1)S(1)}, u32[]{:S(2)}, u32[]{:S(2)}) collective-permute-start(bf16[256,2048]{1,0:T(8,128)(2,1)S(1)} %get-tuple-element.168.refs_1_), channel_id=1, source_target_pairs={{0,16},{16,0},{1,17},{17,1},{2,18},{18,2},{3,19},{19,3},{4,20},{20... | collective-permute-start | bytes 3145736 | tf_op jit(solution)/shard_map/ppermute | solution.py:53
  105.3 15.0 %collective-permute-start.16 = (bf16[2,256,512]{2,1,0:T(8,128)(2,1)S(1)}, bf16[2,256,512]{2,1,0:T(8,128)(2,1)}, u32[]{:S(2)}, u32[]{:S(2)}) collective-permute-start(bf16[2,256,512]{2,1,0:T(8,128)(2,1)S(1)} %project.8), channel_id=1, source_target_pairs={{0,4},{4,0},{8,12},{12,8},{1,5},{5,1},{9,13},{13,9},{2,6},{6,2},{1... | collective-permute-start | bytes 1572872 | tf_op jit(solution)/shard_map/ppermute | solution.py:61
  105.3 26.2 %collective-permute-start.15 = (bf16[2,256,512]{2,1,0:T(8,128)(2,1)S(1)}, bf16[2,256,512]{2,1,0:T(8,128)(2,1)}, u32[]{:S(2)}, u32[]{:S(2)}) collective-permute-start(bf16[2,256,512]{2,1,0:T(8,128)(2,1)S(1)} %get-tuple-element.165), channel_id=1, source_target_pairs={{0,4},{4,0},{8,12},{12,8},{1,5},{5,1},{9,13},{13,9},{2,6},{6,2},{1... | collective-permute-start | bytes 1572872 | tf_op jit(solution)/shard_map/ppermute | solution.py:61
  110.1 38.1 %collective-permute-start.22 = (bf16[2,256,512]{2,1,0:T(8,128)(2,1)S(1)}, bf16[2,256,512]{2,1,0:T(8,128)(2,1)S(1)}, u32[]{:S(2)}, u32[]{:S(2)}) collective-permute-start(bf16[2,256,512]{2,1,0:T(8,128)(2,1)S(1)} %project.9), channel_id=1, source_target_pairs={{0,4},{4,0},{8,12},{12,8},{1,5},{5,1},{9,13},{13,9},{2,6},{6,2},{1... | collective-permute-start | bytes 1572872 | tf_op jit(solution)/shard_map/ppermute | solution.py:61
  116.6 43.8 %collective-permute-start.20 = (bf16[2,128,512]{2,1,0:T(8,128)(2,1)S(1)}, bf16[2,128,512]{2,1,0:T(8,128)(2,1)S(1)}, u32[]{:S(2)}, u32[]{:S(2)}) collective-permute-start(bf16[2,128,512]{2,1,0:T(8,128)(2,1)S(1)} %get-tuple-element.279), channel_id=1, source_target_pairs={{0,16},{16,0},{1,17},{17,1},{2,18},{18,2},{3,19},{19,3},{4,20},{20... | collective-permute-start | bytes 786440 | tf_op jit(solution)/shard_map/ppermute | solution.py:53
  132.5 26.8 %collective-permute-start.19 = (bf16[2,128,512]{2,1,0:T(8,128)(2,1)S(1)}, bf16[2,128,512]{2,1,0:T(8,128)(2,1)S(1)}, u32[]{:S(2)}, u32[]{:S(2)}) collective-permute-start(bf16[2,128,512]{2,1,0:T(8,128)(2,1)S(1)} %add_convert_fusion.2), channel_id=1, source_target_pairs={{0,8},{4,12},{8,0},{12,4},{1,9},{5,13},{9,1},{13,5},{2,10},{6,14},... | collective-permute-start | bytes 786440 | tf_op jit(solution)/shard_map/ppermute | solution.py:61
  137.4 27.5 %collective-permute-start.21 = (bf16[2,128,512]{2,1,0:T(8,128)(2,1)S(1)}, bf16[2,128,512]{2,1,0:T(8,128)(2,1)S(1)}, u32[]{:S(2)}, u32[]{:S(2)}) collective-permute-start(bf16[2,128,512]{2,1,0:T(8,128)(2,1)S(1)} %add_convert_fusion.1), channel_id=1, source_target_pairs={{0,8},{4,12},{8,0},{12,4},{1,9},{5,13},{9,1},{13,5},{2,10},{6,14},... | collective-permute-start | bytes 786440 | tf_op jit(solution)/shard_map/ppermute | solution.py:61
  148.3 19.9 %collective-permute-start.23 = (bf16[2,128,512]{2,1,0:T(8,128)(2,1)S(1)}, bf16[2,128,512]{2,1,0:T(8,128)(2,1)S(1)}, u32[]{:S(2)}, u32[]{:S(2)}) collective-permute-start(bf16[2,128,512]{2,1,0:T(8,128)(2,1)S(1)} %add_convert_fusion), channel_id=1, source_target_pairs={{0,8},{4,12},{8,0},{12,4},{1,9},{5,13},{9,1},{13,5},{2,10},{6,14},... | collective-permute-start | bytes 786440 | tf_op jit(solution)/shard_map/ppermute | solution.py:61
  160.4 28.0 %copy-start.12 = (f32[2,128,512]{2,1,0:T(8,128)}, f32[2,128,512]{2,1,0:T(8,128)S(1)}, u32[]{:S(2)}) copy-start(f32[2,128,512]{2,1,0:T(8,128)S(1)} %get-tuple-element.278.refs_1_) | copy-start | bytes 1572868
  164.9 23.1 %copy-start.22 = (bf16[2,64,4096]{2,1,0:T(8,128)(2,1)S(1)}, bf16[2,64,4096]{2,1,0:T(8,128)(2,1)}, u32[]{:S(2)}) copy-start(bf16[2,64,4096]{2,1,0:T(8,128)(2,1)} %param.28) | copy-start | bytes 3145732
  166.1 22.2 %copy-start.14 = (f32[2,128,512]{2,1,0:T(8,128)}, f32[2,128,512]{2,1,0:T(8,128)S(1)}, u32[]{:S(2)}) copy-start(f32[2,128,512]{2,1,0:T(8,128)S(1)} %get-tuple-element.276.refs_2_) | copy-start | bytes 1572868
  166.1 6.4 %collective-permute-start.24 = (bf16[2,128,512]{2,1,0:T(8,128)(2,1)S(1)}, bf16[2,128,512]{2,1,0:T(8,128)(2,1)S(1)}, u32[]{:S(2)}, u32[]{:S(2)}) collective-permute-start(bf16[2,128,512]{2,1,0:T(8,128)(2,1)S(1)} %get-tuple-element.184), channel_id=1, source_target_pairs={{0,16},{16,0},{1,17},{17,1},{2,18},{18,2},{3,19},{19,3},{4,20},{20... | collective-permute-start | bytes 786440 | tf_op jit(solution)/shard_map/ppermute | solution.py:53
  166.2 10.8 %collective-permute-start.25 = (bf16[2,128,512]{2,1,0:T(8,128)(2,1)S(1)}, bf16[2,128,512]{2,1,0:T(8,128)(2,1)S(1)}, u32[]{:S(2)}, u32[]{:S(2)}) collective-permute-start(bf16[2,128,512]{2,1,0:T(8,128)(2,1)S(1)} %get-tuple-element.185), channel_id=1, source_target_pairs={{0,16},{16,0},{1,17},{17,1},{2,18},{18,2},{3,19},{19,3},{4,20},{20... | collective-permute-start | bytes 786440 | tf_op jit(solution)/shard_map/ppermute | solution.py:53
  178.5 18.5 %copy-start.16 = (f32[2,128,512]{2,1,0:T(8,128)}, f32[2,128,512]{2,1,0:T(8,128)S(1)}, u32[]{:S(2)}) copy-start(f32[2,128,512]{2,1,0:T(8,128)S(1)} %get-tuple-element.274.refs_3_) | copy-start | bytes 1572868
  178.5 9.5 %collective-permute-start.26 = (bf16[2,128,512]{2,1,0:T(8,128)(2,1)}, bf16[2,128,512]{2,1,0:T(8,128)(2,1)S(1)}, u32[]{:S(2)}, u32[]{:S(2)}) collective-permute-start(bf16[2,128,512]{2,1,0:T(8,128)(2,1)} %get-tuple-element.273), channel_id=1, source_target_pairs={{0,16},{16,0},{1,17},{17,1},{2,18},{18,2},{3,19},{19,3},{4,20},{20... | collective-permute-start | bytes 786440 | tf_op jit(solution)/shard_map/ppermute | solution.py:53
  188.2 13.9 %collective-permute-start.27 = (bf16[128,2048]{1,0:T(8,128)(2,1)S(1)}, bf16[128,2048]{1,0:T(8,128)(2,1)S(1)}, u32[]{:S(2)}, u32[]{:S(2)}) collective-permute-start(bf16[128,2048]{1,0:T(8,128)(2,1)S(1)} %pad_maximum_fusion.5), channel_id=1, source_target_pairs={{0,16},{16,0},{1,17},{17,1},{2,18},{18,2},{3,19},{19,3},{4,20},{20... | collective-permute-start | bytes 1572872 | tf_op jit(solution)/shard_map/ppermute | solution.py:53
  202.9 17.1 %collective-permute-start.28 = (bf16[4,256,512]{2,1,0:T(8,128)(2,1)}, bf16[4,256,512]{2,1,0:T(8,128)(2,1)}, u32[]{:S(2)}, u32[]{:S(2)}) collective-permute-start(bf16[4,256,512]{2,1,0:T(8,128)(2,1)} %expert_down.2), channel_id=1, source_target_pairs={{0,16},{16,0},{1,17},{17,1},{2,18},{18,2},{3,19},{19,3},{4,20},{20... | collective-permute-start | bytes 3145736 | tf_op jit(solution)/shard_map/ppermute | solution.py:53
  206.2 13.8 %copy-start.17 = (f32[2,128,512]{2,1,0:T(8,128)S(1)}, f32[2,128,512]{2,1,0:T(8,128)}, u32[]{:S(2)}) copy-start(f32[2,128,512]{2,1,0:T(8,128)} %copy-done.16) | copy-start | bytes 1572868
  222.4 6.0 %collective-permute-start.31 = (bf16[4,384,512]{2,1,0:T(8,128)(2,1)S(1)}, bf16[4,384,512]{2,1,0:T(8,128)(2,1)S(1)}, u32[]{:S(2)}, u32[]{:S(2)}) collective-permute-start(bf16[4,384,512]{2,1,0:T(8,128)(2,1)S(1)} %copy-done.44), channel_id=1, source_target_pairs={{0,1},{1,0},{2,3},{3,2},{4,5},{5,4},{6,7},{7,6},{8,9},{9,8},{10,11... | collective-permute-start | bytes 4718600 | tf_op jit(solution)/shard_map/ppermute | solution.py:57
  222.5 5.9 %collective-permute-start.30 = (bf16[4,384,512]{2,1,0:T(8,128)(2,1)S(1)}, bf16[4,384,512]{2,1,0:T(8,128)(2,1)S(1)}, u32[]{:S(2)}, u32[]{:S(2)}) collective-permute-start(bf16[4,384,512]{2,1,0:T(8,128)(2,1)S(1)} %copy-done.6), channel_id=1, source_target_pairs={{0,1},{1,0},{2,3},{3,2},{4,5},{5,4},{6,7},{7,6},{8,9},{9,8},{10,11... | collective-permute-start | bytes 4718600 | tf_op jit(solution)/shard_map/ppermute | solution.py:57
  223.0 18.0 %collective-permute-start.33 = (bf16[2,256,512]{2,1,0:T(8,128)(2,1)}, bf16[2,256,512]{2,1,0:T(8,128)(2,1)}, u32[]{:S(2)}, u32[]{:S(2)}) collective-permute-start(bf16[2,256,512]{2,1,0:T(8,128)(2,1)} %get-tuple-element.213), channel_id=1, source_target_pairs={{0,2},{1,3},{2,0},{3,1},{4,6},{5,7},{6,4},{7,5},{8,10},{9,11},{10,... | collective-permute-start | bytes 1572872 | tf_op jit(solution)/shard_map/ppermute | solution.py:57
  224.0 4.3 %collective-permute-start.29 = (f32[128,128]{1,0:T(8,128)S(1)}, f32[128,128]{1,0:T(8,128)S(1)}, u32[]{:S(2)}, u32[]{:S(2)}) collective-permute-start(f32[128,128]{1,0:T(8,128)S(1)} %slice.121), channel_id=1, source_target_pairs={{0,16},{16,0},{1,17},{17,1},{2,18},{18,2},{3,19},{19,3},{4,20},{20... | collective-permute-start | bytes 196616 | tf_op jit(solution)/shard_map/ppermute | solution.py:53
  234.1 10.4 %collective-permute-start.32 = (f32[128,768]{1,0:T(8,128)}, f32[128,768]{1,0:T(8,128)}, u32[]{:S(2)}, u32[]{:S(2)}) collective-permute-start(f32[128,768]{1,0:T(8,128)} %get-tuple-element.212), channel_id=1, source_target_pairs={{0,16},{16,0},{1,17},{17,1},{2,18},{18,2},{3,19},{19,3},{4,20},{20... | collective-permute-start | bytes 1179656 | tf_op jit(solution)/shard_map/ppermute | solution.py:53
  245.6 14.8 %collective-permute-start.34 = (f32[128,768]{1,0:T(8,128)}, f32[128,768]{1,0:T(8,128)}, u32[]{:S(2)}, u32[]{:S(2)}) collective-permute-start(f32[128,768]{1,0:T(8,128)} %get-tuple-element.224), channel_id=1, source_target_pairs={{0,16},{16,0},{1,17},{17,1},{2,18},{18,2},{3,19},{19,3},{4,20},{20... | collective-permute-start | bytes 1179656 | tf_op jit(solution)/shard_map/ppermute | solution.py:53
  247.2 14.3 %collective-permute-start.37 = (f32[32,768]{1,0:T(8,128)}, f32[32,768]{1,0:T(8,128)}, u32[]{:S(2)}, u32[]{:S(2)}) collective-permute-start(f32[32,768]{1,0:T(8,128)} %get-tuple-element.315), channel_id=1, source_target_pairs={{0,4},{4,0},{8,12},{12,8},{1,5},{5,1},{9,13},{13,9},{2,6},{6,2},{1... | collective-permute-start | bytes 294920 | tf_op jit(solution)/shard_map/ppermute | solution.py:61
  247.2 14.3 %collective-permute-start.38 = (f32[32,768]{1,0:T(8,128)S(1)}, f32[32,768]{1,0:T(8,128)}, u32[]{:S(2)}, u32[]{:S(2)}) collective-permute-start(f32[32,768]{1,0:T(8,128)S(1)} %get-tuple-element.314), channel_id=1, source_target_pairs={{0,8},{4,12},{8,0},{12,4},{1,9},{5,13},{9,1},{13,5},{2,10},{6,14},... | collective-permute-start | bytes 294920 | tf_op jit(solution)/shard_map/ppermute | solution.py:61
  250.4 11.2 %collective-permute-start.39 = (f32[32,768]{1,0:T(8,128)S(1)}, f32[32,768]{1,0:T(8,128)}, u32[]{:S(2)}, u32[]{:S(2)}) collective-permute-start(f32[32,768]{1,0:T(8,128)S(1)} %get-tuple-element.313), channel_id=1, source_target_pairs={{0,12},{4,8},{8,4},{12,0},{1,13},{5,9},{9,5},{13,1},{2,14},{6,10},... | collective-permute-start | bytes 294920 | tf_op jit(solution)/shard_map/ppermute | solution.py:61
  253.5 21.5 %collective-permute-start.36 = (bf16[2,256,512]{2,1,0:T(8,128)(2,1)}, bf16[2,256,512]{2,1,0:T(8,128)(2,1)S(1)}, u32[]{:S(2)}, u32[]{:S(2)}) collective-permute-start(bf16[2,256,512]{2,1,0:T(8,128)(2,1)} %pad_maximum_fusion.6), channel_id=1, source_target_pairs={{0,1},{1,0},{2,3},{3,2},{4,5},{5,4},{6,7},{7,6},{8,9},{9,8},{10,11... | collective-permute-start | bytes 1572872 | tf_op jit(solution)/shard_map/ppermute | solution.py:57
  261.7 20.0 %collective-permute-start.35 = (f32[128,1536]{1,0:T(8,128)S(1)}, f32[128,1536]{1,0:T(8,128)S(1)}, u32[]{:S(2)}, u32[]{:S(2)}) collective-permute-start(f32[128,1536]{1,0:T(8,128)S(1)} %pad_maximum_fusion.2), channel_id=1, source_target_pairs={{0,16},{16,0},{1,17},{17,1},{2,18},{18,2},{3,19},{19,3},{4,20},{20... | collective-permute-start | bytes 2359304 | tf_op jit(solution)/shard_map/ppermute | solution.py:53
  263.0 6.5 %collective-permute-start.40 = (f32[32,768]{1,0:T(8,128)S(1)}, f32[32,768]{1,0:T(8,128)S(1)}, u32[]{:S(2)}, u32[]{:S(2)}) collective-permute-start(f32[32,768]{1,0:T(8,128)S(1)} %get-tuple-element.307), channel_id=1, source_target_pairs={{0,4},{4,0},{8,12},{12,8},{1,5},{5,1},{9,13},{13,9},{2,6},{6,2},{1... | collective-permute-start | bytes 294920 | tf_op jit(solution)/shard_map/ppermute | solution.py:61
  263.0 11.5 %collective-permute-start.41 = (f32[32,768]{1,0:T(8,128)S(1)}, f32[32,768]{1,0:T(8,128)S(1)}, u32[]{:S(2)}, u32[]{:S(2)}) collective-permute-start(f32[32,768]{1,0:T(8,128)S(1)} %get-tuple-element.306), channel_id=1, source_target_pairs={{0,8},{4,12},{8,0},{12,4},{1,9},{5,13},{9,1},{13,5},{2,10},{6,14},... | collective-permute-start | bytes 294920 | tf_op jit(solution)/shard_map/ppermute | solution.py:61
  266.7 7.9 %collective-permute-start.42 = (f32[32,768]{1,0:T(8,128)S(1)}, f32[32,768]{1,0:T(8,128)S(1)}, u32[]{:S(2)}, u32[]{:S(2)}) collective-permute-start(f32[32,768]{1,0:T(8,128)S(1)} %get-tuple-element.305), channel_id=1, source_target_pairs={{0,12},{4,8},{8,4},{12,0},{1,13},{5,9},{9,5},{13,1},{2,14},{6,10},... | collective-permute-start | bytes 294920 | tf_op jit(solution)/shard_map/ppermute | solution.py:61
  282.9 18.5 %copy-start.57 = (s32[4]{0:T(128)S(1)}, s32[4]{0:T(128)}, u32[]{:S(2)}) copy-start(s32[4]{0:T(128)} %constant.125.clone) | copy-start | bytes 52
  282.9 23.2 %copy-start.27 = (bf16[2,256,512]{2,1,0:T(8,128)(2,1)S(1)}, bf16[2,256,512]{2,1,0:T(8,128)(2,1)}, u32[]{:S(2)}) copy-start(bf16[2,256,512]{2,1,0:T(8,128)(2,1)} %copy-done.25) | copy-start | bytes 1572868
  282.9 10.8 %collective-permute-start.43 = (bf16[128,1536]{1,0:T(8,128)(2,1)S(1)}, bf16[128,1536]{1,0:T(8,128)(2,1)S(1)}, u32[]{:S(2)}, u32[]{:S(2)}) collective-permute-start(bf16[128,1536]{1,0:T(8,128)(2,1)S(1)} %get-tuple-element.251.rows), channel_id=1, source_target_pairs={{0,16},{16,0},{1,17},{17,1},{2,18},{18,2},{3,19},{19,3},{4,20},{20... | collective-permute-start | bytes 1179656 | tf_op jit(solution)/shard_map/ppermute | solution.py:53
  284.2 10.5 %collective-permute-start.44 = (bf16[128,1536]{1,0:T(8,128)(2,1)S(1)}, bf16[128,1536]{1,0:T(8,128)(2,1)S(1)}, u32[]{:S(2)}, u32[]{:S(2)}) collective-permute-start(bf16[128,1536]{1,0:T(8,128)(2,1)S(1)} %get-tuple-element.251.rows), channel_id=1, source_target_pairs={{0,2},{1,3},{2,0},{3,1},{4,6},{5,7},{6,4},{7,5},{8,10},{9,11},{10,... | collective-permute-start | bytes 1179656 | tf_op jit(solution)/shard_map/ppermute | solution.py:57
  294.7 5.7 %collective-permute-start.45 = (bf16[64,1536]{1,0:T(8,128)(2,1)S(1)}, bf16[64,1536]{1,0:T(8,128)(2,1)S(1)}, u32[]{:S(2)}, u32[]{:S(2)}) collective-permute-start(bf16[64,1536]{1,0:T(8,128)(2,1)S(1)} %slice.126), channel_id=1, source_target_pairs={{0,16},{16,0},{1,17},{17,1},{2,18},{18,2},{3,19},{19,3},{4,20},{20... | collective-permute-start | bytes 589832 | tf_op jit(solution)/shard_map/ppermute | solution.py:53
  295.6 5.7 %collective-permute-start.46 = (bf16[64,1536]{1,0:T(8,128)(2,1)S(1)}, bf16[64,1536]{1,0:T(8,128)(2,1)S(1)}, u32[]{:S(2)}, u32[]{:S(2)}) collective-permute-start(bf16[64,1536]{1,0:T(8,128)(2,1)S(1)} %slice.127), channel_id=1, source_target_pairs={{0,2},{1,3},{2,0},{3,1},{4,6},{5,7},{6,4},{7,5},{8,10},{9,11},{10,... | collective-permute-start | bytes 589832 | tf_op jit(solution)/shard_map/ppermute | solution.py:57
  301.4 3.5 collective-permute-start.47
  311.7 24.2 %copy-start.30 = (bf16[2,384,256]{2,1,0:T(8,128)(2,1)}, bf16[2,384,256]{2,1,0:T(8,128)(2,1)S(1)}, u32[]{:S(2)}) copy-start(bf16[2,384,256]{2,1,0:T(8,128)(2,1)S(1)} %get-tuple-element.252) | copy-start | bytes 1179652
  311.7 12.3 %collective-permute-start.50 = (bf16[2,384,256]{2,1,0:T(8,128)(2,1)}, bf16[2,384,256]{2,1,0:T(8,128)(2,1)}, u32[]{:S(2)}, u32[]{:S(2)}) collective-permute-start(bf16[2,384,256]{2,1,0:T(8,128)(2,1)} %get-tuple-element.249), channel_id=1, source_target_pairs={{0,4},{4,0},{8,12},{12,8},{1,5},{5,1},{9,13},{13,9},{2,6},{6,2},{1... | collective-permute-start | bytes 1179656 | tf_op jit(solution)/shard_map/ppermute | solution.py:61
  311.8 24.1 %collective-permute-start.49 = (bf16[2,384,256]{2,1,0:T(8,128)(2,1)}, bf16[2,384,256]{2,1,0:T(8,128)(2,1)}, u32[]{:S(2)}, u32[]{:S(2)}) collective-permute-start(bf16[2,384,256]{2,1,0:T(8,128)(2,1)} %get-tuple-element.253), channel_id=1, source_target_pairs={{0,4},{4,0},{8,12},{12,8},{1,5},{5,1},{9,13},{13,9},{2,6},{6,2},{1... | collective-permute-start | bytes 1179656 | tf_op jit(solution)/shard_map/ppermute | solution.py:61
  318.0 19.7 %copy-start.56 = (s32[64]{0:T(128)S(1)}, s32[64]{0:T(128)}, u32[]{:S(2)}) copy-start(s32[64]{0:T(128)} %copy-done.55) | copy-start | bytes 772
  318.0 20.4 %collective-permute-start.48 = (bf16[128,2048]{1,0:T(8,128)(2,1)S(1)}, bf16[128,2048]{1,0:T(8,128)(2,1)S(1)}, u32[]{:S(2)}, u32[]{:S(2)}) collective-permute-start(bf16[128,2048]{1,0:T(8,128)(2,1)S(1)} %hidden_grad.2), channel_id=1, source_target_pairs={{0,16},{16,0},{1,17},{17,1},{2,18},{18,2},{3,19},{19,3},{4,20},{20... | collective-permute-start | bytes 1572872 | tf_op jit(solution)/shard_map/ppermute | solution.py:53
  325.7 13.9 %collective-permute-start.51 = (bf16[384,256]{1,0:T(8,128)(2,1)}, bf16[384,256]{1,0:T(8,128)(2,1)S(1)}, u32[]{:S(2)}, u32[]{:S(2)}) collective-permute-start(bf16[384,256]{1,0:T(8,128)(2,1)} %fusion.7), channel_id=1, source_target_pairs={{0,8},{4,12},{8,0},{12,4},{1,9},{5,13},{9,1},{13,5},{2,10},{6,14},... | collective-permute-start | bytes 589832 | tf_op jit(solution)/shard_map/ppermute | solution.py:61
  337.6 10.4 %collective-permute-start.52 = (bf16[384,256]{1,0:T(8,128)(2,1)}, bf16[384,256]{1,0:T(8,128)(2,1)S(1)}, u32[]{:S(2)}, u32[]{:S(2)}) collective-permute-start(bf16[384,256]{1,0:T(8,128)(2,1)} %fusion.8), channel_id=1, source_target_pairs={{0,8},{4,12},{8,0},{12,4},{1,9},{5,13},{9,1},{13,5},{2,10},{6,14},... | collective-permute-start | bytes 589832 | tf_op jit(solution)/shard_map/ppermute | solution.py:61
  (48 other events, 261.0 us)
Sparse Core Ops, SparseCore 0:
  178.6 63.6 all-gather.2

commit v5 on v4

--- a/solution.py
+++ b/solution.py
@@ -141,7 +141,7 @@
 
 
 FREE = pl.CostEstimate(flops=0, bytes_accessed=0, transcendentals=0)
-VMEM_BYTES = 48 * 2**20
+VMEM_BYTES = 32 * 2**20
 
 
 def whole(shape):
@@ -428,7 +428,7 @@
             scratch_shapes=[pltpu.VMEM((2 * count, width), BF16)],
         ),
         cost_estimate=FREE,
-        compiler_params=pltpu.CompilerParams(vmem_limit_bytes=VMEM_BYTES),
+        compiler_params=pltpu.CompilerParams(vmem_limit_bytes=48 * 2**20),
         name="expert_hidden",
     )(facts, *hidden, *got, gain[None], gate, up)
 
@@ -460,7 +460,7 @@
             out_specs=pl.BlockSpec((1, rows.shape[0], size), lambda r, facts: (r, 0, 0)),
         ),
         cost_estimate=FREE,
-        compiler_params=pltpu.CompilerParams(vmem_limit_bytes=VMEM_BYTES),
+        compiler_params=pltpu.CompilerParams(vmem_limit_bytes=48 * 2**20),
         name="expert_down",
     )(facts, rows, weight)
 
@@ -624,7 +624,7 @@
     weight_y = order.waits(weight_y)
     weight_y_core = swap_rep(weight_y, 1)
     teacher_y = swap_rep(order.take(teacher), 2)
-    weight_y_core, across_0 = order.waits(weight_y_core, across_0)
+    weight_y_core = order.waits(weight_y_core)
 
     sent_1, mine_1, far_1 = project(
         order.take(sent_rows, kept_rows),
@@ -646,6 +646,7 @@
     (sent_2,) = other_part(order.take(other_sent), other_placer[:sent_count], 0, (sent_count,))
     order.ends(sent_2)
     beside_2 = swap_z(sent_2, 1)
+    across_0 = order.waits(across_0)
     other_kept = swap_x(order.take(kept_rows))
     (sent_3,) = other_part(order.take(other_sent), other_placer[:sent_count], 2, (sent_count,))
     order.ends(sent_3)
@@ -664,19 +665,19 @@
         order.take(other_kept), other_placer[sent_count:], 2, (own_count, own_count)
     )
     order.ends(mine_3)
-    beside_3 = order.waits(beside_3)
+    beside_3, across_1 = order.waits(beside_3, across_1)
     across_3 = swap_z(halved(far_3, beside_3), 2)
     hidden_0 = summed(mine_0, beside_0, across_0)
-    got_0 = swap_x(hidden_0.astype(BF16))
-    hidden_1 = summed(mine_1, beside_1, order.waits(across_1))
-    got_0, across_2 = order.waits(got_0, across_2)
+    hidden_1 = summed(mine_1, beside_1, across_1)
+    got_0, got_1 = (swap_x(order.take(part.astype(BF16))) for part in (hidden_0, hidden_1))
+    across_2, got_0, got_1 = order.waits(across_2, got_0, got_1)
     hidden_2 = summed(mine_2, beside_2, across_2)
-    got_1, got_2 = (swap_x(order.take(part.astype(BF16))) for part in (hidden_1, hidden_2))
-    across_3, got_1, got_2 = order.waits(across_3, got_1, got_2)
+    got_2 = swap_x(hidden_2.astype(BF16))
+    heads = lax.all_gather(order.take(learner_head), ("vocab", "rep"))
+    heads = heads.reshape(4, 4, *learner_head.shape)
+    across_3, got_2 = order.waits(across_3, got_2)
     hidden_3 = summed(mine_3, beside_3, across_3)
     got_3 = swap_x(hidden_3.astype(BF16))
-    heads = lax.all_gather(order.take(learner_head), ("vocab", "rep"))
-    heads = heads.reshape(4, 4, *learner_head.shape)
     got_3 = order.waits(got_3)
     learner_x = swap_x(columns(order.take(learner_own), 1 - ctx_index))
 
@@ -721,7 +722,7 @@
     teacher_own[1], teacher_other[1] = logits_part(order.take(final_rows), teacher, 1)
     order.ends(teacher_own[1])
     scale = lax.rsqrt((squares[:own_count, :1] + other_squares[:, :1]) / width + EPSILON)
-    teacher_got, plane_y = order.waits(teacher_got, plane_y)
+    teacher_got = order.waits(teacher_got)
     part = order.ends((teacher_own[0] + teacher_got) * scale)
     teacher_got = swap_x(order.take(teacher_other[1]))
     teacher_logits = [line_exchange(part)]
@@ -742,6 +743,7 @@
     teacher_lse = teacher_peak + jnp.log(
         jnp.sum(jnp.exp(teacher_logits - teacher_peak), axis=1, keepdims=True)
     )
+    plane_y = order.waits(plane_y)
     plane_core = swap_rep(jnp.stack([plane_here[1], plane_y[1]]), 1)
     learner_other, plane_core = order.waits(learner_other, plane_core)
     learner_logits = learner_own_part + learner_other

time: 358 us -> 336 us (0.939)
  Pallas kernels: 85.1 us -> 69.7 us
  other arithmetic: 30.2 us -> 23 us
  waiting for transfers between devices: 144 us -> 150 us
    ppermute x11, waiting for transfers between devices: 8.52 us -> 23.9 us  [swap_rep(): return lax.ppermute(value, 'rep', [(i, i ^ offset) for i in range(4)])]
    ppermute x24, waiting for transfers between devices: 83 us -> 68.6 us  [swap_z(): return lax.ppermute(value, 'vocab', [(i, i ^ offset) for i in range(4)])]
    ppermute x18, waiting for transfers between devices: 52.4 us -> 57.5 us  [swap_x(): return lax.ppermute(value, 'ctx', [(0, 1), (1, 0)])]
    pallas_call x2, Pallas kernels: 8.4 us -> 4.03 us  [grad_part(): pl.pallas_call(grad_kernel, out_shape=jax.ShapeDtypeStruct((rows.shape[0]...]
    pallas_call x2, Pallas kernels: 6.99 us -> 2.76 us  [logits_part(): pl.pallas_call(logits_kernel, out_shape=[jax.ShapeDtypeStruct((count, til...]
    pallas_call x2, Pallas kernels: 6.85 us -> 3.11 us  [learner_logits_part(): pl.pallas_call(learner_logits_kernel, out_shape=[jax.ShapeDtypeStruct((co...]
    unnamed x120 -> x106, local copies, waits for them, and re-layouts: 13.2 us -> 10.7 us
  transfers between devices with their start and end apart: 54 -> 54, of which waited for: 29 -> 30; matrix products, arithmetic and copies ran while one was open for 8% -> 6% of each run, Pallas kernels for 22% -> 20%
where the time goes in v5:
time: 336 us; the launch traced here: 335 us
  waiting for transfers between devices  150 us (45%)
  Pallas kernels  69.7 us (21%)
  starting transfers between devices  60.4 us (18%)
  other arithmetic  23 us (7%)
  local copies, waits for them, and re-layouts  16.7 us (5%)
  between operations  15.1 us (4%)
    ppermute x24, waiting for transfers between devices, swap_z(): return lax.ppermute(value, 'vocab', [(i, i ^ offset) for i in range(4)])  68.6 us
    ppermute x18, waiting for transfers between devices, swap_x(): return lax.ppermute(value, 'ctx', [(0, 1), (1, 0)])  57.5 us
    ppermute x24, starting transfers between devices, swap_z(): return lax.ppermute(value, 'vocab', [(i, i ^ offset) for i in range(4)])  35.2 us
    ppermute x11, waiting for transfers between devices, swap_rep(): return lax.ppermute(value, 'rep', [(i, i ^ offset) for i in range(4)])  23.9 us
    ppermute x18, starting transfers between devices, swap_x(): return lax.ppermute(value, 'ctx', [(0, 1), (1, 0)])  19.6 us
    pallas_call x6, Pallas kernels, project(): pl.pallas_call(functools.partial(project_kernel, count, parts), out_shape...  19.5 us
    pallas_call x1, Pallas kernels, attend(): pl.pallas_call(attend_kernel, out_shape=jax.ShapeDtypeStruct((seq_dev * p...  12.1 us
    unnamed x106, local copies, waits for them, and re-layouts  10.7 us
  transfers between devices with their start and end apart: 54, of which 30 were waited for; matrix products, arithmetic and copies ran while one was open for 6% of the time, Pallas kernels for 20%

profile of v5, /device:TPU:0, one launch (start us, length us, event | category | flops | bytes accessed | tf_op | source)
XLA Modules:
  0.0 335.4 jit_solution(17796096606247752791)
XLA Ops:
  7.2 1.8 constant_dynamic-slice_fusion.13
  11.8 3.0 collective-permute-start
  14.8 2.6 collective-permute-start.1
  17.4 1.7 collective-permute-start.4
  23.8 1.6 collective-permute-start.3
  29.4 2.2 collective-permute-start.8
  32.8 12.1 %attend.1.heads = bf16[512,2048]{1,0:T(8,128)(2,1)S(1)} custom-call(s32[4]{0:T(128)S(1)} %pad_add_fusion.1.facts, bf16[2,256,2048]{2,1,0:T(8,128)(2,1)S(1)} %copy-done.21, bf16[2,2,512,128]{3,2,1,0:T(8,128)(2,1)S(1)} %pad_maximum_fusion.3.rows), custom_call_target="tpu_custom_call" | custom-call | tf_op jit(solution)/shard_map/attend/pallas_call | solution.py:123
  45.0 2.1 sorted_rows.1
  47.0 1.6 collective-permute-start.11
  48.6 4.1 %project.6 = (bf16[2,256,512]{2,1,0:T(8,128)(2,1)S(1)}, bf16[2,128,512]{2,1,0:T(8,128)(2,1)S(1)}, bf16[2,128,512]{2,1,0:T(8,128)(2,1)S(1)}) custom-call(bf16[256,2048]{1,0:T(8,128)(2,1)S(1)} %get-tuple-element.160.refs_0_, bf16[256,2048]{1,0:T(8,128)(2,1)S(1)} %get-tuple-element.168.refs_1_, bf16[256,128]{1,0:T(8,128)(2,1)S(1)} %get-tuple-element.144.refs_2_, ...), custom_call_target="tpu_custom_call" | custom-call | tf_op jit(solution)/shard_map/project/pallas_call | solution.py:170
  52.7 6.5 %collective-permute-done.8 = bf16[1,384,512]{2,1,0:T(8,128)(2,1)S(1)} collective-permute-done((bf16[1,384,512]{2,1,0:T(8,128)(2,1)S(1)}, bf16[1,384,512]{2,1,0:T(8,128)(2,1)S(1)}, u32[]{:S(2)}, u32[]{:S(2)}) %collective-permute-start.8) | collective-permute-done | bytes 393248 | tf_op jit(solution)/shard_map/ppermute | solution.py:61
  60.6 6.7 %collective-permute-start.10 = (bf16[2,256,512]{2,1,0:T(8,128)(2,1)S(1)}, bf16[2,256,512]{2,1,0:T(8,128)(2,1)S(1)}, u32[]{:S(2)}, u32[]{:S(2)}) collective-permute-start(bf16[2,256,512]{2,1,0:T(8,128)(2,1)S(1)} %get-tuple-element.154), channel_id=1, source_target_pairs={{0,4},{4,0},{8,12},{12,8},{1,5},{5,1},{9,13},{13,9},{2,6},{6,2},{1... | collective-permute-start | bytes 1572872 | tf_op jit(solution)/shard_map/ppermute | solution.py:61
  67.4 3.6 %collective-permute-done.11.refs_0_ = bf16[256,2048]{1,0:T(8,128)(2,1)S(1)} collective-permute-done((bf16[256,2048]{1,0:T(8,128)(2,1)S(1)}, bf16[256,2048]{1,0:T(8,128)(2,1)S(1)}, u32[]{:S(2)}, u32[]{:S(2)}) %collective-permute-start.11) | collective-permute-done | bytes 1048608 | tf_op jit(solution)/shard_map/ppermute | solution.py:53
  70.9 6.4 %collective-permute-done.10 = bf16[2,256,512]{2,1,0:T(8,128)(2,1)S(1)} collective-permute-done((bf16[2,256,512]{2,1,0:T(8,128)(2,1)S(1)}, bf16[2,256,512]{2,1,0:T(8,128)(2,1)S(1)}, u32[]{:S(2)}, u32[]{:S(2)}) %collective-permute-start.10) | collective-permute-done | bytes 524320 | tf_op jit(solution)/shard_map/ppermute | solution.py:61
  77.6 3.7 %collective-permute-start.12 = (bf16[2,128,512]{2,1,0:T(8,128)(2,1)S(1)}, bf16[2,128,512]{2,1,0:T(8,128)(2,1)S(1)}, u32[]{:S(2)}, u32[]{:S(2)}) collective-permute-start(bf16[2,128,512]{2,1,0:T(8,128)(2,1)S(1)} %add_convert_fusion.3), channel_id=1, source_target_pairs={{0,8},{4,12},{8,0},{12,4},{1,9},{5,13},{9,1},{13,5},{2,10},{6,14},... | collective-permute-start | bytes 786440 | tf_op jit(solution)/shard_map/ppermute | solution.py:61
  81.9 4.1 %project.7 = (bf16[2,256,512]{2,1,0:T(8,128)(2,1)S(1)}, bf16[2,128,512]{2,1,0:T(8,128)(2,1)S(1)}, bf16[2,128,512]{2,1,0:T(8,128)(2,1)S(1)}) custom-call(bf16[256,2048]{1,0:T(8,128)(2,1)S(1)} %get-tuple-element.160.refs_0_, bf16[256,2048]{1,0:T(8,128)(2,1)S(1)} %get-tuple-element.168.refs_1_, bf16[256,128]{1,0:T(8,128)(2,1)S(1)} %get-tuple-element.144.refs_2_, ...), custom_call_target="tpu_custom_call" | custom-call | tf_op jit(solution)/shard_map/project/pallas_call | solution.py:170
  85.9 2.9 project.8
  88.8 4.9 %collective-permute-done.12 = bf16[2,128,512]{2,1,0:T(8,128)(2,1)S(1)} collective-permute-done((bf16[2,128,512]{2,1,0:T(8,128)(2,1)S(1)}, bf16[2,128,512]{2,1,0:T(8,128)(2,1)S(1)}, u32[]{:S(2)}, u32[]{:S(2)}) %collective-permute-start.12) | collective-permute-done | bytes 262176 | tf_op jit(solution)/shard_map/ppermute | solution.py:61
  93.7 1.7 collective-permute-start.17
  95.4 2.0 collective-permute-start.15
  97.4 2.8 project.9
  100.3 14.0 %collective-permute-done.18.refs_2_ = bf16[4,384,512]{2,1,0:T(8,128)(2,1)S(1)} collective-permute-done((bf16[4,384,512]{2,1,0:T(8,128)(2,1)S(1)}, bf16[4,384,512]{2,1,0:T(8,128)(2,1)S(1)}, u32[]{:S(2)}, u32[]{:S(2)}) %collective-permute-start.18) | collective-permute-done | bytes 1572896 | tf_op jit(solution)/shard_map/ppermute | solution.py:57
  114.3 7.1 %collective-permute-done.15 = bf16[2,256,512]{2,1,0:T(8,128)(2,1)S(1)} collective-permute-done((bf16[2,256,512]{2,1,0:T(8,128)(2,1)S(1)}, bf16[2,256,512]{2,1,0:T(8,128)(2,1)S(1)}, u32[]{:S(2)}, u32[]{:S(2)}) %collective-permute-start.15) | collective-permute-done | bytes 524320 | tf_op jit(solution)/shard_map/ppermute | solution.py:61
  123.4 2.9 project.10
  126.4 2.1 collective-permute-start.21
  128.5 2.8 project.11
  131.3 8.1 %collective-permute-done.19 = bf16[2,256,512]{2,1,0:T(8,128)(2,1)S(1)} collective-permute-done((bf16[2,256,512]{2,1,0:T(8,128)(2,1)S(1)}, bf16[2,256,512]{2,1,0:T(8,128)(2,1)S(1)}, u32[]{:S(2)}, u32[]{:S(2)}) %collective-permute-start.19) | collective-permute-done | bytes 524320 | tf_op jit(solution)/shard_map/ppermute | solution.py:61
  141.6 4.2 %collective-permute-done.21 = bf16[2,128,512]{2,1,0:T(8,128)(2,1)S(1)} collective-permute-done((bf16[2,128,512]{2,1,0:T(8,128)(2,1)S(1)}, bf16[2,128,512]{2,1,0:T(8,128)(2,1)S(1)}, u32[]{:S(2)}, u32[]{:S(2)}) %collective-permute-start.21) | collective-permute-done | bytes 262176 | tf_op jit(solution)/shard_map/ppermute | solution.py:61
  145.8 3.0 collective-permute-done.22.refs_4_
  148.8 3.2 collective-permute-done.23.refs_5_
  155.6 9.4 %collective-permute-done.24 = bf16[2,128,512]{2,1,0:T(8,128)(2,1)S(1)} collective-permute-done((bf16[2,128,512]{2,1,0:T(8,128)(2,1)S(1)}, bf16[2,128,512]{2,1,0:T(8,128)(2,1)S(1)}, u32[]{:S(2)}, u32[]{:S(2)}) %collective-permute-start.24) | collective-permute-done | bytes 262176 | tf_op jit(solution)/shard_map/ppermute | solution.py:61
  166.8 8.7 %collective-permute-done.26.refs_7_ = bf16[2,128,512]{2,1,0:T(8,128)(2,1)S(1)} collective-permute-done((bf16[2,128,512]{2,1,0:T(8,128)(2,1)S(1)}, bf16[2,128,512]{2,1,0:T(8,128)(2,1)S(1)}, u32[]{:S(2)}, u32[]{:S(2)}) %collective-permute-start.26) | collective-permute-done | bytes 262176 | tf_op jit(solution)/shard_map/ppermute | solution.py:53
  176.3 8.6 %expert_hidden.1.rows = bf16[256,768]{1,0:T(8,128)(2,1)S(1)} custom-call(s32[8]{0:T(128)S(1)} %pad_add_fusion.facts, f32[2,128,512]{2,1,0:T(8,128)S(1)} %copy-done.9, f32[2,128,512]{2,1,0:T(8,128)S(1)} %get-tuple-element.278.refs_1_, f32[2,128,512]{2,1,0:T(8,128)S(1)} %get-tuple-element.276.refs_2_, f32[2,128,512]{2,1,0:T(8,128)S(1)} %get-tuple-element.274.refs_3_, ...), custom_call_target="tpu_custom_call" | custom-call | tf_op jit(solution)/shard_map/expert_hidden/pallas_call | solution.py:418
  184.9 5.0 %expert_down.2 = bf16[4,256,512]{2,1,0:T(8,128)(2,1)} custom-call(s32[4]{0:T(128)S(1)} %get-tuple-element.344.facts, bf16[256,768]{1,0:T(8,128)(2,1)S(1)} %expert_hidden.1.rows, bf16[1,768,4096]{2,1,0:T(8,128)(2,1)} %weight.3), custom_call_target="tpu_custom_call" | custom-call | tf_op jit(solution)/shard_map/expert_down/pallas_call | solution.py:450
  193.6 4.1 %expert_down.3.refs_4_ = bf16[4,256,512]{2,1,0:T(8,128)(2,1)S(1)} custom-call(s32[4]{0:T(128)S(1)} %get-tuple-element.345.facts, bf16[256,768]{1,0:T(8,128)(2,1)S(1)} %expert_hidden.1.rows, bf16[1,768,4096]{2,1,0:T(8,128)(2,1)} %weight.3), custom_call_target="tpu_custom_call" | custom-call | tf_op jit(solution)/shard_map/expert_down/pallas_call | solution.py:450
  197.7 1.8 learner_parts.1
  201.3 6.0 %collective-permute-done.28.refs_5_ = bf16[4,256,512]{2,1,0:T(8,128)(2,1)} collective-permute-done((bf16[4,256,512]{2,1,0:T(8,128)(2,1)}, bf16[4,256,512]{2,1,0:T(8,128)(2,1)}, u32[]{:S(2)}, u32[]{:S(2)}) %collective-permute-start.28) | collective-permute-done | bytes 1048608 | tf_op jit(solution)/shard_map/ppermute | solution.py:53
  207.4 2.3 final_hidden.1
  210.9 3.7 %collective-permute-done.29 = f32[128,128]{1,0:T(8,128)S(1)} collective-permute-done((f32[128,128]{1,0:T(8,128)S(1)}, f32[128,128]{1,0:T(8,128)S(1)}, u32[]{:S(2)}, u32[]{:S(2)}) %collective-permute-start.29) | collective-permute-done | bytes 65568 | tf_op jit(solution)/shard_map/ppermute | solution.py:53
  214.6 1.7 collective-permute-done.30.refs_1_
  217.9 1.8 logits.5
  219.8 8.7 %collective-permute-done.32 = f32[128,768]{1,0:T(8,128)S(1)} collective-permute-done((f32[128,768]{1,0:T(8,128)S(1)}, f32[128,768]{1,0:T(8,128)S(1)}, u32[]{:S(2)}, u32[]{:S(2)}) %collective-permute-start.32) | collective-permute-done | bytes 393248 | tf_op jit(solution)/shard_map/ppermute | solution.py:53
  232.5 1.6 collective-permute-start.37
  234.1 2.7 collective-permute-start.38
  236.8 2.8 copy-done.2
  239.6 1.6 logits.7
  241.1 1.6 logits.6
  244.2 1.6 collective-permute-start.40
  245.8 2.7 collective-permute-start.41
  250.7 2.3 collective-permute-done.40
  253.7 1.9 collective-permute-done.42.other
  255.6 9.6 %collective-permute-done.34 = f32[128,1536]{1,0:T(8,128)S(1)} collective-permute-done((f32[128,1536]{1,0:T(8,128)S(1)}, f32[128,1536]{1,0:T(8,128)S(1)}, u32[]{:S(2)}, u32[]{:S(2)}) %collective-permute-start.34) | collective-permute-done | bytes 786464 | tf_op jit(solution)/shard_map/ppermute | solution.py:53
  268.5 6.7 %collective-permute-done.43.rows = bf16[128,1536]{1,0:T(8,128)(2,1)S(1)} collective-permute-done((bf16[128,1536]{1,0:T(8,128)(2,1)S(1)}, bf16[128,1536]{1,0:T(8,128)(2,1)S(1)}, u32[]{:S(2)}, u32[]{:S(2)}) %collective-permute-start.43) | collective-permute-done | bytes 393248 | tf_op jit(solution)/shard_map/ppermute | solution.py:53
  275.2 1.6 collective-permute-done.44
  278.6 4.0 %collective-permute-done.45 = bf16[64,1536]{1,0:T(8,128)(2,1)S(1)} collective-permute-done((bf16[64,1536]{1,0:T(8,128)(2,1)S(1)}, bf16[64,1536]{1,0:T(8,128)(2,1)S(1)}, u32[]{:S(2)}, u32[]{:S(2)}) %collective-permute-start.45) | collective-permute-done | bytes 196640 | tf_op jit(solution)/shard_map/ppermute | solution.py:53
  283.4 3.4 %collective-permute-done.47.core = bf16[512,1536]{1,0:T(8,128)(2,1)S(1)} collective-permute-done((bf16[512,1536]{1,0:T(8,128)(2,1)S(1)}, bf16[512,1536]{1,0:T(8,128)(2,1)S(1)}, u32[]{:S(2)}, u32[]{:S(2)}) %collective-permute-start.47) | collective-permute-done | bytes 1572896 | tf_op jit(solution)/shard_map/ppermute | solution.py:57
  286.8 4.3 %head_parts.1 = (bf16[2,384,256]{2,1,0:T(8,128)(2,1)}, bf16[2,384,256]{2,1,0:T(8,128)(2,1)}, bf16[2,384,256]{2,1,0:T(8,128)(2,1)S(1)}, bf16[2,384,256]{2,1,0:T(8,128)(2,1)S(1)}) custom-call(s32[4]{0:T(128)S(1)} %broadcast_xor_fusion.facts, bf16[512,1536]{1,0:T(8,128)(2,1)S(1)} %constant_dynamic-update-slice_fusion.2.mine, ...), custom_call_target="tpu_custom_call" | custom-call | tf_op jit(solution)/shard_map/head_parts/pallas_call | solution.py:351
  291.9 2.0 collective-permute-start.49
  293.9 2.8 copy-done.3
  296.7 2.0 hidden_grad.2
  300.2 2.0 hidden_grad.3
  302.3 1.8 collective-permute-done.50
  304.9 10.4 %collective-permute-done.49 = bf16[2,384,256]{2,1,0:T(8,128)(2,1)S(1)} collective-permute-done((bf16[2,384,256]{2,1,0:T(8,128)(2,1)}, bf16[2,384,256]{2,1,0:T(8,128)(2,1)S(1)}, u32[]{:S(2)}, u32[]{:S(2)}) %collective-permute-start.49) | collective-permute-done | bytes 393248 | tf_op jit(solution)/shard_map/ppermute | solution.py:61
  319.7 7.0 %collective-permute-done.52 = bf16[384,256]{1,0:T(8,128)(2,1)} collective-permute-done((bf16[384,256]{1,0:T(8,128)(2,1)}, bf16[384,256]{1,0:T(8,128)(2,1)}, u32[]{:S(2)}, u32[]{:S(2)}) %collective-permute-start.52) | collective-permute-done | bytes 196640 | tf_op jit(solution)/shard_map/ppermute | solution.py:61
  (266 shorter events, 56.7 us)
Async XLA Ops:
  7.2 229.6 %all-gather.3.cloned.1.call-start = ((), (), s32[]{:S(2)}) async-start(), calls=%async_computation | async-start | bytes 6684672 | tf_op jit(solution)/shard_map/all_gather | solution.py:676
  11.8 8.6 %collective-permute-start = (f32[1,2,128]{2,1,0:T(2,128)}, f32[1,2,128]{2,1,0:T(2,128)}, u32[]{:S(2)}, u32[]{:S(2)}) collective-permute-start(f32[1,2,128]{2,1,0:T(2,128)} %maximum_bitcast_fusion), channel_id=1, source_target_pairs={{0,4},{4,0},{8,12},{12,8},{1,5},{5,1},{9,13},{13,9},{2,6},{6,2},{1... | collective-permute-start | bytes 3080 | tf_op jit(solution)/shard_map/ppermute | solution.py:61
  14.8 7.1 %collective-permute-start.1 = (f32[1,2,128]{2,1,0:T(2,128)}, f32[1,2,128]{2,1,0:T(2,128)}, u32[]{:S(2)}, u32[]{:S(2)}) collective-permute-start(f32[1,2,128]{2,1,0:T(2,128)} %maximum_bitcast_fusion), channel_id=1, source_target_pairs={{0,8},{4,12},{8,0},{12,4},{1,9},{5,13},{9,1},{13,5},{2,10},{6,14},... | collective-permute-start | bytes 3080 | tf_op jit(solution)/shard_map/ppermute | solution.py:61
  17.4 5.7 %collective-permute-start.2 = (f32[1,2,128]{2,1,0:T(2,128)}, f32[1,2,128]{2,1,0:T(2,128)}, u32[]{:S(2)}, u32[]{:S(2)}) collective-permute-start(f32[1,2,128]{2,1,0:T(2,128)} %maximum_bitcast_fusion), channel_id=1, source_target_pairs={{0,12},{4,8},{8,4},{12,0},{1,13},{5,9},{9,5},{13,1},{2,14},{6,10},... | collective-permute-start | bytes 3080 | tf_op jit(solution)/shard_map/ppermute | solution.py:61
  17.4 11.9 %collective-permute-start.4 = (bf16[2,2,256,128]{3,2,1,0:T(8,128)(2,1)}, bf16[2,2,256,128]{3,2,1,0:T(8,128)(2,1)}, u32[]{:S(2)}, u32[]{:S(2)}) collective-permute-start(bf16[2,2,256,128]{3,2,1,0:T(8,128)(2,1)} %constant_dynamic-slice_fusion.13), channel_id=1, source_target_pairs={{0,16},{16,0},{1,17},{17,1},{2,18},{18,2},{3,19},{19,3},{4,20},{20... | collective-permute-start | bytes 786440 | tf_op jit(solution)/shard_map/ppermute | solution.py:53
  19.1 12.4 %collective-permute-start.5 = (bf16[2048,512]{1,0:T(8,128)(2,1)}, bf16[2048,512]{1,0:T(8,128)(2,1)}, u32[]{:S(2)}, u32[]{:S(2)}) collective-permute-start(bf16[2048,512]{1,0:T(8,128)(2,1)} %refs_3_.3), channel_id=1, source_target_pairs={{0,1},{1,0},{2,3},{3,2},{4,5},{5,4},{6,7},{7,6},{8,9},{9,8},{10,11... | collective-permute-start | bytes 6291464 | tf_op jit(solution)/shard_map/ppermute | solution.py:57
  20.4 57.0 %collective-permute-start.13 = (bf16[2048,512]{1,0:T(8,128)(2,1)}, bf16[2048,512]{1,0:T(8,128)(2,1)}, u32[]{:S(2)}, u32[]{:S(2)}) collective-permute-start(bf16[2048,512]{1,0:T(8,128)(2,1)} %refs_3_.3), channel_id=1, source_target_pairs={{0,2},{1,3},{2,0},{3,1},{4,6},{5,7},{6,4},{7,5},{8,10},{9,11},{10,... | collective-permute-start | bytes 6291464 | tf_op jit(solution)/shard_map/ppermute | solution.py:57
  22.0 30.8 %collective-permute-start.7 = (bf16[1,384,512]{2,1,0:T(8,128)(2,1)S(1)}, bf16[1,384,512]{2,1,0:T(8,128)(2,1)}, u32[]{:S(2)}, u32[]{:S(2)}) collective-permute-start(bf16[1,384,512]{2,1,0:T(8,128)(2,1)S(1)} %dynamic-slice_bitcast_fusion), channel_id=1, source_target_pairs={{0,4},{4,0},{8,12},{12,8},{1,5},{5,1},{9,13},{13,9},{2,6},{6,2},{1... | collective-permute-start | bytes 1179656 | tf_op jit(solution)/shard_map/ppermute | solution.py:61
  23.8 3.7 %collective-permute-start.3 = (f32[4,2,128]{2,1,0:T(2,128)S(1)}, f32[4,2,128]{2,1,0:T(2,128)S(1)}, u32[]{:S(2)}, u32[]{:S(2)}) collective-permute-start(f32[4,2,128]{2,1,0:T(2,128)S(1)} %pad_maximum_fusion.11), channel_id=1, source_target_pairs={{0,16},{16,0},{1,17},{17,1},{2,18},{18,2},{3,19},{19,3},{4,20},{20... | collective-permute-start | bytes 12296 | tf_op jit(solution)/shard_map/ppermute | solution.py:53
  27.5 17.5 %collective-permute-start.6 = (bf16[4,128,512]{2,1,0:T(8,128)(2,1)S(1)}, bf16[4,128,512]{2,1,0:T(8,128)(2,1)S(1)}, u32[]{:S(2)}, u32[]{:S(2)}) collective-permute-start(bf16[4,128,512]{2,1,0:T(8,128)(2,1)S(1)} %pad_maximum_fusion.4), channel_id=1, source_target_pairs={{0,16},{16,0},{1,17},{17,1},{2,18},{18,2},{3,19},{19,3},{4,20},{20... | collective-permute-start | bytes 1572872 | tf_op jit(solution)/shard_map/ppermute | solution.py:53
  29.4 29.9 %collective-permute-start.8 = (bf16[1,384,512]{2,1,0:T(8,128)(2,1)S(1)}, bf16[1,384,512]{2,1,0:T(8,128)(2,1)S(1)}, u32[]{:S(2)}, u32[]{:S(2)}) collective-permute-start(bf16[1,384,512]{2,1,0:T(8,128)(2,1)S(1)} %dynamic-slice_bitcast_fusion), channel_id=1, source_target_pairs={{0,8},{4,12},{8,0},{12,4},{1,9},{5,13},{9,1},{13,5},{2,10},{6,14},... | collective-permute-start | bytes 1179656 | tf_op jit(solution)/shard_map/ppermute | solution.py:61
  31.5 27.7 %collective-permute-start.9 = (bf16[1,384,512]{2,1,0:T(8,128)(2,1)S(1)}, bf16[1,384,512]{2,1,0:T(8,128)(2,1)S(1)}, u32[]{:S(2)}, u32[]{:S(2)}) collective-permute-start(bf16[1,384,512]{2,1,0:T(8,128)(2,1)S(1)} %dynamic-slice_bitcast_fusion), channel_id=1, source_target_pairs={{0,12},{4,8},{8,4},{12,0},{1,13},{5,9},{9,5},{13,1},{2,14},{6,10},... | collective-permute-start | bytes 1179656 | tf_op jit(solution)/shard_map/ppermute | solution.py:61
  47.0 23.9 %collective-permute-start.11 = (bf16[256,2048]{1,0:T(8,128)(2,1)S(1)}, bf16[256,2048]{1,0:T(8,128)(2,1)S(1)}, u32[]{:S(2)}, u32[]{:S(2)}) collective-permute-start(bf16[256,2048]{1,0:T(8,128)(2,1)S(1)} %get-tuple-element.160.refs_0_), channel_id=1, source_target_pairs={{0,16},{16,0},{1,17},{17,1},{2,18},{18,2},{3,19},{19,3},{4,20},{20... | collective-permute-start | bytes 3145736 | tf_op jit(solution)/shard_map/ppermute | solution.py:53
  60.6 25.3 %copy-start.5 = (bf16[4,384,512]{2,1,0:T(8,128)(2,1)}, bf16[4,384,512]{2,1,0:T(8,128)(2,1)S(1)}, u32[]{:S(2)}) copy-start(bf16[4,384,512]{2,1,0:T(8,128)(2,1)S(1)} %pad_maximum_fusion.refs_0_) | copy-start | bytes 4718596
  60.6 16.7 %collective-permute-start.10 = (bf16[2,256,512]{2,1,0:T(8,128)(2,1)S(1)}, bf16[2,256,512]{2,1,0:T(8,128)(2,1)S(1)}, u32[]{:S(2)}, u32[]{:S(2)}) collective-permute-start(bf16[2,256,512]{2,1,0:T(8,128)(2,1)S(1)} %get-tuple-element.154), channel_id=1, source_target_pairs={{0,4},{4,0},{8,12},{12,8},{1,5},{5,1},{9,13},{13,9},{2,6},{6,2},{1... | collective-permute-start | bytes 1572872 | tf_op jit(solution)/shard_map/ppermute | solution.py:61
  77.4 4.4 %collective-permute-start.14 = (bf16[2048,512]{1,0:T(8,128)(2,1)}, bf16[2048,512]{1,0:T(8,128)(2,1)S(1)}, u32[]{:S(2)}, u32[]{:S(2)}) collective-permute-start(bf16[2048,512]{1,0:T(8,128)(2,1)} %collective-permute-done.13.refs_5_.refs_3_), channel_id=1, source_target_pairs={{0,1},{1,0},{2,3},{3,2},{4,5},{5,4},{6,7},{7,6},{8,9},{9,8},{10,11... | collective-permute-start | bytes 6291464 | tf_op jit(solution)/shard_map/ppermute | solution.py:57
  77.5 36.8 %collective-permute-start.18 = (bf16[4,384,512]{2,1,0:T(8,128)(2,1)S(1)}, bf16[4,384,512]{2,1,0:T(8,128)(2,1)S(1)}, u32[]{:S(2)}, u32[]{:S(2)}) collective-permute-start(bf16[4,384,512]{2,1,0:T(8,128)(2,1)S(1)} %pad_maximum_fusion.refs_0_), channel_id=1, source_target_pairs={{0,2},{1,3},{2,0},{3,1},{4,6},{5,7},{6,4},{7,5},{8,10},{9,11},{10,... | collective-permute-start | bytes 4718600 | tf_op jit(solution)/shard_map/ppermute | solution.py:57
  77.6 16.1 %collective-permute-start.12 = (bf16[2,128,512]{2,1,0:T(8,128)(2,1)S(1)}, bf16[2,128,512]{2,1,0:T(8,128)(2,1)S(1)}, u32[]{:S(2)}, u32[]{:S(2)}) collective-permute-start(bf16[2,128,512]{2,1,0:T(8,128)(2,1)S(1)} %add_convert_fusion.3), channel_id=1, source_target_pairs={{0,8},{4,12},{8,0},{12,4},{1,9},{5,13},{9,1},{13,5},{2,10},{6,14},... | collective-permute-start | bytes 786440 | tf_op jit(solution)/shard_map/ppermute | solution.py:61
  93.7 27.8 %collective-permute-start.17 = (bf16[256,2048]{1,0:T(8,128)(2,1)S(1)}, bf16[256,2048]{1,0:T(8,128)(2,1)S(1)}, u32[]{:S(2)}, u32[]{:S(2)}) collective-permute-start(bf16[256,2048]{1,0:T(8,128)(2,1)S(1)} %get-tuple-element.168.refs_1_), channel_id=1, source_target_pairs={{0,16},{16,0},{1,17},{17,1},{2,18},{18,2},{3,19},{19,3},{4,20},{20... | collective-permute-start | bytes 3145736 | tf_op jit(solution)/shard_map/ppermute | solution.py:53
  95.4 18.9 %collective-permute-start.16 = (bf16[2,256,512]{2,1,0:T(8,128)(2,1)S(1)}, bf16[2,256,512]{2,1,0:T(8,128)(2,1)S(1)}, u32[]{:S(2)}, u32[]{:S(2)}) collective-permute-start(bf16[2,256,512]{2,1,0:T(8,128)(2,1)S(1)} %project.8), channel_id=1, source_target_pairs={{0,4},{4,0},{8,12},{12,8},{1,5},{5,1},{9,13},{13,9},{2,6},{6,2},{1... | collective-permute-start | bytes 1572872 | tf_op jit(solution)/shard_map/ppermute | solution.py:61
  95.4 26.1 %collective-permute-start.15 = (bf16[2,256,512]{2,1,0:T(8,128)(2,1)S(1)}, bf16[2,256,512]{2,1,0:T(8,128)(2,1)S(1)}, u32[]{:S(2)}, u32[]{:S(2)}) collective-permute-start(bf16[2,256,512]{2,1,0:T(8,128)(2,1)S(1)} %get-tuple-element.167), channel_id=1, source_target_pairs={{0,4},{4,0},{8,12},{12,8},{1,5},{5,1},{9,13},{13,9},{2,6},{6,2},{1... | collective-permute-start | bytes 1572872 | tf_op jit(solution)/shard_map/ppermute | solution.py:61
  100.2 39.1 %collective-permute-start.19 = (bf16[2,256,512]{2,1,0:T(8,128)(2,1)S(1)}, bf16[2,256,512]{2,1,0:T(8,128)(2,1)S(1)}, u32[]{:S(2)}, u32[]{:S(2)}) collective-permute-start(bf16[2,256,512]{2,1,0:T(8,128)(2,1)S(1)} %project.9), channel_id=1, source_target_pairs={{0,4},{4,0},{8,12},{12,8},{1,5},{5,1},{9,13},{13,9},{2,6},{6,2},{1... | collective-permute-start | bytes 1572872 | tf_op jit(solution)/shard_map/ppermute | solution.py:61
  121.6 17.8 %collective-permute-start.20 = (bf16[2,128,512]{2,1,0:T(8,128)(2,1)S(1)}, bf16[2,128,512]{2,1,0:T(8,128)(2,1)S(1)}, u32[]{:S(2)}, u32[]{:S(2)}) collective-permute-start(bf16[2,128,512]{2,1,0:T(8,128)(2,1)S(1)} %add_convert_fusion.2), channel_id=1, source_target_pairs={{0,8},{4,12},{8,0},{12,4},{1,9},{5,13},{9,1},{13,5},{2,10},{6,14},... | collective-permute-start | bytes 786440 | tf_op jit(solution)/shard_map/ppermute | solution.py:61
  126.4 19.4 %collective-permute-start.21 = (bf16[2,128,512]{2,1,0:T(8,128)(2,1)S(1)}, bf16[2,128,512]{2,1,0:T(8,128)(2,1)S(1)}, u32[]{:S(2)}, u32[]{:S(2)}) collective-permute-start(bf16[2,128,512]{2,1,0:T(8,128)(2,1)S(1)} %add_convert_fusion.1), channel_id=1, source_target_pairs={{0,8},{4,12},{8,0},{12,4},{1,9},{5,13},{9,1},{13,5},{2,10},{6,14},... | collective-permute-start | bytes 786440 | tf_op jit(solution)/shard_map/ppermute | solution.py:61
  131.3 21.4 %copy-start.33 = (bf16[2,128,512]{2,1,0:T(8,128)(2,1)}, bf16[2,128,512]{2,1,0:T(8,128)(2,1)S(1)}, u32[]{:S(2)}) copy-start(bf16[2,128,512]{2,1,0:T(8,128)(2,1)S(1)} %get-tuple-element.185) | copy-start | bytes 786436
  131.3 21.4 %copy-start.34 = (bf16[2,128,512]{2,1,0:T(8,128)(2,1)}, bf16[2,128,512]{2,1,0:T(8,128)(2,1)S(1)}, u32[]{:S(2)}) copy-start(bf16[2,128,512]{2,1,0:T(8,128)(2,1)S(1)} %get-tuple-element.178) | copy-start | bytes 786436
  139.5 36.8 %copy-start.11 = (f32[2,128,512]{2,1,0:T(8,128)}, f32[2,128,512]{2,1,0:T(8,128)S(1)}, u32[]{:S(2)}) copy-start(f32[2,128,512]{2,1,0:T(8,128)S(1)} %get-tuple-element.278.refs_1_) | copy-start | bytes 1572868
  139.5 9.3 %collective-permute-start.22 = (bf16[2,128,512]{2,1,0:T(8,128)(2,1)S(1)}, bf16[2,128,512]{2,1,0:T(8,128)(2,1)S(1)}, u32[]{:S(2)}, u32[]{:S(2)}) collective-permute-start(bf16[2,128,512]{2,1,0:T(8,128)(2,1)S(1)} %get-tuple-element.181), channel_id=1, source_target_pairs={{0,16},{16,0},{1,17},{17,1},{2,18},{18,2},{3,19},{19,3},{4,20},{20... | collective-permute-start | bytes 786440 | tf_op jit(solution)/shard_map/ppermute | solution.py:53
  140.1 11.9 %collective-permute-start.23 = (bf16[2,128,512]{2,1,0:T(8,128)(2,1)S(1)}, bf16[2,128,512]{2,1,0:T(8,128)(2,1)S(1)}, u32[]{:S(2)}, u32[]{:S(2)}) collective-permute-start(bf16[2,128,512]{2,1,0:T(8,128)(2,1)S(1)} %get-tuple-element.182), channel_id=1, source_target_pairs={{0,16},{16,0},{1,17},{17,1},{2,18},{18,2},{3,19},{19,3},{4,20},{20... | collective-permute-start | bytes 786440 | tf_op jit(solution)/shard_map/ppermute | solution.py:53
  153.5 22.7 %copy-start.13 = (f32[2,128,512]{2,1,0:T(8,128)}, f32[2,128,512]{2,1,0:T(8,128)S(1)}, u32[]{:S(2)}) copy-start(f32[2,128,512]{2,1,0:T(8,128)S(1)} %get-tuple-element.276.refs_2_) | copy-start | bytes 1572868
  153.5 21.9 %copy-start.19 = (bf16[2,64,4096]{2,1,0:T(8,128)(2,1)S(1)}, bf16[2,64,4096]{2,1,0:T(8,128)(2,1)}, u32[]{:S(2)}) copy-start(bf16[2,64,4096]{2,1,0:T(8,128)(2,1)} %param.28) | copy-start | bytes 3145732
  154.8 10.1 %collective-permute-start.24 = (bf16[2,128,512]{2,1,0:T(8,128)(2,1)S(1)}, bf16[2,128,512]{2,1,0:T(8,128)(2,1)S(1)}, u32[]{:S(2)}, u32[]{:S(2)}) collective-permute-start(bf16[2,128,512]{2,1,0:T(8,128)(2,1)S(1)} %add_convert_fusion), channel_id=1, source_target_pairs={{0,8},{4,12},{8,0},{12,4},{1,9},{5,13},{9,1},{13,5},{2,10},{6,14},... | collective-permute-start | bytes 786440 | tf_op jit(solution)/shard_map/ppermute | solution.py:61
  154.9 21.3 %copy-start.9 = (f32[2,128,512]{2,1,0:T(8,128)S(1)}, f32[2,128,512]{2,1,0:T(8,128)}, u32[]{:S(2)}) copy-start(f32[2,128,512]{2,1,0:T(8,128)} %get-tuple-element.280.refs_0_) | copy-start | bytes 1572868
  154.9 21.3 %copy-start.32 = (bf16[2,128,512]{2,1,0:T(8,128)(2,1)S(1)}, bf16[2,128,512]{2,1,0:T(8,128)(2,1)}, u32[]{:S(2)}) copy-start(bf16[2,128,512]{2,1,0:T(8,128)(2,1)} %copy-done.31) | copy-start | bytes 786436
  154.9 21.3 %copy-start.35 = (f32[4096]{0:T(1024)S(1)}, f32[4096]{0:T(1024)}, u32[]{:S(2)}) copy-start(f32[4096]{0:T(1024)} %param.20) | copy-start | bytes 49156
  155.0 10.0 %collective-permute-start.25 = (bf16[2,128,512]{2,1,0:T(8,128)(2,1)}, bf16[2,128,512]{2,1,0:T(8,128)(2,1)S(1)}, u32[]{:S(2)}, u32[]{:S(2)}) collective-permute-start(bf16[2,128,512]{2,1,0:T(8,128)(2,1)} %get-tuple-element.275), channel_id=1, source_target_pairs={{0,16},{16,0},{1,17},{17,1},{2,18},{18,2},{3,19},{19,3},{4,20},{20... | collective-permute-start | bytes 786440 | tf_op jit(solution)/shard_map/ppermute | solution.py:53
  166.1 9.3 %collective-permute-start.26 = (bf16[2,128,512]{2,1,0:T(8,128)(2,1)S(1)}, bf16[2,128,512]{2,1,0:T(8,128)(2,1)S(1)}, u32[]{:S(2)}, u32[]{:S(2)}) collective-permute-start(bf16[2,128,512]{2,1,0:T(8,128)(2,1)S(1)} %get-tuple-element.273), channel_id=1, source_target_pairs={{0,16},{16,0},{1,17},{17,1},{2,18},{18,2},{3,19},{19,3},{4,20},{20... | collective-permute-start | bytes 786440 | tf_op jit(solution)/shard_map/ppermute | solution.py:53
  175.6 14.4 %collective-permute-start.27 = (bf16[128,2048]{1,0:T(8,128)(2,1)S(1)}, bf16[128,2048]{1,0:T(8,128)(2,1)S(1)}, u32[]{:S(2)}, u32[]{:S(2)}) collective-permute-start(bf16[128,2048]{1,0:T(8,128)(2,1)S(1)} %pad_maximum_fusion.5), channel_id=1, source_target_pairs={{0,16},{16,0},{1,17},{17,1},{2,18},{18,2},{3,19},{19,3},{4,20},{20... | collective-permute-start | bytes 1572872 | tf_op jit(solution)/shard_map/ppermute | solution.py:53
  190.7 16.7 %collective-permute-start.28 = (bf16[4,256,512]{2,1,0:T(8,128)(2,1)}, bf16[4,256,512]{2,1,0:T(8,128)(2,1)}, u32[]{:S(2)}, u32[]{:S(2)}) collective-permute-start(bf16[4,256,512]{2,1,0:T(8,128)(2,1)} %expert_down.2), channel_id=1, source_target_pairs={{0,16},{16,0},{1,17},{17,1},{2,18},{18,2},{3,19},{19,3},{4,20},{20... | collective-permute-start | bytes 3145736 | tf_op jit(solution)/shard_map/ppermute | solution.py:53
  209.7 4.9 %collective-permute-start.31 = (bf16[4,384,512]{2,1,0:T(8,128)(2,1)S(1)}, bf16[4,384,512]{2,1,0:T(8,128)(2,1)S(1)}, u32[]{:S(2)}, u32[]{:S(2)}) collective-permute-start(bf16[4,384,512]{2,1,0:T(8,128)(2,1)S(1)} %copy-done.8), channel_id=1, source_target_pairs={{0,1},{1,0},{2,3},{3,2},{4,5},{5,4},{6,7},{7,6},{8,9},{9,8},{10,11... | collective-permute-start | bytes 4718600 | tf_op jit(solution)/shard_map/ppermute | solution.py:57
  209.8 6.5 %collective-permute-start.30 = (bf16[4,384,512]{2,1,0:T(8,128)(2,1)S(1)}, bf16[4,384,512]{2,1,0:T(8,128)(2,1)S(1)}, u32[]{:S(2)}, u32[]{:S(2)}) collective-permute-start(bf16[4,384,512]{2,1,0:T(8,128)(2,1)S(1)} %copy-done.6), channel_id=1, source_target_pairs={{0,1},{1,0},{2,3},{3,2},{4,5},{5,4},{6,7},{7,6},{8,9},{9,8},{10,11... | collective-permute-start | bytes 4718600 | tf_op jit(solution)/shard_map/ppermute | solution.py:57
  210.3 4.3 %collective-permute-start.29 = (f32[128,128]{1,0:T(8,128)S(1)}, f32[128,128]{1,0:T(8,128)S(1)}, u32[]{:S(2)}, u32[]{:S(2)}) collective-permute-start(f32[128,128]{1,0:T(8,128)S(1)} %slice.121), channel_id=1, source_target_pairs={{0,16},{16,0},{1,17},{17,1},{2,18},{18,2},{3,19},{19,3},{4,20},{20... | collective-permute-start | bytes 196616 | tf_op jit(solution)/shard_map/ppermute | solution.py:53
  217.3 11.2 %collective-permute-start.32 = (f32[128,768]{1,0:T(8,128)S(1)}, f32[128,768]{1,0:T(8,128)S(1)}, u32[]{:S(2)}, u32[]{:S(2)}) collective-permute-start(f32[128,768]{1,0:T(8,128)S(1)} %get-tuple-element.212), channel_id=1, source_target_pairs={{0,16},{16,0},{1,17},{17,1},{2,18},{18,2},{3,19},{19,3},{4,20},{20... | collective-permute-start | bytes 1179656 | tf_op jit(solution)/shard_map/ppermute | solution.py:53
  228.6 14.2 %collective-permute-start.33 = (f32[128,768]{1,0:T(8,128)}, f32[128,768]{1,0:T(8,128)}, u32[]{:S(2)}, u32[]{:S(2)}) collective-permute-start(f32[128,768]{1,0:T(8,128)} %get-tuple-element.223), channel_id=1, source_target_pairs={{0,16},{16,0},{1,17},{17,1},{2,18},{18,2},{3,19},{19,3},{4,20},{20... | collective-permute-start | bytes 1179656 | tf_op jit(solution)/shard_map/ppermute | solution.py:53
  229.3 24.2 %collective-permute-start.35 = (bf16[2,256,512]{2,1,0:T(8,128)(2,1)}, bf16[2,256,512]{2,1,0:T(8,128)(2,1)S(1)}, u32[]{:S(2)}, u32[]{:S(2)}) collective-permute-start(bf16[2,256,512]{2,1,0:T(8,128)(2,1)} %copy-done.36), channel_id=1, source_target_pairs={{0,2},{1,3},{2,0},{3,1},{4,6},{5,7},{6,4},{7,5},{8,10},{9,11},{10,... | collective-permute-start | bytes 1572872 | tf_op jit(solution)/shard_map/ppermute | solution.py:57
  232.4 11.5 %collective-permute-start.36 = (f32[32,768]{1,0:T(8,128)}, f32[32,768]{1,0:T(8,128)}, u32[]{:S(2)}, u32[]{:S(2)}) collective-permute-start(f32[32,768]{1,0:T(8,128)} %get-tuple-element.315), channel_id=1, source_target_pairs={{0,4},{4,0},{8,12},{12,8},{1,5},{5,1},{9,13},{13,9},{2,6},{6,2},{1... | collective-permute-start | bytes 294920 | tf_op jit(solution)/shard_map/ppermute | solution.py:61
  232.5 11.4 %collective-permute-start.37 = (f32[32,768]{1,0:T(8,128)}, f32[32,768]{1,0:T(8,128)}, u32[]{:S(2)}, u32[]{:S(2)}) collective-permute-start(f32[32,768]{1,0:T(8,128)} %get-tuple-element.314), channel_id=1, source_target_pairs={{0,8},{4,12},{8,0},{12,4},{1,9},{5,13},{9,1},{13,5},{2,10},{6,14},... | collective-permute-start | bytes 294920 | tf_op jit(solution)/shard_map/ppermute | solution.py:61
  234.1 9.8 %collective-permute-start.38 = (f32[32,768]{1,0:T(8,128)S(1)}, f32[32,768]{1,0:T(8,128)}, u32[]{:S(2)}, u32[]{:S(2)}) collective-permute-start(f32[32,768]{1,0:T(8,128)S(1)} %get-tuple-element.313), channel_id=1, source_target_pairs={{0,12},{4,8},{8,4},{12,0},{1,13},{5,9},{9,5},{13,1},{2,14},{6,10},... | collective-permute-start | bytes 294920 | tf_op jit(solution)/shard_map/ppermute | solution.py:61
  244.0 6.7 %collective-permute-start.39 = (f32[32,768]{1,0:T(8,128)S(1)}, f32[32,768]{1,0:T(8,128)S(1)}, u32[]{:S(2)}, u32[]{:S(2)}) collective-permute-start(f32[32,768]{1,0:T(8,128)S(1)} %get-tuple-element.307), channel_id=1, source_target_pairs={{0,4},{4,0},{8,12},{12,8},{1,5},{5,1},{9,13},{13,9},{2,6},{6,2},{1... | collective-permute-start | bytes 294920 | tf_op jit(solution)/shard_map/ppermute | solution.py:61
  244.2 8.9 %collective-permute-start.40 = (f32[32,768]{1,0:T(8,128)S(1)}, f32[32,768]{1,0:T(8,128)S(1)}, u32[]{:S(2)}, u32[]{:S(2)}) collective-permute-start(f32[32,768]{1,0:T(8,128)S(1)} %get-tuple-element.306), channel_id=1, source_target_pairs={{0,8},{4,12},{8,0},{12,4},{1,9},{5,13},{9,1},{13,5},{2,10},{6,14},... | collective-permute-start | bytes 294920 | tf_op jit(solution)/shard_map/ppermute | solution.py:61
  245.8 7.3 %collective-permute-start.41 = (f32[32,768]{1,0:T(8,128)S(1)}, f32[32,768]{1,0:T(8,128)S(1)}, u32[]{:S(2)}, u32[]{:S(2)}) collective-permute-start(f32[32,768]{1,0:T(8,128)S(1)} %get-tuple-element.305), channel_id=1, source_target_pairs={{0,12},{4,8},{8,4},{12,0},{1,13},{5,9},{9,5},{13,1},{2,14},{6,10},... | collective-permute-start | bytes 294920 | tf_op jit(solution)/shard_map/ppermute | solution.py:61
  248.6 16.7 %collective-permute-start.34 = (f32[128,1536]{1,0:T(8,128)S(1)}, f32[128,1536]{1,0:T(8,128)S(1)}, u32[]{:S(2)}, u32[]{:S(2)}) collective-permute-start(f32[128,1536]{1,0:T(8,128)S(1)} %pad_maximum_fusion.2), channel_id=1, source_target_pairs={{0,16},{16,0},{1,17},{17,1},{2,18},{18,2},{3,19},{19,3},{4,20},{20... | collective-permute-start | bytes 2359304 | tf_op jit(solution)/shard_map/ppermute | solution.py:53
  253.6 2.0 collective-permute-start.42
  266.5 20.4 %copy-start.23 = (bf16[2,256,512]{2,1,0:T(8,128)(2,1)S(1)}, bf16[2,256,512]{2,1,0:T(8,128)(2,1)}, u32[]{:S(2)}) copy-start(bf16[2,256,512]{2,1,0:T(8,128)(2,1)} %copy-done.22) | copy-start | bytes 1572868
  266.5 8.8 %collective-permute-start.43 = (bf16[128,1536]{1,0:T(8,128)(2,1)S(1)}, bf16[128,1536]{1,0:T(8,128)(2,1)S(1)}, u32[]{:S(2)}, u32[]{:S(2)}) collective-permute-start(bf16[128,1536]{1,0:T(8,128)(2,1)S(1)} %get-tuple-element.251.rows), channel_id=1, source_target_pairs={{0,16},{16,0},{1,17},{17,1},{2,18},{18,2},{3,19},{19,3},{4,20},{20... | collective-permute-start | bytes 1179656 | tf_op jit(solution)/shard_map/ppermute | solution.py:53
  267.7 9.2 %collective-permute-start.44 = (bf16[128,1536]{1,0:T(8,128)(2,1)S(1)}, bf16[128,1536]{1,0:T(8,128)(2,1)S(1)}, u32[]{:S(2)}, u32[]{:S(2)}) collective-permute-start(bf16[128,1536]{1,0:T(8,128)(2,1)S(1)} %get-tuple-element.251.rows), channel_id=1, source_target_pairs={{0,2},{1,3},{2,0},{3,1},{4,6},{5,7},{6,4},{7,5},{8,10},{9,11},{10,... | collective-permute-start | bytes 1179656 | tf_op jit(solution)/shard_map/ppermute | solution.py:57
  276.9 5.7 %collective-permute-start.45 = (bf16[64,1536]{1,0:T(8,128)(2,1)S(1)}, bf16[64,1536]{1,0:T(8,128)(2,1)S(1)}, u32[]{:S(2)}, u32[]{:S(2)}) collective-permute-start(bf16[64,1536]{1,0:T(8,128)(2,1)S(1)} %slice.126), channel_id=1, source_target_pairs={{0,16},{16,0},{1,17},{17,1},{2,18},{18,2},{3,19},{19,3},{4,20},{20... | collective-permute-start | bytes 589832 | tf_op jit(solution)/shard_map/ppermute | solution.py:53
  277.6 5.7 %collective-permute-start.46 = (bf16[64,1536]{1,0:T(8,128)(2,1)S(1)}, bf16[64,1536]{1,0:T(8,128)(2,1)S(1)}, u32[]{:S(2)}, u32[]{:S(2)}) collective-permute-start(bf16[64,1536]{1,0:T(8,128)(2,1)S(1)} %slice.127), channel_id=1, source_target_pairs={{0,2},{1,3},{2,0},{3,1},{4,6},{5,7},{6,4},{7,5},{8,10},{9,11},{10,... | collective-permute-start | bytes 589832 | tf_op jit(solution)/shard_map/ppermute | solution.py:57
  283.3 3.5 %collective-permute-start.47 = (bf16[512,1536]{1,0:T(8,128)(2,1)S(1)}, bf16[512,1536]{1,0:T(8,128)(2,1)S(1)}, u32[]{:S(2)}, u32[]{:S(2)}) collective-permute-start(bf16[512,1536]{1,0:T(8,128)(2,1)S(1)} %constant_dynamic-update-slice_fusion.2.mine), channel_id=1, source_target_pairs={{0,1},{1,0},{2,3},{3,2},{4,5},{5,4},{6,7},{7,6},{8,9},{9,8},{10,11... | collective-permute-start | bytes 4718600 | tf_op jit(solution)/shard_map/ppermute | solution.py:57
  291.9 12.2 %collective-permute-start.50 = (bf16[2,384,256]{2,1,0:T(8,128)(2,1)}, bf16[2,384,256]{2,1,0:T(8,128)(2,1)S(1)}, u32[]{:S(2)}, u32[]{:S(2)}) collective-permute-start(bf16[2,384,256]{2,1,0:T(8,128)(2,1)} %get-tuple-element.249), channel_id=1, source_target_pairs={{0,4},{4,0},{8,12},{12,8},{1,5},{5,1},{9,13},{13,9},{2,6},{6,2},{1... | collective-permute-start | bytes 1179656 | tf_op jit(solution)/shard_map/ppermute | solution.py:61
  291.9 23.4 %collective-permute-start.49 = (bf16[2,384,256]{2,1,0:T(8,128)(2,1)}, bf16[2,384,256]{2,1,0:T(8,128)(2,1)S(1)}, u32[]{:S(2)}, u32[]{:S(2)}) collective-permute-start(bf16[2,384,256]{2,1,0:T(8,128)(2,1)} %get-tuple-element.253), channel_id=1, source_target_pairs={{0,4},{4,0},{8,12},{12,8},{1,5},{5,1},{9,13},{13,9},{2,6},{6,2},{1... | collective-permute-start | bytes 1179656 | tf_op jit(solution)/shard_map/ppermute | solution.py:61
  298.7 18.2 %collective-permute-start.48 = (bf16[128,2048]{1,0:T(8,128)(2,1)S(1)}, bf16[128,2048]{1,0:T(8,128)(2,1)S(1)}, u32[]{:S(2)}, u32[]{:S(2)}) collective-permute-start(bf16[128,2048]{1,0:T(8,128)(2,1)S(1)} %hidden_grad.2), channel_id=1, source_target_pairs={{0,16},{16,0},{1,17},{17,1},{2,18},{18,2},{3,19},{19,3},{4,20},{20... | collective-permute-start | bytes 1572872 | tf_op jit(solution)/shard_map/ppermute | solution.py:53
  304.9 13.3 %collective-permute-start.51 = (bf16[384,256]{1,0:T(8,128)(2,1)}, bf16[384,256]{1,0:T(8,128)(2,1)}, u32[]{:S(2)}, u32[]{:S(2)}) collective-permute-start(bf16[384,256]{1,0:T(8,128)(2,1)} %fusion.7), channel_id=1, source_target_pairs={{0,8},{4,12},{8,0},{12,4},{1,9},{5,13},{9,1},{13,5},{2,10},{6,14},... | collective-permute-start | bytes 589832 | tf_op jit(solution)/shard_map/ppermute | solution.py:61
  316.1 10.6 %collective-permute-start.52 = (bf16[384,256]{1,0:T(8,128)(2,1)}, bf16[384,256]{1,0:T(8,128)(2,1)}, u32[]{:S(2)}, u32[]{:S(2)}) collective-permute-start(bf16[384,256]{1,0:T(8,128)(2,1)} %fusion.8), channel_id=1, source_target_pairs={{0,8},{4,12},{8,0},{12,4},{1,9},{5,13},{9,1},{13,5},{2,10},{6,14},... | collective-permute-start | bytes 589832 | tf_op jit(solution)/shard_map/ppermute | solution.py:61
  (41 other events, 299.5 us)
Sparse Core Ops, SparseCore 0:
  153.7 63.3 all-gather.2

commit v6 on v5

--- a/solution.py
+++ b/solution.py
@@ -252,7 +252,7 @@
             out_specs=[whole((count, tile))] * 2,
         ),
         cost_estimate=FREE,
-        compiler_params=pltpu.CompilerParams(vmem_limit_bytes=VMEM_BYTES),
+        compiler_params=pltpu.CompilerParams(vmem_limit_bytes=48 * 2**20),
         name="logits",
     )(facts, rows, *[heads] * rep_count)
 
@@ -380,7 +380,7 @@
         ],
         out_specs=pl.BlockSpec((rows.shape[0], size), lambda r: (0, r)),
         cost_estimate=FREE,
-        compiler_params=pltpu.CompilerParams(vmem_limit_bytes=VMEM_BYTES),
+        compiler_params=pltpu.CompilerParams(vmem_limit_bytes=48 * 2**20),
         name="hidden_grad",
     )(rows, heads)
 

time: 336 us -> 337 us (level)
  Pallas kernels: 69.7 us -> 77.8 us
  local copies, waits for them, and re-layouts: 16.7 us -> 11.2 us
    unnamed x106 -> x102, local copies, waits for them, and re-layouts: 10.7 us -> 5.23 us
    pallas_call x2, Pallas kernels: 4.03 us -> 8.4 us  [grad_part(): pl.pallas_call(grad_kernel, out_shape=jax.ShapeDtypeStruct((rows.shape[0]...]
    pallas_call x2, Pallas kernels: 3.11 us -> 6.81 us  [learner_logits_part(): pl.pallas_call(learner_logits_kernel, out_shape=[jax.ShapeDtypeStruct((co...]
  transfers between devices with their start and end apart: 54 -> 54, of which waited for: 30 -> 29; matrix products, arithmetic and copies ran while one was open for 6% -> 6% of each run, Pallas kernels for 20% -> 22%
where the time goes in v6:
time: 337 us; the launch traced here: 336 us
  waiting for transfers between devices  147 us (44%)
  Pallas kernels  77.8 us (23%)
  starting transfers between devices  61.3 us (18%)
  other arithmetic  23 us (7%)
  between operations  15.2 us (5%)
  local copies, waits for them, and re-layouts  11.2 us (3%)
    ppermute x24, waiting for transfers between devices, swap_z(): return lax.ppermute(value, 'vocab', [(i, i ^ offset) for i in range(4)])  65.8 us
    ppermute x18, waiting for transfers between devices, swap_x(): return lax.ppermute(value, 'ctx', [(0, 1), (1, 0)])  57.8 us
    ppermute x24, starting transfers between devices, swap_z(): return lax.ppermute(value, 'vocab', [(i, i ^ offset) for i in range(4)])  35.9 us
    ppermute x11, waiting for transfers between devices, swap_rep(): return lax.ppermute(value, 'rep', [(i, i ^ offset) for i in range(4)])  23.8 us
    ppermute x18, starting transfers between devices, swap_x(): return lax.ppermute(value, 'ctx', [(0, 1), (1, 0)])  19.7 us
    pallas_call x6, Pallas kernels, project(): pl.pallas_call(functools.partial(project_kernel, count, parts), out_shape...  19.5 us
    pallas_call x1, Pallas kernels, attend(): pl.pallas_call(attend_kernel, out_shape=jax.ShapeDtypeStruct((seq_dev * p...  12.1 us
    pallas_call x2, Pallas kernels, expert_down(): pl.pallas_call(functools.partial(down_kernel, turned), out_shape=jax.Shap...  9.11 us
  transfers between devices with their start and end apart: 54, of which 29 were waited for; matrix products, arithmetic and copies ran while one was open for 6% of the time, Pallas kernels for 22%

profile of v6, /device:TPU:0, one launch (start us, length us, event | category | flops | bytes accessed | tf_op | source)
XLA Modules:
  0.0 336.2 jit_solution(16044812742261518553)
XLA Ops:
  7.2 1.8 constant_dynamic-slice_fusion.13
  11.8 3.0 collective-permute-start
  14.8 2.6 collective-permute-start.1
  17.4 1.7 collective-permute-start.4
  20.5 1.5 collective-permute-start.13
  23.8 1.6 collective-permute-start.3
  29.4 2.2 collective-permute-start.8
  32.9 12.1 %attend.1.heads = bf16[512,2048]{1,0:T(8,128)(2,1)S(1)} custom-call(s32[4]{0:T(128)S(1)} %pad_add_fusion.1.facts, bf16[2,256,2048]{2,1,0:T(8,128)(2,1)S(1)} %copy-done.19, bf16[2,2,512,128]{3,2,1,0:T(8,128)(2,1)S(1)} %pad_maximum_fusion.3.rows), custom_call_target="tpu_custom_call" | custom-call | tf_op jit(solution)/shard_map/attend/pallas_call | solution.py:123
  45.0 2.1 sorted_rows.1
  47.1 1.6 collective-permute-start.11
  48.6 4.1 %project.6 = (bf16[2,256,512]{2,1,0:T(8,128)(2,1)S(1)}, bf16[2,128,512]{2,1,0:T(8,128)(2,1)S(1)}, bf16[2,128,512]{2,1,0:T(8,128)(2,1)S(1)}) custom-call(bf16[256,2048]{1,0:T(8,128)(2,1)S(1)} %get-tuple-element.160.refs_0_, bf16[256,2048]{1,0:T(8,128)(2,1)S(1)} %get-tuple-element.168.refs_1_, bf16[256,128]{1,0:T(8,128)(2,1)S(1)} %get-tuple-element.144.refs_2_, ...), custom_call_target="tpu_custom_call" | custom-call | tf_op jit(solution)/shard_map/project/pallas_call | solution.py:170
  52.8 6.5 %collective-permute-done.8 = bf16[1,384,512]{2,1,0:T(8,128)(2,1)S(1)} collective-permute-done((bf16[1,384,512]{2,1,0:T(8,128)(2,1)S(1)}, bf16[1,384,512]{2,1,0:T(8,128)(2,1)S(1)}, u32[]{:S(2)}, u32[]{:S(2)}) %collective-permute-start.8) | collective-permute-done | bytes 393248 | tf_op jit(solution)/shard_map/ppermute | solution.py:61
  60.6 6.8 %collective-permute-start.10 = (bf16[2,256,512]{2,1,0:T(8,128)(2,1)S(1)}, bf16[2,256,512]{2,1,0:T(8,128)(2,1)S(1)}, u32[]{:S(2)}, u32[]{:S(2)}) collective-permute-start(bf16[2,256,512]{2,1,0:T(8,128)(2,1)S(1)} %get-tuple-element.154), channel_id=1, source_target_pairs={{0,4},{4,0},{8,12},{12,8},{1,5},{5,1},{9,13},{13,9},{2,6},{6,2},{1... | collective-permute-start | bytes 1572872 | tf_op jit(solution)/shard_map/ppermute | solution.py:61
  67.4 3.5 %collective-permute-done.11.refs_0_ = bf16[256,2048]{1,0:T(8,128)(2,1)S(1)} collective-permute-done((bf16[256,2048]{1,0:T(8,128)(2,1)S(1)}, bf16[256,2048]{1,0:T(8,128)(2,1)S(1)}, u32[]{:S(2)}, u32[]{:S(2)}) %collective-permute-start.11) | collective-permute-done | bytes 1048608 | tf_op jit(solution)/shard_map/ppermute | solution.py:53
  70.9 6.5 %collective-permute-done.10 = bf16[2,256,512]{2,1,0:T(8,128)(2,1)S(1)} collective-permute-done((bf16[2,256,512]{2,1,0:T(8,128)(2,1)S(1)}, bf16[2,256,512]{2,1,0:T(8,128)(2,1)S(1)}, u32[]{:S(2)}, u32[]{:S(2)}) %collective-permute-start.10) | collective-permute-done | bytes 524320 | tf_op jit(solution)/shard_map/ppermute | solution.py:61
  77.6 3.7 %collective-permute-start.12 = (bf16[2,128,512]{2,1,0:T(8,128)(2,1)S(1)}, bf16[2,128,512]{2,1,0:T(8,128)(2,1)S(1)}, u32[]{:S(2)}, u32[]{:S(2)}) collective-permute-start(bf16[2,128,512]{2,1,0:T(8,128)(2,1)S(1)} %add_convert_fusion.3), channel_id=1, source_target_pairs={{0,8},{4,12},{8,0},{12,4},{1,9},{5,13},{9,1},{13,5},{2,10},{6,14},... | collective-permute-start | bytes 786440 | tf_op jit(solution)/shard_map/ppermute | solution.py:61
  81.9 4.1 %project.7 = (bf16[2,256,512]{2,1,0:T(8,128)(2,1)S(1)}, bf16[2,128,512]{2,1,0:T(8,128)(2,1)S(1)}, bf16[2,128,512]{2,1,0:T(8,128)(2,1)S(1)}) custom-call(bf16[256,2048]{1,0:T(8,128)(2,1)S(1)} %get-tuple-element.160.refs_0_, bf16[256,2048]{1,0:T(8,128)(2,1)S(1)} %get-tuple-element.168.refs_1_, bf16[256,128]{1,0:T(8,128)(2,1)S(1)} %get-tuple-element.144.refs_2_, ...), custom_call_target="tpu_custom_call" | custom-call | tf_op jit(solution)/shard_map/project/pallas_call | solution.py:170
  86.0 2.9 project.8
  88.9 4.8 %collective-permute-done.12 = bf16[2,128,512]{2,1,0:T(8,128)(2,1)S(1)} collective-permute-done((bf16[2,128,512]{2,1,0:T(8,128)(2,1)S(1)}, bf16[2,128,512]{2,1,0:T(8,128)(2,1)S(1)}, u32[]{:S(2)}, u32[]{:S(2)}) %collective-permute-start.12) | collective-permute-done | bytes 262176 | tf_op jit(solution)/shard_map/ppermute | solution.py:61
  93.7 1.7 collective-permute-start.17
  95.4 2.0 collective-permute-start.15
  97.4 2.8 project.9
  100.3 14.0 %collective-permute-done.18.refs_2_ = bf16[4,384,512]{2,1,0:T(8,128)(2,1)S(1)} collective-permute-done((bf16[4,384,512]{2,1,0:T(8,128)(2,1)S(1)}, bf16[4,384,512]{2,1,0:T(8,128)(2,1)S(1)}, u32[]{:S(2)}, u32[]{:S(2)}) %collective-permute-start.18) | collective-permute-done | bytes 1572896 | tf_op jit(solution)/shard_map/ppermute | solution.py:57
  114.4 7.1 %collective-permute-done.15 = bf16[2,256,512]{2,1,0:T(8,128)(2,1)S(1)} collective-permute-done((bf16[2,256,512]{2,1,0:T(8,128)(2,1)S(1)}, bf16[2,256,512]{2,1,0:T(8,128)(2,1)S(1)}, u32[]{:S(2)}, u32[]{:S(2)}) %collective-permute-start.15) | collective-permute-done | bytes 524320 | tf_op jit(solution)/shard_map/ppermute | solution.py:61
  123.5 2.9 project.10
  126.4 2.1 collective-permute-start.21
  128.5 2.8 project.11
  131.3 8.0 %collective-permute-done.19 = bf16[2,256,512]{2,1,0:T(8,128)(2,1)S(1)} collective-permute-done((bf16[2,256,512]{2,1,0:T(8,128)(2,1)S(1)}, bf16[2,256,512]{2,1,0:T(8,128)(2,1)S(1)}, u32[]{:S(2)}, u32[]{:S(2)}) %collective-permute-start.19) | collective-permute-done | bytes 524320 | tf_op jit(solution)/shard_map/ppermute | solution.py:61
  141.6 4.2 %collective-permute-done.21 = bf16[2,128,512]{2,1,0:T(8,128)(2,1)S(1)} collective-permute-done((bf16[2,128,512]{2,1,0:T(8,128)(2,1)S(1)}, bf16[2,128,512]{2,1,0:T(8,128)(2,1)S(1)}, u32[]{:S(2)}, u32[]{:S(2)}) %collective-permute-start.21) | collective-permute-done | bytes 262176 | tf_op jit(solution)/shard_map/ppermute | solution.py:61
  145.8 3.0 collective-permute-done.22.refs_4_
  148.8 3.2 collective-permute-done.23.refs_5_
  155.5 9.5 %collective-permute-done.24 = bf16[2,128,512]{2,1,0:T(8,128)(2,1)S(1)} collective-permute-done((bf16[2,128,512]{2,1,0:T(8,128)(2,1)S(1)}, bf16[2,128,512]{2,1,0:T(8,128)(2,1)S(1)}, u32[]{:S(2)}, u32[]{:S(2)}) %collective-permute-start.24) | collective-permute-done | bytes 262176 | tf_op jit(solution)/shard_map/ppermute | solution.py:61
  166.7 8.7 %collective-permute-done.26.refs_7_ = bf16[2,128,512]{2,1,0:T(8,128)(2,1)S(1)} collective-permute-done((bf16[2,128,512]{2,1,0:T(8,128)(2,1)S(1)}, bf16[2,128,512]{2,1,0:T(8,128)(2,1)S(1)}, u32[]{:S(2)}, u32[]{:S(2)}) %collective-permute-start.26) | collective-permute-done | bytes 262176 | tf_op jit(solution)/shard_map/ppermute | solution.py:53
  176.3 8.6 %expert_hidden.1.rows = bf16[256,768]{1,0:T(8,128)(2,1)S(1)} custom-call(s32[8]{0:T(128)S(1)} %pad_add_fusion.facts, f32[2,128,512]{2,1,0:T(8,128)S(1)} %copy-done.7, f32[2,128,512]{2,1,0:T(8,128)S(1)} %get-tuple-element.278.refs_1_, f32[2,128,512]{2,1,0:T(8,128)S(1)} %get-tuple-element.276.refs_2_, f32[2,128,512]{2,1,0:T(8,128)S(1)} %get-tuple-element.274.refs_3_, ...), custom_call_target="tpu_custom_call" | custom-call | tf_op jit(solution)/shard_map/expert_hidden/pallas_call | solution.py:418
  184.9 5.0 %expert_down.2 = bf16[4,256,512]{2,1,0:T(8,128)(2,1)} custom-call(s32[4]{0:T(128)S(1)} %get-tuple-element.344.facts, bf16[256,768]{1,0:T(8,128)(2,1)S(1)} %expert_hidden.1.rows, bf16[1,768,4096]{2,1,0:T(8,128)(2,1)} %weight.3), custom_call_target="tpu_custom_call" | custom-call | tf_op jit(solution)/shard_map/expert_down/pallas_call | solution.py:450
  190.7 1.5 collective-permute-start.28
  193.7 4.1 %expert_down.3.refs_4_ = bf16[4,256,512]{2,1,0:T(8,128)(2,1)S(1)} custom-call(s32[4]{0:T(128)S(1)} %get-tuple-element.345.facts, bf16[256,768]{1,0:T(8,128)(2,1)S(1)} %expert_hidden.1.rows, bf16[1,768,4096]{2,1,0:T(8,128)(2,1)} %weight.3), custom_call_target="tpu_custom_call" | custom-call | tf_op jit(solution)/shard_map/expert_down/pallas_call | solution.py:450
  197.8 1.8 learner_parts.1
  201.4 6.0 %collective-permute-done.28.refs_5_ = bf16[4,256,512]{2,1,0:T(8,128)(2,1)} collective-permute-done((bf16[4,256,512]{2,1,0:T(8,128)(2,1)}, bf16[4,256,512]{2,1,0:T(8,128)(2,1)}, u32[]{:S(2)}, u32[]{:S(2)}) %collective-permute-start.28) | collective-permute-done | bytes 1048608 | tf_op jit(solution)/shard_map/ppermute | solution.py:53
  207.4 2.3 final_hidden.1
  210.8 3.8 %collective-permute-done.29 = f32[128,128]{1,0:T(8,128)S(1)} collective-permute-done((f32[128,128]{1,0:T(8,128)S(1)}, f32[128,128]{1,0:T(8,128)S(1)}, u32[]{:S(2)}, u32[]{:S(2)}) %collective-permute-start.29) | collective-permute-done | bytes 65568 | tf_op jit(solution)/shard_map/ppermute | solution.py:53
  214.6 1.6 collective-permute-done.30.refs_1_
  217.9 1.8 logits.5
  219.8 8.6 %collective-permute-done.32 = f32[128,768]{1,0:T(8,128)S(1)} collective-permute-done((f32[128,768]{1,0:T(8,128)S(1)}, f32[128,768]{1,0:T(8,128)S(1)}, u32[]{:S(2)}, u32[]{:S(2)}) %collective-permute-start.32) | collective-permute-done | bytes 393248 | tf_op jit(solution)/shard_map/ppermute | solution.py:53
  232.5 1.6 collective-permute-start.37
  234.2 2.6 collective-permute-start.38
  236.8 3.4 %logits.7 = (f32[128,768]{1,0:T(8,128)S(1)}, f32[128,768]{1,0:T(8,128)S(1)}) custom-call(s32[4]{0:T(128)S(1)} %iota_xor_fusion.facts, bf16[4,256,512]{2,1,0:T(8,128)(2,1)S(1)} %copy-done.16, bf16[4,4,384,512]{3,2,1,0:T(8,128)(2,1)} %bitcast.76, bf16[4,4,384,512]{3,2,1,0:T(8,128)(2,1)} %bitcast.77, bf16[4,4,384,512]{3,2,1,0:T(8,128)(2,1)} %bitcast.78, ...), custom_call_target="tpu_custom_call" | custom-call | tf_op jit(solution)/shard_map/logits/pallas_call | solution.py:241
  240.2 3.4 %logits.6 = (f32[128,768]{1,0:T(8,128)S(1)}, f32[128,768]{1,0:T(8,128)S(1)}) custom-call(s32[4]{0:T(128)S(1)} %iota_xor_fusion.facts, bf16[4,256,512]{2,1,0:T(8,128)(2,1)S(1)} %copy-done.16, bf16[4,4,384,512]{3,2,1,0:T(8,128)(2,1)} %bitcast.80, bf16[4,4,384,512]{3,2,1,0:T(8,128)(2,1)} %bitcast.81, bf16[4,4,384,512]{3,2,1,0:T(8,128)(2,1)} %bitcast.82, ...), custom_call_target="tpu_custom_call" | custom-call | tf_op jit(solution)/shard_map/logits/pallas_call | solution.py:241
  245.0 1.7 collective-permute-start.40
  246.8 2.6 collective-permute-start.41
  251.7 2.2 collective-permute-done.40
  254.5 1.9 collective-permute-done.42.other
  256.4 9.6 %collective-permute-done.34 = f32[128,1536]{1,0:T(8,128)S(1)} collective-permute-done((f32[128,1536]{1,0:T(8,128)S(1)}, f32[128,1536]{1,0:T(8,128)S(1)}, u32[]{:S(2)}, u32[]{:S(2)}) %collective-permute-start.34) | collective-permute-done | bytes 786464 | tf_op jit(solution)/shard_map/ppermute | solution.py:53
  269.4 6.6 %collective-permute-done.43.rows = bf16[128,1536]{1,0:T(8,128)(2,1)S(1)} collective-permute-done((bf16[128,1536]{1,0:T(8,128)(2,1)S(1)}, bf16[128,1536]{1,0:T(8,128)(2,1)S(1)}, u32[]{:S(2)}, u32[]{:S(2)}) %collective-permute-start.43) | collective-permute-done | bytes 393248 | tf_op jit(solution)/shard_map/ppermute | solution.py:53
  276.0 2.3 collective-permute-done.44
  279.5 4.5 %collective-permute-done.45 = bf16[64,1536]{1,0:T(8,128)(2,1)S(1)} collective-permute-done((bf16[64,1536]{1,0:T(8,128)(2,1)S(1)}, bf16[64,1536]{1,0:T(8,128)(2,1)S(1)}, u32[]{:S(2)}, u32[]{:S(2)}) %collective-permute-start.45) | collective-permute-done | bytes 196640 | tf_op jit(solution)/shard_map/ppermute | solution.py:53
  284.2 3.4 %collective-permute-done.47.core = bf16[512,1536]{1,0:T(8,128)(2,1)S(1)} collective-permute-done((bf16[512,1536]{1,0:T(8,128)(2,1)S(1)}, bf16[512,1536]{1,0:T(8,128)(2,1)S(1)}, u32[]{:S(2)}, u32[]{:S(2)}) %collective-permute-start.47) | collective-permute-done | bytes 1572896 | tf_op jit(solution)/shard_map/ppermute | solution.py:57
  287.6 4.3 %head_parts.1 = (bf16[2,384,256]{2,1,0:T(8,128)(2,1)}, bf16[2,384,256]{2,1,0:T(8,128)(2,1)}, bf16[2,384,256]{2,1,0:T(8,128)(2,1)S(1)}, bf16[2,384,256]{2,1,0:T(8,128)(2,1)S(1)}) custom-call(s32[4]{0:T(128)S(1)} %broadcast_xor_fusion.facts, bf16[512,1536]{1,0:T(8,128)(2,1)S(1)} %constant_dynamic-update-slice_fusion.2.mine, ...), custom_call_target="tpu_custom_call" | custom-call | tf_op jit(solution)/shard_map/head_parts/pallas_call | solution.py:351
  292.7 2.0 collective-permute-start.49
  294.7 4.2 %hidden_grad.2 = bf16[128,2048]{1,0:T(8,128)(2,1)S(1)} custom-call(bf16[128,1536]{1,0:T(8,128)(2,1)S(1)} %collective-permute-done.43.rows, bf16[4,4,384,512]{3,2,1,0:T(8,128)(2,1)} %bitcast.84), custom_call_target="tpu_custom_call" | custom-call | tf_op jit(solution)/shard_map/hidden_grad/pallas_call | solution.py:373
  299.0 2.1 collective-permute-start.48
  301.0 4.2 %hidden_grad.3 = bf16[128,2048]{1,0:T(8,128)(2,1)S(1)} custom-call(bf16[128,1536]{1,0:T(8,128)(2,1)S(1)} %get-tuple-element.251.rows, bf16[4,4,384,512]{3,2,1,0:T(8,128)(2,1)} %bitcast.85), custom_call_target="tpu_custom_call" | custom-call | tf_op jit(solution)/shard_map/hidden_grad/pallas_call | solution.py:373
  306.1 9.3 %collective-permute-done.49 = bf16[2,384,256]{2,1,0:T(8,128)(2,1)S(1)} collective-permute-done((bf16[2,384,256]{2,1,0:T(8,128)(2,1)}, bf16[2,384,256]{2,1,0:T(8,128)(2,1)S(1)}, u32[]{:S(2)}, u32[]{:S(2)}) %collective-permute-start.49) | collective-permute-done | bytes 393248 | tf_op jit(solution)/shard_map/ppermute | solution.py:61
  320.5 7.1 %collective-permute-done.52 = bf16[384,256]{1,0:T(8,128)(2,1)} collective-permute-done((bf16[384,256]{1,0:T(8,128)(2,1)}, bf16[384,256]{1,0:T(8,128)(2,1)}, u32[]{:S(2)}, u32[]{:S(2)}) %collective-permute-start.52) | collective-permute-done | bytes 196640 | tf_op jit(solution)/shard_map/ppermute | solution.py:61
  (262 shorter events, 51.9 us)
Async XLA Ops:
  7.2 229.6 %all-gather.3.cloned.1.call-start = ((), (), s32[]{:S(2)}) async-start(), calls=%async_computation | async-start | bytes 6684672 | tf_op jit(solution)/shard_map/all_gather | solution.py:676
  11.8 8.7 %collective-permute-start = (f32[1,2,128]{2,1,0:T(2,128)}, f32[1,2,128]{2,1,0:T(2,128)}, u32[]{:S(2)}, u32[]{:S(2)}) collective-permute-start(f32[1,2,128]{2,1,0:T(2,128)} %maximum_bitcast_fusion), channel_id=1, source_target_pairs={{0,4},{4,0},{8,12},{12,8},{1,5},{5,1},{9,13},{13,9},{2,6},{6,2},{1... | collective-permute-start | bytes 3080 | tf_op jit(solution)/shard_map/ppermute | solution.py:61
  14.8 7.2 %collective-permute-start.1 = (f32[1,2,128]{2,1,0:T(2,128)}, f32[1,2,128]{2,1,0:T(2,128)}, u32[]{:S(2)}, u32[]{:S(2)}) collective-permute-start(f32[1,2,128]{2,1,0:T(2,128)} %maximum_bitcast_fusion), channel_id=1, source_target_pairs={{0,8},{4,12},{8,0},{12,4},{1,9},{5,13},{9,1},{13,5},{2,10},{6,14},... | collective-permute-start | bytes 3080 | tf_op jit(solution)/shard_map/ppermute | solution.py:61
  17.4 5.7 %collective-permute-start.2 = (f32[1,2,128]{2,1,0:T(2,128)}, f32[1,2,128]{2,1,0:T(2,128)}, u32[]{:S(2)}, u32[]{:S(2)}) collective-permute-start(f32[1,2,128]{2,1,0:T(2,128)} %maximum_bitcast_fusion), channel_id=1, source_target_pairs={{0,12},{4,8},{8,4},{12,0},{1,13},{5,9},{9,5},{13,1},{2,14},{6,10},... | collective-permute-start | bytes 3080 | tf_op jit(solution)/shard_map/ppermute | solution.py:61
  17.4 11.9 %collective-permute-start.4 = (bf16[2,2,256,128]{3,2,1,0:T(8,128)(2,1)}, bf16[2,2,256,128]{3,2,1,0:T(8,128)(2,1)}, u32[]{:S(2)}, u32[]{:S(2)}) collective-permute-start(bf16[2,2,256,128]{3,2,1,0:T(8,128)(2,1)} %constant_dynamic-slice_fusion.13), channel_id=1, source_target_pairs={{0,16},{16,0},{1,17},{17,1},{2,18},{18,2},{3,19},{19,3},{4,20},{20... | collective-permute-start | bytes 786440 | tf_op jit(solution)/shard_map/ppermute | solution.py:53
  19.1 12.4 %collective-permute-start.5 = (bf16[2048,512]{1,0:T(8,128)(2,1)}, bf16[2048,512]{1,0:T(8,128)(2,1)}, u32[]{:S(2)}, u32[]{:S(2)}) collective-permute-start(bf16[2048,512]{1,0:T(8,128)(2,1)} %refs_3_.3), channel_id=1, source_target_pairs={{0,1},{1,0},{2,3},{3,2},{4,5},{5,4},{6,7},{7,6},{8,9},{9,8},{10,11... | collective-permute-start | bytes 6291464 | tf_op jit(solution)/shard_map/ppermute | solution.py:57
  20.5 57.0 %collective-permute-start.13 = (bf16[2048,512]{1,0:T(8,128)(2,1)}, bf16[2048,512]{1,0:T(8,128)(2,1)}, u32[]{:S(2)}, u32[]{:S(2)}) collective-permute-start(bf16[2048,512]{1,0:T(8,128)(2,1)} %refs_3_.3), channel_id=1, source_target_pairs={{0,2},{1,3},{2,0},{3,1},{4,6},{5,7},{6,4},{7,5},{8,10},{9,11},{10,... | collective-permute-start | bytes 6291464 | tf_op jit(solution)/shard_map/ppermute | solution.py:57
  22.0 30.8 %collective-permute-start.7 = (bf16[1,384,512]{2,1,0:T(8,128)(2,1)S(1)}, bf16[1,384,512]{2,1,0:T(8,128)(2,1)}, u32[]{:S(2)}, u32[]{:S(2)}) collective-permute-start(bf16[1,384,512]{2,1,0:T(8,128)(2,1)S(1)} %dynamic-slice_bitcast_fusion), channel_id=1, source_target_pairs={{0,4},{4,0},{8,12},{12,8},{1,5},{5,1},{9,13},{13,9},{2,6},{6,2},{1... | collective-permute-start | bytes 1179656 | tf_op jit(solution)/shard_map/ppermute | solution.py:61
  23.8 3.7 %collective-permute-start.3 = (f32[4,2,128]{2,1,0:T(2,128)S(1)}, f32[4,2,128]{2,1,0:T(2,128)S(1)}, u32[]{:S(2)}, u32[]{:S(2)}) collective-permute-start(f32[4,2,128]{2,1,0:T(2,128)S(1)} %pad_maximum_fusion.11), channel_id=1, source_target_pairs={{0,16},{16,0},{1,17},{17,1},{2,18},{18,2},{3,19},{19,3},{4,20},{20... | collective-permute-start | bytes 12296 | tf_op jit(solution)/shard_map/ppermute | solution.py:53
  27.5 17.5 %collective-permute-start.6 = (bf16[4,128,512]{2,1,0:T(8,128)(2,1)S(1)}, bf16[4,128,512]{2,1,0:T(8,128)(2,1)S(1)}, u32[]{:S(2)}, u32[]{:S(2)}) collective-permute-start(bf16[4,128,512]{2,1,0:T(8,128)(2,1)S(1)} %pad_maximum_fusion.4), channel_id=1, source_target_pairs={{0,16},{16,0},{1,17},{17,1},{2,18},{18,2},{3,19},{19,3},{4,20},{20... | collective-permute-start | bytes 1572872 | tf_op jit(solution)/shard_map/ppermute | solution.py:53
  29.4 29.9 %collective-permute-start.8 = (bf16[1,384,512]{2,1,0:T(8,128)(2,1)S(1)}, bf16[1,384,512]{2,1,0:T(8,128)(2,1)S(1)}, u32[]{:S(2)}, u32[]{:S(2)}) collective-permute-start(bf16[1,384,512]{2,1,0:T(8,128)(2,1)S(1)} %dynamic-slice_bitcast_fusion), channel_id=1, source_target_pairs={{0,8},{4,12},{8,0},{12,4},{1,9},{5,13},{9,1},{13,5},{2,10},{6,14},... | collective-permute-start | bytes 1179656 | tf_op jit(solution)/shard_map/ppermute | solution.py:61
  31.5 27.7 %collective-permute-start.9 = (bf16[1,384,512]{2,1,0:T(8,128)(2,1)S(1)}, bf16[1,384,512]{2,1,0:T(8,128)(2,1)S(1)}, u32[]{:S(2)}, u32[]{:S(2)}) collective-permute-start(bf16[1,384,512]{2,1,0:T(8,128)(2,1)S(1)} %dynamic-slice_bitcast_fusion), channel_id=1, source_target_pairs={{0,12},{4,8},{8,4},{12,0},{1,13},{5,9},{9,5},{13,1},{2,14},{6,10},... | collective-permute-start | bytes 1179656 | tf_op jit(solution)/shard_map/ppermute | solution.py:61
  47.1 23.9 %collective-permute-start.11 = (bf16[256,2048]{1,0:T(8,128)(2,1)S(1)}, bf16[256,2048]{1,0:T(8,128)(2,1)S(1)}, u32[]{:S(2)}, u32[]{:S(2)}) collective-permute-start(bf16[256,2048]{1,0:T(8,128)(2,1)S(1)} %get-tuple-element.160.refs_0_), channel_id=1, source_target_pairs={{0,16},{16,0},{1,17},{17,1},{2,18},{18,2},{3,19},{19,3},{4,20},{20... | collective-permute-start | bytes 3145736 | tf_op jit(solution)/shard_map/ppermute | solution.py:53
  60.6 25.4 %copy-start.3 = (bf16[4,384,512]{2,1,0:T(8,128)(2,1)}, bf16[4,384,512]{2,1,0:T(8,128)(2,1)S(1)}, u32[]{:S(2)}) copy-start(bf16[4,384,512]{2,1,0:T(8,128)(2,1)S(1)} %pad_maximum_fusion.refs_0_) | copy-start | bytes 4718596
  60.6 16.8 %collective-permute-start.10 = (bf16[2,256,512]{2,1,0:T(8,128)(2,1)S(1)}, bf16[2,256,512]{2,1,0:T(8,128)(2,1)S(1)}, u32[]{:S(2)}, u32[]{:S(2)}) collective-permute-start(bf16[2,256,512]{2,1,0:T(8,128)(2,1)S(1)} %get-tuple-element.154), channel_id=1, source_target_pairs={{0,4},{4,0},{8,12},{12,8},{1,5},{5,1},{9,13},{13,9},{2,6},{6,2},{1... | collective-permute-start | bytes 1572872 | tf_op jit(solution)/shard_map/ppermute | solution.py:61
  77.5 4.4 %collective-permute-start.14 = (bf16[2048,512]{1,0:T(8,128)(2,1)}, bf16[2048,512]{1,0:T(8,128)(2,1)S(1)}, u32[]{:S(2)}, u32[]{:S(2)}) collective-permute-start(bf16[2048,512]{1,0:T(8,128)(2,1)} %collective-permute-done.13.refs_5_.refs_3_), channel_id=1, source_target_pairs={{0,1},{1,0},{2,3},{3,2},{4,5},{5,4},{6,7},{7,6},{8,9},{9,8},{10,11... | collective-permute-start | bytes 6291464 | tf_op jit(solution)/shard_map/ppermute | solution.py:57
  77.5 36.8 %collective-permute-start.18 = (bf16[4,384,512]{2,1,0:T(8,128)(2,1)S(1)}, bf16[4,384,512]{2,1,0:T(8,128)(2,1)S(1)}, u32[]{:S(2)}, u32[]{:S(2)}) collective-permute-start(bf16[4,384,512]{2,1,0:T(8,128)(2,1)S(1)} %pad_maximum_fusion.refs_0_), channel_id=1, source_target_pairs={{0,2},{1,3},{2,0},{3,1},{4,6},{5,7},{6,4},{7,5},{8,10},{9,11},{10,... | collective-permute-start | bytes 4718600 | tf_op jit(solution)/shard_map/ppermute | solution.py:57
  77.6 16.1 %collective-permute-start.12 = (bf16[2,128,512]{2,1,0:T(8,128)(2,1)S(1)}, bf16[2,128,512]{2,1,0:T(8,128)(2,1)S(1)}, u32[]{:S(2)}, u32[]{:S(2)}) collective-permute-start(bf16[2,128,512]{2,1,0:T(8,128)(2,1)S(1)} %add_convert_fusion.3), channel_id=1, source_target_pairs={{0,8},{4,12},{8,0},{12,4},{1,9},{5,13},{9,1},{13,5},{2,10},{6,14},... | collective-permute-start | bytes 786440 | tf_op jit(solution)/shard_map/ppermute | solution.py:61
  93.7 27.8 %collective-permute-start.17 = (bf16[256,2048]{1,0:T(8,128)(2,1)S(1)}, bf16[256,2048]{1,0:T(8,128)(2,1)S(1)}, u32[]{:S(2)}, u32[]{:S(2)}) collective-permute-start(bf16[256,2048]{1,0:T(8,128)(2,1)S(1)} %get-tuple-element.168.refs_1_), channel_id=1, source_target_pairs={{0,16},{16,0},{1,17},{17,1},{2,18},{18,2},{3,19},{19,3},{4,20},{20... | collective-permute-start | bytes 3145736 | tf_op jit(solution)/shard_map/ppermute | solution.py:53
  95.4 19.0 %collective-permute-start.16 = (bf16[2,256,512]{2,1,0:T(8,128)(2,1)S(1)}, bf16[2,256,512]{2,1,0:T(8,128)(2,1)S(1)}, u32[]{:S(2)}, u32[]{:S(2)}) collective-permute-start(bf16[2,256,512]{2,1,0:T(8,128)(2,1)S(1)} %project.8), channel_id=1, source_target_pairs={{0,4},{4,0},{8,12},{12,8},{1,5},{5,1},{9,13},{13,9},{2,6},{6,2},{1... | collective-permute-start | bytes 1572872 | tf_op jit(solution)/shard_map/ppermute | solution.py:61
  95.4 26.1 %collective-permute-start.15 = (bf16[2,256,512]{2,1,0:T(8,128)(2,1)S(1)}, bf16[2,256,512]{2,1,0:T(8,128)(2,1)S(1)}, u32[]{:S(2)}, u32[]{:S(2)}) collective-permute-start(bf16[2,256,512]{2,1,0:T(8,128)(2,1)S(1)} %get-tuple-element.167), channel_id=1, source_target_pairs={{0,4},{4,0},{8,12},{12,8},{1,5},{5,1},{9,13},{13,9},{2,6},{6,2},{1... | collective-permute-start | bytes 1572872 | tf_op jit(solution)/shard_map/ppermute | solution.py:61
  100.2 39.1 %collective-permute-start.19 = (bf16[2,256,512]{2,1,0:T(8,128)(2,1)S(1)}, bf16[2,256,512]{2,1,0:T(8,128)(2,1)S(1)}, u32[]{:S(2)}, u32[]{:S(2)}) collective-permute-start(bf16[2,256,512]{2,1,0:T(8,128)(2,1)S(1)} %project.9), channel_id=1, source_target_pairs={{0,4},{4,0},{8,12},{12,8},{1,5},{5,1},{9,13},{13,9},{2,6},{6,2},{1... | collective-permute-start | bytes 1572872 | tf_op jit(solution)/shard_map/ppermute | solution.py:61
  121.6 17.8 %collective-permute-start.20 = (bf16[2,128,512]{2,1,0:T(8,128)(2,1)S(1)}, bf16[2,128,512]{2,1,0:T(8,128)(2,1)S(1)}, u32[]{:S(2)}, u32[]{:S(2)}) collective-permute-start(bf16[2,128,512]{2,1,0:T(8,128)(2,1)S(1)} %add_convert_fusion.2), channel_id=1, source_target_pairs={{0,8},{4,12},{8,0},{12,4},{1,9},{5,13},{9,1},{13,5},{2,10},{6,14},... | collective-permute-start | bytes 786440 | tf_op jit(solution)/shard_map/ppermute | solution.py:61
  126.4 19.4 %collective-permute-start.21 = (bf16[2,128,512]{2,1,0:T(8,128)(2,1)S(1)}, bf16[2,128,512]{2,1,0:T(8,128)(2,1)S(1)}, u32[]{:S(2)}, u32[]{:S(2)}) collective-permute-start(bf16[2,128,512]{2,1,0:T(8,128)(2,1)S(1)} %add_convert_fusion.1), channel_id=1, source_target_pairs={{0,8},{4,12},{8,0},{12,4},{1,9},{5,13},{9,1},{13,5},{2,10},{6,14},... | collective-permute-start | bytes 786440 | tf_op jit(solution)/shard_map/ppermute | solution.py:61
  131.3 21.4 %copy-start.31 = (bf16[2,128,512]{2,1,0:T(8,128)(2,1)}, bf16[2,128,512]{2,1,0:T(8,128)(2,1)S(1)}, u32[]{:S(2)}) copy-start(bf16[2,128,512]{2,1,0:T(8,128)(2,1)S(1)} %get-tuple-element.185) | copy-start | bytes 786436
  131.3 21.4 %copy-start.32 = (bf16[2,128,512]{2,1,0:T(8,128)(2,1)}, bf16[2,128,512]{2,1,0:T(8,128)(2,1)S(1)}, u32[]{:S(2)}) copy-start(bf16[2,128,512]{2,1,0:T(8,128)(2,1)S(1)} %get-tuple-element.178) | copy-start | bytes 786436
  139.5 36.7 %copy-start.9 = (f32[2,128,512]{2,1,0:T(8,128)}, f32[2,128,512]{2,1,0:T(8,128)S(1)}, u32[]{:S(2)}) copy-start(f32[2,128,512]{2,1,0:T(8,128)S(1)} %get-tuple-element.278.refs_1_) | copy-start | bytes 1572868
  139.5 9.3 %collective-permute-start.22 = (bf16[2,128,512]{2,1,0:T(8,128)(2,1)S(1)}, bf16[2,128,512]{2,1,0:T(8,128)(2,1)S(1)}, u32[]{:S(2)}, u32[]{:S(2)}) collective-permute-start(bf16[2,128,512]{2,1,0:T(8,128)(2,1)S(1)} %get-tuple-element.181), channel_id=1, source_target_pairs={{0,16},{16,0},{1,17},{17,1},{2,18},{18,2},{3,19},{19,3},{4,20},{20... | collective-permute-start | bytes 786440 | tf_op jit(solution)/shard_map/ppermute | solution.py:53
  140.1 11.9 %collective-permute-start.23 = (bf16[2,128,512]{2,1,0:T(8,128)(2,1)S(1)}, bf16[2,128,512]{2,1,0:T(8,128)(2,1)S(1)}, u32[]{:S(2)}, u32[]{:S(2)}) collective-permute-start(bf16[2,128,512]{2,1,0:T(8,128)(2,1)S(1)} %get-tuple-element.182), channel_id=1, source_target_pairs={{0,16},{16,0},{1,17},{17,1},{2,18},{18,2},{3,19},{19,3},{4,20},{20... | collective-permute-start | bytes 786440 | tf_op jit(solution)/shard_map/ppermute | solution.py:53
  153.5 22.7 %copy-start.11 = (f32[2,128,512]{2,1,0:T(8,128)}, f32[2,128,512]{2,1,0:T(8,128)S(1)}, u32[]{:S(2)}) copy-start(f32[2,128,512]{2,1,0:T(8,128)S(1)} %get-tuple-element.276.refs_2_) | copy-start | bytes 1572868
  153.5 21.9 %copy-start.17 = (bf16[2,64,4096]{2,1,0:T(8,128)(2,1)S(1)}, bf16[2,64,4096]{2,1,0:T(8,128)(2,1)}, u32[]{:S(2)}) copy-start(bf16[2,64,4096]{2,1,0:T(8,128)(2,1)} %param.28) | copy-start | bytes 3145732
  154.9 10.1 %collective-permute-start.24 = (bf16[2,128,512]{2,1,0:T(8,128)(2,1)S(1)}, bf16[2,128,512]{2,1,0:T(8,128)(2,1)S(1)}, u32[]{:S(2)}, u32[]{:S(2)}) collective-permute-start(bf16[2,128,512]{2,1,0:T(8,128)(2,1)S(1)} %add_convert_fusion), channel_id=1, source_target_pairs={{0,8},{4,12},{8,0},{12,4},{1,9},{5,13},{9,1},{13,5},{2,10},{6,14},... | collective-permute-start | bytes 786440 | tf_op jit(solution)/shard_map/ppermute | solution.py:61
  154.9 21.3 %copy-start.7 = (f32[2,128,512]{2,1,0:T(8,128)S(1)}, f32[2,128,512]{2,1,0:T(8,128)}, u32[]{:S(2)}) copy-start(f32[2,128,512]{2,1,0:T(8,128)} %get-tuple-element.280.refs_0_) | copy-start | bytes 1572868
  155.0 21.3 %copy-start.30 = (bf16[2,128,512]{2,1,0:T(8,128)(2,1)S(1)}, bf16[2,128,512]{2,1,0:T(8,128)(2,1)}, u32[]{:S(2)}) copy-start(bf16[2,128,512]{2,1,0:T(8,128)(2,1)} %copy-done.29) | copy-start | bytes 786436
  155.0 21.3 %copy-start.33 = (f32[4096]{0:T(1024)S(1)}, f32[4096]{0:T(1024)}, u32[]{:S(2)}) copy-start(f32[4096]{0:T(1024)} %param.20) | copy-start | bytes 49156
  155.0 10.0 %collective-permute-start.25 = (bf16[2,128,512]{2,1,0:T(8,128)(2,1)}, bf16[2,128,512]{2,1,0:T(8,128)(2,1)S(1)}, u32[]{:S(2)}, u32[]{:S(2)}) collective-permute-start(bf16[2,128,512]{2,1,0:T(8,128)(2,1)} %get-tuple-element.275), channel_id=1, source_target_pairs={{0,16},{16,0},{1,17},{17,1},{2,18},{18,2},{3,19},{19,3},{4,20},{20... | collective-permute-start | bytes 786440 | tf_op jit(solution)/shard_map/ppermute | solution.py:53
  166.2 9.3 %collective-permute-start.26 = (bf16[2,128,512]{2,1,0:T(8,128)(2,1)S(1)}, bf16[2,128,512]{2,1,0:T(8,128)(2,1)S(1)}, u32[]{:S(2)}, u32[]{:S(2)}) collective-permute-start(bf16[2,128,512]{2,1,0:T(8,128)(2,1)S(1)} %get-tuple-element.273), channel_id=1, source_target_pairs={{0,16},{16,0},{1,17},{17,1},{2,18},{18,2},{3,19},{19,3},{4,20},{20... | collective-permute-start | bytes 786440 | tf_op jit(solution)/shard_map/ppermute | solution.py:53
  175.6 14.3 %collective-permute-start.27 = (bf16[128,2048]{1,0:T(8,128)(2,1)S(1)}, bf16[128,2048]{1,0:T(8,128)(2,1)S(1)}, u32[]{:S(2)}, u32[]{:S(2)}) collective-permute-start(bf16[128,2048]{1,0:T(8,128)(2,1)S(1)} %pad_maximum_fusion.5), channel_id=1, source_target_pairs={{0,16},{16,0},{1,17},{17,1},{2,18},{18,2},{3,19},{19,3},{4,20},{20... | collective-permute-start | bytes 1572872 | tf_op jit(solution)/shard_map/ppermute | solution.py:53
  190.7 16.7 %collective-permute-start.28 = (bf16[4,256,512]{2,1,0:T(8,128)(2,1)}, bf16[4,256,512]{2,1,0:T(8,128)(2,1)}, u32[]{:S(2)}, u32[]{:S(2)}) collective-permute-start(bf16[4,256,512]{2,1,0:T(8,128)(2,1)} %expert_down.2), channel_id=1, source_target_pairs={{0,16},{16,0},{1,17},{17,1},{2,18},{18,2},{3,19},{19,3},{4,20},{20... | collective-permute-start | bytes 3145736 | tf_op jit(solution)/shard_map/ppermute | solution.py:53
  209.8 4.9 %collective-permute-start.31 = (bf16[4,384,512]{2,1,0:T(8,128)(2,1)S(1)}, bf16[4,384,512]{2,1,0:T(8,128)(2,1)S(1)}, u32[]{:S(2)}, u32[]{:S(2)}) collective-permute-start(bf16[4,384,512]{2,1,0:T(8,128)(2,1)S(1)} %copy-done.6), channel_id=1, source_target_pairs={{0,1},{1,0},{2,3},{3,2},{4,5},{5,4},{6,7},{7,6},{8,9},{9,8},{10,11... | collective-permute-start | bytes 4718600 | tf_op jit(solution)/shard_map/ppermute | solution.py:57
  209.8 6.3 %collective-permute-start.30 = (bf16[4,384,512]{2,1,0:T(8,128)(2,1)S(1)}, bf16[4,384,512]{2,1,0:T(8,128)(2,1)S(1)}, u32[]{:S(2)}, u32[]{:S(2)}) collective-permute-start(bf16[4,384,512]{2,1,0:T(8,128)(2,1)S(1)} %copy-done.4), channel_id=1, source_target_pairs={{0,1},{1,0},{2,3},{3,2},{4,5},{5,4},{6,7},{7,6},{8,9},{9,8},{10,11... | collective-permute-start | bytes 4718600 | tf_op jit(solution)/shard_map/ppermute | solution.py:57
  210.3 4.3 %collective-permute-start.29 = (f32[128,128]{1,0:T(8,128)S(1)}, f32[128,128]{1,0:T(8,128)S(1)}, u32[]{:S(2)}, u32[]{:S(2)}) collective-permute-start(f32[128,128]{1,0:T(8,128)S(1)} %slice.121), channel_id=1, source_target_pairs={{0,16},{16,0},{1,17},{17,1},{2,18},{18,2},{3,19},{19,3},{4,20},{20... | collective-permute-start | bytes 196616 | tf_op jit(solution)/shard_map/ppermute | solution.py:53
  217.2 11.3 %collective-permute-start.32 = (f32[128,768]{1,0:T(8,128)S(1)}, f32[128,768]{1,0:T(8,128)S(1)}, u32[]{:S(2)}, u32[]{:S(2)}) collective-permute-start(f32[128,768]{1,0:T(8,128)S(1)} %get-tuple-element.212), channel_id=1, source_target_pairs={{0,16},{16,0},{1,17},{17,1},{2,18},{18,2},{3,19},{19,3},{4,20},{20... | collective-permute-start | bytes 1179656 | tf_op jit(solution)/shard_map/ppermute | solution.py:53
  228.5 15.2 %collective-permute-start.33 = (f32[128,768]{1,0:T(8,128)}, f32[128,768]{1,0:T(8,128)}, u32[]{:S(2)}, u32[]{:S(2)}) collective-permute-start(f32[128,768]{1,0:T(8,128)} %get-tuple-element.223), channel_id=1, source_target_pairs={{0,16},{16,0},{1,17},{17,1},{2,18},{18,2},{3,19},{19,3},{4,20},{20... | collective-permute-start | bytes 1179656 | tf_op jit(solution)/shard_map/ppermute | solution.py:53
  229.2 25.1 %collective-permute-start.35 = (bf16[2,256,512]{2,1,0:T(8,128)(2,1)}, bf16[2,256,512]{2,1,0:T(8,128)(2,1)S(1)}, u32[]{:S(2)}, u32[]{:S(2)}) collective-permute-start(bf16[2,256,512]{2,1,0:T(8,128)(2,1)} %copy-done.34), channel_id=1, source_target_pairs={{0,2},{1,3},{2,0},{3,1},{4,6},{5,7},{6,4},{7,5},{8,10},{9,11},{10,... | collective-permute-start | bytes 1572872 | tf_op jit(solution)/shard_map/ppermute | solution.py:57
  232.4 12.4 %collective-permute-start.36 = (f32[32,768]{1,0:T(8,128)}, f32[32,768]{1,0:T(8,128)}, u32[]{:S(2)}, u32[]{:S(2)}) collective-permute-start(f32[32,768]{1,0:T(8,128)} %get-tuple-element.315), channel_id=1, source_target_pairs={{0,4},{4,0},{8,12},{12,8},{1,5},{5,1},{9,13},{13,9},{2,6},{6,2},{1... | collective-permute-start | bytes 294920 | tf_op jit(solution)/shard_map/ppermute | solution.py:61
  232.5 12.3 %collective-permute-start.37 = (f32[32,768]{1,0:T(8,128)}, f32[32,768]{1,0:T(8,128)}, u32[]{:S(2)}, u32[]{:S(2)}) collective-permute-start(f32[32,768]{1,0:T(8,128)} %get-tuple-element.314), channel_id=1, source_target_pairs={{0,8},{4,12},{8,0},{12,4},{1,9},{5,13},{9,1},{13,5},{2,10},{6,14},... | collective-permute-start | bytes 294920 | tf_op jit(solution)/shard_map/ppermute | solution.py:61
  234.2 10.7 %collective-permute-start.38 = (f32[32,768]{1,0:T(8,128)S(1)}, f32[32,768]{1,0:T(8,128)}, u32[]{:S(2)}, u32[]{:S(2)}) collective-permute-start(f32[32,768]{1,0:T(8,128)S(1)} %get-tuple-element.313), channel_id=1, source_target_pairs={{0,12},{4,8},{8,4},{12,0},{1,13},{5,9},{9,5},{13,1},{2,14},{6,10},... | collective-permute-start | bytes 294920 | tf_op jit(solution)/shard_map/ppermute | solution.py:61
  244.9 6.7 %collective-permute-start.39 = (f32[32,768]{1,0:T(8,128)S(1)}, f32[32,768]{1,0:T(8,128)S(1)}, u32[]{:S(2)}, u32[]{:S(2)}) collective-permute-start(f32[32,768]{1,0:T(8,128)S(1)} %get-tuple-element.307), channel_id=1, source_target_pairs={{0,4},{4,0},{8,12},{12,8},{1,5},{5,1},{9,13},{13,9},{2,6},{6,2},{1... | collective-permute-start | bytes 294920 | tf_op jit(solution)/shard_map/ppermute | solution.py:61
  245.0 8.9 %collective-permute-start.40 = (f32[32,768]{1,0:T(8,128)S(1)}, f32[32,768]{1,0:T(8,128)S(1)}, u32[]{:S(2)}, u32[]{:S(2)}) collective-permute-start(f32[32,768]{1,0:T(8,128)S(1)} %get-tuple-element.306), channel_id=1, source_target_pairs={{0,8},{4,12},{8,0},{12,4},{1,9},{5,13},{9,1},{13,5},{2,10},{6,14},... | collective-permute-start | bytes 294920 | tf_op jit(solution)/shard_map/ppermute | solution.py:61
  246.8 7.1 %collective-permute-start.41 = (f32[32,768]{1,0:T(8,128)S(1)}, f32[32,768]{1,0:T(8,128)S(1)}, u32[]{:S(2)}, u32[]{:S(2)}) collective-permute-start(f32[32,768]{1,0:T(8,128)S(1)} %get-tuple-element.305), channel_id=1, source_target_pairs={{0,12},{4,8},{8,4},{12,0},{1,13},{5,9},{9,5},{13,1},{2,14},{6,10},... | collective-permute-start | bytes 294920 | tf_op jit(solution)/shard_map/ppermute | solution.py:61
  249.5 16.6 %collective-permute-start.34 = (f32[128,1536]{1,0:T(8,128)S(1)}, f32[128,1536]{1,0:T(8,128)S(1)}, u32[]{:S(2)}, u32[]{:S(2)}) collective-permute-start(f32[128,1536]{1,0:T(8,128)S(1)} %pad_maximum_fusion.2), channel_id=1, source_target_pairs={{0,16},{16,0},{1,17},{17,1},{2,18},{18,2},{3,19},{19,3},{4,20},{20... | collective-permute-start | bytes 2359304 | tf_op jit(solution)/shard_map/ppermute | solution.py:53
  254.4 2.0 collective-permute-start.42
  267.3 20.3 %copy-start.21 = (bf16[2,256,512]{2,1,0:T(8,128)(2,1)S(1)}, bf16[2,256,512]{2,1,0:T(8,128)(2,1)}, u32[]{:S(2)}) copy-start(bf16[2,256,512]{2,1,0:T(8,128)(2,1)} %copy-done.20) | copy-start | bytes 1572868
  267.3 8.7 %collective-permute-start.43 = (bf16[128,1536]{1,0:T(8,128)(2,1)S(1)}, bf16[128,1536]{1,0:T(8,128)(2,1)S(1)}, u32[]{:S(2)}, u32[]{:S(2)}) collective-permute-start(bf16[128,1536]{1,0:T(8,128)(2,1)S(1)} %get-tuple-element.251.rows), channel_id=1, source_target_pairs={{0,16},{16,0},{1,17},{17,1},{2,18},{18,2},{3,19},{19,3},{4,20},{20... | collective-permute-start | bytes 1179656 | tf_op jit(solution)/shard_map/ppermute | solution.py:53
  268.6 9.7 %collective-permute-start.44 = (bf16[128,1536]{1,0:T(8,128)(2,1)S(1)}, bf16[128,1536]{1,0:T(8,128)(2,1)S(1)}, u32[]{:S(2)}, u32[]{:S(2)}) collective-permute-start(bf16[128,1536]{1,0:T(8,128)(2,1)S(1)} %get-tuple-element.251.rows), channel_id=1, source_target_pairs={{0,2},{1,3},{2,0},{3,1},{4,6},{5,7},{6,4},{7,5},{8,10},{9,11},{10,... | collective-permute-start | bytes 1179656 | tf_op jit(solution)/shard_map/ppermute | solution.py:57
  278.3 5.7 %collective-permute-start.45 = (bf16[64,1536]{1,0:T(8,128)(2,1)S(1)}, bf16[64,1536]{1,0:T(8,128)(2,1)S(1)}, u32[]{:S(2)}, u32[]{:S(2)}) collective-permute-start(bf16[64,1536]{1,0:T(8,128)(2,1)S(1)} %slice.126), channel_id=1, source_target_pairs={{0,16},{16,0},{1,17},{17,1},{2,18},{18,2},{3,19},{19,3},{4,20},{20... | collective-permute-start | bytes 589832 | tf_op jit(solution)/shard_map/ppermute | solution.py:53
  278.4 5.7 %collective-permute-start.46 = (bf16[64,1536]{1,0:T(8,128)(2,1)S(1)}, bf16[64,1536]{1,0:T(8,128)(2,1)S(1)}, u32[]{:S(2)}, u32[]{:S(2)}) collective-permute-start(bf16[64,1536]{1,0:T(8,128)(2,1)S(1)} %slice.127), channel_id=1, source_target_pairs={{0,2},{1,3},{2,0},{3,1},{4,6},{5,7},{6,4},{7,5},{8,10},{9,11},{10,... | collective-permute-start | bytes 589832 | tf_op jit(solution)/shard_map/ppermute | solution.py:57
  284.1 3.5 %collective-permute-start.47 = (bf16[512,1536]{1,0:T(8,128)(2,1)S(1)}, bf16[512,1536]{1,0:T(8,128)(2,1)S(1)}, u32[]{:S(2)}, u32[]{:S(2)}) collective-permute-start(bf16[512,1536]{1,0:T(8,128)(2,1)S(1)} %constant_dynamic-update-slice_fusion.2.mine), channel_id=1, source_target_pairs={{0,1},{1,0},{2,3},{3,2},{4,5},{5,4},{6,7},{7,6},{8,9},{9,8},{10,11... | collective-permute-start | bytes 4718600 | tf_op jit(solution)/shard_map/ppermute | solution.py:57
  292.7 12.5 %collective-permute-start.50 = (bf16[2,384,256]{2,1,0:T(8,128)(2,1)}, bf16[2,384,256]{2,1,0:T(8,128)(2,1)S(1)}, u32[]{:S(2)}, u32[]{:S(2)}) collective-permute-start(bf16[2,384,256]{2,1,0:T(8,128)(2,1)} %get-tuple-element.249), channel_id=1, source_target_pairs={{0,4},{4,0},{8,12},{12,8},{1,5},{5,1},{9,13},{13,9},{2,6},{6,2},{1... | collective-permute-start | bytes 1179656 | tf_op jit(solution)/shard_map/ppermute | solution.py:61
  292.7 22.7 %collective-permute-start.49 = (bf16[2,384,256]{2,1,0:T(8,128)(2,1)}, bf16[2,384,256]{2,1,0:T(8,128)(2,1)S(1)}, u32[]{:S(2)}, u32[]{:S(2)}) collective-permute-start(bf16[2,384,256]{2,1,0:T(8,128)(2,1)} %get-tuple-element.253), channel_id=1, source_target_pairs={{0,4},{4,0},{8,12},{12,8},{1,5},{5,1},{9,13},{13,9},{2,6},{6,2},{1... | collective-permute-start | bytes 1179656 | tf_op jit(solution)/shard_map/ppermute | solution.py:61
  299.0 18.8 %collective-permute-start.48 = (bf16[128,2048]{1,0:T(8,128)(2,1)S(1)}, bf16[128,2048]{1,0:T(8,128)(2,1)S(1)}, u32[]{:S(2)}, u32[]{:S(2)}) collective-permute-start(bf16[128,2048]{1,0:T(8,128)(2,1)S(1)} %hidden_grad.2), channel_id=1, source_target_pairs={{0,16},{16,0},{1,17},{17,1},{2,18},{18,2},{3,19},{19,3},{4,20},{20... | collective-permute-start | bytes 1572872 | tf_op jit(solution)/shard_map/ppermute | solution.py:53
  306.1 12.9 %collective-permute-start.51 = (bf16[384,256]{1,0:T(8,128)(2,1)}, bf16[384,256]{1,0:T(8,128)(2,1)}, u32[]{:S(2)}, u32[]{:S(2)}) collective-permute-start(bf16[384,256]{1,0:T(8,128)(2,1)} %fusion.7), channel_id=1, source_target_pairs={{0,8},{4,12},{8,0},{12,4},{1,9},{5,13},{9,1},{13,5},{2,10},{6,14},... | collective-permute-start | bytes 589832 | tf_op jit(solution)/shard_map/ppermute | solution.py:61
  316.2 11.4 %collective-permute-start.52 = (bf16[384,256]{1,0:T(8,128)(2,1)}, bf16[384,256]{1,0:T(8,128)(2,1)}, u32[]{:S(2)}, u32[]{:S(2)}) collective-permute-start(bf16[384,256]{1,0:T(8,128)(2,1)} %fusion.8), channel_id=1, source_target_pairs={{0,8},{4,12},{8,0},{12,4},{1,9},{5,13},{9,1},{13,5},{2,10},{6,14},... | collective-permute-start | bytes 589832 | tf_op jit(solution)/shard_map/ppermute | solution.py:61
  (39 other events, 295.8 us)
Sparse Core Ops, SparseCore 0:
  153.7 63.2 all-gather.2
